TPU v7x, 256 devices: a whole 4x4x8 slice. The times are simulated.
256 devices in a mesh: slide: 64 (over z, y, core), seq: 4 (over x).
Axes of the slice: x: 4, y: 4, z: 8, core: 2. Of those that a mesh axis runs over, the one named last changes fastest.
Arguments:
- embeddings: bfloat16 [64, 512, 1536], P('slide', 'seq'), may hold values from -30 to 30
- tile_counts: int32 [64], P('slide'), may hold values from 256 to 512, as said below
- masked_tiles: int32 [64, 128], P('slide'), may hold values from 0 to 511, as said below
- w_in: bfloat16 [1536, 768], replicated, may hold values from -0.15625 to 0.15625
- norm_gain: float32 [768], replicated, may hold values from 0.25 to 1.75
- w_qkv: bfloat16 [768, 2304], replicated, may hold values from -1 to 1
- w_out: bfloat16 [768, 768], replicated, may hold values from -0.21875 to 0.21875
Outputs:
- grad_weights: float32 [3072, 768], P(('slide', 'seq'))
- loss_sum: float32 [], replicated
Inputs may be any that keep to these rules, and one draw needn't show every extreme that they name: `tile_counts`: number of real tiles of each slide; positions at or past it are padding. `masked_tiles`: each slide's 128 positions are distinct and below that slide's tile count.
All inputs are finite; a program needn't handle non-finite values.
Results may differ from a plain program's by a relative error of at most 0.02.
Values may be sent and summed in bfloat16 or wider, within the bound.
No kernel may reach another device: no remote copies, remote signals or barrier semaphores. Data moves between devices by JAX's collectives and lax.ppermute only.
A program may use at most 128 MiB of HBM per device.

v0:
```python
import math

import jax
import jax.numpy as jnp
from jax import lax
from jax.sharding import PartitionSpec as P

HEADS = 16
RATE = 4


NORM_EPS = 1e-06
NEG_FILL = -1e30


def dilate(array):
    row_count = array.shape[0] // RATE
    head_size = array.shape[-1]
    grouped = array.reshape(row_count, RATE, HEADS // RATE, RATE, head_size)
    picked = jnp.diagonal(grouped, axis1=1, axis2=3)
    return jnp.transpose(picked, (0, 1, 3, 2)).reshape(row_count, HEADS, head_size)


def spread(far_grads):
    row_count = far_grads.shape[0]
    head_size = far_grads.shape[-1]
    grouped = far_grads.reshape(row_count, HEADS // RATE, RATE, head_size)
    identity = jnp.arange(RATE)[:, None] == jnp.arange(RATE)[None, :]
    placed = jnp.where(
        identity[None, :, None, :, None], grouped[:, None], jnp.zeros((), far_grads.dtype)
    )
    return placed.reshape(row_count * RATE, HEADS, head_size)


def key_mask(head_index, query_pos, key_pos, real_count, far_count):
    near_mask = (key_pos[None, :] < real_count) | (key_pos[None, :] == query_pos[:, None])
    offset = head_index % RATE
    far_pos = jnp.arange(far_count, dtype=jnp.int32) * RATE + offset
    far_mask = (query_pos % RATE == offset)[:, None] & (far_pos < real_count)[None, :]
    return jnp.concatenate([near_mask, far_mask], axis=1)


def softmax_rows(query_head, key_head, allowed):
    scores = jnp.dot(query_head, key_head.T, preferred_element_type=jnp.float32) / math.sqrt(
        query_head.shape[-1]
    )
    scores = jnp.where(allowed, scores, NEG_FILL)
    row_max = jnp.max(scores, axis=1, keepdims=True)
    numerators = jnp.where(allowed, jnp.exp(scores - row_max), 0.0)
    return numerators / jnp.sum(numerators, axis=1, keepdims=True)


def by_head(array):
    return jnp.transpose(array, (1, 0, 2))


def attend(queries, keys_all, values_all, query_pos, real_count):
    far_count = keys_all.shape[0] - queries.shape[0]

    def per_head(pieces):
        query_head, key_head, value_head, head_index = pieces
        weights_f = softmax_rows(
            query_head, key_head, key_mask(head_index, query_pos, query_pos, real_count, far_count)
        )
        return jnp.dot(
            weights_f.astype(jnp.bfloat16), value_head, preferred_element_type=jnp.float32
        )

    outputs = lax.map(
        per_head,
        (
            by_head(queries),
            by_head(keys_all),
            by_head(values_all),
            jnp.arange(HEADS, dtype=jnp.int32),
        ),
    )
    return by_head(outputs).reshape(queries.shape[0], -1).astype(jnp.bfloat16)


def attend_back(queries, keys_all, values_all, grad_attended, query_pos, real_count):
    far_count = keys_all.shape[0] - queries.shape[0]
    grad_heads = by_head(grad_attended.reshape(queries.shape))

    def per_head(pieces):
        query_head, key_head, value_head, grad_head, head_index = pieces
        weights_f = softmax_rows(
            query_head, key_head, key_mask(head_index, query_pos, query_pos, real_count, far_count)
        )
        grad_values = jnp.dot(
            weights_f.astype(jnp.bfloat16).T, grad_head, preferred_element_type=jnp.float32
        )
        grad_probs = jnp.dot(grad_head, value_head.T, preferred_element_type=jnp.float32)
        row_dots = jnp.sum(weights_f * grad_probs, axis=1, keepdims=True)
        grad_scores = (
            weights_f * (grad_probs - row_dots) / math.sqrt(query_head.shape[-1])
        ).astype(jnp.bfloat16)
        grad_query = jnp.dot(grad_scores, key_head, preferred_element_type=jnp.float32)
        grad_keys = jnp.dot(grad_scores.T, query_head, preferred_element_type=jnp.float32)
        return (grad_query, grad_keys, grad_values)

    grad_query, grad_keys, grad_values = lax.map(
        per_head,
        (
            by_head(queries),
            by_head(keys_all),
            by_head(values_all),
            grad_heads,
            jnp.arange(HEADS, dtype=jnp.int32),
        ),
    )
    return (by_head(grad_query), by_head(grad_keys), by_head(grad_values))


def project(inputs, w_in, norm_gain, w_qkv):
    hidden = jnp.dot(inputs, w_in, preferred_element_type=jnp.float32).astype(jnp.bfloat16)
    hidden_f = hidden.astype(jnp.float32)
    scale_rows = lax.rsqrt(jnp.mean(hidden_f * hidden_f, axis=-1, keepdims=True) + NORM_EPS)
    normed = (hidden_f * scale_rows * norm_gain).astype(jnp.bfloat16)
    projected = jnp.dot(normed, w_qkv, preferred_element_type=jnp.float32).astype(jnp.bfloat16)
    return (hidden, normed, projected)


def per_device(embeddings, tile_counts, masked_tiles, w_in, norm_gain, w_qkv, w_out):
    tiles = embeddings[0]
    real_count = tile_counts[0]
    masked = masked_tiles[0]
    tok_rows = tiles.shape[0]
    width = w_out.shape[0]
    head_size = width // HEADS
    positions = lax.axis_index("seq") * tok_rows + jnp.arange(tok_rows, dtype=jnp.int32)
    masked_flag = jnp.any(positions[:, None] == masked[None, :], axis=1)
    inputs = jnp.where(masked_flag[:, None], jnp.zeros((), jnp.bfloat16), tiles)
    hidden, normed, projected = project(inputs, w_in, norm_gain, w_qkv)
    queries = projected[:, :width].reshape(tok_rows, HEADS, head_size)
    keys_near = projected[:, width : 2 * width].reshape(tok_rows, HEADS, head_size)
    values_near = projected[:, 2 * width :].reshape(tok_rows, HEADS, head_size)
    far_keys, far_values = (
        lax.all_gather(dilate(keys_near), "seq", axis=0, tiled=True),
        lax.all_gather(dilate(values_near), "seq", axis=0, tiled=True),
    )
    keys_all = jnp.concatenate([keys_near, far_keys], 0)
    values_all = jnp.concatenate([values_near, far_values], 0)
    attended = attend(queries, keys_all, values_all, positions, real_count)
    mixed = (
        hidden.astype(jnp.float32) + jnp.dot(attended, w_out, preferred_element_type=jnp.float32)
    ).astype(jnp.bfloat16)
    predicted = jnp.dot(mixed, w_in.T, preferred_element_type=jnp.float32)
    error_rows = jnp.where(masked_flag[:, None], predicted - tiles.astype(jnp.float32), 0.0)
    inv_count = 1.0 / (lax.axis_size("slide") * masked.shape[0])
    loss_part = jnp.sum(error_rows * error_rows) * inv_count
    grad_pred = (2.0 * inv_count * error_rows).astype(jnp.bfloat16)
    grad_mixed = jnp.dot(grad_pred, w_in, preferred_element_type=jnp.float32).astype(jnp.bfloat16)
    grad_attended = jnp.dot(grad_mixed, w_out.T, preferred_element_type=jnp.float32).astype(
        jnp.bfloat16
    )
    grad_query, grad_keys_all, grad_values_all = attend_back(
        queries, keys_all, values_all, grad_attended, positions, real_count
    )
    far_key_grads, far_value_grads = (
        lax.psum_scatter(grad_keys_all[tok_rows:], "seq", scatter_dimension=0, tiled=True),
        lax.psum_scatter(grad_values_all[tok_rows:], "seq", scatter_dimension=0, tiled=True),
    )
    grad_keys = grad_keys_all[:tok_rows] + spread(far_key_grads)
    grad_values = grad_values_all[:tok_rows] + spread(far_value_grads)
    grad_projected = jnp.concatenate(
        [
            grad_query.reshape(tok_rows, width),
            grad_keys.reshape(tok_rows, width),
            grad_values.reshape(tok_rows, width),
        ],
        axis=1,
    ).astype(jnp.bfloat16)
    weight_terms = jnp.concatenate(
        [
            jnp.dot(grad_projected.T, normed, preferred_element_type=jnp.float32),
            jnp.dot(grad_mixed.T, attended, preferred_element_type=jnp.float32),
        ],
        axis=0,
    )
    gradients = lax.psum_scatter(weight_terms, ("slide", "seq"), scatter_dimension=0, tiled=True)
    loss_total = lax.psum(loss_part, ("slide", "seq"))
    return (gradients, loss_total)


def solution(mesh):
    in_specs = (P("slide", "seq", None), P("slide"), P("slide", None), P(), P(), P(), P())
    out_specs = (P(("slide", "seq"), None), P())
    return jax.shard_map(
        per_device, mesh=mesh, in_specs=in_specs, out_specs=out_specs, check_vma=False
    )
```

profile of v0, /device:TPU:2, one launch (start us, length us, event | category | flops | bytes accessed | tf_op | source)
XLA Modules:
  0.0 1860.9 jit_solution(9342787829598683582)
XLA Ops:
  25.9 14.3 all_gather.7
  51.9 13.5 all_gather.6
  76.1 109.5 %while.34 = (s32[]{:T(128)}, bf16[16,128,48]{1,2,0:T(8,128)(2,1)}, s32[]{:T(128)}, s32[16]{0:T(128)S(1)}, bf16[16,128,48]{2,1,0:T(8,128)(2,1)}, /*index=5*/bf16[...) while((s32[]{:T(128)}, bf16[16,128,48]{1,2,0:T(8,128)(2,1)}, ...), condition=%wide.region_5.6_spmd.clone.clone, body=%wide.region_2.5_spmd.clone.clone.sunk | while | flops 6768781 | bytes 719366 | solution.py:69
  197.4 182.8 %while.35 = (s32[]{:T(128)}, bf16[16,128,48]{1,2,0:T(8,128)(2,1)}, f32[16,256,48]{1,2,0:T(8,128)}, f32[16,256,48]{1,2,0:T(8,128)}, s32[]{:T(128)}, /*index=5*/s3...) while((s32[]{:T(128)}, bf16[16,128,48]{1,2,0:T(8,128)(2,1)}, ...), condition=%wide.region_10.11_spmd.clone.clone, body=%wide.region_6.10_spmd.clone.clone.sunk | while | flops 16926732 | bytes 1832990 | solution.py:102
  398.3 14.8 reduce-scatter.5.cloned.1.call-done
  413.1 28.6 %reduce-scatter.7.cloned.1.call-done = f32[32,16,48]{2,1,0:T(8,128)} async-done(((f32[128,16,48]{2,1,0:T(8,128)}), f32[32,16,48]{2,1,0:T(8,128)}) %reduce-scatter.7.cloned.1.call-update) | async-done | bytes 98320 | tf_op jit(solution)/shard_map/reduce_scatter | solution.py:162
  455.8 8.0 pad_maximum_fusion
  463.8 719.8 %fusion.8 = f32[16,768]{1,0:T(8,128)} fusion(f32[3072,768]{1,0:T(8,128)} %pad_maximum_fusion), kind=kCustom, calls=%all-reduce-scatter | all-reduce-scatter fusion | flops 3145729 | bytes 9486336
  1188.9 13.7 collective-permute-start.1
  1202.6 13.1 collective-permute-start.10
  1221.2 11.5 collective-permute-start.11
  1232.7 13.1 collective-permute-start.12
  1245.8 13.1 collective-permute-start.13
  1259.0 13.1 collective-permute-start.14
  1272.1 13.1 collective-permute-start.15
  1285.2 13.1 collective-permute-start.16
  1298.4 13.1 collective-permute-start.17
  1311.5 13.1 collective-permute-start.18
  1324.7 13.1 collective-permute-start.19
  1337.8 13.1 collective-permute-start.2
  1351.0 13.1 collective-permute-start.20
  1364.1 13.1 collective-permute-start.21
  1377.2 13.1 collective-permute-start.22
  1390.4 13.1 collective-permute-start.23
  1403.5 13.1 collective-permute-start.24
  1416.7 13.1 collective-permute-start.25
  1429.8 13.1 collective-permute-start.26
  1443.0 13.1 collective-permute-start.27
  1456.1 13.1 collective-permute-start.28
  1469.2 13.1 collective-permute-start.29
  1482.4 13.1 collective-permute-start.3
  1507.3 7.1 collective-permute-start.33
  1533.4 6.0 collective-permute-start.4
  1539.5 5.4 collective-permute-start.40
  1549.8 5.3 collective-permute-start.42
  1555.1 6.4 collective-permute-start.43
  1564.8 5.6 collective-permute-start.45
  1579.1 6.5 collective-permute-start.5
  1585.6 5.8 collective-permute-start.50
  1596.1 7.2 collective-permute-start.52
  1603.3 6.6 collective-permute-start.53
  1621.7 8.3 collective-permute-start.6
  1630.0 6.5 collective-permute-start.60
  1641.7 6.9 collective-permute-start.62
  1653.3 13.1 collective-permute-start.8
  1666.4 13.1 collective-permute-start.9
  1680.1 76.5 %psum.7 = f32[]{:T(128)} all-reduce(f32[]{:T(128)S(6)} %mul.79), channel_id=1, replica_groups=mesh['slide'=64,'seq'=4] {'slide','seq'}, use_global_device_ids=true, to_apply=%region_15.16 | all-reduce | flops 1 | bytes 8 | tf_op jit(solution)/shard_map/psum | solution.py:182
  1756.7 95.8 %concatenate.45 = f32[1036,768]{1,0:T(8,128)} concatenate(f32[12,768]{1,0:T(8,128)} %collective-permute-done.63, f32[16,768]{1,0:T(8,128)} %collective-permute-done.62, f32[16,768]{1,0:T(8,128)} %collective-permute-done.61, f32[16,768]{1,0:T(8,128)} %collective-permute-done.60, f32[16,768]{1,0:T(8,128)} %collective-permute-done.59, f32[16,768]{1,0:T(8,128)} %collective-permute-done.58, ...), dimensions={0} | concatenate | bytes 6365184
  (498 shorter events, 403.2 us)
Async XLA Ops:
  7.2 405.9 %reduce-scatter.5.cloned.1.call-start = ((), (), s32[]{:S(2)}) async-start(), calls=%async_computation.2 | async-start | bytes 1310720 | tf_op jit(solution)/shard_map/reduce_scatter | solution.py:161
  386.1 55.5 %reduce-scatter.7.cloned.1.call-start = ((), (), s32[]{:S(2)}) async-start(), calls=%async_computation.3 | async-start | bytes 1310720 | tf_op jit(solution)/shard_map/reduce_scatter | solution.py:162
  1183.6 62.2 %collective-permute-start = (f32[16,768]{1,0:T(8,128)}, f32[16,768]{1,0:T(8,128)}, u32[]{:S(2)}, u32[]{:S(2)}) collective-permute-start(f32[16,768]{1,0:T(8,128)} %fusion.8), channel_id=1, source_target_pairs={{0,1},{1,2},{2,3},{3,4},{4,5},{5,6},{6,7},{7,8},{8,9},{9,10},{10,1... | collective-permute-start | bytes 147464
  1188.9 70.1 %collective-permute-start.1 = (f32[16,768]{1,0:T(8,128)}, f32[16,768]{1,0:T(8,128)}, u32[]{:S(2)}, u32[]{:S(2)}) collective-permute-start(f32[16,768]{1,0:T(8,128)} %fusion.8), channel_id=1, source_target_pairs={{0,2},{1,3},{2,4},{3,5},{4,6},{5,7},{6,8},{7,9},{8,10},{9,11},{10,... | collective-permute-start | bytes 147464
  1202.6 69.5 %collective-permute-start.10 = (f32[16,768]{1,0:T(8,128)}, f32[16,768]{1,0:T(8,128)}, u32[]{:S(2)}, u32[]{:S(2)}) collective-permute-start(f32[16,768]{1,0:T(8,128)} %fusion.8), channel_id=1, source_target_pairs={{0,11},{1,12},{2,13},{3,14},{4,15},{5,16},{6,17},{7,18},{8,19},{9,... | collective-permute-start | bytes 147464
  1221.2 64.0 %collective-permute-start.11 = (f32[16,768]{1,0:T(8,128)}, f32[16,768]{1,0:T(8,128)}, u32[]{:S(2)}, u32[]{:S(2)}) collective-permute-start(f32[16,768]{1,0:T(8,128)} %fusion.8), channel_id=1, source_target_pairs={{0,12},{1,13},{2,14},{3,15},{4,16},{5,17},{6,18},{7,19},{8,20},{9,... | collective-permute-start | bytes 147464
  1232.7 65.7 %collective-permute-start.12 = (f32[16,768]{1,0:T(8,128)}, f32[16,768]{1,0:T(8,128)}, u32[]{:S(2)}, u32[]{:S(2)}) collective-permute-start(f32[16,768]{1,0:T(8,128)} %fusion.8), channel_id=1, source_target_pairs={{0,13},{1,14},{2,15},{3,16},{4,17},{5,18},{6,19},{7,20},{8,21},{9,... | collective-permute-start | bytes 147464
  1245.8 65.7 %collective-permute-start.13 = (f32[16,768]{1,0:T(8,128)}, f32[16,768]{1,0:T(8,128)}, u32[]{:S(2)}, u32[]{:S(2)}) collective-permute-start(f32[16,768]{1,0:T(8,128)} %fusion.8), channel_id=1, source_target_pairs={{0,14},{1,15},{2,16},{3,17},{4,18},{5,19},{6,20},{7,21},{8,22},{9,... | collective-permute-start | bytes 147464
  1259.0 65.7 %collective-permute-start.14 = (f32[16,768]{1,0:T(8,128)}, f32[16,768]{1,0:T(8,128)}, u32[]{:S(2)}, u32[]{:S(2)}) collective-permute-start(f32[16,768]{1,0:T(8,128)} %fusion.8), channel_id=1, source_target_pairs={{0,15},{1,16},{2,17},{3,18},{4,19},{5,20},{6,21},{7,22},{8,23},{9,... | collective-permute-start | bytes 147464
  1272.1 65.7 %collective-permute-start.15 = (f32[16,768]{1,0:T(8,128)}, f32[16,768]{1,0:T(8,128)}, u32[]{:S(2)}, u32[]{:S(2)}) collective-permute-start(f32[16,768]{1,0:T(8,128)} %fusion.8), channel_id=1, source_target_pairs={{0,16},{1,17},{2,18},{3,19},{4,20},{5,21},{6,22},{7,23},{8,24},{9,... | collective-permute-start | bytes 147464
  1285.2 65.7 %collective-permute-start.16 = (f32[16,768]{1,0:T(8,128)}, f32[16,768]{1,0:T(8,128)}, u32[]{:S(2)}, u32[]{:S(2)}) collective-permute-start(f32[16,768]{1,0:T(8,128)} %fusion.8), channel_id=1, source_target_pairs={{0,17},{1,18},{2,19},{3,20},{4,21},{5,22},{6,23},{7,24},{8,25},{9,... | collective-permute-start | bytes 147464
  1298.4 65.7 %collective-permute-start.17 = (f32[16,768]{1,0:T(8,128)}, f32[16,768]{1,0:T(8,128)}, u32[]{:S(2)}, u32[]{:S(2)}) collective-permute-start(f32[16,768]{1,0:T(8,128)} %fusion.8), channel_id=1, source_target_pairs={{0,18},{1,19},{2,20},{3,21},{4,22},{5,23},{6,24},{7,25},{8,26},{9,... | collective-permute-start | bytes 147464
  1311.5 65.7 %collective-permute-start.18 = (f32[16,768]{1,0:T(8,128)}, f32[16,768]{1,0:T(8,128)}, u32[]{:S(2)}, u32[]{:S(2)}) collective-permute-start(f32[16,768]{1,0:T(8,128)} %fusion.8), channel_id=1, source_target_pairs={{0,19},{1,20},{2,21},{3,22},{4,23},{5,24},{6,25},{7,26},{8,27},{9,... | collective-permute-start | bytes 147464
  1324.7 65.7 %collective-permute-start.19 = (f32[16,768]{1,0:T(8,128)}, f32[16,768]{1,0:T(8,128)}, u32[]{:S(2)}, u32[]{:S(2)}) collective-permute-start(f32[16,768]{1,0:T(8,128)} %fusion.8), channel_id=1, source_target_pairs={{0,20},{1,21},{2,22},{3,23},{4,24},{5,25},{6,26},{7,27},{8,28},{9,... | collective-permute-start | bytes 147464
  1337.8 65.7 %collective-permute-start.2 = (f32[16,768]{1,0:T(8,128)}, f32[16,768]{1,0:T(8,128)}, u32[]{:S(2)}, u32[]{:S(2)}) collective-permute-start(f32[16,768]{1,0:T(8,128)} %fusion.8), channel_id=1, source_target_pairs={{0,3},{1,4},{2,5},{3,6},{4,7},{5,8},{6,9},{7,10},{8,11},{9,12},{10... | collective-permute-start | bytes 147464
  1351.0 65.7 %collective-permute-start.20 = (f32[16,768]{1,0:T(8,128)}, f32[16,768]{1,0:T(8,128)}, u32[]{:S(2)}, u32[]{:S(2)}) collective-permute-start(f32[16,768]{1,0:T(8,128)} %fusion.8), channel_id=1, source_target_pairs={{0,21},{1,22},{2,23},{3,24},{4,25},{5,26},{6,27},{7,28},{8,29},{9,... | collective-permute-start | bytes 147464
  1364.1 65.7 %collective-permute-start.21 = (f32[16,768]{1,0:T(8,128)}, f32[16,768]{1,0:T(8,128)}, u32[]{:S(2)}, u32[]{:S(2)}) collective-permute-start(f32[16,768]{1,0:T(8,128)} %fusion.8), channel_id=1, source_target_pairs={{0,22},{1,23},{2,24},{3,25},{4,26},{5,27},{6,28},{7,29},{8,30},{9,... | collective-permute-start | bytes 147464
  1377.2 65.7 %collective-permute-start.22 = (f32[16,768]{1,0:T(8,128)}, f32[16,768]{1,0:T(8,128)}, u32[]{:S(2)}, u32[]{:S(2)}) collective-permute-start(f32[16,768]{1,0:T(8,128)} %fusion.8), channel_id=1, source_target_pairs={{0,23},{1,24},{2,25},{3,26},{4,27},{5,28},{6,29},{7,30},{8,31},{9,... | collective-permute-start | bytes 147464
  1390.4 65.7 %collective-permute-start.23 = (f32[16,768]{1,0:T(8,128)}, f32[16,768]{1,0:T(8,128)}, u32[]{:S(2)}, u32[]{:S(2)}) collective-permute-start(f32[16,768]{1,0:T(8,128)} %fusion.8), channel_id=1, source_target_pairs={{0,24},{1,25},{2,26},{3,27},{4,28},{5,29},{6,30},{7,31},{8,32},{9,... | collective-permute-start | bytes 147464
  1403.5 65.7 %collective-permute-start.24 = (f32[16,768]{1,0:T(8,128)}, f32[16,768]{1,0:T(8,128)}, u32[]{:S(2)}, u32[]{:S(2)}) collective-permute-start(f32[16,768]{1,0:T(8,128)} %fusion.8), channel_id=1, source_target_pairs={{0,25},{1,26},{2,27},{3,28},{4,29},{5,30},{6,31},{7,32},{8,33},{9,... | collective-permute-start | bytes 147464
  1416.7 65.7 %collective-permute-start.25 = (f32[16,768]{1,0:T(8,128)}, f32[16,768]{1,0:T(8,128)}, u32[]{:S(2)}, u32[]{:S(2)}) collective-permute-start(f32[16,768]{1,0:T(8,128)} %fusion.8), channel_id=1, source_target_pairs={{0,26},{1,27},{2,28},{3,29},{4,30},{5,31},{6,32},{7,33},{8,34},{9,... | collective-permute-start | bytes 147464
  1429.8 65.7 %collective-permute-start.26 = (f32[16,768]{1,0:T(8,128)}, f32[16,768]{1,0:T(8,128)}, u32[]{:S(2)}, u32[]{:S(2)}) collective-permute-start(f32[16,768]{1,0:T(8,128)} %fusion.8), channel_id=1, source_target_pairs={{0,27},{1,28},{2,29},{3,30},{4,31},{5,32},{6,33},{7,34},{8,35},{9,... | collective-permute-start | bytes 147464
  1443.0 56.1 %collective-permute-start.27 = (f32[16,768]{1,0:T(8,128)}, f32[16,768]{1,0:T(8,128)}, u32[]{:S(2)}, u32[]{:S(2)}) collective-permute-start(f32[16,768]{1,0:T(8,128)} %fusion.8), channel_id=1, source_target_pairs={{0,28},{1,29},{2,30},{3,31},{4,32},{5,33},{6,34},{7,35},{8,36},{9,... | collective-permute-start | bytes 147464
  1456.1 46.6 %collective-permute-start.28 = (f32[16,768]{1,0:T(8,128)}, f32[16,768]{1,0:T(8,128)}, u32[]{:S(2)}, u32[]{:S(2)}) collective-permute-start(f32[16,768]{1,0:T(8,128)} %fusion.8), channel_id=1, source_target_pairs={{0,29},{1,30},{2,31},{3,32},{4,33},{5,34},{6,35},{7,36},{8,37},{9,... | collective-permute-start | bytes 147464
  1469.2 38.0 %collective-permute-start.29 = (f32[16,768]{1,0:T(8,128)}, f32[16,768]{1,0:T(8,128)}, u32[]{:S(2)}, u32[]{:S(2)}) collective-permute-start(f32[16,768]{1,0:T(8,128)} %fusion.8), channel_id=1, source_target_pairs={{0,30},{1,31},{2,32},{3,33},{4,34},{5,35},{6,36},{7,37},{8,38},{9,... | collective-permute-start | bytes 147464
  1482.4 32.0 %collective-permute-start.3 = (f32[16,768]{1,0:T(8,128)}, f32[16,768]{1,0:T(8,128)}, u32[]{:S(2)}, u32[]{:S(2)}) collective-permute-start(f32[16,768]{1,0:T(8,128)} %fusion.8), channel_id=1, source_target_pairs={{0,4},{1,5},{2,6},{3,7},{4,8},{5,9},{6,10},{7,11},{8,12},{9,13},{1... | collective-permute-start | bytes 147464
  1499.0 21.7 %collective-permute-start.31 = (f32[16,768]{1,0:T(8,128)}, f32[16,768]{1,0:T(8,128)}, u32[]{:S(2)}, u32[]{:S(2)}) collective-permute-start(f32[16,768]{1,0:T(8,128)} %fusion.8), channel_id=1, source_target_pairs={{0,32},{1,33},{2,34},{3,35},{4,36},{5,37},{6,38},{7,39},{8,40},{9,... | collective-permute-start | bytes 147464
  1502.7 22.2 %collective-permute-start.32 = (f32[16,768]{1,0:T(8,128)}, f32[16,768]{1,0:T(8,128)}, u32[]{:S(2)}, u32[]{:S(2)}) collective-permute-start(f32[16,768]{1,0:T(8,128)} %fusion.8), channel_id=1, source_target_pairs={{0,33},{1,34},{2,35},{3,36},{4,37},{5,38},{6,39},{7,40},{8,41},{9,... | collective-permute-start | bytes 147464
  1528.0 21.8 %collective-permute-start.38 = (f32[16,768]{1,0:T(8,128)}, f32[16,768]{1,0:T(8,128)}, u32[]{:S(2)}, u32[]{:S(2)}) collective-permute-start(f32[16,768]{1,0:T(8,128)} %fusion.8), channel_id=1, source_target_pairs={{0,39},{1,40},{2,41},{3,42},{4,43},{5,44},{6,45},{7,46},{8,47},{9,... | collective-permute-start | bytes 147464
  1531.2 23.9 %collective-permute-start.39 = (f32[16,768]{1,0:T(8,128)}, f32[16,768]{1,0:T(8,128)}, u32[]{:S(2)}, u32[]{:S(2)}) collective-permute-start(f32[16,768]{1,0:T(8,128)} %fusion.8), channel_id=1, source_target_pairs={{0,40},{1,41},{2,42},{3,43},{4,44},{5,45},{6,46},{7,47},{8,48},{9,... | collective-permute-start | bytes 147464
  1533.4 28.1 %collective-permute-start.4 = (f32[16,768]{1,0:T(8,128)}, f32[16,768]{1,0:T(8,128)}, u32[]{:S(2)}, u32[]{:S(2)}) collective-permute-start(f32[16,768]{1,0:T(8,128)} %fusion.8), channel_id=1, source_target_pairs={{0,5},{1,6},{2,7},{3,8},{4,9},{5,10},{6,11},{7,12},{8,13},{9,14},{... | collective-permute-start | bytes 147464
  1539.5 25.3 %collective-permute-start.40 = (f32[16,768]{1,0:T(8,128)}, f32[16,768]{1,0:T(8,128)}, u32[]{:S(2)}, u32[]{:S(2)}) collective-permute-start(f32[16,768]{1,0:T(8,128)} %fusion.8), channel_id=1, source_target_pairs={{0,41},{1,42},{2,43},{3,44},{4,45},{5,46},{6,47},{7,48},{8,49},{9,... | collective-permute-start | bytes 147464
  1544.9 25.5 %collective-permute-start.41 = (f32[16,768]{1,0:T(8,128)}, f32[16,768]{1,0:T(8,128)}, u32[]{:S(2)}, u32[]{:S(2)}) collective-permute-start(f32[16,768]{1,0:T(8,128)} %fusion.8), channel_id=1, source_target_pairs={{0,42},{1,43},{2,44},{3,45},{4,46},{5,47},{6,48},{7,49},{8,50},{9,... | collective-permute-start | bytes 147464
  1549.8 22.4 %collective-permute-start.42 = (f32[16,768]{1,0:T(8,128)}, f32[16,768]{1,0:T(8,128)}, u32[]{:S(2)}, u32[]{:S(2)}) collective-permute-start(f32[16,768]{1,0:T(8,128)} %fusion.8), channel_id=1, source_target_pairs={{0,43},{1,44},{2,45},{3,46},{4,47},{5,48},{6,49},{7,50},{8,51},{9,... | collective-permute-start | bytes 147464
  1574.1 22.0 %collective-permute-start.48 = (f32[16,768]{1,0:T(8,128)}, f32[16,768]{1,0:T(8,128)}, u32[]{:S(2)}, u32[]{:S(2)}) collective-permute-start(f32[16,768]{1,0:T(8,128)} %fusion.8), channel_id=1, source_target_pairs={{0,49},{1,50},{2,51},{3,52},{4,53},{5,54},{6,55},{7,56},{8,57},{9,... | collective-permute-start | bytes 147464
  1576.1 27.2 %collective-permute-start.49 = (f32[16,768]{1,0:T(8,128)}, f32[16,768]{1,0:T(8,128)}, u32[]{:S(2)}, u32[]{:S(2)}) collective-permute-start(f32[16,768]{1,0:T(8,128)} %fusion.8), channel_id=1, source_target_pairs={{0,50},{1,51},{2,52},{3,53},{4,54},{5,55},{6,56},{7,57},{8,58},{9,... | collective-permute-start | bytes 147464
  1579.1 30.8 %collective-permute-start.5 = (f32[16,768]{1,0:T(8,128)}, f32[16,768]{1,0:T(8,128)}, u32[]{:S(2)}, u32[]{:S(2)}) collective-permute-start(f32[16,768]{1,0:T(8,128)} %fusion.8), channel_id=1, source_target_pairs={{0,6},{1,7},{2,8},{3,9},{4,10},{5,11},{6,12},{7,13},{8,14},{9,15},... | collective-permute-start | bytes 147464
  1585.6 26.5 %collective-permute-start.50 = (f32[16,768]{1,0:T(8,128)}, f32[16,768]{1,0:T(8,128)}, u32[]{:S(2)}, u32[]{:S(2)}) collective-permute-start(f32[16,768]{1,0:T(8,128)} %fusion.8), channel_id=1, source_target_pairs={{0,51},{1,52},{2,53},{3,54},{4,55},{5,56},{6,57},{7,58},{8,59},{9,... | collective-permute-start | bytes 147464
  1591.4 22.7 %collective-permute-start.51 = (f32[16,768]{1,0:T(8,128)}, f32[16,768]{1,0:T(8,128)}, u32[]{:S(2)}, u32[]{:S(2)}) collective-permute-start(f32[16,768]{1,0:T(8,128)} %fusion.8), channel_id=1, source_target_pairs={{0,52},{1,53},{2,54},{3,55},{4,56},{5,57},{6,58},{7,59},{8,60},{9,... | collective-permute-start | bytes 147464
  1617.9 23.8 %collective-permute-start.58 = (f32[16,768]{1,0:T(8,128)}, f32[16,768]{1,0:T(8,128)}, u32[]{:S(2)}, u32[]{:S(2)}) collective-permute-start(f32[16,768]{1,0:T(8,128)} %fusion.8), channel_id=1, source_target_pairs={{0,59},{1,60},{2,61},{3,62},{4,63},{5,64},{6,65},{7,66},{8,67},{9,... | collective-permute-start | bytes 147464
  1619.8 28.8 %collective-permute-start.59 = (f32[16,768]{1,0:T(8,128)}, f32[16,768]{1,0:T(8,128)}, u32[]{:S(2)}, u32[]{:S(2)}) collective-permute-start(f32[16,768]{1,0:T(8,128)} %fusion.8), channel_id=1, source_target_pairs={{0,60},{1,61},{2,62},{3,63},{4,64},{5,65},{6,66},{7,67},{8,68},{9,... | collective-permute-start | bytes 147464
  1621.7 31.6 %collective-permute-start.6 = (f32[16,768]{1,0:T(8,128)}, f32[16,768]{1,0:T(8,128)}, u32[]{:S(2)}, u32[]{:S(2)}) collective-permute-start(f32[16,768]{1,0:T(8,128)} %fusion.8), channel_id=1, source_target_pairs={{0,7},{1,8},{2,9},{3,10},{4,11},{5,12},{6,13},{7,14},{8,15},{9,16}... | collective-permute-start | bytes 147464
  1630.0 36.4 %collective-permute-start.60 = (f32[16,768]{1,0:T(8,128)}, f32[16,768]{1,0:T(8,128)}, u32[]{:S(2)}, u32[]{:S(2)}) collective-permute-start(f32[16,768]{1,0:T(8,128)} %fusion.8), channel_id=1, source_target_pairs={{0,61},{1,62},{2,63},{3,64},{4,65},{5,66},{6,67},{7,68},{8,69},{9,... | collective-permute-start | bytes 147464
  1636.6 120.1 %collective-permute-start.61 = (f32[16,768]{1,0:T(8,128)}, f32[16,768]{1,0:T(8,128)}, u32[]{:S(2)}, u32[]{:S(2)}) collective-permute-start(f32[16,768]{1,0:T(8,128)} %fusion.8), channel_id=1, source_target_pairs={{0,62},{1,63},{2,64},{3,65},{4,66},{5,67},{6,68},{7,69},{8,70},{9,... | collective-permute-start | bytes 147464
  1641.7 115.0 %collective-permute-start.62 = (f32[16,768]{1,0:T(8,128)}, f32[16,768]{1,0:T(8,128)}, u32[]{:S(2)}, u32[]{:S(2)}) collective-permute-start(f32[16,768]{1,0:T(8,128)} %fusion.8), channel_id=1, source_target_pairs={{0,63},{1,64},{2,65},{3,66},{4,67},{5,68},{6,69},{7,70},{8,71},{9,... | collective-permute-start | bytes 147464
  1648.6 108.1 %collective-permute-start.7 = (f32[16,768]{1,0:T(8,128)}, f32[16,768]{1,0:T(8,128)}, u32[]{:S(2)}, u32[]{:S(2)}) collective-permute-start(f32[16,768]{1,0:T(8,128)} %fusion.8), channel_id=1, source_target_pairs={{0,8},{1,9},{2,10},{3,11},{4,12},{5,13},{6,14},{7,15},{8,16},{9,17... | collective-permute-start | bytes 147464
  1653.3 103.4 %collective-permute-start.8 = (f32[16,768]{1,0:T(8,128)}, f32[16,768]{1,0:T(8,128)}, u32[]{:S(2)}, u32[]{:S(2)}) collective-permute-start(f32[16,768]{1,0:T(8,128)} %fusion.8), channel_id=1, source_target_pairs={{0,9},{1,10},{2,11},{3,12},{4,13},{5,14},{6,15},{7,16},{8,17},{9,1... | collective-permute-start | bytes 147464
  1666.4 90.3 %collective-permute-start.9 = (f32[16,768]{1,0:T(8,128)}, f32[16,768]{1,0:T(8,128)}, u32[]{:S(2)}, u32[]{:S(2)}) collective-permute-start(f32[16,768]{1,0:T(8,128)} %fusion.8), channel_id=1, source_target_pairs={{0,10},{1,11},{2,12},{3,13},{4,14},{5,15},{6,16},{7,17},{8,18},{9,... | collective-permute-start | bytes 147464
  (25 other events, 319.6 us)
Sparse Core Ops, SparseCore 0:
  386.3 26.7 reduce-scatter.4
  415.8 25.8 reduce-scatter.6
where the time goes:
time: 1880 us; the launch traced here: 1860 us
  blocking collectives  824 us (44%)
  starting transfers between devices  495 us (26%)
  matrix products  180 us (10%)
  local copies, waits for them, and re-layouts  175 us (9%)
  other arithmetic  68.5 us (4%)
  loops' own time  60.4 us (3%)
  waiting for transfers between devices  43.6 us (2%)
    unnamed x1, blocking collectives  720 us
    unnamed x64, starting transfers between devices  495 us
    unnamed x20, local copies, waits for them, and re-layouts  105 us
    psum x1, blocking collectives, per_device(): loss_total = lax.psum(loss_part, ('slide', 'seq'))  76.5 us
  transfers between devices with their start and end apart: 66, of which 2 were waited for; matrix products, arithmetic and copies ran while one was open for 1% of the time, Pallas kernels for 0%

commit v1 on v0

v1 whole, which is shorter than its diff:
```python
import math

import numpy as np
import jax
import jax.numpy as jnp
from jax import lax
from jax.experimental import pallas as pl
from jax.experimental.pallas import tpu as pltpu
from jax.sharding import PartitionSpec as P

HEADS = 16
RATE = 4
HD = 48
D = 768
TOK = 128
N_SEQ = 4
GROUPS = HEADS // RATE
FAR = TOK // RATE
NORM_EPS = 1e-06
NEG_FILL = -1e30
SCALE = 1.0 / math.sqrt(HD)
BF = jnp.bfloat16
F32 = jnp.float32
HALF = 384
SUB = 96
SECTIONS = 12
XROWS = SECTIONS * SUB + 16
NZ, NY, NC = 8, 4, 2


def dot(a, b, dims):
    return lax.dot_general(a, b, (dims, ((), ())), preferred_element_type=F32)


def nn(a, b):
    return dot(a, b, ((1,), (0,)))


def nt(a, b):
    return dot(a, b, ((1,), (1,)))


def tn(a, b):
    return dot(a, b, ((0,), (0,)))


def iota(shape, dim):
    return lax.broadcasted_iota(jnp.int32, shape, dim)


def class_major(index):
    return (index & (FAR - 1)) * RATE + (index >> 5)


def split_rows(value, shape, first):
    high = value.astype(BF).astype(F32)
    rest = value - high
    mid = rest.astype(BF).astype(F32)
    low = rest - mid
    row = iota(shape, 0)
    return jnp.where(
        row == first,
        high,
        jnp.where(row == first + 1, mid, jnp.where(row == first + 2, low, 0.0)),
    )


def masked_rows(pos0, masked):
    positions = pos0 + class_major(iota((TOK, TOK), 0))
    hits = jnp.where(positions == masked, 1.0, 0.0)
    return jnp.max(hits, axis=1, keepdims=True) > 0.5


def prep_kernel(s_ref, tiles_ref, masked_ref, w_in_ref, gain_ref, tiles_out, hidden_out, normed_out):
    pos0 = s_ref[0] * TOK
    shape = (TOK, TOK)
    order = (iota(shape, 1) == class_major(iota(shape, 0))).astype(F32).astype(BF)
    tiles = nn(order, tiles_ref[...]).astype(BF)
    tiles_out[...] = tiles
    flag = masked_rows(pos0, masked_ref[...])
    inputs = jnp.where(flag, 0.0, tiles.astype(F32)).astype(BF)
    hidden = nn(inputs, w_in_ref[...]).astype(BF)
    hidden_out[...] = hidden
    hidden_f = hidden.astype(F32)
    scale_rows = lax.rsqrt(jnp.mean(hidden_f * hidden_f, axis=1, keepdims=True) + NORM_EPS)
    normed_out[...] = (hidden_f * scale_rows * gain_ref[...]).astype(BF)


def window(group):
    return (group * RATE * HD) // 128 * 128


def head_masks(group):
    lane = iota((TOK, 256), 1) + window(group)
    row_class = iota((TOK, 256), 0) >> 5
    masks = []
    for r in range(RATE):
        first = (group * RATE + r) * HD
        masks.append((lane >= first) & (lane < first + HD))
    picked = masks[0] & (row_class == 0)
    for r in range(1, RATE):
        picked = picked | (masks[r] & (row_class == r))
    return masks, picked


def keep(mask, value):
    return jnp.where(mask, value, jnp.zeros((), value.dtype))


def by_class(own_class, pieces):
    out = pieces[0]
    for r in range(1, RATE):
        out = jnp.where(own_class == r, pieces[r], out)
    return out


def forward_kernel(
    s_ref, proj_ref, hidden_ref, tiles_ref, masked_ref, n0, n1, n2, n3, w_in_ref, w_qkv_ref, w_out_ref,
    pn_ref, fk_ref, fv_ref, pnear_ref, pfar_ref, att_ref, gm_ref, ga_ref, loss_ref,
    att_acc,
):
    seq = s_ref[0]
    count = s_ref[1]
    pos0 = seq * TOK
    for shift, ref in enumerate((n0, n1, n2, n3)):
        pn_ref[(seq - shift) & 3] = ref[...]
    pn_all = pn_ref[...].reshape(N_SEQ * TOK, D)
    for part, far_ref in enumerate((fk_ref, fv_ref)):
        for block in range(D // 256):
            first = (1 + part) * D + block * 256
            every = nn(pn_all, w_qkv_ref[:, first : first + 256])
            lane_head = iota((FAR, 256), 1) + block * 256
            lane_class = (lane_head // HD) & 3
            for src in range(N_SEQ):
                base = src * TOK
                pieces = [every[base + FAR * r : base + FAR * (r + 1)] for r in range(RATE)]
                far_ref[src * FAR : (src + 1) * FAR, block * 256 : (block + 1) * 256] = by_class(
                    lane_class, pieces
                ).astype(BF)

    square = (TOK, TOK)
    key_pos = pos0 + class_major(iota(square, 0))
    query_pos = pos0 + class_major(iota(square, 1))
    near_ok = (key_pos < count) | (key_pos == query_pos)
    far_row = iota(square, 0)
    far_ok = (far_row >> 5) * TOK + (far_row & (FAR - 1)) * RATE + (iota(square, 1) >> 5) < count
    own_class = iota((1, TOK), 1) >> 5

    att_acc[...] = jnp.zeros_like(att_acc)
    for g in range(GROUPS):
        lo = window(g)
        win = slice(lo, lo + 256)
        masks, picked = head_masks(g)
        q = proj_ref[:, lo : lo + 256]
        k = proj_ref[:, D + lo : D + lo + 256]
        v = proj_ref[:, 2 * D + lo : 2 * D + lo + 256]
        q_stack = jnp.concatenate([keep(m, q) for m in masks], 0)
        near = nt(k, q_stack)
        far = jnp.where(far_ok, nt(fk_ref[:, win], keep(picked, q)) * SCALE, NEG_FILL)
        far_max = jnp.max(far, axis=0, keepdims=True)
        scores = [
            jnp.where(near_ok, near[:, TOK * r : TOK * (r + 1)] * SCALE, NEG_FILL) for r in range(RATE)
        ]
        tops = []
        for r in range(RATE):
            top = jnp.max(scores[r], axis=0, keepdims=True)
            tops.append(jnp.where(own_class == r, jnp.maximum(top, far_max), top))
        exps = [jnp.exp(scores[r] - tops[r]) for r in range(RATE)]
        far_exp = jnp.exp(far - by_class(own_class, tops))
        far_sum = jnp.sum(far_exp, axis=0, keepdims=True)
        inverse = []
        for r in range(RATE):
            total = jnp.sum(exps[r], axis=0, keepdims=True)
            inverse.append(1.0 / jnp.where(own_class == r, total + far_sum, total))
        probs = [exps[r] * inverse[r] for r in range(RATE)]
        far_probs = far_exp * by_class(own_class, inverse)
        for r in range(RATE):
            pnear_ref[g, :, TOK * r : TOK * (r + 1)] = probs[r]
        pfar_ref[g] = far_probs
        att = tn(
            jnp.concatenate([p.astype(BF) for p in probs], 0),
            jnp.concatenate([keep(m, v) for m in masks], 0),
        )
        att_acc[:, win] += att + keep(picked, tn(far_probs.astype(BF), fv_ref[:, win]))

    attended = att_acc[...].astype(BF)
    att_ref[...] = attended
    mixed = (hidden_ref[...].astype(F32) + nn(attended, w_out_ref[...])).astype(BF)
    flag = masked_rows(pos0, masked_ref[...])
    error = jnp.where(flag, nt(mixed, w_in_ref[...]) - tiles_ref[...].astype(F32), 0.0)
    inv_count = s_ref[3].astype(F32)
    inv_count = 1.0 / inv_count
    loss = jnp.sum(jnp.sum(error * error, axis=1, keepdims=True), axis=0, keepdims=True) * inv_count
    loss_ref[...] = split_rows(jnp.broadcast_to(loss, (16, 128)), (16, 128), 0).astype(BF)
    grad_pred = (2.0 * inv_count * error).astype(BF)
    grad_mixed = nn(grad_pred, w_in_ref[...]).astype(BF)
    gm_ref[...] = grad_mixed
    ga_ref[...] = nt(grad_mixed, w_out_ref[...]).astype(BF)


def backward_kernel(
    proj_ref, fk_ref, fv_ref, pnear_ref, pfar_ref, gm_ref, ga_ref, loss_ref, spread_ref,
    x_ref,
    gq, gk, gv, gkf, gvf,
):
    own_class = iota((1, TOK), 1) >> 5
    for ref in (gq, gk, gv, gkf, gvf):
        ref[...] = jnp.zeros_like(ref)
    for g in range(GROUPS):
        lo = window(g)
        win = slice(lo, lo + 256)
        masks, picked = head_masks(g)
        q = proj_ref[:, lo : lo + 256]
        k = proj_ref[:, D + lo : D + lo + 256]
        v = proj_ref[:, 2 * D + lo : 2 * D + lo + 256]
        ga = ga_ref[:, win]
        fk = fk_ref[:, win]
        fv = fv_ref[:, win]
        ga_stack = jnp.concatenate([keep(m, ga) for m in masks], 0)
        ga_picked = keep(picked, ga)
        near = nt(v, ga_stack)
        far = nt(fv, ga_picked)
        probs = [pnear_ref[g, :, TOK * r : TOK * (r + 1)] for r in range(RATE)]
        far_probs = pfar_ref[g]
        far_dot = jnp.sum(far_probs * far, axis=0, keepdims=True)
        grads = [near[:, TOK * r : TOK * (r + 1)] for r in range(RATE)]
        dots = []
        for r in range(RATE):
            own = jnp.sum(probs[r] * grads[r], axis=0, keepdims=True)
            dots.append(jnp.where(own_class == r, own + far_dot, own))
        scores = [(probs[r] * (grads[r] - dots[r]) * SCALE).astype(BF) for r in range(RATE)]
        far_scores = (far_probs * (far - by_class(own_class, dots)) * SCALE).astype(BF)
        gq[:, win] += tn(
            jnp.concatenate(scores, 0), jnp.concatenate([keep(m, k) for m in masks], 0)
        ) + keep(picked, tn(far_scores, fk))
        gk[:, win] += nn(
            jnp.concatenate(scores, 1), jnp.concatenate([keep(m, q) for m in masks], 0)
        )
        gv[:, win] += nn(jnp.concatenate([p.astype(BF) for p in probs], 1), ga_stack)
        gkf[:, win] += nn(far_scores, keep(picked, q))
        gvf[:, win] += nn(far_probs.astype(BF), ga_picked)
    place = spread_ref[...]
    section = 0
    for ref in (gq, gk, gv, gkf, gvf, gm_ref):
        for half in range(2):
            turned = nt(place, ref[:, half * HALF : (half + 1) * HALF].astype(BF)).astype(BF)
            for j in range(N_SEQ):
                x_ref[j, section * SUB : (section + 1) * SUB] = turned[j * SUB : (j + 1) * SUB]
            section += 1
    for j in range(N_SEQ):
        x_ref[j, SECTIONS * SUB :] = loss_ref[...]


def product_kernel(s_ref, x_ref, pn_ref, a0, a1, a2, a3, order_ref, out_ref, left, att, res):
    seq = s_ref[0]
    core = s_ref[2]
    for shift, ref in enumerate((a0, a1, a2, a3)):
        att[pl.ds(((seq - shift) & 3) * TOK, TOK)] = ref[...]
    for src in range(N_SEQ):
        left[0 : 2 * SUB, src * TOK : (src + 1) * TOK] = x_ref[src, 0 : 2 * SUB]
        left[6 * SUB : 8 * SUB, src * TOK : (src + 1) * TOK] = x_ref[src, 10 * SUB : 12 * SUB]
    shape = (SUB, TOK)
    row = iota(shape, 0)
    lane_class = iota(shape, 1) >> 5
    core_row = jnp.where(row >= 48, 1, 0)
    row_y = (row - 48 * core_row) // 12
    row_class = ((row_y & 1) << 1) + core_row
    spots = [(row_class == r) & (lane_class == r) for r in range(RATE)]
    for part in range(2):
        for half in range(2):
            near_at = (2 + 2 * part + half) * SUB
            far_at = (6 + 2 * part + half) * SUB
            far = x_ref[0, far_at : far_at + SUB].astype(F32)
            for src in range(1, N_SEQ):
                far = far + x_ref[src, far_at : far_at + SUB].astype(F32)
            turns = [far] + [pltpu.roll(far, FAR * t, 1) for t in range(1, RATE)]
            for src in range(N_SEQ):
                total = x_ref[src, near_at : near_at + SUB].astype(F32)
                for r in range(RATE):
                    total = total + jnp.where(spots[r], turns[(r - src) & 3], 0.0)
                left[near_at : near_at + SUB, src * TOK : (src + 1) * TOK] = total.astype(BF)
    right = pn_ref[...].reshape(N_SEQ * TOK, D)
    res[0 : 6 * SUB] = nn(left[0 : 6 * SUB], right).astype(BF)
    res[6 * SUB :] = nn(left[6 * SUB :], att[...]).astype(BF)
    loss = x_ref[0, SECTIONS * SUB :].astype(F32)
    for src in range(1, N_SEQ):
        loss = loss + x_ref[src, SECTIONS * SUB :].astype(F32)
    loss = jnp.sum(jnp.sum(loss, axis=0, keepdims=True)[:, 0:1], axis=0, keepdims=True)
    tail = split_rows(jnp.broadcast_to(loss, (16, D)), (16, D), 0).astype(BF)
    whole = res[...]
    for c in range(NC):
        spot = (core + c) & 1
        out_ref[spot, 0:HALF] = nn(order_ref[c * HALF : (c + 1) * HALF], whole).astype(BF)
        out_ref[spot, HALF : HALF + 16] = tail


def core_kernel(mine_ref, other_ref, out_ref):
    for y in range(NY):
        rows = slice(y * SUB, (y + 1) * SUB)
        out_ref[y, 0:SUB] = (mine_ref[0, rows].astype(F32) + other_ref[rows].astype(F32)).astype(BF)
    tail = mine_ref[0, HALF:].astype(F32) + other_ref[HALF:].astype(F32)
    loss = jnp.sum(tail, axis=0, keepdims=True)
    rows = split_rows(jnp.broadcast_to(loss, (16, D)), (16, D), 0).astype(BF)
    for y in range(NY):
        out_ref[y, SUB:] = rows


def y_kernel(in_ref, order_ref, out_ref):
    total = in_ref[0].astype(F32)
    for src in range(1, NY):
        total = total + in_ref[src].astype(F32)
    loss = jnp.sum(total[SUB:], axis=0, keepdims=True)
    rows = split_rows(jnp.broadcast_to(loss, (16, D)), (16, D), 0)
    total = jnp.concatenate([total[:SUB], rows], 0).astype(BF)
    out_ref[...] = nn(order_ref[...], total).astype(BF).reshape(NZ, 16, D)


def z_kernel(in_ref, out_ref, loss_ref):
    total = in_ref[0].astype(F32)
    for src in range(1, NZ):
        total = total + in_ref[src].astype(F32)
    out_ref[...] = total[0:12]
    loss_ref[...] = jnp.sum(total[12:15, 0:1], axis=0, keepdims=True)


def spread_order():
    place = np.zeros((HALF, HALF), np.float32)
    for row in range(HALF):
        j, rest = divmod(row, SUB)
        c, rest = divmod(rest, 48)
        y, r = divmod(rest, 12)
        place[row, (y * NC + c) * HD + j * 12 + r] = 1.0
    return jnp.asarray(place, BF)


def product_order():
    place = np.zeros((D, D), np.float32)
    for row in range(D):
        c, rest = divmod(row, HALF)
        y, rest = divmod(rest, SUB)
        z, r = divmod(rest, 12)
        place[row, z * SUB + c * 48 + y * 12 + r] = 1.0
    return jnp.asarray(place, BF)


def pad_order():
    place = np.zeros((NZ * 16, SUB + 16), np.float32)
    for z in range(NZ):
        for r in range(12):
            place[z * 16 + r, z * 12 + r] = 1.0
        for r in range(3):
            place[z * 16 + 12 + r, SUB + r] = 1.0
    return jnp.asarray(place, BF)


SMEM = pl.BlockSpec(memory_space=pltpu.SMEM)
VMEM = pl.BlockSpec(memory_space=pltpu.VMEM)


def call(kernel, out_shapes, args, scratch=(), flops=1_000_000):
    specs = [SMEM if a.dtype == jnp.int32 and a.ndim == 1 else VMEM for a in args]
    single = not isinstance(out_shapes, (list, tuple))
    return pl.pallas_call(
        kernel,
        out_shape=out_shapes,
        in_specs=specs,
        out_specs=VMEM if single else [VMEM] * len(out_shapes),
        scratch_shapes=list(scratch),
        compiler_params=pltpu.CompilerParams(vmem_limit_bytes=48 * 1024 * 1024),
        cost_estimate=pl.CostEstimate(flops=flops, bytes_accessed=1_000_000, transcendentals=0),
    )(*args)


def shape(*dims, dtype=BF):
    return jax.ShapeDtypeStruct(dims, dtype)


def slide_at(z, y, c):
    return (z * NY + y) * NC + c


CORE_PAIRS = [(i, i ^ 1) for i in range(NZ * NY * NC)]
Y_GROUPS = [[slide_at(z, y, c) for y in range(NY)] for z in range(NZ) for c in range(NC)]
Z_GROUPS = [[slide_at(z, y, c) for z in range(NZ)] for y in range(NY) for c in range(NC)]


def gather_seq(array):
    return [array] + [
        lax.ppermute(array, "seq", [(k, (k + t) % N_SEQ) for k in range(N_SEQ)]) for t in range(1, N_SEQ)
    ]


def per_device(embeddings, tile_counts, masked_tiles, w_in, norm_gain, w_qkv, w_out):
    seq = lax.axis_index("seq")
    core = lax.axis_index("slide") % NC
    scale = lax.axis_size("slide") * masked_tiles.shape[1]
    scalars = jnp.stack(
        [seq.astype(jnp.int32), tile_counts[0], core.astype(jnp.int32), jnp.int32(scale)]
    )
    tiles, hidden, normed = call(
        prep_kernel,
        [shape(TOK, 2 * D), shape(TOK, D), shape(TOK, D)],
        (scalars, embeddings[0], masked_tiles, w_in, norm_gain.reshape(1, D)),
    )
    spread_norms = gather_seq(normed)
    projected = jnp.dot(normed, w_qkv, preferred_element_type=F32).astype(BF)
    pn, fk, fv, pnear, pfar, attended, grad_mixed, grad_attended, loss = call(
        forward_kernel,
        [
            shape(N_SEQ, TOK, D),
            shape(TOK, D),
            shape(TOK, D),
            shape(GROUPS, TOK, RATE * TOK, dtype=F32),
            shape(GROUPS, TOK, TOK, dtype=F32),
            shape(TOK, D),
            shape(TOK, D),
            shape(TOK, D),
            shape(16, 128),
        ],
        (scalars, projected, hidden, tiles, masked_tiles, *spread_norms, w_in, w_qkv, w_out),
        [pltpu.VMEM((TOK, D), F32)],
    )
    spread_att = gather_seq(attended)
    sent = call(
        backward_kernel,
        shape(N_SEQ, XROWS, TOK),
        (projected, fk, fv, pnear, pfar, grad_mixed, grad_attended, loss, spread_order()),
        [pltpu.VMEM((TOK, D), F32)] * 5,
    )
    got = lax.all_to_all(sent, "seq", 0, 0, tiled=True)
    halves = call(
        product_kernel,
        shape(NC, HALF + 16, D),
        (scalars, got, pn, *spread_att, product_order()),
        [pltpu.VMEM((D, N_SEQ * TOK), BF), pltpu.VMEM((N_SEQ * TOK, D), BF), pltpu.VMEM((D, D), BF)],
    )
    other = lax.ppermute(halves[1], "slide", CORE_PAIRS)
    by_y = call(core_kernel, shape(NY, SUB + 16, D), (halves, other))
    by_y = lax.all_to_all(by_y, "slide", 0, 0, tiled=True, axis_index_groups=Y_GROUPS)
    by_z = call(y_kernel, shape(NZ, 16, D), (by_y, pad_order()))
    by_z = lax.all_to_all(by_z, "slide", 0, 0, tiled=True, axis_index_groups=Z_GROUPS)
    gradients, loss_total = call(z_kernel, [shape(12, D, dtype=F32), shape(1, 1, dtype=F32)], (by_z,))
    return (gradients, loss_total[0, 0])


def solution(mesh):
    in_specs = (P("slide", "seq", None), P("slide"), P("slide", None), P(), P(), P(), P())
    out_specs = (P(("slide", "seq"), None), P())
    return jax.shard_map(
        per_device, mesh=mesh, in_specs=in_specs, out_specs=out_specs, check_vma=False
    )
```

time: 1880 us -> 106 us (0.06)
  blocking collectives: 824 us -> 33.8 us
  starting transfers between devices: 495 us -> 16 us
  matrix products: 180 us -> 2.65 us
  local copies, waits for them, and re-layouts: 175 us -> 7.93 us
  other arithmetic: 68.5 us -> 0.08 us
  loops' own time: 60.4 us -> 0 us
    unnamed x1 -> x0, blocking collectives: 720 us -> none
    unnamed x64 -> x0, starting transfers between devices: 495 us -> none
    dot_general x119 -> x1, matrix products: 180 us -> 2.65 us  [per_device(): projected = jnp.dot(normed, w_qkv, preferred_element_type=F32).astype(BF)]
    unnamed x20 -> x26, local copies, waits for them, and re-layouts: 105 us -> 7.19 us
    psum x1 -> x0, blocking collectives: 76.5 us -> none  [per_device(): loss_total = lax.psum(loss_part, ('slide', 'seq'))]
    another operation x2 -> x0, loops' own time: 60.4 us -> none  [the longest x1 32.1 us: attend_back(): lax.map(per_head, (by_head(queries), by_head(keys_all), by_head(values_al...]
    reduce_scatter x2 -> x0, waiting for transfers between devices: 43.4 us -> none  [the longest x1 28.6 us: per_device(): lax.psum_scatter(grad_values_all[tok_rows:], 'seq', scatter_dimension=0,...]
    all_to_all x0 -> x2, blocking collectives: none -> 33.8 us  [the longest x1 18 us: per_device(): lax.all_to_all(by_z, 'slide', 0, 0, tiled=True, axis_index_groups=Z_GROUPS)]
  transfers between devices with their start and end apart: 66 -> 8, of which waited for: 2 -> 5; matrix products, arithmetic and copies ran while one was open for 1% -> 3% of each run, Pallas kernels for 0% -> 0%
where the time goes in v1:
time: 106 us
  blocking collectives  33.8 us (32%)
  waiting for transfers between devices  26.7 us (25%)
  Pallas kernels  17 us (16%)
  starting transfers between devices  16 us (15%)
  local copies, waits for them, and re-layouts  7.93 us (7%)
  matrix products  2.65 us (2%)
  between operations  1.4 us (1%)
    ppermute x6, waiting for transfers between devices, gather_seq(): lax.ppermute(array, 'seq', [(k, (k + t) % N_SEQ) for k in range(N_SEQ)])  24.7 us
    all_to_all x1, blocking collectives, per_device(): lax.all_to_all(by_z, 'slide', 0, 0, tiled=True, axis_index_groups=Z_GROUPS)  18 us
    pallas_call x7, Pallas kernels, call(): pl.pallas_call(kernel, out_shape=out_shapes, in_specs=specs, out_specs=VM...  17 us
    all_to_all x1, blocking collectives, per_device(): lax.all_to_all(by_y, 'slide', 0, 0, tiled=True, axis_index_groups=Y_GROUPS)  15.8 us
    ppermute x6, starting transfers between devices, gather_seq(): lax.ppermute(array, 'seq', [(k, (k + t) % N_SEQ) for k in range(N_SEQ)])  9.54 us
    unnamed x26, local copies, waits for them, and re-layouts  7.19 us
    all_to_all x1, starting transfers between devices, per_device(): got = lax.all_to_all(sent, 'seq', 0, 0, tiled=True)  6.32 us
    dot_general x1, matrix products, per_device(): projected = jnp.dot(normed, w_qkv, preferred_element_type=F32).astype(BF)  2.65 us
  transfers between devices with their start and end apart: 8, of which 5 were waited for; matrix products, arithmetic and copies ran while one was open for 3% of the time, Pallas kernels for 0%

profile of v1, /device:TPU:2, one launch (start us, length us, event | category | flops | bytes accessed | tf_op | source)
XLA Modules:
  0.0 105.6 jit_solution(1176903399370168395)
XLA Ops:
  1.3 0.7 reshape.7.gain_ref
  2.0 0.1 pad_add_fusion.s_ref
  2.1 0.0 copy-start.9
  2.1 0.0 copy-start
  2.1 1.7 %copy-done = bf16[1536,768]{1,0:T(8,128)(2,1)S(1)} copy-done((bf16[1536,768]{1,0:T(8,128)(2,1)S(1)}, bf16[1536,768]{1,0:T(8,128)(2,1)}, u32[]{:S(2)}) %copy-start) | copy-done | bytes 2359320
  3.7 0.0 copy-start.2
  3.7 1.0 copy-done.2
  4.7 0.0 copy-start.11
  4.7 0.7 copy-done.11
  5.4 1.3 %shard_map.113 = (bf16[128,1536]{1,0:T(8,128)(2,1)S(1)}, bf16[128,768]{1,0:T(8,128)(2,1)S(1)}, bf16[128,768]{1,0:T(8,128)(2,1)S(1)}) custom-call(s32[4]{0:T(128)S(1)} %pad_add_fusion.s_ref, bf16[128,1536]{1,0:T(8,128)(2,1)S(1)} %bitcast.8, s32[1,128]{1,0:T(1,128)S(1)} %copy-done.11, bf16[1536,768]{1,0:T(8,128)(2,1)S(1)} %copy-done, f32[1,768]{1,0:T(1,128)S(1)} %reshape.7.gain_ref), custom_call_target="tpu_custom_call" | custom-call | flops 1000000 | bytes 1000000 | tf_op jit(solution)/shard_map/pallas_call | solution.py:363
  6.7 0.0 copy-start.12
  6.7 2.3 %collective-permute-start.2 = (bf16[128,768]{1,0:T(8,128)(2,1)S(1)}, bf16[128,768]{1,0:T(8,128)(2,1)S(1)}, u32[]{:S(2)}, u32[]{:S(2)}) collective-permute-start(bf16[128,768]{1,0:T(8,128)(2,1)S(1)} %get-tuple-element.16.n0), channel_id=1, source_target_pairs={{0,3},{1,0},{2,1},{3,2},{4,7},{5,4},{6,5},{7,6},{8,11},{9,8},{10,9... | collective-permute-start | bytes 589832 | tf_op jit(solution)/shard_map/ppermute | solution.py:389
  9.1 0.7 collective-permute-start.1
  9.8 1.8 %collective-permute-start = (bf16[128,768]{1,0:T(8,128)(2,1)S(1)}, bf16[128,768]{1,0:T(8,128)(2,1)S(1)}, u32[]{:S(2)}, u32[]{:S(2)}) collective-permute-start(bf16[128,768]{1,0:T(8,128)(2,1)S(1)} %get-tuple-element.16.n0), channel_id=1, source_target_pairs={{0,1},{1,2},{2,3},{3,0},{4,5},{5,6},{6,7},{7,4},{8,9},{9,10},{10,1... | collective-permute-start | bytes 589832 | tf_op jit(solution)/shard_map/ppermute | solution.py:389
  11.6 2.7 %convolution_convert_fusion.proj_ref = bf16[128,2304]{1,0:T(8,128)(2,1)S(1)} fusion(bf16[128,768]{1,0:T(8,128)(2,1)S(1)} %get-tuple-element.16.n0, bf16[768,2304]{1,0:T(8,128)(2,1)} %w_qkv_ref.1), kind=kOutput, calls=%fused_computation | convolution fusion | flops 453279744 | bytes 4325376 | tf_op jit(solution)/shard_map/dot_general | solution.py:406
  14.2 0.0 collective-permute-done.2.n3
  14.2 4.4 %collective-permute-done.1.n2 = bf16[128,768]{1,0:T(8,128)(2,1)S(1)} collective-permute-done((bf16[128,768]{1,0:T(8,128)(2,1)S(1)}, bf16[128,768]{1,0:T(8,128)(2,1)S(1)}, u32[]{:S(2)}, u32[]{:S(2)}) %collective-permute-start.1) | collective-permute-done | bytes 196640 | tf_op jit(solution)/shard_map/ppermute | solution.py:389
  18.6 0.9 collective-permute-done.n1
  19.5 0.0 copy-done.9
  19.5 0.0 copy-done.12
  19.5 0.0 copy-start.3
  19.5 7.9 %shard_map.114 = (bf16[4,128,768]{2,1,0:T(8,128)(2,1)S(1)}, bf16[128,768]{1,0:T(8,128)(2,1)S(1)}, bf16[128,768]{1,0:T(8,128)(2,1)S(1)}, f32[4,128,512]{2,1,0:T(8...) custom-call(s32[4]{0:T(128)S(1)} %pad_add_fusion.s_ref, ...), custom_call_target="tpu_custom_call" | custom-call | flops 1000000 | bytes 1000000 | tf_op jit(solution)/shard_map/pallas_call | solution.py:363
  27.4 0.0 copy-done.3
  27.5 4.2 %shard_map.115 = bf16[4,1168,128]{2,1,0:T(8,128)(2,1)} custom-call(bf16[128,2304]{1,0:T(8,128)(2,1)S(1)} %convolution_convert_fusion.proj_ref, bf16[128,768]{1,0:T(8,128)(2,1)S(1)} %get-tuple-element.19.fk_ref, bf16[128,768]{1,0:T(8,128)(2,1)S(1)} %get-tuple-element.20.fv_ref, f32[4,128,512]{2,1,0:T(8,128)S(1)} %get-tuple-element.21.pnear_ref, ...), custom_call_target="tpu_custom_call" | custom-call | flops 1000000 | bytes 1000000 | tf_op jit(solution)/shard_map/pallas_call | solution.py:363
  31.6 6.3 %all-to-all-start = ((bf16[4,1168,128]{2,1,0:T(8,128)(2,1)}), bf16[4,1168,128]{2,1,0:T(8,128)(2,1)S(1)}, u32[]{:S(2)}, u32[]{:S(2)}) async-start(bf16[4,1168,128]{2,1,0:T(8,128)(2,1)} %shard_map.115), calls=%async_computation | async-start | bytes 2392064 | tf_op jit(solution)/shard_map/all_to_all | solution.py:430
  37.9 0.1 collective-permute-start.5
  38.1 2.8 %collective-permute-start.4 = (bf16[128,768]{1,0:T(8,128)(2,1)S(1)}, bf16[128,768]{1,0:T(8,128)(2,1)S(1)}, u32[]{:S(2)}, u32[]{:S(2)}) collective-permute-start(bf16[128,768]{1,0:T(8,128)(2,1)S(1)} %get-tuple-element.27.a0), channel_id=1, source_target_pairs={{0,2},{1,3},{2,0},{3,1},{4,6},{5,7},{6,4},{7,5},{8,10},{9,11},{10,... | collective-permute-start | bytes 589832 | tf_op jit(solution)/shard_map/ppermute | solution.py:389
  40.9 1.8 %collective-permute-start.3 = (bf16[128,768]{1,0:T(8,128)(2,1)S(1)}, bf16[128,768]{1,0:T(8,128)(2,1)S(1)}, u32[]{:S(2)}, u32[]{:S(2)}) collective-permute-start(bf16[128,768]{1,0:T(8,128)(2,1)S(1)} %get-tuple-element.27.a0), channel_id=1, source_target_pairs={{0,1},{1,2},{2,3},{3,0},{4,5},{5,6},{6,7},{7,4},{8,9},{9,10},{10,1... | collective-permute-start | bytes 589832 | tf_op jit(solution)/shard_map/ppermute | solution.py:389
  42.6 14.9 %collective-permute-done.5.a3 = bf16[128,768]{1,0:T(8,128)(2,1)S(1)} collective-permute-done((bf16[128,768]{1,0:T(8,128)(2,1)S(1)}, bf16[128,768]{1,0:T(8,128)(2,1)S(1)}, u32[]{:S(2)}, u32[]{:S(2)}) %collective-permute-start.5) | collective-permute-done | bytes 196640 | tf_op jit(solution)/shard_map/ppermute | solution.py:389
  57.5 4.6 %collective-permute-done.4.a2 = bf16[128,768]{1,0:T(8,128)(2,1)S(1)} collective-permute-done((bf16[128,768]{1,0:T(8,128)(2,1)S(1)}, bf16[128,768]{1,0:T(8,128)(2,1)S(1)}, u32[]{:S(2)}, u32[]{:S(2)}) %collective-permute-start.4) | collective-permute-done | bytes 196640 | tf_op jit(solution)/shard_map/ppermute | solution.py:389
  62.1 0.7 copy-done.4
  62.8 0.0 collective-permute-done.3.a1
  62.8 0.7 copy-done.6
  63.4 0.0 all-to-all-done.x_ref
  63.4 0.0 copy-done.1
  63.5 0.9 copy-done.5
  64.4 0.9 copy-done.7
  65.3 0.7 copy-done.10
  66.0 2.5 %shard_map.116.mine_ref = bf16[2,400,768]{2,1,0:T(8,128)(2,1)S(1)} custom-call(s32[4]{0:T(128)S(1)} %copy-done.10, bf16[4,1168,128]{2,1,0:T(8,128)(2,1)S(1)} %all-to-all-done.x_ref, bf16[4,128,768]{2,1,0:T(8,128)(2,1)S(1)} %get-tuple-element.26.pn_ref, bf16[128,768]{1,0:T(8,128)(2,1)S(1)} %get-tuple-element.27.a0, bf16[128,768]{1,0:T(8,128)(2,1)S(1)} %copy-done.7, ...), custom_call_target="tpu_custom_call" | custom-call | flops 1000000 | bytes 1000000 | tf_op jit(solution)/shard_map/pallas_call | solution.py:363
  68.5 0.1 collective-permute-start.6
  68.6 2.0 %collective-permute-done.6.other_ref = bf16[400,768]{1,0:T(8,128)(2,1)S(1)} collective-permute-done((bf16[400,768]{1,0:T(8,128)(2,1)S(1)}, bf16[400,768]{1,0:T(8,128)(2,1)S(1)}, u32[]{:S(2)}, u32[]{:S(2)}) %collective-permute-start.6) | collective-permute-done | bytes 614432 | tf_op jit(solution)/shard_map/ppermute | solution.py:437
  70.6 0.2 shard_map.117
  70.8 0.0 copy-start.8
  70.8 15.8 %all_to_all.15.in_ref = bf16[4,112,768]{2,1,0:T(8,128)(2,1)S(1)} all-to-all(bf16[4,112,768]{2,1,0:T(8,128)(2,1)S(1)} %shard_map.117), channel_id=1, replica_groups={{0,8,16,24},{4,12,20,28},{32,40,48,56},{36,44,52,60},{64,72,80,88},{68,..., dimensions={0} | all-to-all | bytes 1376256 | tf_op jit(solution)/shard_map/all_to_all | solution.py:439
  86.6 0.0 copy-done.8
  86.6 0.3 shard_map.118
  86.9 18.0 %all_to_all.16.in_ref = bf16[8,16,768]{2,1,0:T(8,128)(2,1)S(1)} all-to-all(bf16[8,16,768]{2,1,0:T(8,128)(2,1)S(1)} %shard_map.118), channel_id=1, replica_groups={{0,32,64,96,128,160,192,224},{4,36,68,100,132,164,196,228},{8,40,72,104..., dimensions={0} | all-to-all | bytes 393216 | tf_op jit(solution)/shard_map/all_to_all | solution.py:441
  104.9 0.7 shard_map.119
  (7 shorter events, 0.1 us)
Async XLA Ops:
  2.1 17.4 %copy-start.9 = (s32[4]{0:T(128)}, s32[4]{0:T(128)S(1)}, u32[]{:S(2)}) copy-start(s32[4]{0:T(128)S(1)} %pad_add_fusion.s_ref) | copy-start | bytes 52
  2.1 1.7 %copy-start = (bf16[1536,768]{1,0:T(8,128)(2,1)S(1)}, bf16[1536,768]{1,0:T(8,128)(2,1)}, u32[]{:S(2)}) copy-start(bf16[1536,768]{1,0:T(8,128)(2,1)} %w_in_ref.3) | copy-start | bytes 7077892
  3.7 1.0 copy-start.2
  4.7 0.7 copy-start.11
  6.7 12.8 %copy-start.12 = (s32[1,128]{1,0:T(1,128)S(1)}, s32[1,128]{1,0:T(1,128)}, u32[]{:S(2)}) copy-start(s32[1,128]{1,0:T(1,128)} %masked_ref.3) | copy-start | bytes 1540
  6.7 7.5 %collective-permute-start.2 = (bf16[128,768]{1,0:T(8,128)(2,1)S(1)}, bf16[128,768]{1,0:T(8,128)(2,1)S(1)}, u32[]{:S(2)}, u32[]{:S(2)}) collective-permute-start(bf16[128,768]{1,0:T(8,128)(2,1)S(1)} %get-tuple-element.16.n0), channel_id=1, source_target_pairs={{0,3},{1,0},{2,1},{3,2},{4,7},{5,4},{6,5},{7,6},{8,11},{9,8},{10,9... | collective-permute-start | bytes 589832 | tf_op jit(solution)/shard_map/ppermute | solution.py:389
  9.1 9.5 %collective-permute-start.1 = (bf16[128,768]{1,0:T(8,128)(2,1)S(1)}, bf16[128,768]{1,0:T(8,128)(2,1)S(1)}, u32[]{:S(2)}, u32[]{:S(2)}) collective-permute-start(bf16[128,768]{1,0:T(8,128)(2,1)S(1)} %get-tuple-element.16.n0), channel_id=1, source_target_pairs={{0,2},{1,3},{2,0},{3,1},{4,6},{5,7},{6,4},{7,5},{8,10},{9,11},{10,... | collective-permute-start | bytes 589832 | tf_op jit(solution)/shard_map/ppermute | solution.py:389
  9.8 9.7 %collective-permute-start = (bf16[128,768]{1,0:T(8,128)(2,1)S(1)}, bf16[128,768]{1,0:T(8,128)(2,1)S(1)}, u32[]{:S(2)}, u32[]{:S(2)}) collective-permute-start(bf16[128,768]{1,0:T(8,128)(2,1)S(1)} %get-tuple-element.16.n0), channel_id=1, source_target_pairs={{0,1},{1,2},{2,3},{3,0},{4,5},{5,6},{6,7},{7,4},{8,9},{9,10},{10,1... | collective-permute-start | bytes 589832 | tf_op jit(solution)/shard_map/ppermute | solution.py:389
  19.5 8.0 %copy-start.3 = (bf16[384,384]{1,0:T(8,128)(2,1)S(1)}, bf16[384,384]{1,0:T(8,128)(2,1)}, u32[]{:S(2)}) copy-start(bf16[384,384]{1,0:T(8,128)(2,1)} %constant.30.clone.spread_ref) | copy-start | bytes 884740
  31.6 31.8 %copy-start.1 = (bf16[768,768]{1,0:T(8,128)(2,1)S(1)}, bf16[768,768]{1,0:T(8,128)(2,1)}, u32[]{:S(2)}) copy-start(bf16[768,768]{1,0:T(8,128)(2,1)} %constant.31.clone.order_ref) | copy-start | bytes 3538948
  31.6 31.8 %all-to-all-start = ((bf16[4,1168,128]{2,1,0:T(8,128)(2,1)}), bf16[4,1168,128]{2,1,0:T(8,128)(2,1)S(1)}, u32[]{:S(2)}, u32[]{:S(2)}) async-start(bf16[4,1168,128]{2,1,0:T(8,128)(2,1)} %shard_map.115), calls=%async_computation | async-start | bytes 2392064 | tf_op jit(solution)/shard_map/all_to_all | solution.py:430
  37.9 19.6 %collective-permute-start.5 = (bf16[128,768]{1,0:T(8,128)(2,1)S(1)}, bf16[128,768]{1,0:T(8,128)(2,1)S(1)}, u32[]{:S(2)}, u32[]{:S(2)}) collective-permute-start(bf16[128,768]{1,0:T(8,128)(2,1)S(1)} %get-tuple-element.27.a0), channel_id=1, source_target_pairs={{0,3},{1,0},{2,1},{3,2},{4,7},{5,4},{6,5},{7,6},{8,11},{9,8},{10,9... | collective-permute-start | bytes 589832 | tf_op jit(solution)/shard_map/ppermute | solution.py:389
  38.1 24.0 %collective-permute-start.4 = (bf16[128,768]{1,0:T(8,128)(2,1)S(1)}, bf16[128,768]{1,0:T(8,128)(2,1)S(1)}, u32[]{:S(2)}, u32[]{:S(2)}) collective-permute-start(bf16[128,768]{1,0:T(8,128)(2,1)S(1)} %get-tuple-element.27.a0), channel_id=1, source_target_pairs={{0,2},{1,3},{2,0},{3,1},{4,6},{5,7},{6,4},{7,5},{8,10},{9,11},{10,... | collective-permute-start | bytes 589832 | tf_op jit(solution)/shard_map/ppermute | solution.py:389
  40.9 21.9 %collective-permute-start.3 = (bf16[128,768]{1,0:T(8,128)(2,1)S(1)}, bf16[128,768]{1,0:T(8,128)(2,1)S(1)}, u32[]{:S(2)}, u32[]{:S(2)}) collective-permute-start(bf16[128,768]{1,0:T(8,128)(2,1)S(1)} %get-tuple-element.27.a0), channel_id=1, source_target_pairs={{0,1},{1,2},{2,3},{3,0},{4,5},{5,6},{6,7},{7,4},{8,9},{9,10},{10,1... | collective-permute-start | bytes 589832 | tf_op jit(solution)/shard_map/ppermute | solution.py:389
  62.1 0.7 copy-start.4
  62.8 0.7 copy-start.6
  63.4 0.9 copy-start.5
  64.4 0.9 copy-start.7
  65.3 0.7 copy-start.10
  68.5 2.1 %collective-permute-start.6 = (bf16[400,768]{1,0:T(8,128)(2,1)S(1)}, bf16[400,768]{1,0:T(8,128)(2,1)S(1)}, u32[]{:S(2)}, u32[]{:S(2)}) collective-permute-start(bf16[400,768]{1,0:T(8,128)(2,1)S(1)} %slice_bitcast_fusion), channel_id=1, source_target_pairs={{0,4},{4,0},{8,12},{12,8},{16,20},{20,16},{24,28},{28,24},{32,36},... | collective-permute-start | bytes 1843208 | tf_op jit(solution)/shard_map/ppermute | solution.py:437
  70.8 15.8 %copy-start.8 = (bf16[128,112]{1,0:T(8,128)(2,1)S(1)}, bf16[128,112]{1,0:T(8,128)(2,1)}, u32[]{:S(2)}) copy-start(bf16[128,112]{1,0:T(8,128)(2,1)} %constant.32.clone.order_ref) | copy-start | bytes 86020

commit v2 on v1

v2 whole, which is shorter than its diff:
```python
import functools
import math

import numpy as np
import jax
import jax.numpy as jnp
from jax import lax
from jax.experimental import pallas as pl
from jax.experimental.pallas import tpu as pltpu
from jax.sharding import PartitionSpec as P

HEADS = 16
RATE = 4
HD = 48
D = 768
TOK = 128
N_SEQ = 4
GROUPS = HEADS // RATE
FAR = TOK // RATE
NORM_EPS = 1e-06
NEG_FILL = -1e30
SCALE = 1.0 / math.sqrt(HD)
BF = jnp.bfloat16
F32 = jnp.float32
HALF = 384
SUB = 96
SECTIONS = 12
XROWS = SECTIONS * SUB + 16
NZ, NY, NC = 8, 4, 2


def dot(a, b, dims):
    return lax.dot_general(a, b, (dims, ((), ())), preferred_element_type=F32)


def nn(a, b):
    return dot(a, b, ((1,), (0,)))


def nt(a, b):
    return dot(a, b, ((1,), (1,)))


def tn(a, b):
    return dot(a, b, ((0,), (0,)))


def iota(shape, dim):
    return lax.broadcasted_iota(jnp.int32, shape, dim)


def class_major(index):
    return (index & (FAR - 1)) * RATE + (index >> 5)


def split_rows(value, shape, first):
    high = value.astype(BF).astype(F32)
    rest = value - high
    mid = rest.astype(BF).astype(F32)
    low = rest - mid
    row = iota(shape, 0)
    return jnp.where(
        row == first,
        high,
        jnp.where(row == first + 1, mid, jnp.where(row == first + 2, low, 0.0)),
    )


def prep_kernel(
    tiles_hbm, masked_hbm, gain_hbm, w_in_hbm, tiles_out, hidden_out, normed_out, flag_out,
    raw, masked, gain, w_in, sems,
):
    blocks = w_in_hbm.shape[0] // 256
    loads = [
        pltpu.make_async_copy(tiles_hbm.at[0], raw, sems.at[0]),
        pltpu.make_async_copy(masked_hbm, masked, sems.at[1]),
        pltpu.make_async_copy(gain_hbm, gain, sems.at[2]),
    ]
    chunks = [
        pltpu.make_async_copy(
            w_in_hbm.at[256 * i : 256 * (i + 1)], w_in.at[256 * i : 256 * (i + 1)], sems.at[3 + i]
        )
        for i in range(blocks)
    ]
    for copy in loads + chunks:
        copy.start()
    pos0 = lax.axis_index("seq") * TOK
    shape = (TOK, TOK)
    order = (iota(shape, 1) == class_major(iota(shape, 0))).astype(F32).astype(BF)
    loads[1].wait()
    positions = pos0 + class_major(iota(shape, 0))
    hits = jnp.where(positions == masked[...], 1.0, 0.0)
    hit = jnp.max(hits, axis=1, keepdims=True)
    flag_out[...] = jnp.broadcast_to(hit, shape)
    flag = hit > 0.5
    loads[0].wait()
    hidden = jnp.zeros((TOK, D), F32)
    for i in range(blocks):
        cols = slice(256 * i, 256 * (i + 1))
        tiles = nn(order, raw[:, cols])
        tiles_out[:, cols] = tiles.astype(BF)
        chunks[i].wait()
        hidden += nn(jnp.where(flag, 0.0, tiles).astype(BF), w_in[cols])
    hidden = hidden.astype(BF)
    hidden_out[...] = hidden
    hidden_f = hidden.astype(F32)
    scale_rows = lax.rsqrt(jnp.mean(hidden_f * hidden_f, axis=1, keepdims=True) + NORM_EPS)
    loads[2].wait()
    normed_out[...] = (hidden_f * scale_rows * gain[...].reshape(1, D)).astype(BF)


def window(group):
    return (group * RATE * HD) // 128 * 128


def head_masks(group):
    lane = iota((TOK, 256), 1) + window(group)
    row_class = iota((TOK, 256), 0) >> 5
    masks = []
    for r in range(RATE):
        first = (group * RATE + r) * HD
        masks.append((lane >= first) & (lane < first + HD))
    picked = masks[0] & (row_class == 0)
    for r in range(1, RATE):
        picked = picked | (masks[r] & (row_class == r))
    return masks, picked


def keep(mask, value):
    return jnp.where(mask, value, jnp.zeros((), value.dtype))


def by_class(own_class, pieces):
    out = pieces[0]
    for r in range(1, RATE):
        out = jnp.where(own_class == r, pieces[r], out)
    return out


def near_kernel(count_ref, normed_ref, w_qkv_ref, proj_ref, exp_ref, top_ref, sum_ref):
    count = count_ref[0]
    pos0 = lax.axis_index("seq") * TOK
    normed = normed_ref[...]
    for block in range(3 * D // 256):
        cols = slice(block * 256, (block + 1) * 256)
        proj_ref[:, cols] = nn(normed, w_qkv_ref[:, cols]).astype(BF)
    square = (TOK, TOK)
    key_pos = pos0 + class_major(iota(square, 0))
    query_pos = pos0 + class_major(iota(square, 1))
    near_ok = (key_pos < count) | (key_pos == query_pos)
    for g in range(GROUPS):
        lo = window(g)
        masks, _ = head_masks(g)
        q = proj_ref[:, lo : lo + 256]
        k = proj_ref[:, D + lo : D + lo + 256]
        near = nt(k, jnp.concatenate([keep(m, q) for m in masks], 0))
        for r in range(RATE):
            head = g * RATE + r
            scores = jnp.where(near_ok, near[:, TOK * r : TOK * (r + 1)] * SCALE, NEG_FILL)
            top = jnp.max(scores, axis=0, keepdims=True)
            exps = jnp.exp(scores - top)
            exp_ref[g, :, TOK * r : TOK * (r + 1)] = exps
            top_ref[head : head + 1] = top
            sum_ref[head : head + 1] = jnp.sum(exps, axis=0, keepdims=True)


def far_kernel(
    count_ref, n0, n1, n2, n3, proj_ref, exp_ref, top_ref, sum_ref, w_qkv_ref,
    pn_ref, fk_ref, fv_ref, pnear_ref, pfar_ref, att_ref,
    att_acc,
):
    count = count_ref[0]
    seq = lax.axis_index("seq")
    for turn, ref in enumerate((n0, n1, n2, n3)):
        pn_ref[(seq - turn) & 3] = ref[...]
    pn_all = pn_ref[...].reshape(N_SEQ * TOK, D)
    for part, far_ref in enumerate((fk_ref, fv_ref)):
        for block in range(D // 256):
            first = (1 + part) * D + block * 256
            every = nn(pn_all, w_qkv_ref[:, first : first + 256])
            lane_class = ((iota((FAR, 256), 1) + block * 256) // HD) & 3
            for src in range(N_SEQ):
                base = src * TOK
                pieces = [every[base + FAR * r : base + FAR * (r + 1)] for r in range(RATE)]
                far_ref[src * FAR : (src + 1) * FAR, block * 256 : (block + 1) * 256] = by_class(
                    lane_class, pieces
                ).astype(BF)

    square = (TOK, TOK)
    far_row = iota(square, 0)
    far_ok = (far_row >> 5) * TOK + (far_row & (FAR - 1)) * RATE + (iota(square, 1) >> 5) < count
    own_class = iota((1, TOK), 1) >> 5

    att_acc[...] = jnp.zeros_like(att_acc)
    for g in range(GROUPS):
        lo = window(g)
        win = slice(lo, lo + 256)
        masks, picked = head_masks(g)
        q = proj_ref[:, lo : lo + 256]
        v = proj_ref[:, 2 * D + lo : 2 * D + lo + 256]
        far = jnp.where(far_ok, nt(fk_ref[:, win], keep(picked, q)) * SCALE, NEG_FILL)
        heads = range(g * RATE, (g + 1) * RATE)
        near_tops = [top_ref[h : h + 1] for h in heads]
        near_sums = [sum_ref[h : h + 1] for h in heads]
        top = jnp.maximum(jnp.max(far, axis=0, keepdims=True), by_class(own_class, near_tops))
        shrink = jnp.exp(by_class(own_class, near_tops) - top)
        far_exp = jnp.exp(far - top)
        total = by_class(own_class, near_sums) * shrink + jnp.sum(far_exp, axis=0, keepdims=True)
        far_probs = far_exp / total
        probs = []
        for r in range(RATE):
            factor = jnp.where(own_class == r, shrink / total, 1.0 / near_sums[r])
            probs.append(exp_ref[g, :, TOK * r : TOK * (r + 1)] * factor)
            pnear_ref[g, :, TOK * r : TOK * (r + 1)] = probs[r]
        pfar_ref[g] = far_probs
        att = tn(
            jnp.concatenate([p.astype(BF) for p in probs], 0),
            jnp.concatenate([keep(m, v) for m in masks], 0),
        )
        att_acc[:, win] += att + keep(picked, tn(far_probs.astype(BF), fv_ref[:, win]))
    att_ref[...] = att_acc[...].astype(BF)


def backward_kernel(
    inv_count,
    proj_ref, fk_ref, fv_ref, pnear_ref, pfar_ref, att_ref, hidden_ref, tiles_ref, flag_ref, spread_ref,
    w_in_ref, w_out_ref,
    x0, x1, x2, x3,
    gq, gk, gv, gkf, gvf, ga_ref, turned,
):
    seq = lax.axis_index("seq")
    mixed = (hidden_ref[...].astype(F32) + nn(att_ref[...], w_out_ref[...])).astype(BF)
    flag = flag_ref[:, 0:1] > 0.5
    error = jnp.where(flag, nt(mixed, w_in_ref[...]) - tiles_ref[...].astype(F32), 0.0)
    loss = jnp.sum(jnp.sum(error * error, axis=1, keepdims=True), axis=0, keepdims=True) * inv_count
    tail = split_rows(jnp.broadcast_to(loss, (16, 128)), (16, 128), 0).astype(BF)
    grad_pred = (2.0 * inv_count * error).astype(BF)
    grad_mixed = nn(grad_pred, w_in_ref[...]).astype(BF)
    ga_ref[...] = nt(grad_mixed, w_out_ref[...]).astype(BF)

    own_class = iota((1, TOK), 1) >> 5
    for ref in (gq, gk, gv, gkf, gvf):
        ref[...] = jnp.zeros_like(ref)
    for g in range(GROUPS):
        lo = window(g)
        win = slice(lo, lo + 256)
        masks, picked = head_masks(g)
        q = proj_ref[:, lo : lo + 256]
        k = proj_ref[:, D + lo : D + lo + 256]
        v = proj_ref[:, 2 * D + lo : 2 * D + lo + 256]
        ga = ga_ref[:, win]
        fk = fk_ref[:, win]
        fv = fv_ref[:, win]
        ga_stack = jnp.concatenate([keep(m, ga) for m in masks], 0)
        ga_picked = keep(picked, ga)
        near = nt(v, ga_stack)
        far = nt(fv, ga_picked)
        probs = [pnear_ref[g, :, TOK * r : TOK * (r + 1)] for r in range(RATE)]
        far_probs = pfar_ref[g]
        far_dot = jnp.sum(far_probs * far, axis=0, keepdims=True)
        grads = [near[:, TOK * r : TOK * (r + 1)] for r in range(RATE)]
        dots = []
        for r in range(RATE):
            own = jnp.sum(probs[r] * grads[r], axis=0, keepdims=True)
            dots.append(jnp.where(own_class == r, own + far_dot, own))
        scores = [(probs[r] * (grads[r] - dots[r]) * SCALE).astype(BF) for r in range(RATE)]
        far_scores = (far_probs * (far - by_class(own_class, dots)) * SCALE).astype(BF)
        gq[:, win] += tn(
            jnp.concatenate(scores, 0), jnp.concatenate([keep(m, k) for m in masks], 0)
        ) + keep(picked, tn(far_scores, fk))
        gk[:, win] += nn(
            jnp.concatenate(scores, 1), jnp.concatenate([keep(m, q) for m in masks], 0)
        )
        gv[:, win] += nn(jnp.concatenate([p.astype(BF) for p in probs], 1), ga_stack)
        gkf[:, win] += nn(far_scores, keep(picked, q))
        gvf[:, win] += nn(far_probs.astype(BF), ga_picked)
    place = spread_ref[...]
    section = 0
    for value in (gq, gk, gv, gkf, gvf, grad_mixed):
        for half in range(2):
            piece = value[:, half * HALF : (half + 1) * HALF].astype(BF)
            turned[section] = nt(place, piece).astype(BF)
            section += 1
    for turn, ref in enumerate((x0, x1, x2, x3)):
        first = pl.multiple_of(((seq + turn) & 3) * SUB, 16)
        for section in range(SECTIONS):
            ref[section * SUB : (section + 1) * SUB] = turned[section, pl.ds(first, SUB)]
        ref[SECTIONS * SUB :] = tail


def product_kernel(
    x0, x1, x2, x3, pn_ref, a0, a1, a2, a3, order_ref, mine_ref, other_ref, got, left, att, res
):
    seq = lax.axis_index("seq")
    core = lax.axis_index("slide") & 1
    for turn, (ref, x_ref) in enumerate(zip((a0, a1, a2, a3), (x0, x1, x2, x3))):
        src = (seq - turn) & 3
        att[pl.ds(pl.multiple_of(src * TOK, TOK), TOK)] = ref[...]
        got[src] = x_ref[...]
    for src in range(N_SEQ):
        left[0 : 2 * SUB, src * TOK : (src + 1) * TOK] = got[src, 0 : 2 * SUB]
        left[6 * SUB : 8 * SUB, src * TOK : (src + 1) * TOK] = got[src, 10 * SUB : 12 * SUB]
    shape = (SUB, TOK)
    row = iota(shape, 0)
    lane_class = iota(shape, 1) >> 5
    core_row = jnp.where(row >= 48, 1, 0)
    row_y = (row - 48 * core_row) // 12
    row_class = ((row_y & 1) << 1) + core_row
    spots = [(row_class == r) & (lane_class == r) for r in range(RATE)]
    for part in range(2):
        for half in range(2):
            near_at = (2 + 2 * part + half) * SUB
            far_at = (6 + 2 * part + half) * SUB
            far = got[0, far_at : far_at + SUB].astype(F32)
            for src in range(1, N_SEQ):
                far = far + got[src, far_at : far_at + SUB].astype(F32)
            turns = [far] + [pltpu.roll(far, FAR * t, 1) for t in range(1, RATE)]
            for src in range(N_SEQ):
                total = got[src, near_at : near_at + SUB].astype(F32)
                for r in range(RATE):
                    total = total + jnp.where(spots[r], turns[(r - src) & 3], 0.0)
                left[near_at : near_at + SUB, src * TOK : (src + 1) * TOK] = total.astype(BF)
    right = pn_ref[...].reshape(N_SEQ * TOK, D)
    res[0 : 6 * SUB] = nn(left[0 : 6 * SUB], right).astype(BF)
    res[6 * SUB :] = nn(left[6 * SUB :], att[...]).astype(BF)
    loss = got[0, SECTIONS * SUB :].astype(F32)
    for src in range(1, N_SEQ):
        loss = loss + got[src, SECTIONS * SUB :].astype(F32)
    loss = jnp.sum(loss, axis=0, keepdims=True)[:, 0:1]
    tail = split_rows(jnp.broadcast_to(loss, (16, D)), (16, D), 0).astype(BF)
    whole = res[...]
    for turn, ref in enumerate((mine_ref, other_ref)):
        first = pl.multiple_of(((core + turn) & 1) * HALF, HALF)
        ref[0:HALF] = nn(order_ref[pl.ds(first, HALF)], whole).astype(BF)
        ref[HALF:] = tail


def core_kernel(mine_ref, other_ref, y0, y1, y2, y3):
    y = (lax.axis_index("slide") >> 1) & 3
    loss = jnp.sum(mine_ref[HALF:].astype(F32) + other_ref[HALF:].astype(F32), axis=0, keepdims=True)
    tail = split_rows(jnp.broadcast_to(loss, (16, D)), (16, D), 0).astype(BF)
    for turn, ref in enumerate((y0, y1, y2, y3)):
        rows = pl.ds(pl.multiple_of(((y + turn) & 3) * SUB, 16), SUB)
        ref[0:SUB] = (mine_ref[rows].astype(F32) + other_ref[rows].astype(F32)).astype(BF)
        ref[SUB:] = tail


def y_kernel(y0, y1, y2, y3, order_ref, out_ref):
    total = y0[...].astype(F32) + y1[...].astype(F32) + y2[...].astype(F32) + y3[...].astype(F32)
    loss = jnp.sum(total[SUB:], axis=0, keepdims=True)
    rows = split_rows(jnp.broadcast_to(loss, (16, D)), (16, D), 0)
    total = jnp.concatenate([total[:SUB], rows], 0).astype(BF)
    out_ref[...] = nn(order_ref[...], total).astype(BF).reshape(NZ, 16, D)


def z_kernel(in_ref, out_ref, loss_ref):
    total = in_ref[0].astype(F32)
    for src in range(1, NZ):
        total = total + in_ref[src].astype(F32)
    out_ref[...] = total[0:12]
    loss_ref[...] = jnp.sum(total[12:15, 0:1], axis=0, keepdims=True)


def spread_order():
    place = np.zeros((HALF, HALF), np.float32)
    for row in range(HALF):
        j, rest = divmod(row, SUB)
        c, rest = divmod(rest, 48)
        y, r = divmod(rest, 12)
        place[row, (y * NC + c) * HD + j * 12 + r] = 1.0
    return jnp.asarray(place, BF)


def product_order():
    place = np.zeros((D, D), np.float32)
    for row in range(D):
        c, rest = divmod(row, HALF)
        y, rest = divmod(rest, SUB)
        z, r = divmod(rest, 12)
        place[row, z * SUB + c * 48 + y * 12 + r] = 1.0
    return jnp.asarray(place, BF)


def pad_order():
    place = np.zeros((NZ * 16, SUB + 16), np.float32)
    for z in range(NZ):
        for r in range(12):
            place[z * 16 + r, z * 12 + r] = 1.0
        for r in range(3):
            place[z * 16 + 12 + r, SUB + r] = 1.0
    return jnp.asarray(place, BF)


SMEM = pl.BlockSpec(memory_space=pltpu.SMEM)
VMEM = pl.BlockSpec(memory_space=pltpu.VMEM)
HBM = pl.BlockSpec(memory_space=pltpu.HBM)


def call(kernel, out_shapes, args, scratch=(), micros=1.0, specs=None):
    if specs is None:
        specs = [SMEM if a.dtype == jnp.int32 else VMEM for a in args]
    return pl.pallas_call(
        kernel,
        out_shape=out_shapes,
        in_specs=specs,
        out_specs=[VMEM] * len(out_shapes),
        scratch_shapes=list(scratch),
        compiler_params=pltpu.CompilerParams(vmem_limit_bytes=24 * 1024 * 1024),
        cost_estimate=pl.CostEstimate(
            flops=int(micros * 1.0e9), bytes_accessed=int(micros * 1.0e6), transcendentals=0
        ),
    )(*args)


def shape(*dims, dtype=BF):
    return jax.ShapeDtypeStruct(dims, dtype)


def slide_at(z, y, c):
    return (z * NY + y) * NC + c


CORE_PAIRS = [(i, i ^ 1) for i in range(NZ * NY * NC)]
Z_GROUPS = [[slide_at(z, y, c) for z in range(NZ)] for y in range(NY) for c in range(NC)]
SEQ_TURNS = [[(k, (k + t) % N_SEQ) for k in range(N_SEQ)] for t in range(N_SEQ)]
Y_TURNS = [
    [
        (slide_at(z, y, c), slide_at(z, (y + t) % NY, c))
        for z in range(NZ)
        for y in range(NY)
        for c in range(NC)
    ]
    for t in range(NY)
]


def swap(arrays, axis, turns):
    return [arrays[0]] + [lax.ppermute(arrays[t], axis, turns[t]) for t in range(1, len(arrays))]


def per_device(embeddings, tile_counts, masked_tiles, w_in, norm_gain, w_qkv, w_out):
    inv_count = 1.0 / (lax.axis_size("slide") * masked_tiles.shape[1])
    tiles, hidden, normed, flag = call(
        prep_kernel,
        [shape(TOK, 2 * D), shape(TOK, D), shape(TOK, D), shape(TOK, TOK, dtype=F32)],
        (embeddings, masked_tiles, norm_gain, w_in),
        [
            pltpu.VMEM((TOK, 2 * D), BF),
            pltpu.VMEM((1, TOK), jnp.int32),
            pltpu.VMEM((D,), F32),
            pltpu.VMEM((2 * D, D), BF),
            pltpu.SemaphoreType.DMA((3 + 2 * D // 256,)),
        ],
        2.0,
        [HBM] * 4,
    )
    norms = swap([normed] * N_SEQ, "seq", SEQ_TURNS)
    scores = shape(GROUPS, TOK, RATE * TOK, dtype=F32)
    rows = shape(HEADS, TOK, dtype=F32)
    projected, exps, tops, sums = call(
        near_kernel, [shape(TOK, 3 * D), scores, rows, rows], (tile_counts, normed, w_qkv), (), 5.0
    )
    pn, fk, fv, pnear, pfar, attended = call(
        far_kernel,
        [
            shape(N_SEQ, TOK, D),
            shape(TOK, D),
            shape(TOK, D),
            scores,
            shape(GROUPS, TOK, TOK, dtype=F32),
            shape(TOK, D),
        ],
        (tile_counts, *norms, projected, exps, tops, sums, w_qkv),
        [pltpu.VMEM((TOK, D), F32)],
        4.0,
    )
    atts = swap([attended] * N_SEQ, "seq", SEQ_TURNS)
    sent = call(
        functools.partial(backward_kernel, inv_count),
        [shape(XROWS, TOK)] * N_SEQ,
        (projected, fk, fv, pnear, pfar, attended, hidden, tiles, flag, spread_order(), w_in, w_out),
        [pltpu.VMEM((TOK, D), F32)] * 5
        + [pltpu.VMEM((TOK, D), BF), pltpu.VMEM((SECTIONS, HALF, TOK), BF)],
        8.0,
    )
    got = swap(sent, "seq", SEQ_TURNS)
    mine, other = call(
        product_kernel,
        [shape(HALF + 16, D)] * 2,
        (*got, pn, *atts, product_order()),
        [
            pltpu.VMEM((N_SEQ, XROWS, TOK), BF),
            pltpu.VMEM((D, N_SEQ * TOK), BF),
            pltpu.VMEM((N_SEQ * TOK, D), BF),
            pltpu.VMEM((D, D), BF),
        ],
        3.0,
    )
    other = lax.ppermute(other, "slide", CORE_PAIRS)
    by_y = call(core_kernel, [shape(SUB + 16, D)] * NY, (mine, other))
    by_y = swap(by_y, "slide", Y_TURNS)
    (by_z,) = call(y_kernel, [shape(NZ, 16, D)], (*by_y, pad_order()))
    by_z = lax.all_to_all(by_z, "slide", 0, 0, tiled=True, axis_index_groups=Z_GROUPS)
    gradients, loss = call(z_kernel, [shape(12, D, dtype=F32), shape(1, 1, dtype=F32)], (by_z,))
    return (gradients, loss[0, 0])


def solution(mesh):
    in_specs = (P("slide", "seq", None), P("slide"), P("slide", None), P(), P(), P(), P())
    out_specs = (P(("slide", "seq"), None), P())
    return jax.shard_map(
        per_device, mesh=mesh, in_specs=in_specs, out_specs=out_specs, check_vma=False
    )
```

time: 106 us -> 91.8 us (0.87)
  blocking collectives: 33.8 us -> 18.2 us
  waiting for transfers between devices: 26.7 us -> 32.2 us
  starting transfers between devices: 16 us -> 20.1 us
  local copies, waits for them, and re-layouts: 7.93 us -> 4.17 us
  matrix products: 2.65 us -> 0 us
  Pallas kernels: 17 us -> 14.9 us
    all_to_all x1 -> x0, blocking collectives: 15.8 us -> none  [per_device(): lax.all_to_all(by_y, 'slide', 0, 0, tiled=True, axis_index_groups=Y_GROUPS)]
    ppermute x7 -> x13, starting transfers between devices: 9.63 us -> 20.1 us  [the longest x12 20 us: swap(): lax.ppermute(arrays[t], axis, turns[t])]
    all_to_all x1 -> x0, starting transfers between devices: 6.32 us -> none  [per_device(): got = lax.all_to_all(sent, 'seq', 0, 0, tiled=True)]
    ppermute x7 -> x13, waiting for transfers between devices: 26.7 us -> 32.2 us  [the longest x12 30.2 us: swap(): lax.ppermute(arrays[t], axis, turns[t])]
    unnamed x26 -> x20, local copies, waits for them, and re-layouts: 7.19 us -> 4.17 us
    dot_general x1 -> x0, matrix products: 2.65 us -> none  [per_device(): projected = jnp.dot(normed, w_qkv, preferred_element_type=F32).astype(BF)]
    pallas_call x7 -> x8, Pallas kernels: 17 us -> 14.9 us  [call(): pl.pallas_call(kernel, out_shape=out_shapes, in_specs=specs, out_specs=[V...]
  transfers between devices with their start and end apart: 8 -> 13, of which waited for: 5 -> 8; matrix products, arithmetic and copies ran while one was open for 3% -> 0% of each run, Pallas kernels for 0% -> 6%
where the time goes in v2:
time: 91.8 us; the launch traced here: 91 us
  waiting for transfers between devices  32.2 us (35%)
  starting transfers between devices  20.1 us (22%)
  blocking collectives  18.2 us (20%)
  Pallas kernels  14.9 us (16%)
  local copies, waits for them, and re-layouts  4.17 us (5%)
  between operations  1.4 us (2%)
    ppermute x12, waiting for transfers between devices, swap(): lax.ppermute(arrays[t], axis, turns[t])  30.2 us
    ppermute x12, starting transfers between devices, swap(): lax.ppermute(arrays[t], axis, turns[t])  20 us
    all_to_all x1, blocking collectives, per_device(): lax.all_to_all(by_z, 'slide', 0, 0, tiled=True, axis_index_groups=Z_GROUPS)  18.2 us
    pallas_call x8, Pallas kernels, call(): pl.pallas_call(kernel, out_shape=out_shapes, in_specs=specs, out_specs=[V...  14.9 us
    unnamed x20, local copies, waits for them, and re-layouts  4.17 us
    ppermute x1, waiting for transfers between devices, per_device(): other = lax.ppermute(other, 'slide', CORE_PAIRS)  2.03 us
  transfers between devices with their start and end apart: 13, of which 8 were waited for; matrix products, arithmetic and copies ran while one was open for 0% of the time, Pallas kernels for 6%

profile of v2, /device:TPU:2, one launch (start us, length us, event | category | flops | bytes accessed | tf_op | source)
XLA Modules:
  0.0 91.0 jit_solution(591988975621875178)
XLA Ops:
  0.6 0.0 copy-start
  0.6 0.0 copy-start.1
  0.7 1.8 %copy-done.1 = bf16[1536,768]{1,0:T(8,128)(2,1)S(1)} copy-done((bf16[1536,768]{1,0:T(8,128)(2,1)S(1)}, bf16[1536,768]{1,0:T(8,128)(2,1)}, u32[]{:S(2)}) %copy-start.1) | copy-done | bytes 2359320
  2.5 1.0 %copy-done.4 = bf16[1,128,1536]{2,1,0:T(8,128)(2,1)S(1)} copy-done((bf16[1,128,1536]{2,1,0:T(8,128)(2,1)S(1)}, bf16[1,128,1536]{2,1,0:T(8,128)(2,1)}, u32[]{:S(2)}) %copy-start.4) | copy-done | bytes 393240
  3.5 0.7 copy-done.5
  4.1 0.7 copy-done.6
  4.8 3.2 %shard_map.113 = (bf16[128,1536]{1,0:T(8,128)(2,1)S(1)}, bf16[128,768]{1,0:T(8,128)(2,1)S(1)}, bf16[128,768]{1,0:T(8,128)(2,1)S(1)}, f32[128,128]{1,0:T(8,128)S(1)}) custom-call(bf16[1,128,1536]{2,1,0:T(8,128)(2,1)S(1)} %copy-done.4, s32[1,128]{1,0:T(1,128)S(1)} %copy-done.6, f32[768]{0:T(1024)S(1)} %copy-done.5, bf16[1536,768]{1,0:T(8,128)(2,1)S(1)} %copy-done.1), custom_call_target="tpu_custom_call" | custom-call | flops 2000000000 | bytes 2000000 | tf_op jit(solution)/shard_map/pallas_call | solution.py:402
  8.0 2.3 %collective-permute-start.2 = (bf16[128,768]{1,0:T(8,128)(2,1)S(1)}, bf16[128,768]{1,0:T(8,128)(2,1)S(1)}, u32[]{:S(2)}, u32[]{:S(2)}) collective-permute-start(bf16[128,768]{1,0:T(8,128)(2,1)S(1)} %get-tuple-element.28.normed_ref.n0), channel_id=1, source_target_pairs={{0,3},{1,0},{2,1},{3,2},{4,7},{5,4},{6,5},{7,6},{8,11},{9,8},{10,9... | collective-permute-start | bytes 589832 | tf_op jit(solution)/shard_map/ppermute | solution.py:438
  10.3 0.7 collective-permute-start.1
  11.0 1.8 %collective-permute-start = (bf16[128,768]{1,0:T(8,128)(2,1)S(1)}, bf16[128,768]{1,0:T(8,128)(2,1)S(1)}, u32[]{:S(2)}, u32[]{:S(2)}) collective-permute-start(bf16[128,768]{1,0:T(8,128)(2,1)S(1)} %get-tuple-element.28.normed_ref.n0), channel_id=1, source_target_pairs={{0,1},{1,2},{2,3},{3,0},{4,5},{5,6},{6,7},{7,4},{8,9},{9,10},{10,1... | collective-permute-start | bytes 589832 | tf_op jit(solution)/shard_map/ppermute | solution.py:438
  13.5 0.0 copy-done
  13.5 1.0 %shard_map.114 = (bf16[128,2304]{1,0:T(8,128)(2,1)S(1)}, f32[4,128,512]{2,1,0:T(8,128)S(1)}, f32[16,128]{1,0:T(8,128)S(1)}, f32[16,128]{1,0:T(8,128)S(1)}) custom-call(s32[1]{0:T(128)S(6)} %copy.12.count_ref, bf16[128,768]{1,0:T(8,128)(2,1)S(1)} %get-tuple-element.28.normed_ref.n0, bf16[768,2304]{1,0:T(8,128)(2,1)S(1)} %copy-done), custom_call_target="tpu_custom_call" | custom-call | flops 5000000000 | bytes 5000000 | tf_op jit(solution)/shard_map/pallas_call | solution.py:402
  14.5 0.4 collective-permute-done.2.n3
  14.9 4.9 %collective-permute-done.1.n2 = bf16[128,768]{1,0:T(8,128)(2,1)S(1)} collective-permute-done((bf16[128,768]{1,0:T(8,128)(2,1)S(1)}, bf16[128,768]{1,0:T(8,128)(2,1)S(1)}, u32[]{:S(2)}, u32[]{:S(2)}) %collective-permute-start.1) | collective-permute-done | bytes 196640 | tf_op jit(solution)/shard_map/ppermute | solution.py:438
  19.8 0.9 collective-permute-done.n1
  20.7 2.7 %shard_map.115 = (bf16[4,128,768]{2,1,0:T(8,128)(2,1)S(1)}, bf16[128,768]{1,0:T(8,128)(2,1)S(1)}, bf16[128,768]{1,0:T(8,128)(2,1)S(1)}, f32[4,128,512]{2,1,0:T(8...) custom-call(s32[1]{0:T(128)S(6)} %copy.12.count_ref, ...), custom_call_target="tpu_custom_call" | custom-call | flops 4000000000 | bytes 4000000 | tf_op jit(solution)/shard_map/pallas_call | solution.py:402
  23.5 2.8 %collective-permute-start.8 = (bf16[128,768]{1,0:T(8,128)(2,1)S(1)}, bf16[128,768]{1,0:T(8,128)(2,1)S(1)}, u32[]{:S(2)}, u32[]{:S(2)}) collective-permute-start(bf16[128,768]{1,0:T(8,128)(2,1)S(1)} %get-tuple-element.37.att_ref.a0), channel_id=1, source_target_pairs={{0,3},{1,0},{2,1},{3,2},{4,7},{5,4},{6,5},{7,6},{8,11},{9,8},{10,9... | collective-permute-start | bytes 589832 | tf_op jit(solution)/shard_map/ppermute | solution.py:438
  26.3 0.0 copy-done.2
  26.3 0.0 copy-done.3
  26.3 0.0 copy-done.8
  26.3 4.7 %shard_map.116 = (bf16[1168,128]{1,0:T(8,128)(2,1)S(1)}, bf16[1168,128]{1,0:T(8,128)(2,1)S(1)}, bf16[1168,128]{1,0:T(8,128)(2,1)S(1)}, bf16[1168,128]{1,0:T(8,128)(2,1)S(1)}) custom-call(bf16[128,2304]{1,0:T(8,128)(2,1)S(1)} %get-tuple-element.29.proj_ref, bf16[128,768]{1,0:T(8,128)(2,1)S(1)} %get-tuple-element.33.fk_ref, ...), custom_call_target="tpu_custom_call" | custom-call | flops 8000000000 | bytes 8000000 | tf_op jit(solution)/shard_map/pallas_call | solution.py:402
  30.9 0.1 collective-permute-start.3
  31.0 2.6 %collective-permute-start.4 = (bf16[1168,128]{1,0:T(8,128)(2,1)S(1)}, bf16[1168,128]{1,0:T(8,128)(2,1)S(1)}, u32[]{:S(2)}, u32[]{:S(2)}) collective-permute-start(bf16[1168,128]{1,0:T(8,128)(2,1)S(1)} %get-tuple-element.43), channel_id=1, source_target_pairs={{0,2},{1,3},{2,0},{3,1},{4,6},{5,7},{6,4},{7,5},{8,10},{9,11},{10,... | collective-permute-start | bytes 897032 | tf_op jit(solution)/shard_map/ppermute | solution.py:438
  33.7 0.3 collective-permute-start.5
  33.9 2.0 %collective-permute-start.7 = (bf16[128,768]{1,0:T(8,128)(2,1)S(1)}, bf16[128,768]{1,0:T(8,128)(2,1)S(1)}, u32[]{:S(2)}, u32[]{:S(2)}) collective-permute-start(bf16[128,768]{1,0:T(8,128)(2,1)S(1)} %get-tuple-element.37.att_ref.a0), channel_id=1, source_target_pairs={{0,2},{1,3},{2,0},{3,1},{4,6},{5,7},{6,4},{7,5},{8,10},{9,11},{10,... | collective-permute-start | bytes 589832 | tf_op jit(solution)/shard_map/ppermute | solution.py:438
  36.0 0.0 collective-permute-done.8.a3
  36.0 1.5 %collective-permute-start.6 = (bf16[128,768]{1,0:T(8,128)(2,1)S(1)}, bf16[128,768]{1,0:T(8,128)(2,1)S(1)}, u32[]{:S(2)}, u32[]{:S(2)}) collective-permute-start(bf16[128,768]{1,0:T(8,128)(2,1)S(1)} %get-tuple-element.37.att_ref.a0), channel_id=1, source_target_pairs={{0,1},{1,2},{2,3},{3,0},{4,5},{5,6},{6,7},{7,4},{8,9},{9,10},{10,1... | collective-permute-start | bytes 589832 | tf_op jit(solution)/shard_map/ppermute | solution.py:438
  37.5 14.7 %collective-permute-done.7.a2 = bf16[128,768]{1,0:T(8,128)(2,1)S(1)} collective-permute-done((bf16[128,768]{1,0:T(8,128)(2,1)S(1)}, bf16[128,768]{1,0:T(8,128)(2,1)S(1)}, u32[]{:S(2)}, u32[]{:S(2)}) %collective-permute-start.7) | collective-permute-done | bytes 196640 | tf_op jit(solution)/shard_map/ppermute | solution.py:438
  52.2 2.4 %collective-permute-done.6.a1 = bf16[128,768]{1,0:T(8,128)(2,1)S(1)} collective-permute-done((bf16[128,768]{1,0:T(8,128)(2,1)S(1)}, bf16[128,768]{1,0:T(8,128)(2,1)S(1)}, u32[]{:S(2)}, u32[]{:S(2)}) %collective-permute-start.6) | collective-permute-done | bytes 196640 | tf_op jit(solution)/shard_map/ppermute | solution.py:438
  54.6 0.0 collective-permute-done.3.x1
  54.6 0.0 collective-permute-done.4.x2
  54.7 0.0 collective-permute-done.5.x3
  54.7 0.0 copy-done.7
  54.7 2.2 %shard_map.117 = (bf16[400,768]{1,0:T(8,128)(2,1)S(1)}, bf16[400,768]{1,0:T(8,128)(2,1)S(1)}) custom-call(bf16[1168,128]{1,0:T(8,128)(2,1)S(1)} %get-tuple-element.41.x0, bf16[1168,128]{1,0:T(8,128)(2,1)S(1)} %collective-permute-done.3.x1, bf16[1168,128]{1,0:T(8,128)(2,1)S(1)} %collective-permute-done.4.x2, bf16[1168,128]{1,0:T(8,128)(2,1)S(1)} %collective-permute-done.5.x3, ...), custom_call_target="tpu_custom_call" | custom-call | flops 3000000000 | bytes 3000000 | tf_op jit(solution)/shard_map/pallas_call | solution.py:402
  56.9 0.0 copy-start.9
  56.9 0.1 collective-permute-start.9
  57.0 2.0 %collective-permute-done.9.other_ref = bf16[400,768]{1,0:T(8,128)(2,1)S(1)} collective-permute-done((bf16[400,768]{1,0:T(8,128)(2,1)S(1)}, bf16[400,768]{1,0:T(8,128)(2,1)S(1)}, u32[]{:S(2)}, u32[]{:S(2)}) %collective-permute-start.9) | collective-permute-done | bytes 614432 | tf_op jit(solution)/shard_map/ppermute | solution.py:499
  59.0 0.2 shard_map.118
  59.2 1.7 %collective-permute-start.10 = (bf16[112,768]{1,0:T(8,128)(2,1)S(1)}, bf16[112,768]{1,0:T(8,128)(2,1)S(1)}, u32[]{:S(2)}, u32[]{:S(2)}) collective-permute-start(bf16[112,768]{1,0:T(8,128)(2,1)S(1)} %get-tuple-element.49), channel_id=1, source_target_pairs={{0,8},{4,12},{8,16},{12,20},{16,24},{20,28},{24,0},{28,4},{32,40},... | collective-permute-start | bytes 516104 | tf_op jit(solution)/shard_map/ppermute | solution.py:438
  60.8 2.9 %collective-permute-start.11 = (bf16[112,768]{1,0:T(8,128)(2,1)S(1)}, bf16[112,768]{1,0:T(8,128)(2,1)S(1)}, u32[]{:S(2)}, u32[]{:S(2)}) collective-permute-start(bf16[112,768]{1,0:T(8,128)(2,1)S(1)} %get-tuple-element.50), channel_id=1, source_target_pairs={{0,16},{4,20},{8,24},{12,28},{16,0},{20,4},{24,8},{28,12},{32,48},... | collective-permute-start | bytes 516104 | tf_op jit(solution)/shard_map/ppermute | solution.py:438
  63.7 1.3 %collective-permute-start.12 = (bf16[112,768]{1,0:T(8,128)(2,1)S(1)}, bf16[112,768]{1,0:T(8,128)(2,1)S(1)}, u32[]{:S(2)}, u32[]{:S(2)}) collective-permute-start(bf16[112,768]{1,0:T(8,128)(2,1)S(1)} %get-tuple-element.51), channel_id=1, source_target_pairs={{0,24},{4,28},{8,0},{12,4},{16,8},{20,12},{24,16},{28,20},{32,56},... | collective-permute-start | bytes 516104 | tf_op jit(solution)/shard_map/ppermute | solution.py:438
  65.1 1.9 %collective-permute-done.10.y1 = bf16[112,768]{1,0:T(8,128)(2,1)S(1)} collective-permute-done((bf16[112,768]{1,0:T(8,128)(2,1)S(1)}, bf16[112,768]{1,0:T(8,128)(2,1)S(1)}, u32[]{:S(2)}, u32[]{:S(2)}) %collective-permute-start.10) | collective-permute-done | bytes 172064 | tf_op jit(solution)/shard_map/ppermute | solution.py:438
  67.0 4.9 %collective-permute-done.11.y2 = bf16[112,768]{1,0:T(8,128)(2,1)S(1)} collective-permute-done((bf16[112,768]{1,0:T(8,128)(2,1)S(1)}, bf16[112,768]{1,0:T(8,128)(2,1)S(1)}, u32[]{:S(2)}, u32[]{:S(2)}) %collective-permute-start.11) | collective-permute-done | bytes 172064 | tf_op jit(solution)/shard_map/ppermute | solution.py:438
  71.8 0.0 collective-permute-done.12.y3
  71.8 0.0 copy-done.9
  71.8 0.3 shard_map.119
  72.1 18.2 %all_to_all.5.in_ref = bf16[8,16,768]{2,1,0:T(8,128)(2,1)S(1)} all-to-all(bf16[8,16,768]{2,1,0:T(8,128)(2,1)S(1)} %shard_map.119), channel_id=1, replica_groups={{0,32,64,96,128,160,192,224},{4,36,68,100,132,164,196,228},{8,40,72,104..., dimensions={0} | all-to-all | bytes 393216 | tf_op jit(solution)/shard_map/all_to_all | solution.py:503
  90.3 0.7 shard_map.120
  (7 shorter events, 0.0 us)
Async XLA Ops:
  0.6 12.9 %copy-start = (bf16[768,2304]{1,0:T(8,128)(2,1)S(1)}, bf16[768,2304]{1,0:T(8,128)(2,1)}, u32[]{:S(2)}) copy-start(bf16[768,2304]{1,0:T(8,128)(2,1)} %w_qkv_ref.3) | copy-start | bytes 10616836
  0.6 1.8 %copy-start.1 = (bf16[1536,768]{1,0:T(8,128)(2,1)S(1)}, bf16[1536,768]{1,0:T(8,128)(2,1)}, u32[]{:S(2)}) copy-start(bf16[1536,768]{1,0:T(8,128)(2,1)} %w_in_ref.1) | copy-start | bytes 7077892
  2.5 1.0 %copy-start.4 = (bf16[1,128,1536]{2,1,0:T(8,128)(2,1)S(1)}, bf16[1,128,1536]{2,1,0:T(8,128)(2,1)}, u32[]{:S(2)}) copy-start(bf16[1,128,1536]{2,1,0:T(8,128)(2,1)} %tiles_hbm.1) | copy-start | bytes 1179652
  3.5 0.7 copy-start.5
  4.1 0.7 copy-start.6
  8.0 6.9 %collective-permute-start.2 = (bf16[128,768]{1,0:T(8,128)(2,1)S(1)}, bf16[128,768]{1,0:T(8,128)(2,1)S(1)}, u32[]{:S(2)}, u32[]{:S(2)}) collective-permute-start(bf16[128,768]{1,0:T(8,128)(2,1)S(1)} %get-tuple-element.28.normed_ref.n0), channel_id=1, source_target_pairs={{0,3},{1,0},{2,1},{3,2},{4,7},{5,4},{6,5},{7,6},{8,11},{9,8},{10,9... | collective-permute-start | bytes 589832 | tf_op jit(solution)/shard_map/ppermute | solution.py:438
  10.3 9.5 %collective-permute-start.1 = (bf16[128,768]{1,0:T(8,128)(2,1)S(1)}, bf16[128,768]{1,0:T(8,128)(2,1)S(1)}, u32[]{:S(2)}, u32[]{:S(2)}) collective-permute-start(bf16[128,768]{1,0:T(8,128)(2,1)S(1)} %get-tuple-element.28.normed_ref.n0), channel_id=1, source_target_pairs={{0,2},{1,3},{2,0},{3,1},{4,6},{5,7},{6,4},{7,5},{8,10},{9,11},{10,... | collective-permute-start | bytes 589832 | tf_op jit(solution)/shard_map/ppermute | solution.py:438
  11.0 9.7 %collective-permute-start = (bf16[128,768]{1,0:T(8,128)(2,1)S(1)}, bf16[128,768]{1,0:T(8,128)(2,1)S(1)}, u32[]{:S(2)}, u32[]{:S(2)}) collective-permute-start(bf16[128,768]{1,0:T(8,128)(2,1)S(1)} %get-tuple-element.28.normed_ref.n0), channel_id=1, source_target_pairs={{0,1},{1,2},{2,3},{3,0},{4,5},{5,6},{6,7},{7,4},{8,9},{9,10},{10,1... | collective-permute-start | bytes 589832 | tf_op jit(solution)/shard_map/ppermute | solution.py:438
  20.7 5.5 %copy-start.2 = (bf16[1536,768]{1,0:T(8,128)(2,1)S(1)}, bf16[1536,768]{1,0:T(8,128)(2,1)}, u32[]{:S(2)}) copy-start(bf16[1536,768]{1,0:T(8,128)(2,1)} %w_in_ref.1) | copy-start | bytes 7077892
  20.7 5.5 %copy-start.3 = (bf16[768,768]{1,0:T(8,128)(2,1)S(1)}, bf16[768,768]{1,0:T(8,128)(2,1)}, u32[]{:S(2)}) copy-start(bf16[768,768]{1,0:T(8,128)(2,1)} %w_out_ref.1) | copy-start | bytes 3538948
  20.7 5.5 %copy-start.8 = (bf16[384,384]{1,0:T(8,128)(2,1)S(1)}, bf16[384,384]{1,0:T(8,128)(2,1)}, u32[]{:S(2)}) copy-start(bf16[384,384]{1,0:T(8,128)(2,1)} %constant.6.clone.spread_ref) | copy-start | bytes 884740
  23.5 12.5 %collective-permute-start.8 = (bf16[128,768]{1,0:T(8,128)(2,1)S(1)}, bf16[128,768]{1,0:T(8,128)(2,1)S(1)}, u32[]{:S(2)}, u32[]{:S(2)}) collective-permute-start(bf16[128,768]{1,0:T(8,128)(2,1)S(1)} %get-tuple-element.37.att_ref.a0), channel_id=1, source_target_pairs={{0,3},{1,0},{2,1},{3,2},{4,7},{5,4},{6,5},{7,6},{8,11},{9,8},{10,9... | collective-permute-start | bytes 589832 | tf_op jit(solution)/shard_map/ppermute | solution.py:438
  26.3 28.4 %copy-start.7 = (bf16[768,768]{1,0:T(8,128)(2,1)S(1)}, bf16[768,768]{1,0:T(8,128)(2,1)}, u32[]{:S(2)}) copy-start(bf16[768,768]{1,0:T(8,128)(2,1)} %constant.7.clone.order_ref) | copy-start | bytes 3538948
  30.9 23.7 %collective-permute-start.3 = (bf16[1168,128]{1,0:T(8,128)(2,1)S(1)}, bf16[1168,128]{1,0:T(8,128)(2,1)S(1)}, u32[]{:S(2)}, u32[]{:S(2)}) collective-permute-start(bf16[1168,128]{1,0:T(8,128)(2,1)S(1)} %get-tuple-element.42), channel_id=1, source_target_pairs={{0,1},{1,2},{2,3},{3,0},{4,5},{5,6},{6,7},{7,4},{8,9},{9,10},{10,1... | collective-permute-start | bytes 897032 | tf_op jit(solution)/shard_map/ppermute | solution.py:438
  31.0 23.6 %collective-permute-start.4 = (bf16[1168,128]{1,0:T(8,128)(2,1)S(1)}, bf16[1168,128]{1,0:T(8,128)(2,1)S(1)}, u32[]{:S(2)}, u32[]{:S(2)}) collective-permute-start(bf16[1168,128]{1,0:T(8,128)(2,1)S(1)} %get-tuple-element.43), channel_id=1, source_target_pairs={{0,2},{1,3},{2,0},{3,1},{4,6},{5,7},{6,4},{7,5},{8,10},{9,11},{10,... | collective-permute-start | bytes 897032 | tf_op jit(solution)/shard_map/ppermute | solution.py:438
  33.7 21.0 %collective-permute-start.5 = (bf16[1168,128]{1,0:T(8,128)(2,1)S(1)}, bf16[1168,128]{1,0:T(8,128)(2,1)S(1)}, u32[]{:S(2)}, u32[]{:S(2)}) collective-permute-start(bf16[1168,128]{1,0:T(8,128)(2,1)S(1)} %get-tuple-element.44), channel_id=1, source_target_pairs={{0,3},{1,0},{2,1},{3,2},{4,7},{5,4},{6,5},{7,6},{8,11},{9,8},{10,9... | collective-permute-start | bytes 897032 | tf_op jit(solution)/shard_map/ppermute | solution.py:438
  33.9 18.3 %collective-permute-start.7 = (bf16[128,768]{1,0:T(8,128)(2,1)S(1)}, bf16[128,768]{1,0:T(8,128)(2,1)S(1)}, u32[]{:S(2)}, u32[]{:S(2)}) collective-permute-start(bf16[128,768]{1,0:T(8,128)(2,1)S(1)} %get-tuple-element.37.att_ref.a0), channel_id=1, source_target_pairs={{0,2},{1,3},{2,0},{3,1},{4,6},{5,7},{6,4},{7,5},{8,10},{9,11},{10,... | collective-permute-start | bytes 589832 | tf_op jit(solution)/shard_map/ppermute | solution.py:438
  36.0 18.7 %collective-permute-start.6 = (bf16[128,768]{1,0:T(8,128)(2,1)S(1)}, bf16[128,768]{1,0:T(8,128)(2,1)S(1)}, u32[]{:S(2)}, u32[]{:S(2)}) collective-permute-start(bf16[128,768]{1,0:T(8,128)(2,1)S(1)} %get-tuple-element.37.att_ref.a0), channel_id=1, source_target_pairs={{0,1},{1,2},{2,3},{3,0},{4,5},{5,6},{6,7},{7,4},{8,9},{9,10},{10,1... | collective-permute-start | bytes 589832 | tf_op jit(solution)/shard_map/ppermute | solution.py:438
  56.9 14.9 %copy-start.9 = (bf16[128,112]{1,0:T(8,128)(2,1)S(1)}, bf16[128,112]{1,0:T(8,128)(2,1)}, u32[]{:S(2)}) copy-start(bf16[128,112]{1,0:T(8,128)(2,1)} %constant.8.clone.order_ref) | copy-start | bytes 86020
  56.9 2.1 %collective-permute-start.9 = (bf16[400,768]{1,0:T(8,128)(2,1)S(1)}, bf16[400,768]{1,0:T(8,128)(2,1)S(1)}, u32[]{:S(2)}, u32[]{:S(2)}) collective-permute-start(bf16[400,768]{1,0:T(8,128)(2,1)S(1)} %get-tuple-element.47), channel_id=1, source_target_pairs={{0,4},{4,0},{8,12},{12,8},{16,20},{20,16},{24,28},{28,24},{32,36},... | collective-permute-start | bytes 1843208 | tf_op jit(solution)/shard_map/ppermute | solution.py:499
  59.2 7.8 %collective-permute-start.10 = (bf16[112,768]{1,0:T(8,128)(2,1)S(1)}, bf16[112,768]{1,0:T(8,128)(2,1)S(1)}, u32[]{:S(2)}, u32[]{:S(2)}) collective-permute-start(bf16[112,768]{1,0:T(8,128)(2,1)S(1)} %get-tuple-element.49), channel_id=1, source_target_pairs={{0,8},{4,12},{8,16},{12,20},{16,24},{20,28},{24,0},{28,4},{32,40},... | collective-permute-start | bytes 516104 | tf_op jit(solution)/shard_map/ppermute | solution.py:438
  60.8 11.0 %collective-permute-start.11 = (bf16[112,768]{1,0:T(8,128)(2,1)S(1)}, bf16[112,768]{1,0:T(8,128)(2,1)S(1)}, u32[]{:S(2)}, u32[]{:S(2)}) collective-permute-start(bf16[112,768]{1,0:T(8,128)(2,1)S(1)} %get-tuple-element.50), channel_id=1, source_target_pairs={{0,16},{4,20},{8,24},{12,28},{16,0},{20,4},{24,8},{28,12},{32,48},... | collective-permute-start | bytes 516104 | tf_op jit(solution)/shard_map/ppermute | solution.py:438
  63.7 8.1 %collective-permute-start.12 = (bf16[112,768]{1,0:T(8,128)(2,1)S(1)}, bf16[112,768]{1,0:T(8,128)(2,1)S(1)}, u32[]{:S(2)}, u32[]{:S(2)}) collective-permute-start(bf16[112,768]{1,0:T(8,128)(2,1)S(1)} %get-tuple-element.51), channel_id=1, source_target_pairs={{0,24},{4,28},{8,0},{12,4},{16,8},{20,12},{24,16},{28,20},{32,56},... | collective-permute-start | bytes 516104 | tf_op jit(solution)/shard_map/ppermute | solution.py:438

commit v3 on v2

--- a/solution.py
+++ b/solution.py
@@ -24,7 +24,8 @@
 F32 = jnp.float32
 HALF = 384
 SUB = 96
-SECTIONS = 12
+SECTIONS = 10
+YROWS = 80
 XROWS = SECTIONS * SUB + 16
 NZ, NY, NC = 8, 4, 2
 
@@ -221,23 +222,33 @@
     att_ref[...] = att_acc[...].astype(BF)
 
 
-def backward_kernel(
+def chain_kernel(
     inv_count,
-    proj_ref, fk_ref, fv_ref, pnear_ref, pfar_ref, att_ref, hidden_ref, tiles_ref, flag_ref, spread_ref,
-    w_in_ref, w_out_ref,
-    x0, x1, x2, x3,
-    gq, gk, gv, gkf, gvf, ga_ref, turned,
+    att_ref, hidden_ref, tiles_ref, flag_ref, w_in_ref, w_out_ref, order_ref,
+    ga_ref, loss_ref, mine_ref, other_ref,
 ):
-    seq = lax.axis_index("seq")
-    mixed = (hidden_ref[...].astype(F32) + nn(att_ref[...], w_out_ref[...])).astype(BF)
+    core = lax.axis_index("slide") & 1
+    attended = att_ref[...]
+    mixed = (hidden_ref[...].astype(F32) + nn(attended, w_out_ref[...])).astype(BF)
     flag = flag_ref[:, 0:1] > 0.5
     error = jnp.where(flag, nt(mixed, w_in_ref[...]) - tiles_ref[...].astype(F32), 0.0)
     loss = jnp.sum(jnp.sum(error * error, axis=1, keepdims=True), axis=0, keepdims=True) * inv_count
-    tail = split_rows(jnp.broadcast_to(loss, (16, 128)), (16, 128), 0).astype(BF)
+    loss_ref[...] = split_rows(jnp.broadcast_to(loss, (16, 128)), (16, 128), 0).astype(BF)
     grad_pred = (2.0 * inv_count * error).astype(BF)
     grad_mixed = nn(grad_pred, w_in_ref[...]).astype(BF)
     ga_ref[...] = nt(grad_mixed, w_out_ref[...]).astype(BF)
-
+    for turn, ref in enumerate((mine_ref, other_ref)):
+        first = pl.multiple_of(((core + turn) & 1) * HALF, HALF)
+        left = nt(order_ref[pl.ds(first, HALF)], grad_mixed).astype(BF)
+        ref[...] = nn(left, attended).astype(BF)
+
+
+def backward_kernel(
+    proj_ref, fk_ref, fv_ref, pnear_ref, pfar_ref, ga_ref, loss_ref, spread_ref,
+    x0, x1, x2, x3,
+    gq, gk, gv, gkf, gvf, turned,
+):
+    seq = lax.axis_index("seq")
     own_class = iota((1, TOK), 1) >> 5
     for ref in (gq, gk, gv, gkf, gvf):
         ref[...] = jnp.zeros_like(ref)
@@ -276,7 +287,7 @@
         gvf[:, win] += nn(far_probs.astype(BF), ga_picked)
     place = spread_ref[...]
     section = 0
-    for value in (gq, gk, gv, gkf, gvf, grad_mixed):
+    for value in (gq, gk, gv, gkf, gvf):
         for half in range(2):
             piece = value[:, half * HALF : (half + 1) * HALF].astype(BF)
             turned[section] = nt(place, piece).astype(BF)
@@ -285,21 +296,16 @@
         first = pl.multiple_of(((seq + turn) & 3) * SUB, 16)
         for section in range(SECTIONS):
             ref[section * SUB : (section + 1) * SUB] = turned[section, pl.ds(first, SUB)]
-        ref[SECTIONS * SUB :] = tail
-
-
-def product_kernel(
-    x0, x1, x2, x3, pn_ref, a0, a1, a2, a3, order_ref, mine_ref, other_ref, got, left, att, res
-):
+        ref[SECTIONS * SUB :] = loss_ref[...]
+
+
+def product_kernel(x0, x1, x2, x3, pn_ref, order_ref, mine_ref, other_ref, got, left):
     seq = lax.axis_index("seq")
     core = lax.axis_index("slide") & 1
-    for turn, (ref, x_ref) in enumerate(zip((a0, a1, a2, a3), (x0, x1, x2, x3))):
-        src = (seq - turn) & 3
-        att[pl.ds(pl.multiple_of(src * TOK, TOK), TOK)] = ref[...]
-        got[src] = x_ref[...]
+    for turn, x_ref in enumerate((x0, x1, x2, x3)):
+        got[(seq - turn) & 3] = x_ref[...]
     for src in range(N_SEQ):
         left[0 : 2 * SUB, src * TOK : (src + 1) * TOK] = got[src, 0 : 2 * SUB]
-        left[6 * SUB : 8 * SUB, src * TOK : (src + 1) * TOK] = got[src, 10 * SUB : 12 * SUB]
     shape = (SUB, TOK)
     row = iota(shape, 0)
     lane_class = iota(shape, 1) >> 5
@@ -320,37 +326,58 @@
                 for r in range(RATE):
                     total = total + jnp.where(spots[r], turns[(r - src) & 3], 0.0)
                 left[near_at : near_at + SUB, src * TOK : (src + 1) * TOK] = total.astype(BF)
-    right = pn_ref[...].reshape(N_SEQ * TOK, D)
-    res[0 : 6 * SUB] = nn(left[0 : 6 * SUB], right).astype(BF)
-    res[6 * SUB :] = nn(left[6 * SUB :], att[...]).astype(BF)
+    whole = nn(left[...], pn_ref[...].reshape(N_SEQ * TOK, D)).astype(BF)
     loss = got[0, SECTIONS * SUB :].astype(F32)
     for src in range(1, N_SEQ):
         loss = loss + got[src, SECTIONS * SUB :].astype(F32)
     loss = jnp.sum(loss, axis=0, keepdims=True)[:, 0:1]
-    tail = split_rows(jnp.broadcast_to(loss, (16, D)), (16, D), 0).astype(BF)
-    whole = res[...]
+    tail = split_rows(jnp.broadcast_to(loss, (YROWS, D)), (YROWS, D), 72)
     for turn, ref in enumerate((mine_ref, other_ref)):
-        first = pl.multiple_of(((core + turn) & 1) * HALF, HALF)
-        ref[0:HALF] = nn(order_ref[pl.ds(first, HALF)], whole).astype(BF)
-        ref[HALF:] = tail
+        first = pl.multiple_of(((core + turn) & 1) * NY * YROWS, NY * YROWS)
+        half = nn(order_ref[pl.ds(first, NY * YROWS)], whole)
+        for y in range(NY):
+            rows = slice(y * YROWS, (y + 1) * YROWS)
+            ref[rows] = (half[rows] + tail).astype(BF)
+
+
+def resplit(total):
+    row = iota(total.shape, 0)
+    loss = jnp.sum(jnp.where(row >= 72, total, 0.0), axis=0, keepdims=True)
+    pieces = split_rows(jnp.broadcast_to(loss, total.shape), total.shape, 72)
+    return jnp.where(row >= 72, pieces, total), loss
 
 
 def core_kernel(mine_ref, other_ref, y0, y1, y2, y3):
     y = (lax.axis_index("slide") >> 1) & 3
-    loss = jnp.sum(mine_ref[HALF:].astype(F32) + other_ref[HALF:].astype(F32), axis=0, keepdims=True)
-    tail = split_rows(jnp.broadcast_to(loss, (16, D)), (16, D), 0).astype(BF)
+    for turn, ref in enumerate((y0, y1, y2, y3)):
+        rows = pl.ds(pl.multiple_of(((y + turn) & 3) * YROWS, 16), YROWS)
+        ref[...] = resplit(mine_ref[rows].astype(F32) + other_ref[rows].astype(F32))[0].astype(BF)
+
+
+def y_kernel(y0, y1, y2, y3, o0, o1, o2, o3, order_ref, out_ref):
+    total = y0[...].astype(F32) + y1[...].astype(F32) + y2[...].astype(F32) + y3[...].astype(F32)
+    total, loss = resplit(total)
+    out_ref[0:6] = nn(order_ref[...], total.astype(BF)).astype(BF).reshape(6, 16, D)
+    out = o0[...].astype(F32) + o1[...].astype(F32) + o2[...].astype(F32) + o3[...].astype(F32)
+    tail = split_rows(jnp.broadcast_to(loss, (16, D)), (16, D), 12)
+    for half in range(2):
+        out_ref[6 + half] = (out[16 * half : 16 * (half + 1)] + tail).astype(BF)
+
+
+def out_core_kernel(mine_ref, other_ref, y0, y1, y2, y3):
+    y = (lax.axis_index("slide") >> 1) & 3
     for turn, ref in enumerate((y0, y1, y2, y3)):
         rows = pl.ds(pl.multiple_of(((y + turn) & 3) * SUB, 16), SUB)
-        ref[0:SUB] = (mine_ref[rows].astype(F32) + other_ref[rows].astype(F32)).astype(BF)
-        ref[SUB:] = tail
-
-
-def y_kernel(y0, y1, y2, y3, order_ref, out_ref):
+        ref[...] = (mine_ref[rows].astype(F32) + other_ref[rows].astype(F32)).astype(BF)
+
+
+def out_y_kernel(y0, y1, y2, y3, order_ref, x0, x1, x2, x3):
+    seq = lax.axis_index("seq")
     total = y0[...].astype(F32) + y1[...].astype(F32) + y2[...].astype(F32) + y3[...].astype(F32)
-    loss = jnp.sum(total[SUB:], axis=0, keepdims=True)
-    rows = split_rows(jnp.broadcast_to(loss, (16, D)), (16, D), 0)
-    total = jnp.concatenate([total[:SUB], rows], 0).astype(BF)
-    out_ref[...] = nn(order_ref[...], total).astype(BF).reshape(NZ, 16, D)
+    total = total.astype(BF)
+    for turn, ref in enumerate((x0, x1, x2, x3)):
+        rows = pl.ds(pl.multiple_of(((seq + turn) & 3) * 32, 32), 32)
+        ref[...] = nn(order_ref[rows], total).astype(BF)
 
 
 def z_kernel(in_ref, out_ref, loss_ref):
@@ -372,22 +399,44 @@
 
 
 def product_order():
+    place = np.zeros((NC * NY * YROWS, 6 * SUB), np.float32)
+    for c in range(NC):
+        for y in range(NY):
+            for z in range(6):
+                for r in range(12):
+                    place[(c * NY + y) * YROWS + z * 12 + r, z * SUB + c * 48 + y * 12 + r] = 1.0
+    return jnp.asarray(place, BF)
+
+
+def out_order():
     place = np.zeros((D, D), np.float32)
-    for row in range(D):
-        c, rest = divmod(row, HALF)
-        y, rest = divmod(rest, SUB)
-        z, r = divmod(rest, 12)
-        place[row, z * SUB + c * 48 + y * 12 + r] = 1.0
+    row = 0
+    for c in range(NC):
+        for y in range(NY):
+            for j in range(N_SEQ):
+                for half in range(2):
+                    for r in range(12):
+                        place[row, (half * 8 + y * NC + c) * HD + j * 12 + r] = 1.0
+                        row += 1
     return jnp.asarray(place, BF)
 
 
+def out_pad_order():
+    place = np.zeros((N_SEQ * 32, SUB), np.float32)
+    for j in range(N_SEQ):
+        for half in range(2):
+            for r in range(12):
+                place[j * 32 + half * 16 + r, j * 24 + half * 12 + r] = 1.0
+    return jnp.asarray(place, BF)
+
+
 def pad_order():
-    place = np.zeros((NZ * 16, SUB + 16), np.float32)
-    for z in range(NZ):
+    place = np.zeros((SUB, YROWS), np.float32)
+    for z in range(6):
         for r in range(12):
             place[z * 16 + r, z * 12 + r] = 1.0
         for r in range(3):
-            place[z * 16 + 12 + r, SUB + r] = 1.0
+            place[z * 16 + 12 + r, 72 + r] = 1.0
     return jnp.asarray(place, BF)
 
 
@@ -396,7 +445,7 @@
 HBM = pl.BlockSpec(memory_space=pltpu.HBM)
 
 
-def call(kernel, out_shapes, args, scratch=(), micros=1.0, specs=None):
+def call(kernel, out_shapes, args, scratch=(), micros=1.0, specs=None, grant=24):
     if specs is None:
         specs = [SMEM if a.dtype == jnp.int32 else VMEM for a in args]
     return pl.pallas_call(
@@ -405,7 +454,7 @@
         in_specs=specs,
         out_specs=[VMEM] * len(out_shapes),
         scratch_shapes=list(scratch),
-        compiler_params=pltpu.CompilerParams(vmem_limit_bytes=24 * 1024 * 1024),
+        compiler_params=pltpu.CompilerParams(vmem_limit_bytes=grant * 1024 * 1024),
         cost_estimate=pl.CostEstimate(
             flops=int(micros * 1.0e9), bytes_accessed=int(micros * 1.0e6), transcendentals=0
         ),
@@ -453,6 +502,7 @@
         ],
         2.0,
         [HBM] * 4,
+        60,
     )
     norms = swap([normed] * N_SEQ, "seq", SEQ_TURNS)
     scores = shape(GROUPS, TOK, RATE * TOK, dtype=F32)
@@ -474,32 +524,37 @@
         [pltpu.VMEM((TOK, D), F32)],
         4.0,
     )
-    atts = swap([attended] * N_SEQ, "seq", SEQ_TURNS)
+    grad_attended, loss, out_mine, out_other = call(
+        functools.partial(chain_kernel, inv_count),
+        [shape(TOK, D), shape(16, 128), shape(HALF, D), shape(HALF, D)],
+        (attended, hidden, tiles, flag, w_in, w_out, out_order()),
+        (),
+        3.0,
+    )
+    out_other = lax.ppermute(out_other, "slide", CORE_PAIRS)
     sent = call(
-        functools.partial(backward_kernel, inv_count),
+        backward_kernel,
         [shape(XROWS, TOK)] * N_SEQ,
-        (projected, fk, fv, pnear, pfar, attended, hidden, tiles, flag, spread_order(), w_in, w_out),
-        [pltpu.VMEM((TOK, D), F32)] * 5
-        + [pltpu.VMEM((TOK, D), BF), pltpu.VMEM((SECTIONS, HALF, TOK), BF)],
-        8.0,
+        (projected, fk, fv, pnear, pfar, grad_attended, loss, spread_order()),
+        [pltpu.VMEM((TOK, D), F32)] * 5 + [pltpu.VMEM((SECTIONS, HALF, TOK), BF)],
+        4.0,
     )
     got = swap(sent, "seq", SEQ_TURNS)
+    out = call(out_core_kernel, [shape(SUB, D)] * NY, (out_mine, out_other))
+    out = swap(out, "slide", Y_TURNS)
+    out = call(out_y_kernel, [shape(32, D)] * N_SEQ, (*out, out_pad_order()))
+    out = swap(out, "seq", SEQ_TURNS)
     mine, other = call(
         product_kernel,
-        [shape(HALF + 16, D)] * 2,
-        (*got, pn, *atts, product_order()),
-        [
-            pltpu.VMEM((N_SEQ, XROWS, TOK), BF),
-            pltpu.VMEM((D, N_SEQ * TOK), BF),
-            pltpu.VMEM((N_SEQ * TOK, D), BF),
-            pltpu.VMEM((D, D), BF),
-        ],
+        [shape(NY * YROWS, D)] * 2,
+        (*got, pn, product_order()),
+        [pltpu.VMEM((N_SEQ, XROWS, TOK), BF), pltpu.VMEM((6 * SUB, N_SEQ * TOK), BF)],
         3.0,
     )
     other = lax.ppermute(other, "slide", CORE_PAIRS)
-    by_y = call(core_kernel, [shape(SUB + 16, D)] * NY, (mine, other))
+    by_y = call(core_kernel, [shape(YROWS, D)] * NY, (mine, other))
     by_y = swap(by_y, "slide", Y_TURNS)
-    (by_z,) = call(y_kernel, [shape(NZ, 16, D)], (*by_y, pad_order()))
+    (by_z,) = call(y_kernel, [shape(NZ, 16, D)], (*by_y, *out, pad_order()))
     by_z = lax.all_to_all(by_z, "slide", 0, 0, tiled=True, axis_index_groups=Z_GROUPS)
     gradients, loss = call(z_kernel, [shape(12, D, dtype=F32), shape(1, 1, dtype=F32)], (by_z,))
     return (gradients, loss[0, 0])

time: 91.8 us -> 87.9 us (0.958)
  the two profiles are of different devices: /device:TPU:2 before, /device:TPU:24 now
where the time goes in v3:
time: 87.9 us; the launch traced here: 87.7 us
  waiting for transfers between devices  27.3 us (31%)
  starting transfers between devices  23.2 us (26%)
  blocking collectives  18 us (20%)
  Pallas kernels  16.7 us (19%)
  between operations  1.52 us (2%)
  local copies, waits for them, and re-layouts  0.97 us (1%)
    ppermute x15, waiting for transfers between devices, swap(): lax.ppermute(arrays[t], axis, turns[t])  27.3 us
    ppermute x15, starting transfers between devices, swap(): lax.ppermute(arrays[t], axis, turns[t])  23.1 us
    all_to_all x1, blocking collectives, per_device(): lax.all_to_all(by_z, 'slide', 0, 0, tiled=True, axis_index_groups=Z_GROUPS)  18 us
    pallas_call x11, Pallas kernels, call(): pl.pallas_call(kernel, out_shape=out_shapes, in_specs=specs, out_specs=[V...  16.7 us
  transfers between devices with their start and end apart: 17, of which 9 were waited for; matrix products, arithmetic and copies ran while one was open for 0% of the time, Pallas kernels for 4%

profile of v3, /device:TPU:24, one launch (start us, length us, event | category | flops | bytes accessed | tf_op | source)
XLA Modules:
  0.0 87.7 jit_solution(7916689963458511960)
XLA Ops:
  0.6 3.8 %shard_map.131 = (bf16[128,1536]{1,0:T(8,128)(2,1)}, bf16[128,768]{1,0:T(8,128)(2,1)}, bf16[128,768]{1,0:T(8,128)(2,1)}, f32[128,128]{1,0:T(8,128)}) custom-call(bf16[1,128,1536]{2,1,0:T(8,128)(2,1)} %tiles_hbm.1, s32[1,128]{1,0:T(1,128)} %masked_hbm.1, f32[768]{0:T(1024)} %gain_hbm.1, bf16[1536,768]{1,0:T(8,128)(2,1)} %w_in_ref.1), custom_call_target="tpu_custom_call" | custom-call | flops 2000000000 | bytes 2000000 | tf_op jit(solution)/shard_map/pallas_call | solution.py:451
  4.5 2.8 %collective-permute-start.2 = (bf16[128,768]{1,0:T(8,128)(2,1)}, bf16[128,768]{1,0:T(8,128)(2,1)S(1)}, u32[]{:S(2)}, u32[]{:S(2)}) collective-permute-start(bf16[128,768]{1,0:T(8,128)(2,1)} %get-tuple-element.40.normed_ref.n0), channel_id=1, source_target_pairs={{0,3},{1,0},{2,1},{3,2},{4,7},{5,4},{6,5},{7,6},{8,11},{9,8},{10,9... | collective-permute-start | bytes 589832 | tf_op jit(solution)/shard_map/ppermute | solution.py:487
  7.3 0.8 collective-permute-start.1
  8.1 0.9 %collective-permute-start = (bf16[128,768]{1,0:T(8,128)(2,1)}, bf16[128,768]{1,0:T(8,128)(2,1)S(1)}, u32[]{:S(2)}, u32[]{:S(2)}) collective-permute-start(bf16[128,768]{1,0:T(8,128)(2,1)} %get-tuple-element.40.normed_ref.n0), channel_id=1, source_target_pairs={{0,1},{1,2},{2,3},{3,0},{4,5},{5,6},{6,7},{7,4},{8,9},{9,10},{10,1... | collective-permute-start | bytes 589832 | tf_op jit(solution)/shard_map/ppermute | solution.py:487
  9.7 0.9 %copy-done.3 = bf16[128,768]{1,0:T(8,128)(2,1)S(1)} copy-done((bf16[128,768]{1,0:T(8,128)(2,1)S(1)}, bf16[128,768]{1,0:T(8,128)(2,1)}, u32[]{:S(2)}) %copy-start.3) | copy-done | bytes 196632
  10.6 1.0 %shard_map.132 = (bf16[128,2304]{1,0:T(8,128)(2,1)S(1)}, f32[4,128,512]{2,1,0:T(8,128)S(1)}, f32[16,128]{1,0:T(8,128)S(1)}, f32[16,128]{1,0:T(8,128)S(1)}) custom-call(s32[1]{0:T(128)S(6)} %copy.14.count_ref, bf16[128,768]{1,0:T(8,128)(2,1)S(1)} %copy-done.3, bf16[768,2304]{1,0:T(8,128)(2,1)S(1)} %copy-done), custom_call_target="tpu_custom_call" | custom-call | flops 5000000000 | bytes 5000000 | tf_op jit(solution)/shard_map/pallas_call | solution.py:451
  11.6 4.5 %collective-permute-done.2.n3 = bf16[128,768]{1,0:T(8,128)(2,1)S(1)} collective-permute-done((bf16[128,768]{1,0:T(8,128)(2,1)}, bf16[128,768]{1,0:T(8,128)(2,1)S(1)}, u32[]{:S(2)}, u32[]{:S(2)}) %collective-permute-start.2) | collective-permute-done | bytes 196640 | tf_op jit(solution)/shard_map/ppermute | solution.py:487
  16.0 0.9 collective-permute-done.1.n2
  16.9 2.7 %collective-permute-done.n1 = bf16[128,768]{1,0:T(8,128)(2,1)S(1)} collective-permute-done((bf16[128,768]{1,0:T(8,128)(2,1)}, bf16[128,768]{1,0:T(8,128)(2,1)S(1)}, u32[]{:S(2)}, u32[]{:S(2)}) %collective-permute-start) | collective-permute-done | bytes 196640 | tf_op jit(solution)/shard_map/ppermute | solution.py:487
  19.6 2.7 %shard_map.133 = (bf16[4,128,768]{2,1,0:T(8,128)(2,1)S(1)}, bf16[128,768]{1,0:T(8,128)(2,1)S(1)}, bf16[128,768]{1,0:T(8,128)(2,1)S(1)}, f32[4,128,512]{2,1,0:T(8...) custom-call(s32[1]{0:T(128)S(6)} %copy.14.count_ref, bf16[128,768]{1,0:T(8,128)(2,1)S(1)} %copy-done.3, ...), custom_call_target="tpu_custom_call" | custom-call | flops 4000000000 | bytes 4000000 | tf_op jit(solution)/shard_map/pallas_call | solution.py:451
  22.4 0.0 copy-start.6
  22.4 2.7 %shard_map.134 = (bf16[128,768]{1,0:T(8,128)(2,1)S(1)}, bf16[16,128]{1,0:T(8,128)(2,1)S(1)}, bf16[384,768]{1,0:T(8,128)(2,1)S(1)}, bf16[384,768]{1,0:T(8,128)(2,1)S(1)}) custom-call(bf16[128,768]{1,0:T(8,128)(2,1)S(1)} %get-tuple-element.49.att_ref, bf16[128,768]{1,0:T(8,128)(2,1)S(1)} %copy-done.10, bf16[128,1536]{1,0:T(8,128)(2,1)S(1)} %copy-done.9, ...), custom_call_target="tpu_custom_call" | custom-call | flops 3000000000 | bytes 3000000 | tf_op jit(solution)/shard_map/pallas_call | solution.py:451
  25.1 0.0 copy-start.5
  25.2 3.0 %shard_map.135 = (bf16[976,128]{1,0:T(8,128)(2,1)S(1)}, bf16[976,128]{1,0:T(8,128)(2,1)S(1)}, bf16[976,128]{1,0:T(8,128)(2,1)S(1)}, bf16[976,128]{1,0:T(8,128)(2,1)S(1)}) custom-call(bf16[128,2304]{1,0:T(8,128)(2,1)S(1)} %get-tuple-element.41.proj_ref, bf16[128,768]{1,0:T(8,128)(2,1)S(1)} %get-tuple-element.45.fk_ref, ...), custom_call_target="tpu_custom_call" | custom-call | flops 4000000000 | bytes 4000000 | tf_op jit(solution)/shard_map/pallas_call | solution.py:451
  28.1 0.1 collective-permute-start.3
  28.2 2.1 %collective-permute-start.4 = (bf16[976,128]{1,0:T(8,128)(2,1)S(1)}, bf16[976,128]{1,0:T(8,128)(2,1)S(1)}, u32[]{:S(2)}, u32[]{:S(2)}) collective-permute-start(bf16[976,128]{1,0:T(8,128)(2,1)S(1)} %get-tuple-element.57), channel_id=1, source_target_pairs={{0,2},{1,3},{2,0},{3,1},{4,6},{5,7},{6,4},{7,5},{8,10},{9,11},{10,... | collective-permute-start | bytes 749576 | tf_op jit(solution)/shard_map/ppermute | solution.py:487
  30.4 1.3 %collective-permute-start.5 = (bf16[976,128]{1,0:T(8,128)(2,1)S(1)}, bf16[976,128]{1,0:T(8,128)(2,1)S(1)}, u32[]{:S(2)}, u32[]{:S(2)}) collective-permute-start(bf16[976,128]{1,0:T(8,128)(2,1)S(1)} %get-tuple-element.58), channel_id=1, source_target_pairs={{0,3},{1,0},{2,1},{3,2},{4,7},{5,4},{6,5},{7,6},{8,11},{9,8},{10,9... | collective-permute-start | bytes 749576 | tf_op jit(solution)/shard_map/ppermute | solution.py:487
  31.7 0.0 collective-permute-start.10
  31.7 11.0 %collective-permute-done.3.x1 = bf16[976,128]{1,0:T(8,128)(2,1)S(1)} collective-permute-done((bf16[976,128]{1,0:T(8,128)(2,1)S(1)}, bf16[976,128]{1,0:T(8,128)(2,1)S(1)}, u32[]{:S(2)}, u32[]{:S(2)}) %collective-permute-start.3) | collective-permute-done | bytes 249888 | tf_op jit(solution)/shard_map/ppermute | solution.py:487
  42.7 0.0 collective-permute-done.4.x2
  42.7 0.6 collective-permute-done.5.x3
  43.3 1.9 %shard_map.136 = (bf16[320,768]{1,0:T(8,128)(2,1)S(1)}, bf16[320,768]{1,0:T(8,128)(2,1)S(1)}) custom-call(bf16[976,128]{1,0:T(8,128)(2,1)S(1)} %get-tuple-element.55.x0, bf16[976,128]{1,0:T(8,128)(2,1)S(1)} %collective-permute-done.3.x1, bf16[976,128]{1,0:T(8,128)(2,1)S(1)} %collective-permute-done.4.x2, bf16[976,128]{1,0:T(8,128)(2,1)S(1)} %collective-permute-done.5.x3, ...), custom_call_target="tpu_custom_call" | custom-call | flops 3000000000 | bytes 3000000 | tf_op jit(solution)/shard_map/pallas_call | solution.py:451
  45.3 0.1 collective-permute-start.6
  45.4 0.0 collective-permute-done.10.other_ref
  45.4 0.2 shard_map.138
  45.6 0.0 copy-start.7
  45.6 0.3 collective-permute-start.11
  45.9 2.6 %collective-permute-start.12 = (bf16[96,768]{1,0:T(8,128)(2,1)S(1)}, bf16[96,768]{1,0:T(8,128)(2,1)S(1)}, u32[]{:S(2)}, u32[]{:S(2)}) collective-permute-start(bf16[96,768]{1,0:T(8,128)(2,1)S(1)} %get-tuple-element.70), channel_id=1, source_target_pairs={{0,16},{4,20},{8,24},{12,28},{16,0},{20,4},{24,8},{28,12},{32,48},... | collective-permute-start | bytes 442376 | tf_op jit(solution)/shard_map/ppermute | solution.py:487
  48.5 0.0 collective-permute-start.13
  48.5 0.2 shard_map.137
  48.7 0.0 copy-start.8
  48.7 3.3 %collective-permute-start.7 = (bf16[80,768]{1,0:T(8,128)(2,1)S(1)}, bf16[80,768]{1,0:T(8,128)(2,1)S(1)}, u32[]{:S(2)}, u32[]{:S(2)}) collective-permute-start(bf16[80,768]{1,0:T(8,128)(2,1)S(1)} %get-tuple-element.63), channel_id=1, source_target_pairs={{0,8},{4,12},{8,16},{12,20},{16,24},{20,28},{24,0},{28,4},{32,40},... | collective-permute-start | bytes 368648 | tf_op jit(solution)/shard_map/ppermute | solution.py:487
  52.0 0.2 collective-permute-start.8
  52.2 0.1 collective-permute-done.11.y1
  52.3 3.6 %collective-permute-start.9 = (bf16[80,768]{1,0:T(8,128)(2,1)S(1)}, bf16[80,768]{1,0:T(8,128)(2,1)S(1)}, u32[]{:S(2)}, u32[]{:S(2)}) collective-permute-start(bf16[80,768]{1,0:T(8,128)(2,1)S(1)} %get-tuple-element.65), channel_id=1, source_target_pairs={{0,24},{4,28},{8,0},{12,4},{16,8},{20,12},{24,16},{28,20},{32,56},... | collective-permute-start | bytes 368648 | tf_op jit(solution)/shard_map/ppermute | solution.py:487
  55.9 3.1 %collective-permute-done.13.y3 = bf16[96,768]{1,0:T(8,128)(2,1)S(1)} collective-permute-done((bf16[96,768]{1,0:T(8,128)(2,1)S(1)}, bf16[96,768]{1,0:T(8,128)(2,1)S(1)}, u32[]{:S(2)}, u32[]{:S(2)}) %collective-permute-start.13) | collective-permute-done | bytes 147488 | tf_op jit(solution)/shard_map/ppermute | solution.py:487
  59.0 0.3 shard_map.139
  59.2 0.3 collective-permute-start.14
  59.6 3.6 %collective-permute-start.15 = (bf16[32,768]{1,0:T(8,128)(2,1)S(1)}, bf16[32,768]{1,0:T(8,128)(2,1)S(1)}, u32[]{:S(2)}, u32[]{:S(2)}) collective-permute-start(bf16[32,768]{1,0:T(8,128)(2,1)S(1)} %get-tuple-element.74), channel_id=1, source_target_pairs={{0,2},{1,3},{2,0},{3,1},{4,6},{5,7},{6,4},{7,5},{8,10},{9,11},{10,... | collective-permute-start | bytes 147464 | tf_op jit(solution)/shard_map/ppermute | solution.py:487
  63.1 1.5 %collective-permute-done.14.o1 = bf16[32,768]{1,0:T(8,128)(2,1)S(1)} collective-permute-done((bf16[32,768]{1,0:T(8,128)(2,1)S(1)}, bf16[32,768]{1,0:T(8,128)(2,1)S(1)}, u32[]{:S(2)}, u32[]{:S(2)}) %collective-permute-start.14) | collective-permute-done | bytes 49184 | tf_op jit(solution)/shard_map/ppermute | solution.py:487
  64.6 1.1 %collective-permute-start.16 = (bf16[32,768]{1,0:T(8,128)(2,1)S(1)}, bf16[32,768]{1,0:T(8,128)(2,1)S(1)}, u32[]{:S(2)}, u32[]{:S(2)}) collective-permute-start(bf16[32,768]{1,0:T(8,128)(2,1)S(1)} %get-tuple-element.75), channel_id=1, source_target_pairs={{0,3},{1,0},{2,1},{3,2},{4,7},{5,4},{6,5},{7,6},{8,11},{9,8},{10,9... | collective-permute-start | bytes 147464 | tf_op jit(solution)/shard_map/ppermute | solution.py:487
  65.8 3.0 %collective-permute-done.16.o3 = bf16[32,768]{1,0:T(8,128)(2,1)S(1)} collective-permute-done((bf16[32,768]{1,0:T(8,128)(2,1)S(1)}, bf16[32,768]{1,0:T(8,128)(2,1)S(1)}, u32[]{:S(2)}, u32[]{:S(2)}) %collective-permute-start.16) | collective-permute-done | bytes 49184 | tf_op jit(solution)/shard_map/ppermute | solution.py:487
  68.7 0.0 collective-permute-done.7.y1
  68.7 0.0 collective-permute-done.8.y2
  68.7 0.0 collective-permute-done.9.y3
  68.7 0.3 shard_map.140
  69.0 18.0 %all_to_all.5.in_ref = bf16[8,16,768]{2,1,0:T(8,128)(2,1)S(1)} all-to-all(bf16[8,16,768]{2,1,0:T(8,128)(2,1)S(1)} %shard_map.140), channel_id=1, replica_groups={{0,32,64,96,128,160,192,224},{4,36,68,100,132,164,196,228},{8,40,72,104..., dimensions={0} | all-to-all | bytes 393216 | tf_op jit(solution)/shard_map/all_to_all | solution.py:558
  87.1 0.7 shard_map.141
  (22 shorter events, 0.0 us)
Async XLA Ops:
  0.6 9.0 %copy-start = (bf16[768,2304]{1,0:T(8,128)(2,1)S(1)}, bf16[768,2304]{1,0:T(8,128)(2,1)}, u32[]{:S(2)}) copy-start(bf16[768,2304]{1,0:T(8,128)(2,1)} %w_qkv_ref.3) | copy-start | bytes 10616836
  4.5 11.6 %collective-permute-start.2 = (bf16[128,768]{1,0:T(8,128)(2,1)}, bf16[128,768]{1,0:T(8,128)(2,1)S(1)}, u32[]{:S(2)}, u32[]{:S(2)}) collective-permute-start(bf16[128,768]{1,0:T(8,128)(2,1)} %get-tuple-element.40.normed_ref.n0), channel_id=1, source_target_pairs={{0,3},{1,0},{2,1},{3,2},{4,7},{5,4},{6,5},{7,6},{8,11},{9,8},{10,9... | collective-permute-start | bytes 589832 | tf_op jit(solution)/shard_map/ppermute | solution.py:487
  7.3 9.6 %collective-permute-start.1 = (bf16[128,768]{1,0:T(8,128)(2,1)}, bf16[128,768]{1,0:T(8,128)(2,1)S(1)}, u32[]{:S(2)}, u32[]{:S(2)}) collective-permute-start(bf16[128,768]{1,0:T(8,128)(2,1)} %get-tuple-element.40.normed_ref.n0), channel_id=1, source_target_pairs={{0,2},{1,3},{2,0},{3,1},{4,6},{5,7},{6,4},{7,5},{8,10},{9,11},{10,... | collective-permute-start | bytes 589832 | tf_op jit(solution)/shard_map/ppermute | solution.py:487
  8.1 11.5 %collective-permute-start = (bf16[128,768]{1,0:T(8,128)(2,1)}, bf16[128,768]{1,0:T(8,128)(2,1)S(1)}, u32[]{:S(2)}, u32[]{:S(2)}) collective-permute-start(bf16[128,768]{1,0:T(8,128)(2,1)} %get-tuple-element.40.normed_ref.n0), channel_id=1, source_target_pairs={{0,1},{1,2},{2,3},{3,0},{4,5},{5,6},{6,7},{7,4},{8,9},{9,10},{10,1... | collective-permute-start | bytes 589832 | tf_op jit(solution)/shard_map/ppermute | solution.py:487
  9.7 0.9 %copy-start.3 = (bf16[128,768]{1,0:T(8,128)(2,1)S(1)}, bf16[128,768]{1,0:T(8,128)(2,1)}, u32[]{:S(2)}) copy-start(bf16[128,768]{1,0:T(8,128)(2,1)} %get-tuple-element.40.normed_ref.n0) | copy-start | bytes 589828
  19.6 2.8 %copy-start.1 = (bf16[1536,768]{1,0:T(8,128)(2,1)S(1)}, bf16[1536,768]{1,0:T(8,128)(2,1)}, u32[]{:S(2)}) copy-start(bf16[1536,768]{1,0:T(8,128)(2,1)} %w_in_ref.1) | copy-start | bytes 7077892
  19.6 2.8 %copy-start.2 = (bf16[768,768]{1,0:T(8,128)(2,1)S(1)}, bf16[768,768]{1,0:T(8,128)(2,1)}, u32[]{:S(2)}) copy-start(bf16[768,768]{1,0:T(8,128)(2,1)} %w_out_ref.1) | copy-start | bytes 3538948
  19.6 2.8 %copy-start.4 = (bf16[768,768]{1,0:T(8,128)(2,1)S(1)}, bf16[768,768]{1,0:T(8,128)(2,1)}, u32[]{:S(2)}) copy-start(bf16[768,768]{1,0:T(8,128)(2,1)} %constant.10.clone.order_ref) | copy-start | bytes 3538948
  19.6 2.8 %copy-start.9 = (bf16[128,1536]{1,0:T(8,128)(2,1)S(1)}, bf16[128,1536]{1,0:T(8,128)(2,1)}, u32[]{:S(2)}) copy-start(bf16[128,1536]{1,0:T(8,128)(2,1)} %get-tuple-element.51.tiles_ref) | copy-start | bytes 1179652
  19.6 2.8 %copy-start.10 = (bf16[128,768]{1,0:T(8,128)(2,1)S(1)}, bf16[128,768]{1,0:T(8,128)(2,1)}, u32[]{:S(2)}) copy-start(bf16[128,768]{1,0:T(8,128)(2,1)} %get-tuple-element.50.hidden_ref) | copy-start | bytes 589828
  19.6 2.8 %copy-start.11 = (f32[128,128]{1,0:T(8,128)S(1)}, f32[128,128]{1,0:T(8,128)}, u32[]{:S(2)}) copy-start(f32[128,128]{1,0:T(8,128)} %get-tuple-element.52.flag_ref) | copy-start | bytes 196612
  22.4 2.7 %copy-start.6 = (bf16[384,384]{1,0:T(8,128)(2,1)S(1)}, bf16[384,384]{1,0:T(8,128)(2,1)}, u32[]{:S(2)}) copy-start(bf16[384,384]{1,0:T(8,128)(2,1)} %constant.11.clone.spread_ref) | copy-start | bytes 884740
  25.1 18.2 %copy-start.5 = (bf16[640,576]{1,0:T(8,128)(2,1)S(1)}, bf16[640,576]{1,0:T(8,128)(2,1)}, u32[]{:S(2)}) copy-start(bf16[640,576]{1,0:T(8,128)(2,1)} %constant.13.clone.order_ref) | copy-start | bytes 2211844
  28.1 14.6 %collective-permute-start.3 = (bf16[976,128]{1,0:T(8,128)(2,1)S(1)}, bf16[976,128]{1,0:T(8,128)(2,1)S(1)}, u32[]{:S(2)}, u32[]{:S(2)}) collective-permute-start(bf16[976,128]{1,0:T(8,128)(2,1)S(1)} %get-tuple-element.56), channel_id=1, source_target_pairs={{0,1},{1,2},{2,3},{3,0},{4,5},{5,6},{6,7},{7,4},{8,9},{9,10},{10,1... | collective-permute-start | bytes 749576 | tf_op jit(solution)/shard_map/ppermute | solution.py:487
  28.2 14.5 %collective-permute-start.4 = (bf16[976,128]{1,0:T(8,128)(2,1)S(1)}, bf16[976,128]{1,0:T(8,128)(2,1)S(1)}, u32[]{:S(2)}, u32[]{:S(2)}) collective-permute-start(bf16[976,128]{1,0:T(8,128)(2,1)S(1)} %get-tuple-element.57), channel_id=1, source_target_pairs={{0,2},{1,3},{2,0},{3,1},{4,6},{5,7},{6,4},{7,5},{8,10},{9,11},{10,... | collective-permute-start | bytes 749576 | tf_op jit(solution)/shard_map/ppermute | solution.py:487
  30.4 13.0 %collective-permute-start.5 = (bf16[976,128]{1,0:T(8,128)(2,1)S(1)}, bf16[976,128]{1,0:T(8,128)(2,1)S(1)}, u32[]{:S(2)}, u32[]{:S(2)}) collective-permute-start(bf16[976,128]{1,0:T(8,128)(2,1)S(1)} %get-tuple-element.58), channel_id=1, source_target_pairs={{0,3},{1,0},{2,1},{3,2},{4,7},{5,4},{6,5},{7,6},{8,11},{9,8},{10,9... | collective-permute-start | bytes 749576 | tf_op jit(solution)/shard_map/ppermute | solution.py:487
  31.7 13.7 %collective-permute-start.10 = (bf16[384,768]{1,0:T(8,128)(2,1)S(1)}, bf16[384,768]{1,0:T(8,128)(2,1)S(1)}, u32[]{:S(2)}, u32[]{:S(2)}) collective-permute-start(bf16[384,768]{1,0:T(8,128)(2,1)S(1)} %get-tuple-element.67), channel_id=1, source_target_pairs={{0,4},{4,0},{8,12},{12,8},{16,20},{20,16},{24,28},{28,24},{32,36},... | collective-permute-start | bytes 1769480 | tf_op jit(solution)/shard_map/ppermute | solution.py:534
  45.3 3.2 %collective-permute-start.6 = (bf16[320,768]{1,0:T(8,128)(2,1)S(1)}, bf16[320,768]{1,0:T(8,128)(2,1)S(1)}, u32[]{:S(2)}, u32[]{:S(2)}) collective-permute-start(bf16[320,768]{1,0:T(8,128)(2,1)S(1)} %get-tuple-element.61), channel_id=1, source_target_pairs={{0,4},{4,0},{8,12},{12,8},{16,20},{20,16},{24,28},{28,24},{32,36},... | collective-permute-start | bytes 1474568 | tf_op jit(solution)/shard_map/ppermute | solution.py:554
  45.6 13.4 %copy-start.7 = (bf16[128,96]{1,0:T(8,128)(2,1)S(1)}, bf16[128,96]{1,0:T(8,128)(2,1)}, u32[]{:S(2)}) copy-start(bf16[128,96]{1,0:T(8,128)(2,1)} %constant.12.clone.order_ref) | copy-start | bytes 73732
  45.6 6.7 %collective-permute-start.11 = (bf16[96,768]{1,0:T(8,128)(2,1)S(1)}, bf16[96,768]{1,0:T(8,128)(2,1)S(1)}, u32[]{:S(2)}, u32[]{:S(2)}) collective-permute-start(bf16[96,768]{1,0:T(8,128)(2,1)S(1)} %get-tuple-element.69), channel_id=1, source_target_pairs={{0,8},{4,12},{8,16},{12,20},{16,24},{20,28},{24,0},{28,4},{32,40},... | collective-permute-start | bytes 442376 | tf_op jit(solution)/shard_map/ppermute | solution.py:487
  45.9 10.0 %collective-permute-start.12 = (bf16[96,768]{1,0:T(8,128)(2,1)S(1)}, bf16[96,768]{1,0:T(8,128)(2,1)S(1)}, u32[]{:S(2)}, u32[]{:S(2)}) collective-permute-start(bf16[96,768]{1,0:T(8,128)(2,1)S(1)} %get-tuple-element.70), channel_id=1, source_target_pairs={{0,16},{4,20},{8,24},{12,28},{16,0},{20,4},{24,8},{28,12},{32,48},... | collective-permute-start | bytes 442376 | tf_op jit(solution)/shard_map/ppermute | solution.py:487
  48.5 10.5 %collective-permute-start.13 = (bf16[96,768]{1,0:T(8,128)(2,1)S(1)}, bf16[96,768]{1,0:T(8,128)(2,1)S(1)}, u32[]{:S(2)}, u32[]{:S(2)}) collective-permute-start(bf16[96,768]{1,0:T(8,128)(2,1)S(1)} %get-tuple-element.71), channel_id=1, source_target_pairs={{0,24},{4,28},{8,0},{12,4},{16,8},{20,12},{24,16},{28,20},{32,56},... | collective-permute-start | bytes 442376 | tf_op jit(solution)/shard_map/ppermute | solution.py:487
  48.7 20.1 %copy-start.8 = (bf16[96,80]{1,0:T(8,128)(2,1)S(1)}, bf16[96,80]{1,0:T(8,128)(2,1)}, u32[]{:S(2)}) copy-start(bf16[96,80]{1,0:T(8,128)(2,1)} %constant.14.clone.order_ref) | copy-start | bytes 46084
  48.7 20.0 %collective-permute-start.7 = (bf16[80,768]{1,0:T(8,128)(2,1)S(1)}, bf16[80,768]{1,0:T(8,128)(2,1)S(1)}, u32[]{:S(2)}, u32[]{:S(2)}) collective-permute-start(bf16[80,768]{1,0:T(8,128)(2,1)S(1)} %get-tuple-element.63), channel_id=1, source_target_pairs={{0,8},{4,12},{8,16},{12,20},{16,24},{20,28},{24,0},{28,4},{32,40},... | collective-permute-start | bytes 368648 | tf_op jit(solution)/shard_map/ppermute | solution.py:487
  52.0 16.7 %collective-permute-start.8 = (bf16[80,768]{1,0:T(8,128)(2,1)S(1)}, bf16[80,768]{1,0:T(8,128)(2,1)S(1)}, u32[]{:S(2)}, u32[]{:S(2)}) collective-permute-start(bf16[80,768]{1,0:T(8,128)(2,1)S(1)} %get-tuple-element.64), channel_id=1, source_target_pairs={{0,16},{4,20},{8,24},{12,28},{16,0},{20,4},{24,8},{28,12},{32,48},... | collective-permute-start | bytes 368648 | tf_op jit(solution)/shard_map/ppermute | solution.py:487
  52.3 16.4 %collective-permute-start.9 = (bf16[80,768]{1,0:T(8,128)(2,1)S(1)}, bf16[80,768]{1,0:T(8,128)(2,1)S(1)}, u32[]{:S(2)}, u32[]{:S(2)}) collective-permute-start(bf16[80,768]{1,0:T(8,128)(2,1)S(1)} %get-tuple-element.65), channel_id=1, source_target_pairs={{0,24},{4,28},{8,0},{12,4},{16,8},{20,12},{24,16},{28,20},{32,56},... | collective-permute-start | bytes 368648 | tf_op jit(solution)/shard_map/ppermute | solution.py:487
  59.2 5.4 %collective-permute-start.14 = (bf16[32,768]{1,0:T(8,128)(2,1)S(1)}, bf16[32,768]{1,0:T(8,128)(2,1)S(1)}, u32[]{:S(2)}, u32[]{:S(2)}) collective-permute-start(bf16[32,768]{1,0:T(8,128)(2,1)S(1)} %get-tuple-element.73), channel_id=1, source_target_pairs={{0,1},{1,2},{2,3},{3,0},{4,5},{5,6},{6,7},{7,4},{8,9},{9,10},{10,1... | collective-permute-start | bytes 147464 | tf_op jit(solution)/shard_map/ppermute | solution.py:487
  59.6 6.2 %collective-permute-start.15 = (bf16[32,768]{1,0:T(8,128)(2,1)S(1)}, bf16[32,768]{1,0:T(8,128)(2,1)S(1)}, u32[]{:S(2)}, u32[]{:S(2)}) collective-permute-start(bf16[32,768]{1,0:T(8,128)(2,1)S(1)} %get-tuple-element.74), channel_id=1, source_target_pairs={{0,2},{1,3},{2,0},{3,1},{4,6},{5,7},{6,4},{7,5},{8,10},{9,11},{10,... | collective-permute-start | bytes 147464 | tf_op jit(solution)/shard_map/ppermute | solution.py:487
  64.6 4.1 %collective-permute-start.16 = (bf16[32,768]{1,0:T(8,128)(2,1)S(1)}, bf16[32,768]{1,0:T(8,128)(2,1)S(1)}, u32[]{:S(2)}, u32[]{:S(2)}) collective-permute-start(bf16[32,768]{1,0:T(8,128)(2,1)S(1)} %get-tuple-element.75), channel_id=1, source_target_pairs={{0,3},{1,0},{2,1},{3,2},{4,7},{5,4},{6,5},{7,6},{8,11},{9,8},{10,9... | collective-permute-start | bytes 147464 | tf_op jit(solution)/shard_map/ppermute | solution.py:487

commit v4 on v3

--- a/solution.py
+++ b/solution.py
@@ -67,14 +67,23 @@
     )
 
 
+def class_order():
+    shape = (TOK, TOK)
+    return (iota(shape, 1) == class_major(iota(shape, 0))).astype(F32).astype(BF)
+
+
+def masked_rows(positions, masked):
+    hits = jnp.where(positions == masked, 1.0, 0.0)
+    return jnp.broadcast_to(jnp.max(hits, axis=1, keepdims=True), (TOK, TOK))
+
+
 def prep_kernel(
-    tiles_hbm, masked_hbm, gain_hbm, w_in_hbm, tiles_out, hidden_out, normed_out, flag_out,
-    raw, masked, gain, w_in, sems,
+    tiles_hbm, masked_hbm, gain_hbm, w_in_hbm, hidden_out, normed_out, tiles, masked, gain, w_in, sems
 ):
     blocks = w_in_hbm.shape[0] // 256
     loads = [
-        pltpu.make_async_copy(tiles_hbm.at[0], raw, sems.at[0]),
-        pltpu.make_async_copy(masked_hbm, masked, sems.at[1]),
+        pltpu.make_async_copy(masked_hbm, masked, sems.at[0]),
+        pltpu.make_async_copy(tiles_hbm.at[0], tiles, sems.at[1]),
         pltpu.make_async_copy(gain_hbm, gain, sems.at[2]),
     ]
     chunks = [
@@ -85,26 +94,19 @@
     ]
     for copy in loads + chunks:
         copy.start()
-    pos0 = lax.axis_index("seq") * TOK
-    shape = (TOK, TOK)
-    order = (iota(shape, 1) == class_major(iota(shape, 0))).astype(F32).astype(BF)
+    order = class_order()
+    positions = lax.axis_index("seq") * TOK + iota((TOK, TOK), 0)
+    loads[0].wait()
+    flag = masked_rows(positions, masked[...])[:, 0:1] > 0.5
     loads[1].wait()
-    positions = pos0 + class_major(iota(shape, 0))
-    hits = jnp.where(positions == masked[...], 1.0, 0.0)
-    hit = jnp.max(hits, axis=1, keepdims=True)
-    flag_out[...] = jnp.broadcast_to(hit, shape)
-    flag = hit > 0.5
-    loads[0].wait()
     hidden = jnp.zeros((TOK, D), F32)
     for i in range(blocks):
         cols = slice(256 * i, 256 * (i + 1))
-        tiles = nn(order, raw[:, cols])
-        tiles_out[:, cols] = tiles.astype(BF)
+        inputs = jnp.where(flag, jnp.zeros((), BF), tiles[:, cols])
         chunks[i].wait()
-        hidden += nn(jnp.where(flag, 0.0, tiles).astype(BF), w_in[cols])
-    hidden = hidden.astype(BF)
-    hidden_out[...] = hidden
-    hidden_f = hidden.astype(F32)
+        hidden += nn(inputs, w_in[cols])
+    hidden_f = nn(order, hidden.astype(BF))
+    hidden_out[...] = hidden_f.astype(BF)
     scale_rows = lax.rsqrt(jnp.mean(hidden_f * hidden_f, axis=1, keepdims=True) + NORM_EPS)
     loads[2].wait()
     normed_out[...] = (hidden_f * scale_rows * gain[...].reshape(1, D)).astype(BF)
@@ -138,9 +140,14 @@
     return out
 
 
-def near_kernel(count_ref, normed_ref, w_qkv_ref, proj_ref, exp_ref, top_ref, sum_ref):
+def near_kernel(
+    count_ref, normed_ref, w_qkv_ref, tiles_ref, masked_ref,
+    proj_ref, exp_ref, top_ref, sum_ref, tiles_out, flag_ref,
+):
     count = count_ref[0]
     pos0 = lax.axis_index("seq") * TOK
+    flag_ref[...] = masked_rows(pos0 + class_major(iota((TOK, TOK), 0)), masked_ref[...])
+    tiles_out[...] = nn(class_order(), tiles_ref[0]).astype(BF)
     normed = normed_ref[...]
     for block in range(3 * D // 256):
         cols = slice(block * 256, (block + 1) * 256)
@@ -299,7 +306,7 @@
         ref[SECTIONS * SUB :] = loss_ref[...]
 
 
-def product_kernel(x0, x1, x2, x3, pn_ref, order_ref, mine_ref, other_ref, got, left):
+def product_kernel(x0, x1, x2, x3, pn_ref, order_ref, wait_ref, mine_ref, other_ref, got, left):
     seq = lax.axis_index("seq")
     core = lax.axis_index("slide") & 1
     for turn, x_ref in enumerate((x0, x1, x2, x3)):
@@ -347,7 +354,7 @@
     return jnp.where(row >= 72, pieces, total), loss
 
 
-def core_kernel(mine_ref, other_ref, y0, y1, y2, y3):
+def core_kernel(mine_ref, other_ref, wait1, wait2, wait3, y0, y1, y2, y3):
     y = (lax.axis_index("slide") >> 1) & 3
     for turn, ref in enumerate((y0, y1, y2, y3)):
         rows = pl.ds(pl.multiple_of(((y + turn) & 3) * YROWS, 16), YROWS)
@@ -364,7 +371,7 @@
         out_ref[6 + half] = (out[16 * half : 16 * (half + 1)] + tail).astype(BF)
 
 
-def out_core_kernel(mine_ref, other_ref, y0, y1, y2, y3):
+def out_core_kernel(mine_ref, other_ref, wait_ref, y0, y1, y2, y3):
     y = (lax.axis_index("slide") >> 1) & 3
     for turn, ref in enumerate((y0, y1, y2, y3)):
         rows = pl.ds(pl.multiple_of(((y + turn) & 3) * SUB, 16), SUB)
@@ -443,11 +450,13 @@
 SMEM = pl.BlockSpec(memory_space=pltpu.SMEM)
 VMEM = pl.BlockSpec(memory_space=pltpu.VMEM)
 HBM = pl.BlockSpec(memory_space=pltpu.HBM)
-
-
-def call(kernel, out_shapes, args, scratch=(), micros=1.0, specs=None, grant=24):
+ANY = pl.BlockSpec(memory_space=pl.ANY)
+
+
+def call(kernel, out_shapes, args, scratch=(), micros=1.0, specs=None, grant=24, unread=0):
     if specs is None:
         specs = [SMEM if a.dtype == jnp.int32 else VMEM for a in args]
+        specs = specs[: len(specs) - unread] + [ANY] * unread
     return pl.pallas_call(
         kernel,
         out_shape=out_shapes,
@@ -489,9 +498,9 @@
 
 def per_device(embeddings, tile_counts, masked_tiles, w_in, norm_gain, w_qkv, w_out):
     inv_count = 1.0 / (lax.axis_size("slide") * masked_tiles.shape[1])
-    tiles, hidden, normed, flag = call(
+    hidden, normed = call(
         prep_kernel,
-        [shape(TOK, 2 * D), shape(TOK, D), shape(TOK, D), shape(TOK, TOK, dtype=F32)],
+        [shape(TOK, D), shape(TOK, D)],
         (embeddings, masked_tiles, norm_gain, w_in),
         [
             pltpu.VMEM((TOK, 2 * D), BF),
@@ -507,8 +516,13 @@
     norms = swap([normed] * N_SEQ, "seq", SEQ_TURNS)
     scores = shape(GROUPS, TOK, RATE * TOK, dtype=F32)
     rows = shape(HEADS, TOK, dtype=F32)
-    projected, exps, tops, sums = call(
-        near_kernel, [shape(TOK, 3 * D), scores, rows, rows], (tile_counts, normed, w_qkv), (), 5.0
+    projected, exps, tops, sums, tiles, flag = call(
+        near_kernel,
+        [shape(TOK, 3 * D), scores, rows, rows, shape(TOK, 2 * D), shape(TOK, TOK, dtype=F32)],
+        (tile_counts, normed, w_qkv, embeddings, masked_tiles),
+        (),
+        5.0,
+        [SMEM] + [VMEM] * 4,
     )
     pn, fk, fv, pnear, pfar, attended = call(
         far_kernel,
@@ -540,19 +554,20 @@
         4.0,
     )
     got = swap(sent, "seq", SEQ_TURNS)
-    out = call(out_core_kernel, [shape(SUB, D)] * NY, (out_mine, out_other))
+    out = call(out_core_kernel, [shape(SUB, D)] * NY, (out_mine, out_other, sent[0]), unread=1)
     out = swap(out, "slide", Y_TURNS)
-    out = call(out_y_kernel, [shape(32, D)] * N_SEQ, (*out, out_pad_order()))
-    out = swap(out, "seq", SEQ_TURNS)
+    out_sums = call(out_y_kernel, [shape(32, D)] * N_SEQ, (*out, out_pad_order()))
+    out = swap(out_sums, "seq", SEQ_TURNS)
     mine, other = call(
         product_kernel,
         [shape(NY * YROWS, D)] * 2,
-        (*got, pn, product_order()),
+        (*got, pn, product_order(), out_sums[0]),
         [pltpu.VMEM((N_SEQ, XROWS, TOK), BF), pltpu.VMEM((6 * SUB, N_SEQ * TOK), BF)],
         3.0,
+        unread=1,
     )
     other = lax.ppermute(other, "slide", CORE_PAIRS)
-    by_y = call(core_kernel, [shape(YROWS, D)] * NY, (mine, other))
+    by_y = call(core_kernel, [shape(YROWS, D)] * NY, (mine, other, *out[1:]), unread=3)
     by_y = swap(by_y, "slide", Y_TURNS)
     (by_z,) = call(y_kernel, [shape(NZ, 16, D)], (*by_y, *out, pad_order()))
     by_z = lax.all_to_all(by_z, "slide", 0, 0, tiled=True, axis_index_groups=Z_GROUPS)

time: 87.9 us -> 83.4 us (0.949)
  the two profiles are of different devices: /device:TPU:24 before, /device:TPU:2 now
where the time goes in v4:
time: 83.4 us; the launch traced here: 81.8 us
  starting transfers between devices  27.2 us (33%)
  blocking collectives  18 us (22%)
  waiting for transfers between devices  17.6 us (21%)
  Pallas kernels  16.4 us (20%)
  between operations  1.53 us (2%)
  local copies, waits for them, and re-layouts  0.97 us (1%)
    ppermute x15, starting transfers between devices, swap(): lax.ppermute(arrays[t], axis, turns[t])  27 us
    all_to_all x1, blocking collectives, per_device(): lax.all_to_all(by_z, 'slide', 0, 0, tiled=True, axis_index_groups=Z_GROUPS)  18 us
    ppermute x15, waiting for transfers between devices, swap(): lax.ppermute(arrays[t], axis, turns[t])  17.6 us
    pallas_call x11, Pallas kernels, call(): pl.pallas_call(kernel, out_shape=out_shapes, in_specs=specs, out_specs=[V...  16.4 us
  transfers between devices with their start and end apart: 17, of which 10 were waited for; matrix products, arithmetic and copies ran while one was open for 0% of the time, Pallas kernels for 5%

profile of v4, /device:TPU:2, one launch (start us, length us, event | category | flops | bytes accessed | tf_op | source)
XLA Modules:
  0.0 81.8 jit_solution(12354860542290756585)
XLA Ops:
  0.7 3.4 %shard_map.131 = (bf16[128,768]{1,0:T(8,128)(2,1)}, bf16[128,768]{1,0:T(8,128)(2,1)}) custom-call(bf16[1,128,1536]{2,1,0:T(8,128)(2,1)} %tiles_ref.1, s32[1,128]{1,0:T(1,128)} %masked_ref.1, f32[768]{0:T(1024)} %gain_hbm.1, bf16[1536,768]{1,0:T(8,128)(2,1)} %w_in_ref.1), custom_call_target="tpu_custom_call" | custom-call | flops 2000000000 | bytes 2000000 | tf_op jit(solution)/shard_map/pallas_call | solution.py:460
  4.1 2.3 %collective-permute-start.2 = (bf16[128,768]{1,0:T(8,128)(2,1)}, bf16[128,768]{1,0:T(8,128)(2,1)S(1)}, u32[]{:S(2)}, u32[]{:S(2)}) collective-permute-start(bf16[128,768]{1,0:T(8,128)(2,1)} %get-tuple-element.40.normed_ref.n0), channel_id=1, source_target_pairs={{0,3},{1,0},{2,1},{3,2},{4,7},{5,4},{6,5},{7,6},{8,11},{9,8},{10,9... | collective-permute-start | bytes 589832 | tf_op jit(solution)/shard_map/ppermute | solution.py:496
  6.4 0.7 collective-permute-start.1
  7.1 1.8 %collective-permute-start = (bf16[128,768]{1,0:T(8,128)(2,1)}, bf16[128,768]{1,0:T(8,128)(2,1)S(1)}, u32[]{:S(2)}, u32[]{:S(2)}) collective-permute-start(bf16[128,768]{1,0:T(8,128)(2,1)} %get-tuple-element.40.normed_ref.n0), channel_id=1, source_target_pairs={{0,1},{1,2},{2,3},{3,0},{4,5},{5,6},{6,7},{7,4},{8,9},{9,10},{10,1... | collective-permute-start | bytes 589832 | tf_op jit(solution)/shard_map/ppermute | solution.py:496
  9.6 0.9 %copy-done.4 = bf16[128,768]{1,0:T(8,128)(2,1)S(1)} copy-done((bf16[128,768]{1,0:T(8,128)(2,1)S(1)}, bf16[128,768]{1,0:T(8,128)(2,1)}, u32[]{:S(2)}) %copy-start.4) | copy-done | bytes 196632
  10.5 1.2 %shard_map.132 = (bf16[128,2304]{1,0:T(8,128)(2,1)S(1)}, f32[4,128,512]{2,1,0:T(8,128)S(1)}, f32[16,128]{1,0:T(8,128)S(1)}, f32[16,128]{1,0:T(8,128)S(1)}, bf16[...) custom-call(s32[1]{0:T(128)S(6)} %copy.14.count_ref, bf16[128,768]{1,0:T(8,128)(2,1)S(1)} %copy-done.4, ...), custom_call_target="tpu_custom_call" | custom-call | flops 5000000000 | bytes 5000000 | tf_op jit(solution)/shard_map/pallas_call | solution.py:460
  11.7 0.0 collective-permute-done.2.n3
  11.7 4.5 %collective-permute-done.1.n2 = bf16[128,768]{1,0:T(8,128)(2,1)S(1)} collective-permute-done((bf16[128,768]{1,0:T(8,128)(2,1)}, bf16[128,768]{1,0:T(8,128)(2,1)S(1)}, u32[]{:S(2)}, u32[]{:S(2)}) %collective-permute-start.1) | collective-permute-done | bytes 196640 | tf_op jit(solution)/shard_map/ppermute | solution.py:496
  16.2 0.9 %collective-permute-done.n1 = bf16[128,768]{1,0:T(8,128)(2,1)S(1)} collective-permute-done((bf16[128,768]{1,0:T(8,128)(2,1)}, bf16[128,768]{1,0:T(8,128)(2,1)S(1)}, u32[]{:S(2)}, u32[]{:S(2)}) %collective-permute-start) | collective-permute-done | bytes 196640 | tf_op jit(solution)/shard_map/ppermute | solution.py:496
  17.1 2.7 %shard_map.133 = (bf16[4,128,768]{2,1,0:T(8,128)(2,1)S(1)}, bf16[128,768]{1,0:T(8,128)(2,1)S(1)}, bf16[128,768]{1,0:T(8,128)(2,1)S(1)}, f32[4,128,512]{2,1,0:T(8...) custom-call(s32[1]{0:T(128)S(6)} %copy.14.count_ref, bf16[128,768]{1,0:T(8,128)(2,1)S(1)} %copy-done.4, ...), custom_call_target="tpu_custom_call" | custom-call | flops 4000000000 | bytes 4000000 | tf_op jit(solution)/shard_map/pallas_call | solution.py:460
  19.8 0.0 copy-start.8
  19.8 2.7 %shard_map.134 = (bf16[128,768]{1,0:T(8,128)(2,1)S(1)}, bf16[16,128]{1,0:T(8,128)(2,1)S(1)}, bf16[384,768]{1,0:T(8,128)(2,1)S(1)}, bf16[384,768]{1,0:T(8,128)(2,1)S(1)}) custom-call(bf16[128,768]{1,0:T(8,128)(2,1)S(1)} %get-tuple-element.49.att_ref, bf16[128,768]{1,0:T(8,128)(2,1)S(1)} %copy-done.11, bf16[128,1536]{1,0:T(8,128)(2,1)S(1)} %get-tuple-element.51.tiles_ref, ...), custom_call_target="tpu_custom_call" | custom-call | flops 3000000000 | bytes 3000000 | tf_op jit(solution)/shard_map/pallas_call | solution.py:460
  22.5 0.1 collective-permute-start.6
  22.7 3.0 %shard_map.135 = (bf16[976,128]{1,0:T(8,128)(2,1)S(1)}, bf16[976,128]{1,0:T(8,128)(2,1)S(1)}, bf16[976,128]{1,0:T(8,128)(2,1)S(1)}, bf16[976,128]{1,0:T(8,128)(2,1)S(1)}) custom-call(bf16[128,2304]{1,0:T(8,128)(2,1)S(1)} %get-tuple-element.41.proj_ref, bf16[128,768]{1,0:T(8,128)(2,1)S(1)} %get-tuple-element.45.fk_ref, ...), custom_call_target="tpu_custom_call" | custom-call | flops 4000000000 | bytes 4000000 | tf_op jit(solution)/shard_map/pallas_call | solution.py:460
  25.6 0.0 copy-start.9
  25.7 0.2 shard_map.136
  25.8 0.0 copy-start.7
  25.8 1.8 %collective-permute-start.7 = (bf16[96,768]{1,0:T(8,128)(2,1)S(1)}, bf16[96,768]{1,0:T(8,128)(2,1)S(1)}, u32[]{:S(2)}, u32[]{:S(2)}) collective-permute-start(bf16[96,768]{1,0:T(8,128)(2,1)S(1)} %get-tuple-element.63), channel_id=1, source_target_pairs={{0,8},{4,12},{8,16},{12,20},{16,24},{20,28},{24,0},{28,4},{32,40},... | collective-permute-start | bytes 442376 | tf_op jit(solution)/shard_map/ppermute | solution.py:496
  27.7 1.5 %collective-permute-start.3 = (bf16[976,128]{1,0:T(8,128)(2,1)S(1)}, bf16[976,128]{1,0:T(8,128)(2,1)S(1)}, u32[]{:S(2)}, u32[]{:S(2)}) collective-permute-start(bf16[976,128]{1,0:T(8,128)(2,1)S(1)} %get-tuple-element.56), channel_id=1, source_target_pairs={{0,1},{1,2},{2,3},{3,0},{4,5},{5,6},{6,7},{7,4},{8,9},{9,10},{10,1... | collective-permute-start | bytes 749576 | tf_op jit(solution)/shard_map/ppermute | solution.py:496
  29.1 3.3 %collective-permute-start.4 = (bf16[976,128]{1,0:T(8,128)(2,1)S(1)}, bf16[976,128]{1,0:T(8,128)(2,1)S(1)}, u32[]{:S(2)}, u32[]{:S(2)}) collective-permute-start(bf16[976,128]{1,0:T(8,128)(2,1)S(1)} %get-tuple-element.57), channel_id=1, source_target_pairs={{0,2},{1,3},{2,0},{3,1},{4,6},{5,7},{6,4},{7,5},{8,10},{9,11},{10,... | collective-permute-start | bytes 749576 | tf_op jit(solution)/shard_map/ppermute | solution.py:496
  32.4 0.1 collective-permute-start.5
  32.5 2.9 %collective-permute-start.8 = (bf16[96,768]{1,0:T(8,128)(2,1)S(1)}, bf16[96,768]{1,0:T(8,128)(2,1)S(1)}, u32[]{:S(2)}, u32[]{:S(2)}) collective-permute-start(bf16[96,768]{1,0:T(8,128)(2,1)S(1)} %get-tuple-element.64), channel_id=1, source_target_pairs={{0,16},{4,20},{8,24},{12,28},{16,0},{20,4},{24,8},{28,12},{32,48},... | collective-permute-start | bytes 442376 | tf_op jit(solution)/shard_map/ppermute | solution.py:496
  35.4 0.0 collective-permute-done.7.y1
  35.4 1.3 %collective-permute-start.9 = (bf16[96,768]{1,0:T(8,128)(2,1)S(1)}, bf16[96,768]{1,0:T(8,128)(2,1)S(1)}, u32[]{:S(2)}, u32[]{:S(2)}) collective-permute-start(bf16[96,768]{1,0:T(8,128)(2,1)S(1)} %get-tuple-element.65), channel_id=1, source_target_pairs={{0,24},{4,28},{8,0},{12,4},{16,8},{20,12},{24,16},{28,20},{32,56},... | collective-permute-start | bytes 442376 | tf_op jit(solution)/shard_map/ppermute | solution.py:496
  36.8 2.6 %collective-permute-done.8.y2 = bf16[96,768]{1,0:T(8,128)(2,1)S(1)} collective-permute-done((bf16[96,768]{1,0:T(8,128)(2,1)S(1)}, bf16[96,768]{1,0:T(8,128)(2,1)S(1)}, u32[]{:S(2)}, u32[]{:S(2)}) %collective-permute-start.8) | collective-permute-done | bytes 147488 | tf_op jit(solution)/shard_map/ppermute | solution.py:496
  39.3 2.3 %collective-permute-done.9.y3 = bf16[96,768]{1,0:T(8,128)(2,1)S(1)} collective-permute-done((bf16[96,768]{1,0:T(8,128)(2,1)S(1)}, bf16[96,768]{1,0:T(8,128)(2,1)S(1)}, u32[]{:S(2)}, u32[]{:S(2)}) %collective-permute-start.9) | collective-permute-done | bytes 147488 | tf_op jit(solution)/shard_map/ppermute | solution.py:496
  41.6 0.3 shard_map.137
  41.9 0.0 collective-permute-done.3.x1
  41.9 2.0 %collective-permute-done.5.x3 = bf16[976,128]{1,0:T(8,128)(2,1)S(1)} collective-permute-done((bf16[976,128]{1,0:T(8,128)(2,1)S(1)}, bf16[976,128]{1,0:T(8,128)(2,1)S(1)}, u32[]{:S(2)}, u32[]{:S(2)}) %collective-permute-start.5) | collective-permute-done | bytes 249888 | tf_op jit(solution)/shard_map/ppermute | solution.py:496
  43.9 2.0 %shard_map.138 = (bf16[320,768]{1,0:T(8,128)(2,1)S(1)}, bf16[320,768]{1,0:T(8,128)(2,1)S(1)}) custom-call(bf16[976,128]{1,0:T(8,128)(2,1)S(1)} %get-tuple-element.55.wait_ref.x0, bf16[976,128]{1,0:T(8,128)(2,1)S(1)} %collective-permute-done.3.x1, bf16[976,128]{1,0:T(8,128)(2,1)S(1)} %collective-permute-done.4.x2, ...), custom_call_target="tpu_custom_call" | custom-call | flops 3000000000 | bytes 3000000 | tf_op jit(solution)/shard_map/pallas_call | solution.py:460
  45.9 0.0 copy-start.10
  45.9 0.1 collective-permute-start.10
  46.0 0.7 collective-permute-start.11
  46.7 3.2 %collective-permute-start.12 = (bf16[32,768]{1,0:T(8,128)(2,1)S(1)}, bf16[32,768]{1,0:T(8,128)(2,1)S(1)}, u32[]{:S(2)}, u32[]{:S(2)}) collective-permute-start(bf16[32,768]{1,0:T(8,128)(2,1)S(1)} %get-tuple-element.70), channel_id=1, source_target_pairs={{0,2},{1,3},{2,0},{3,1},{4,6},{5,7},{6,4},{7,5},{8,10},{9,11},{10,... | collective-permute-start | bytes 147464 | tf_op jit(solution)/shard_map/ppermute | solution.py:496
  49.9 1.7 %collective-permute-start.13 = (bf16[32,768]{1,0:T(8,128)(2,1)S(1)}, bf16[32,768]{1,0:T(8,128)(2,1)S(1)}, u32[]{:S(2)}, u32[]{:S(2)}) collective-permute-start(bf16[32,768]{1,0:T(8,128)(2,1)S(1)} %get-tuple-element.71), channel_id=1, source_target_pairs={{0,3},{1,0},{2,1},{3,2},{4,7},{5,4},{6,5},{7,6},{8,11},{9,8},{10,9... | collective-permute-start | bytes 147464 | tf_op jit(solution)/shard_map/ppermute | solution.py:496
  51.6 0.0 collective-permute-done.11.wait1.o1
  51.6 1.1 %collective-permute-done.12.wait2.o2 = bf16[32,768]{1,0:T(8,128)(2,1)S(1)} collective-permute-done((bf16[32,768]{1,0:T(8,128)(2,1)S(1)}, bf16[32,768]{1,0:T(8,128)(2,1)S(1)}, u32[]{:S(2)}, u32[]{:S(2)}) %collective-permute-start.12) | collective-permute-done | bytes 49184 | tf_op jit(solution)/shard_map/ppermute | solution.py:496
  52.7 1.3 %collective-permute-done.13.wait3.o3 = bf16[32,768]{1,0:T(8,128)(2,1)S(1)} collective-permute-done((bf16[32,768]{1,0:T(8,128)(2,1)S(1)}, bf16[32,768]{1,0:T(8,128)(2,1)S(1)}, u32[]{:S(2)}, u32[]{:S(2)}) %collective-permute-start.13) | collective-permute-done | bytes 49184 | tf_op jit(solution)/shard_map/ppermute | solution.py:496
  54.0 0.2 shard_map.139
  54.2 1.6 %collective-permute-start.14 = (bf16[80,768]{1,0:T(8,128)(2,1)S(1)}, bf16[80,768]{1,0:T(8,128)(2,1)S(1)}, u32[]{:S(2)}, u32[]{:S(2)}) collective-permute-start(bf16[80,768]{1,0:T(8,128)(2,1)S(1)} %get-tuple-element.73), channel_id=1, source_target_pairs={{0,8},{4,12},{8,16},{12,20},{16,24},{20,28},{24,0},{28,4},{32,40},... | collective-permute-start | bytes 368648 | tf_op jit(solution)/shard_map/ppermute | solution.py:496
  55.8 1.7 %collective-permute-start.15 = (bf16[80,768]{1,0:T(8,128)(2,1)S(1)}, bf16[80,768]{1,0:T(8,128)(2,1)S(1)}, u32[]{:S(2)}, u32[]{:S(2)}) collective-permute-start(bf16[80,768]{1,0:T(8,128)(2,1)S(1)} %get-tuple-element.74), channel_id=1, source_target_pairs={{0,16},{4,20},{8,24},{12,28},{16,0},{20,4},{24,8},{28,12},{32,48},... | collective-permute-start | bytes 368648 | tf_op jit(solution)/shard_map/ppermute | solution.py:496
  57.5 2.3 %collective-permute-start.16 = (bf16[80,768]{1,0:T(8,128)(2,1)S(1)}, bf16[80,768]{1,0:T(8,128)(2,1)S(1)}, u32[]{:S(2)}, u32[]{:S(2)}) collective-permute-start(bf16[80,768]{1,0:T(8,128)(2,1)S(1)} %get-tuple-element.75), channel_id=1, source_target_pairs={{0,24},{4,28},{8,0},{12,4},{16,8},{20,12},{24,16},{28,20},{32,56},... | collective-permute-start | bytes 368648 | tf_op jit(solution)/shard_map/ppermute | solution.py:496
  59.8 1.4 %collective-permute-done.14.y1 = bf16[80,768]{1,0:T(8,128)(2,1)S(1)} collective-permute-done((bf16[80,768]{1,0:T(8,128)(2,1)S(1)}, bf16[80,768]{1,0:T(8,128)(2,1)S(1)}, u32[]{:S(2)}, u32[]{:S(2)}) %collective-permute-start.14) | collective-permute-done | bytes 122912 | tf_op jit(solution)/shard_map/ppermute | solution.py:496
  61.2 1.3 %collective-permute-done.15.y2 = bf16[80,768]{1,0:T(8,128)(2,1)S(1)} collective-permute-done((bf16[80,768]{1,0:T(8,128)(2,1)S(1)}, bf16[80,768]{1,0:T(8,128)(2,1)S(1)}, u32[]{:S(2)}, u32[]{:S(2)}) %collective-permute-start.15) | collective-permute-done | bytes 122912 | tf_op jit(solution)/shard_map/ppermute | solution.py:496
  62.5 0.4 collective-permute-done.16.y3
  62.9 0.3 shard_map.140
  63.1 18.0 %all_to_all.5.in_ref = bf16[8,16,768]{2,1,0:T(8,128)(2,1)S(1)} all-to-all(bf16[8,16,768]{2,1,0:T(8,128)(2,1)S(1)} %shard_map.140), channel_id=1, replica_groups={{0,32,64,96,128,160,192,224},{4,36,68,100,132,164,196,228},{8,40,72,104..., dimensions={0} | all-to-all | bytes 393216 | tf_op jit(solution)/shard_map/all_to_all | solution.py:573
  81.2 0.7 shard_map.141
  (22 shorter events, 0.0 us)
Async XLA Ops:
  0.6 8.9 %copy-start.5 = (s32[1,128]{1,0:T(1,128)S(1)}, s32[1,128]{1,0:T(1,128)}, u32[]{:S(2)}) copy-start(s32[1,128]{1,0:T(1,128)} %masked_ref.1) | copy-start | bytes 1540
  0.6 8.9 %copy-start.3 = (bf16[1,128,1536]{2,1,0:T(8,128)(2,1)S(1)}, bf16[1,128,1536]{2,1,0:T(8,128)(2,1)}, u32[]{:S(2)}) copy-start(bf16[1,128,1536]{2,1,0:T(8,128)(2,1)} %tiles_ref.1) | copy-start | bytes 1179652
  0.7 8.9 %copy-start = (bf16[768,2304]{1,0:T(8,128)(2,1)S(1)}, bf16[768,2304]{1,0:T(8,128)(2,1)}, u32[]{:S(2)}) copy-start(bf16[768,2304]{1,0:T(8,128)(2,1)} %w_qkv_ref.3) | copy-start | bytes 10616836
  4.1 7.6 %collective-permute-start.2 = (bf16[128,768]{1,0:T(8,128)(2,1)}, bf16[128,768]{1,0:T(8,128)(2,1)S(1)}, u32[]{:S(2)}, u32[]{:S(2)}) collective-permute-start(bf16[128,768]{1,0:T(8,128)(2,1)} %get-tuple-element.40.normed_ref.n0), channel_id=1, source_target_pairs={{0,3},{1,0},{2,1},{3,2},{4,7},{5,4},{6,5},{7,6},{8,11},{9,8},{10,9... | collective-permute-start | bytes 589832 | tf_op jit(solution)/shard_map/ppermute | solution.py:496
  6.4 9.7 %collective-permute-start.1 = (bf16[128,768]{1,0:T(8,128)(2,1)}, bf16[128,768]{1,0:T(8,128)(2,1)S(1)}, u32[]{:S(2)}, u32[]{:S(2)}) collective-permute-start(bf16[128,768]{1,0:T(8,128)(2,1)} %get-tuple-element.40.normed_ref.n0), channel_id=1, source_target_pairs={{0,2},{1,3},{2,0},{3,1},{4,6},{5,7},{6,4},{7,5},{8,10},{9,11},{10,... | collective-permute-start | bytes 589832 | tf_op jit(solution)/shard_map/ppermute | solution.py:496
  7.1 9.9 %collective-permute-start = (bf16[128,768]{1,0:T(8,128)(2,1)}, bf16[128,768]{1,0:T(8,128)(2,1)S(1)}, u32[]{:S(2)}, u32[]{:S(2)}) collective-permute-start(bf16[128,768]{1,0:T(8,128)(2,1)} %get-tuple-element.40.normed_ref.n0), channel_id=1, source_target_pairs={{0,1},{1,2},{2,3},{3,0},{4,5},{5,6},{6,7},{7,4},{8,9},{9,10},{10,1... | collective-permute-start | bytes 589832 | tf_op jit(solution)/shard_map/ppermute | solution.py:496
  9.6 0.9 %copy-start.4 = (bf16[128,768]{1,0:T(8,128)(2,1)S(1)}, bf16[128,768]{1,0:T(8,128)(2,1)}, u32[]{:S(2)}) copy-start(bf16[128,768]{1,0:T(8,128)(2,1)} %get-tuple-element.40.normed_ref.n0) | copy-start | bytes 589828
  17.1 2.7 %copy-start.1 = (bf16[1536,768]{1,0:T(8,128)(2,1)S(1)}, bf16[1536,768]{1,0:T(8,128)(2,1)}, u32[]{:S(2)}) copy-start(bf16[1536,768]{1,0:T(8,128)(2,1)} %w_in_ref.1) | copy-start | bytes 7077892
  17.1 2.7 %copy-start.2 = (bf16[768,768]{1,0:T(8,128)(2,1)S(1)}, bf16[768,768]{1,0:T(8,128)(2,1)}, u32[]{:S(2)}) copy-start(bf16[768,768]{1,0:T(8,128)(2,1)} %w_out_ref.1) | copy-start | bytes 3538948
  17.1 2.8 %copy-start.6 = (bf16[768,768]{1,0:T(8,128)(2,1)S(1)}, bf16[768,768]{1,0:T(8,128)(2,1)}, u32[]{:S(2)}) copy-start(bf16[768,768]{1,0:T(8,128)(2,1)} %constant.10.clone.order_ref) | copy-start | bytes 3538948
  17.1 2.8 %copy-start.11 = (bf16[128,768]{1,0:T(8,128)(2,1)S(1)}, bf16[128,768]{1,0:T(8,128)(2,1)}, u32[]{:S(2)}) copy-start(bf16[128,768]{1,0:T(8,128)(2,1)} %get-tuple-element.50.hidden_ref) | copy-start | bytes 589828
  19.8 2.8 %copy-start.8 = (bf16[384,384]{1,0:T(8,128)(2,1)S(1)}, bf16[384,384]{1,0:T(8,128)(2,1)}, u32[]{:S(2)}) copy-start(bf16[384,384]{1,0:T(8,128)(2,1)} %constant.11.clone.spread_ref) | copy-start | bytes 884740
  22.5 3.1 %collective-permute-start.6 = (bf16[384,768]{1,0:T(8,128)(2,1)S(1)}, bf16[384,768]{1,0:T(8,128)(2,1)S(1)}, u32[]{:S(2)}, u32[]{:S(2)}) collective-permute-start(bf16[384,768]{1,0:T(8,128)(2,1)S(1)} %get-tuple-element.61), channel_id=1, source_target_pairs={{0,4},{4,0},{8,12},{12,8},{16,20},{20,16},{24,28},{28,24},{32,36},... | collective-permute-start | bytes 1769480 | tf_op jit(solution)/shard_map/ppermute | solution.py:548
  25.6 16.0 %copy-start.9 = (bf16[128,96]{1,0:T(8,128)(2,1)S(1)}, bf16[128,96]{1,0:T(8,128)(2,1)}, u32[]{:S(2)}) copy-start(bf16[128,96]{1,0:T(8,128)(2,1)} %constant.12.clone.order_ref) | copy-start | bytes 73732
  25.8 18.1 %copy-start.7 = (bf16[640,576]{1,0:T(8,128)(2,1)S(1)}, bf16[640,576]{1,0:T(8,128)(2,1)}, u32[]{:S(2)}) copy-start(bf16[640,576]{1,0:T(8,128)(2,1)} %constant.13.clone.order_ref) | copy-start | bytes 2211844
  25.8 9.6 %collective-permute-start.7 = (bf16[96,768]{1,0:T(8,128)(2,1)S(1)}, bf16[96,768]{1,0:T(8,128)(2,1)S(1)}, u32[]{:S(2)}, u32[]{:S(2)}) collective-permute-start(bf16[96,768]{1,0:T(8,128)(2,1)S(1)} %get-tuple-element.63), channel_id=1, source_target_pairs={{0,8},{4,12},{8,16},{12,20},{16,24},{20,28},{24,0},{28,4},{32,40},... | collective-permute-start | bytes 442376 | tf_op jit(solution)/shard_map/ppermute | solution.py:496
  27.7 14.2 %collective-permute-start.3 = (bf16[976,128]{1,0:T(8,128)(2,1)S(1)}, bf16[976,128]{1,0:T(8,128)(2,1)S(1)}, u32[]{:S(2)}, u32[]{:S(2)}) collective-permute-start(bf16[976,128]{1,0:T(8,128)(2,1)S(1)} %get-tuple-element.56), channel_id=1, source_target_pairs={{0,1},{1,2},{2,3},{3,0},{4,5},{5,6},{6,7},{7,4},{8,9},{9,10},{10,1... | collective-permute-start | bytes 749576 | tf_op jit(solution)/shard_map/ppermute | solution.py:496
  29.1 12.7 %collective-permute-start.4 = (bf16[976,128]{1,0:T(8,128)(2,1)S(1)}, bf16[976,128]{1,0:T(8,128)(2,1)S(1)}, u32[]{:S(2)}, u32[]{:S(2)}) collective-permute-start(bf16[976,128]{1,0:T(8,128)(2,1)S(1)} %get-tuple-element.57), channel_id=1, source_target_pairs={{0,2},{1,3},{2,0},{3,1},{4,6},{5,7},{6,4},{7,5},{8,10},{9,11},{10,... | collective-permute-start | bytes 749576 | tf_op jit(solution)/shard_map/ppermute | solution.py:496
  32.4 11.5 %collective-permute-start.5 = (bf16[976,128]{1,0:T(8,128)(2,1)S(1)}, bf16[976,128]{1,0:T(8,128)(2,1)S(1)}, u32[]{:S(2)}, u32[]{:S(2)}) collective-permute-start(bf16[976,128]{1,0:T(8,128)(2,1)S(1)} %get-tuple-element.58), channel_id=1, source_target_pairs={{0,3},{1,0},{2,1},{3,2},{4,7},{5,4},{6,5},{7,6},{8,11},{9,8},{10,9... | collective-permute-start | bytes 749576 | tf_op jit(solution)/shard_map/ppermute | solution.py:496
  32.5 6.8 %collective-permute-start.8 = (bf16[96,768]{1,0:T(8,128)(2,1)S(1)}, bf16[96,768]{1,0:T(8,128)(2,1)S(1)}, u32[]{:S(2)}, u32[]{:S(2)}) collective-permute-start(bf16[96,768]{1,0:T(8,128)(2,1)S(1)} %get-tuple-element.64), channel_id=1, source_target_pairs={{0,16},{4,20},{8,24},{12,28},{16,0},{20,4},{24,8},{28,12},{32,48},... | collective-permute-start | bytes 442376 | tf_op jit(solution)/shard_map/ppermute | solution.py:496
  35.4 6.2 %collective-permute-start.9 = (bf16[96,768]{1,0:T(8,128)(2,1)S(1)}, bf16[96,768]{1,0:T(8,128)(2,1)S(1)}, u32[]{:S(2)}, u32[]{:S(2)}) collective-permute-start(bf16[96,768]{1,0:T(8,128)(2,1)S(1)} %get-tuple-element.65), channel_id=1, source_target_pairs={{0,24},{4,28},{8,0},{12,4},{16,8},{20,12},{24,16},{28,20},{32,56},... | collective-permute-start | bytes 442376 | tf_op jit(solution)/shard_map/ppermute | solution.py:496
  45.9 17.0 %copy-start.10 = (bf16[96,80]{1,0:T(8,128)(2,1)S(1)}, bf16[96,80]{1,0:T(8,128)(2,1)}, u32[]{:S(2)}) copy-start(bf16[96,80]{1,0:T(8,128)(2,1)} %constant.14.clone.order_ref) | copy-start | bytes 46084
  45.9 8.1 %collective-permute-start.10 = (bf16[320,768]{1,0:T(8,128)(2,1)S(1)}, bf16[320,768]{1,0:T(8,128)(2,1)S(1)}, u32[]{:S(2)}, u32[]{:S(2)}) collective-permute-start(bf16[320,768]{1,0:T(8,128)(2,1)S(1)} %get-tuple-element.68), channel_id=1, source_target_pairs={{0,4},{4,0},{8,12},{12,8},{16,20},{20,16},{24,28},{28,24},{32,36},... | collective-permute-start | bytes 1474568 | tf_op jit(solution)/shard_map/ppermute | solution.py:569
  46.0 5.7 %collective-permute-start.11 = (bf16[32,768]{1,0:T(8,128)(2,1)S(1)}, bf16[32,768]{1,0:T(8,128)(2,1)S(1)}, u32[]{:S(2)}, u32[]{:S(2)}) collective-permute-start(bf16[32,768]{1,0:T(8,128)(2,1)S(1)} %get-tuple-element.69), channel_id=1, source_target_pairs={{0,1},{1,2},{2,3},{3,0},{4,5},{5,6},{6,7},{7,4},{8,9},{9,10},{10,1... | collective-permute-start | bytes 147464 | tf_op jit(solution)/shard_map/ppermute | solution.py:496
  46.7 6.1 %collective-permute-start.12 = (bf16[32,768]{1,0:T(8,128)(2,1)S(1)}, bf16[32,768]{1,0:T(8,128)(2,1)S(1)}, u32[]{:S(2)}, u32[]{:S(2)}) collective-permute-start(bf16[32,768]{1,0:T(8,128)(2,1)S(1)} %get-tuple-element.70), channel_id=1, source_target_pairs={{0,2},{1,3},{2,0},{3,1},{4,6},{5,7},{6,4},{7,5},{8,10},{9,11},{10,... | collective-permute-start | bytes 147464 | tf_op jit(solution)/shard_map/ppermute | solution.py:496
  49.9 4.1 %collective-permute-start.13 = (bf16[32,768]{1,0:T(8,128)(2,1)S(1)}, bf16[32,768]{1,0:T(8,128)(2,1)S(1)}, u32[]{:S(2)}, u32[]{:S(2)}) collective-permute-start(bf16[32,768]{1,0:T(8,128)(2,1)S(1)} %get-tuple-element.71), channel_id=1, source_target_pairs={{0,3},{1,0},{2,1},{3,2},{4,7},{5,4},{6,5},{7,6},{8,11},{9,8},{10,9... | collective-permute-start | bytes 147464 | tf_op jit(solution)/shard_map/ppermute | solution.py:496
  54.2 7.0 %collective-permute-start.14 = (bf16[80,768]{1,0:T(8,128)(2,1)S(1)}, bf16[80,768]{1,0:T(8,128)(2,1)S(1)}, u32[]{:S(2)}, u32[]{:S(2)}) collective-permute-start(bf16[80,768]{1,0:T(8,128)(2,1)S(1)} %get-tuple-element.73), channel_id=1, source_target_pairs={{0,8},{4,12},{8,16},{12,20},{16,24},{20,28},{24,0},{28,4},{32,40},... | collective-permute-start | bytes 368648 | tf_op jit(solution)/shard_map/ppermute | solution.py:496
  55.8 6.7 %collective-permute-start.15 = (bf16[80,768]{1,0:T(8,128)(2,1)S(1)}, bf16[80,768]{1,0:T(8,128)(2,1)S(1)}, u32[]{:S(2)}, u32[]{:S(2)}) collective-permute-start(bf16[80,768]{1,0:T(8,128)(2,1)S(1)} %get-tuple-element.74), channel_id=1, source_target_pairs={{0,16},{4,20},{8,24},{12,28},{16,0},{20,4},{24,8},{28,12},{32,48},... | collective-permute-start | bytes 368648 | tf_op jit(solution)/shard_map/ppermute | solution.py:496
  57.5 5.3 %collective-permute-start.16 = (bf16[80,768]{1,0:T(8,128)(2,1)S(1)}, bf16[80,768]{1,0:T(8,128)(2,1)S(1)}, u32[]{:S(2)}, u32[]{:S(2)}) collective-permute-start(bf16[80,768]{1,0:T(8,128)(2,1)S(1)} %get-tuple-element.75), channel_id=1, source_target_pairs={{0,24},{4,28},{8,0},{12,4},{16,8},{20,12},{24,16},{28,20},{32,56},... | collective-permute-start | bytes 368648 | tf_op jit(solution)/shard_map/ppermute | solution.py:496

commit v5 on v4

--- a/solution.py
+++ b/solution.py
@@ -181,18 +181,21 @@
     seq = lax.axis_index("seq")
     for turn, ref in enumerate((n0, n1, n2, n3)):
         pn_ref[(seq - turn) & 3] = ref[...]
-    pn_all = pn_ref[...].reshape(N_SEQ * TOK, D)
+    others = jnp.concatenate([n1[...], n2[...], n3[...]], 0)
     for part, far_ref in enumerate((fk_ref, fv_ref)):
         for block in range(D // 256):
+            cols = slice(block * 256, (block + 1) * 256)
             first = (1 + part) * D + block * 256
-            every = nn(pn_all, w_qkv_ref[:, first : first + 256])
+            every = nn(others, w_qkv_ref[:, first : first + 256]).astype(BF)
             lane_class = ((iota((FAR, 256), 1) + block * 256) // HD) & 3
-            for src in range(N_SEQ):
-                base = src * TOK
-                pieces = [every[base + FAR * r : base + FAR * (r + 1)] for r in range(RATE)]
-                far_ref[src * FAR : (src + 1) * FAR, block * 256 : (block + 1) * 256] = by_class(
-                    lane_class, pieces
-                ).astype(BF)
+            for turn in range(N_SEQ):
+                if turn == 0:
+                    rows = proj_ref[:, first : first + 256]
+                else:
+                    rows = every[(turn - 1) * TOK : turn * TOK]
+                pieces = [rows[FAR * r : FAR * (r + 1)] for r in range(RATE)]
+                place = pl.multiple_of(((seq - turn) & 3) * FAR, FAR)
+                far_ref[pl.ds(place, FAR), cols] = by_class(lane_class, pieces)
 
     square = (TOK, TOK)
     far_row = iota(square, 0)
@@ -231,10 +234,9 @@
 
 def chain_kernel(
     inv_count,
-    att_ref, hidden_ref, tiles_ref, flag_ref, w_in_ref, w_out_ref, order_ref,
-    ga_ref, loss_ref, mine_ref, other_ref,
+    att_ref, hidden_ref, tiles_ref, flag_ref, w_in_ref, w_out_ref,
+    ga_ref, loss_ref, gm_ref,
 ):
-    core = lax.axis_index("slide") & 1
     attended = att_ref[...]
     mixed = (hidden_ref[...].astype(F32) + nn(attended, w_out_ref[...])).astype(BF)
     flag = flag_ref[:, 0:1] > 0.5
@@ -244,10 +246,15 @@
     grad_pred = (2.0 * inv_count * error).astype(BF)
     grad_mixed = nn(grad_pred, w_in_ref[...]).astype(BF)
     ga_ref[...] = nt(grad_mixed, w_out_ref[...]).astype(BF)
+    gm_ref[...] = grad_mixed
+
+
+def out_kernel(gm_ref, att_ref, order_ref, mine_ref, other_ref):
+    core = lax.axis_index("slide") & 1
     for turn, ref in enumerate((mine_ref, other_ref)):
         first = pl.multiple_of(((core + turn) & 1) * HALF, HALF)
-        left = nt(order_ref[pl.ds(first, HALF)], grad_mixed).astype(BF)
-        ref[...] = nn(left, attended).astype(BF)
+        left = nt(order_ref[pl.ds(first, HALF)], gm_ref[...]).astype(BF)
+        ref[...] = nn(left, att_ref[...]).astype(BF)
 
 
 def backward_kernel(
@@ -306,7 +313,7 @@
         ref[SECTIONS * SUB :] = loss_ref[...]
 
 
-def product_kernel(x0, x1, x2, x3, pn_ref, order_ref, wait_ref, mine_ref, other_ref, got, left):
+def product_kernel(x0, x1, x2, x3, pn_ref, order_ref, wait0, wait1, wait2, mine_ref, other_ref, got, left):
     seq = lax.axis_index("seq")
     core = lax.axis_index("slide") & 1
     for turn, x_ref in enumerate((x0, x1, x2, x3)):
@@ -354,7 +361,7 @@
     return jnp.where(row >= 72, pieces, total), loss
 
 
-def core_kernel(mine_ref, other_ref, wait1, wait2, wait3, y0, y1, y2, y3):
+def core_kernel(mine_ref, other_ref, wait_ref, y0, y1, y2, y3):
     y = (lax.axis_index("slide") >> 1) & 3
     for turn, ref in enumerate((y0, y1, y2, y3)):
         rows = pl.ds(pl.multiple_of(((y + turn) & 3) * YROWS, 16), YROWS)
@@ -493,7 +500,8 @@
 
 
 def swap(arrays, axis, turns):
-    return [arrays[0]] + [lax.ppermute(arrays[t], axis, turns[t]) for t in range(1, len(arrays))]
+    got = {t: lax.ppermute(arrays[t], axis, turns[t]) for t in (2, 1, 3)}
+    return [arrays[0], got[1], got[2], got[3]]
 
 
 def per_device(embeddings, tile_counts, masked_tiles, w_in, norm_gain, w_qkv, w_out):
@@ -538,14 +546,13 @@
         [pltpu.VMEM((TOK, D), F32)],
         4.0,
     )
-    grad_attended, loss, out_mine, out_other = call(
+    grad_attended, loss, grad_mixed = call(
         functools.partial(chain_kernel, inv_count),
-        [shape(TOK, D), shape(16, 128), shape(HALF, D), shape(HALF, D)],
-        (attended, hidden, tiles, flag, w_in, w_out, out_order()),
+        [shape(TOK, D), shape(16, 128), shape(TOK, D)],
+        (attended, hidden, tiles, flag, w_in, w_out),
         (),
         3.0,
     )
-    out_other = lax.ppermute(out_other, "slide", CORE_PAIRS)
     sent = call(
         backward_kernel,
         [shape(XROWS, TOK)] * N_SEQ,
@@ -554,20 +561,25 @@
         4.0,
     )
     got = swap(sent, "seq", SEQ_TURNS)
+    out_mine, out_other = call(
+        out_kernel, [shape(HALF, D)] * 2, (grad_mixed, attended, out_order())
+    )
+    out_other = lax.ppermute(out_other, "slide", CORE_PAIRS)
     out = call(out_core_kernel, [shape(SUB, D)] * NY, (out_mine, out_other, sent[0]), unread=1)
     out = swap(out, "slide", Y_TURNS)
+    out_rows = out
     out_sums = call(out_y_kernel, [shape(32, D)] * N_SEQ, (*out, out_pad_order()))
     out = swap(out_sums, "seq", SEQ_TURNS)
     mine, other = call(
         product_kernel,
         [shape(NY * YROWS, D)] * 2,
-        (*got, pn, product_order(), out_sums[0]),
+        (*got, pn, product_order(), *out_rows[1:]),
         [pltpu.VMEM((N_SEQ, XROWS, TOK), BF), pltpu.VMEM((6 * SUB, N_SEQ * TOK), BF)],
         3.0,
-        unread=1,
+        unread=3,
     )
     other = lax.ppermute(other, "slide", CORE_PAIRS)
-    by_y = call(core_kernel, [shape(YROWS, D)] * NY, (mine, other, *out[1:]), unread=3)
+    by_y = call(core_kernel, [shape(YROWS, D)] * NY, (mine, other, out_sums[0]), unread=1)
     by_y = swap(by_y, "slide", Y_TURNS)
     (by_z,) = call(y_kernel, [shape(NZ, 16, D)], (*by_y, *out, pad_order()))
     by_z = lax.all_to_all(by_z, "slide", 0, 0, tiled=True, axis_index_groups=Z_GROUPS)

time: 83.4 us -> 88 us (1.055)
  the two profiles are of different devices: /device:TPU:2 before, /device:TPU:8 now
where the time goes in v5:
time: 88 us; the launch traced here: 87.8 us
  waiting for transfers between devices  32.2 us (37%)
  starting transfers between devices  18.6 us (21%)
  blocking collectives  18 us (20%)
  Pallas kernels  16.5 us (19%)
  between operations  1.51 us (2%)
  local copies, waits for them, and re-layouts  0.97 us (1%)
    ppermute x15, waiting for transfers between devices, swap(): got = {t: lax.ppermute(arrays[t], axis, turns[t]) for t in (2, 1, 3)}  30.7 us
    ppermute x15, starting transfers between devices, swap(): got = {t: lax.ppermute(arrays[t], axis, turns[t]) for t in (2, 1, 3)}  18.4 us
    all_to_all x1, blocking collectives, per_device(): lax.all_to_all(by_z, 'slide', 0, 0, tiled=True, axis_index_groups=Z_GROUPS)  18 us
    pallas_call x12, Pallas kernels, call(): pl.pallas_call(kernel, out_shape=out_shapes, in_specs=specs, out_specs=[V...  16.5 us
  transfers between devices with their start and end apart: 17, of which 9 were waited for; matrix products, arithmetic and copies ran while one was open for 0% of the time, Pallas kernels for 5%

profile of v5, /device:TPU:8, one launch (start us, length us, event | category | flops | bytes accessed | tf_op | source)
XLA Modules:
  0.0 87.8 jit_solution(9628444739806263185)
XLA Ops:
  0.7 3.4 %shard_map.131 = (bf16[128,768]{1,0:T(8,128)(2,1)}, bf16[128,768]{1,0:T(8,128)(2,1)}) custom-call(bf16[1,128,1536]{2,1,0:T(8,128)(2,1)} %tiles_ref.1, s32[1,128]{1,0:T(1,128)} %masked_ref.1, f32[768]{0:T(1024)} %gain_hbm.1, bf16[1536,768]{1,0:T(8,128)(2,1)} %w_in_ref.1), custom_call_target="tpu_custom_call" | custom-call | flops 2000000000 | bytes 2000000 | tf_op jit(solution)/shard_map/pallas_call | solution.py:467
  4.1 2.8 %collective-permute-start.2 = (bf16[128,768]{1,0:T(8,128)(2,1)}, bf16[128,768]{1,0:T(8,128)(2,1)S(1)}, u32[]{:S(2)}, u32[]{:S(2)}) collective-permute-start(bf16[128,768]{1,0:T(8,128)(2,1)} %get-tuple-element.41.normed_ref.n0), channel_id=1, source_target_pairs={{0,3},{1,0},{2,1},{3,2},{4,7},{5,4},{6,5},{7,6},{8,11},{9,8},{10,9... | collective-permute-start | bytes 589832 | tf_op jit(solution)/shard_map/ppermute | solution.py:503
  6.9 0.8 collective-permute-start.1
  7.7 0.9 %collective-permute-start = (bf16[128,768]{1,0:T(8,128)(2,1)}, bf16[128,768]{1,0:T(8,128)(2,1)S(1)}, u32[]{:S(2)}, u32[]{:S(2)}) collective-permute-start(bf16[128,768]{1,0:T(8,128)(2,1)} %get-tuple-element.41.normed_ref.n0), channel_id=1, source_target_pairs={{0,1},{1,2},{2,3},{3,0},{4,5},{5,6},{6,7},{7,4},{8,9},{9,10},{10,1... | collective-permute-start | bytes 589832 | tf_op jit(solution)/shard_map/ppermute | solution.py:503
  9.3 0.9 %copy-done.4 = bf16[128,768]{1,0:T(8,128)(2,1)S(1)} copy-done((bf16[128,768]{1,0:T(8,128)(2,1)S(1)}, bf16[128,768]{1,0:T(8,128)(2,1)}, u32[]{:S(2)}) %copy-start.4) | copy-done | bytes 196632
  10.2 1.2 %shard_map.132 = (bf16[128,2304]{1,0:T(8,128)(2,1)S(1)}, f32[4,128,512]{2,1,0:T(8,128)S(1)}, f32[16,128]{1,0:T(8,128)S(1)}, f32[16,128]{1,0:T(8,128)S(1)}, bf16[...) custom-call(s32[1]{0:T(128)S(6)} %copy.14.count_ref, bf16[128,768]{1,0:T(8,128)(2,1)S(1)} %copy-done.4, ...), custom_call_target="tpu_custom_call" | custom-call | flops 5000000000 | bytes 5000000 | tf_op jit(solution)/shard_map/pallas_call | solution.py:467
  11.4 4.3 %collective-permute-done.2.n3 = bf16[128,768]{1,0:T(8,128)(2,1)S(1)} collective-permute-done((bf16[128,768]{1,0:T(8,128)(2,1)}, bf16[128,768]{1,0:T(8,128)(2,1)S(1)}, u32[]{:S(2)}, u32[]{:S(2)}) %collective-permute-start.2) | collective-permute-done | bytes 196640 | tf_op jit(solution)/shard_map/ppermute | solution.py:503
  15.6 0.9 collective-permute-done.1.n2
  16.5 2.7 %collective-permute-done.n1 = bf16[128,768]{1,0:T(8,128)(2,1)S(1)} collective-permute-done((bf16[128,768]{1,0:T(8,128)(2,1)}, bf16[128,768]{1,0:T(8,128)(2,1)S(1)}, u32[]{:S(2)}, u32[]{:S(2)}) %collective-permute-start) | collective-permute-done | bytes 196640 | tf_op jit(solution)/shard_map/ppermute | solution.py:503
  19.2 2.4 %shard_map.133 = (bf16[4,128,768]{2,1,0:T(8,128)(2,1)S(1)}, bf16[128,768]{1,0:T(8,128)(2,1)S(1)}, bf16[128,768]{1,0:T(8,128)(2,1)S(1)}, f32[4,128,512]{2,1,0:T(8...) custom-call(s32[1]{0:T(128)S(6)} %copy.14.count_ref, bf16[128,768]{1,0:T(8,128)(2,1)S(1)} %copy-done.4, ...), custom_call_target="tpu_custom_call" | custom-call | flops 4000000000 | bytes 4000000 | tf_op jit(solution)/shard_map/pallas_call | solution.py:467
  21.7 0.0 copy-start.6
  21.7 1.7 %shard_map.134 = (bf16[128,768]{1,0:T(8,128)(2,1)S(1)}, bf16[16,128]{1,0:T(8,128)(2,1)S(1)}, bf16[128,768]{1,0:T(8,128)(2,1)S(1)}) custom-call(bf16[128,768]{1,0:T(8,128)(2,1)S(1)} %get-tuple-element.50.att_ref, bf16[128,768]{1,0:T(8,128)(2,1)S(1)} %copy-done.11, bf16[128,1536]{1,0:T(8,128)(2,1)S(1)} %get-tuple-element.52.tiles_ref, ...), custom_call_target="tpu_custom_call" | custom-call | flops 3000000000 | bytes 3000000 | tf_op jit(solution)/shard_map/pallas_call | solution.py:467
  23.4 0.0 copy-start.8
  23.4 1.4 %shard_map.136 = (bf16[384,768]{1,0:T(8,128)(2,1)S(1)}, bf16[384,768]{1,0:T(8,128)(2,1)S(1)}) custom-call(bf16[128,768]{1,0:T(8,128)(2,1)S(1)} %get-tuple-element.61.gm_ref, bf16[128,768]{1,0:T(8,128)(2,1)S(1)} %get-tuple-element.50.att_ref, bf16[768,768]{1,0:T(8,128)(2,1)S(1)} %copy-done.6), custom_call_target="tpu_custom_call" | custom-call | flops 1000000000 | bytes 1000000 | tf_op jit(solution)/shard_map/pallas_call | solution.py:467
  24.8 0.1 collective-permute-start.6
  24.9 3.0 %shard_map.135 = (bf16[976,128]{1,0:T(8,128)(2,1)S(1)}, bf16[976,128]{1,0:T(8,128)(2,1)S(1)}, bf16[976,128]{1,0:T(8,128)(2,1)S(1)}, bf16[976,128]{1,0:T(8,128)(2,1)S(1)}) custom-call(bf16[128,2304]{1,0:T(8,128)(2,1)S(1)} %get-tuple-element.42.proj_ref, bf16[128,768]{1,0:T(8,128)(2,1)S(1)} %get-tuple-element.46.fk_ref, ...), custom_call_target="tpu_custom_call" | custom-call | flops 4000000000 | bytes 4000000 | tf_op jit(solution)/shard_map/pallas_call | solution.py:467
  27.8 0.0 copy-start.7
  27.9 0.3 collective-permute-start.3
  28.1 2.2 %collective-permute-start.4 = (bf16[976,128]{1,0:T(8,128)(2,1)S(1)}, bf16[976,128]{1,0:T(8,128)(2,1)S(1)}, u32[]{:S(2)}, u32[]{:S(2)}) collective-permute-start(bf16[976,128]{1,0:T(8,128)(2,1)S(1)} %get-tuple-element.58), channel_id=1, source_target_pairs={{0,2},{1,3},{2,0},{3,1},{4,6},{5,7},{6,4},{7,5},{8,10},{9,11},{10,... | collective-permute-start | bytes 749576 | tf_op jit(solution)/shard_map/ppermute | solution.py:503
  30.3 1.3 %collective-permute-start.5 = (bf16[976,128]{1,0:T(8,128)(2,1)S(1)}, bf16[976,128]{1,0:T(8,128)(2,1)S(1)}, u32[]{:S(2)}, u32[]{:S(2)}) collective-permute-start(bf16[976,128]{1,0:T(8,128)(2,1)S(1)} %get-tuple-element.59), channel_id=1, source_target_pairs={{0,3},{1,0},{2,1},{3,2},{4,7},{5,4},{6,5},{7,6},{8,11},{9,8},{10,9... | collective-permute-start | bytes 749576 | tf_op jit(solution)/shard_map/ppermute | solution.py:503
  31.6 0.0 collective-permute-done.6.other_ref
  31.6 0.1 shard_map.137
  31.8 1.7 %collective-permute-start.7 = (bf16[96,768]{1,0:T(8,128)(2,1)S(1)}, bf16[96,768]{1,0:T(8,128)(2,1)S(1)}, u32[]{:S(2)}, u32[]{:S(2)}) collective-permute-start(bf16[96,768]{1,0:T(8,128)(2,1)S(1)} %get-tuple-element.64), channel_id=1, source_target_pairs={{0,8},{4,12},{8,16},{12,20},{16,24},{20,28},{24,0},{28,4},{32,40},... | collective-permute-start | bytes 442376 | tf_op jit(solution)/shard_map/ppermute | solution.py:503
  33.4 0.9 %collective-permute-start.8 = (bf16[96,768]{1,0:T(8,128)(2,1)S(1)}, bf16[96,768]{1,0:T(8,128)(2,1)S(1)}, u32[]{:S(2)}, u32[]{:S(2)}) collective-permute-start(bf16[96,768]{1,0:T(8,128)(2,1)S(1)} %get-tuple-element.65), channel_id=1, source_target_pairs={{0,16},{4,20},{8,24},{12,28},{16,0},{20,4},{24,8},{28,12},{32,48},... | collective-permute-start | bytes 442376 | tf_op jit(solution)/shard_map/ppermute | solution.py:503
  34.4 8.8 %collective-permute-done.3.x1 = bf16[976,128]{1,0:T(8,128)(2,1)S(1)} collective-permute-done((bf16[976,128]{1,0:T(8,128)(2,1)S(1)}, bf16[976,128]{1,0:T(8,128)(2,1)S(1)}, u32[]{:S(2)}, u32[]{:S(2)}) %collective-permute-start.3) | collective-permute-done | bytes 249888 | tf_op jit(solution)/shard_map/ppermute | solution.py:503
  43.1 0.4 collective-permute-start.9
  43.6 0.0 collective-permute-done.4.x2
  43.6 0.2 collective-permute-done.5.x3
  43.7 0.0 collective-permute-done.7.wait0.y1
  43.7 0.0 collective-permute-done.8.wait1.y2
  43.7 4.8 %collective-permute-done.9.wait2.y3 = bf16[96,768]{1,0:T(8,128)(2,1)S(1)} collective-permute-done((bf16[96,768]{1,0:T(8,128)(2,1)S(1)}, bf16[96,768]{1,0:T(8,128)(2,1)S(1)}, u32[]{:S(2)}, u32[]{:S(2)}) %collective-permute-start.9) | collective-permute-done | bytes 147488 | tf_op jit(solution)/shard_map/ppermute | solution.py:503
  48.6 2.0 %shard_map.138 = (bf16[320,768]{1,0:T(8,128)(2,1)S(1)}, bf16[320,768]{1,0:T(8,128)(2,1)S(1)}) custom-call(bf16[976,128]{1,0:T(8,128)(2,1)S(1)} %get-tuple-element.56.wait_ref.x0, bf16[976,128]{1,0:T(8,128)(2,1)S(1)} %collective-permute-done.3.x1, bf16[976,128]{1,0:T(8,128)(2,1)S(1)} %collective-permute-done.4.x2, ...), custom_call_target="tpu_custom_call" | custom-call | flops 3000000000 | bytes 3000000 | tf_op jit(solution)/shard_map/pallas_call | solution.py:467
  50.5 0.1 collective-permute-start.10
  50.7 0.3 shard_map.139
  50.9 0.0 copy-start.10
  50.9 1.6 %collective-permute-done.10.other_ref = bf16[320,768]{1,0:T(8,128)(2,1)S(1)} collective-permute-done((bf16[320,768]{1,0:T(8,128)(2,1)S(1)}, bf16[320,768]{1,0:T(8,128)(2,1)S(1)}, u32[]{:S(2)}, u32[]{:S(2)}) %collective-permute-start.10) | collective-permute-done | bytes 491552 | tf_op jit(solution)/shard_map/ppermute | solution.py:581
  52.5 0.2 shard_map.140
  52.7 1.7 %collective-permute-start.11 = (bf16[80,768]{1,0:T(8,128)(2,1)S(1)}, bf16[80,768]{1,0:T(8,128)(2,1)S(1)}, u32[]{:S(2)}, u32[]{:S(2)}) collective-permute-start(bf16[80,768]{1,0:T(8,128)(2,1)S(1)} %get-tuple-element.72), channel_id=1, source_target_pairs={{0,8},{4,12},{8,16},{12,20},{16,24},{20,28},{24,0},{28,4},{32,40},... | collective-permute-start | bytes 368648 | tf_op jit(solution)/shard_map/ppermute | solution.py:503
  54.3 2.0 %collective-permute-start.12 = (bf16[80,768]{1,0:T(8,128)(2,1)S(1)}, bf16[80,768]{1,0:T(8,128)(2,1)S(1)}, u32[]{:S(2)}, u32[]{:S(2)}) collective-permute-start(bf16[80,768]{1,0:T(8,128)(2,1)S(1)} %get-tuple-element.73), channel_id=1, source_target_pairs={{0,16},{4,20},{8,24},{12,28},{16,0},{20,4},{24,8},{28,12},{32,48},... | collective-permute-start | bytes 368648 | tf_op jit(solution)/shard_map/ppermute | solution.py:503
  56.4 2.5 %collective-permute-start.13 = (bf16[80,768]{1,0:T(8,128)(2,1)S(1)}, bf16[80,768]{1,0:T(8,128)(2,1)S(1)}, u32[]{:S(2)}, u32[]{:S(2)}) collective-permute-start(bf16[80,768]{1,0:T(8,128)(2,1)S(1)} %get-tuple-element.74), channel_id=1, source_target_pairs={{0,24},{4,28},{8,0},{12,4},{16,8},{20,12},{24,16},{28,20},{32,56},... | collective-permute-start | bytes 368648 | tf_op jit(solution)/shard_map/ppermute | solution.py:503
  58.9 0.0 collective-permute-start.14
  58.9 0.9 collective-permute-start.15
  59.8 5.0 %collective-permute-done.14.o1 = bf16[32,768]{1,0:T(8,128)(2,1)S(1)} collective-permute-done((bf16[32,768]{1,0:T(8,128)(2,1)S(1)}, bf16[32,768]{1,0:T(8,128)(2,1)S(1)}, u32[]{:S(2)}, u32[]{:S(2)}) %collective-permute-start.14) | collective-permute-done | bytes 49184 | tf_op jit(solution)/shard_map/ppermute | solution.py:503
  64.7 4.1 %collective-permute-done.16.o3 = bf16[32,768]{1,0:T(8,128)(2,1)S(1)} collective-permute-done((bf16[32,768]{1,0:T(8,128)(2,1)S(1)}, bf16[32,768]{1,0:T(8,128)(2,1)S(1)}, u32[]{:S(2)}, u32[]{:S(2)}) %collective-permute-start.16) | collective-permute-done | bytes 49184 | tf_op jit(solution)/shard_map/ppermute | solution.py:503
  68.8 0.0 collective-permute-done.11.y1
  68.8 0.3 shard_map.141
  69.1 18.0 %all_to_all.5.in_ref = bf16[8,16,768]{2,1,0:T(8,128)(2,1)S(1)} all-to-all(bf16[8,16,768]{2,1,0:T(8,128)(2,1)S(1)} %shard_map.141), channel_id=1, replica_groups={{0,32,64,96,128,160,192,224},{4,36,68,100,132,164,196,228},{8,40,72,104..., dimensions={0} | all-to-all | bytes 393216 | tf_op jit(solution)/shard_map/all_to_all | solution.py:585
  87.2 0.7 shard_map.142
  (23 shorter events, 0.0 us)
Async XLA Ops:
  0.6 8.6 %copy-start.5 = (s32[1,128]{1,0:T(1,128)S(1)}, s32[1,128]{1,0:T(1,128)}, u32[]{:S(2)}) copy-start(s32[1,128]{1,0:T(1,128)} %masked_ref.1) | copy-start | bytes 1540
  0.6 8.6 %copy-start.3 = (bf16[1,128,1536]{2,1,0:T(8,128)(2,1)S(1)}, bf16[1,128,1536]{2,1,0:T(8,128)(2,1)}, u32[]{:S(2)}) copy-start(bf16[1,128,1536]{2,1,0:T(8,128)(2,1)} %tiles_ref.1) | copy-start | bytes 1179652
  0.7 8.6 %copy-start = (bf16[768,2304]{1,0:T(8,128)(2,1)S(1)}, bf16[768,2304]{1,0:T(8,128)(2,1)}, u32[]{:S(2)}) copy-start(bf16[768,2304]{1,0:T(8,128)(2,1)} %w_qkv_ref.3) | copy-start | bytes 10616836
  4.1 11.6 %collective-permute-start.2 = (bf16[128,768]{1,0:T(8,128)(2,1)}, bf16[128,768]{1,0:T(8,128)(2,1)S(1)}, u32[]{:S(2)}, u32[]{:S(2)}) collective-permute-start(bf16[128,768]{1,0:T(8,128)(2,1)} %get-tuple-element.41.normed_ref.n0), channel_id=1, source_target_pairs={{0,3},{1,0},{2,1},{3,2},{4,7},{5,4},{6,5},{7,6},{8,11},{9,8},{10,9... | collective-permute-start | bytes 589832 | tf_op jit(solution)/shard_map/ppermute | solution.py:503
  6.9 9.6 %collective-permute-start.1 = (bf16[128,768]{1,0:T(8,128)(2,1)}, bf16[128,768]{1,0:T(8,128)(2,1)S(1)}, u32[]{:S(2)}, u32[]{:S(2)}) collective-permute-start(bf16[128,768]{1,0:T(8,128)(2,1)} %get-tuple-element.41.normed_ref.n0), channel_id=1, source_target_pairs={{0,2},{1,3},{2,0},{3,1},{4,6},{5,7},{6,4},{7,5},{8,10},{9,11},{10,... | collective-permute-start | bytes 589832 | tf_op jit(solution)/shard_map/ppermute | solution.py:503
  7.7 11.5 %collective-permute-start = (bf16[128,768]{1,0:T(8,128)(2,1)}, bf16[128,768]{1,0:T(8,128)(2,1)S(1)}, u32[]{:S(2)}, u32[]{:S(2)}) collective-permute-start(bf16[128,768]{1,0:T(8,128)(2,1)} %get-tuple-element.41.normed_ref.n0), channel_id=1, source_target_pairs={{0,1},{1,2},{2,3},{3,0},{4,5},{5,6},{6,7},{7,4},{8,9},{9,10},{10,1... | collective-permute-start | bytes 589832 | tf_op jit(solution)/shard_map/ppermute | solution.py:503
  9.3 0.9 %copy-start.4 = (bf16[128,768]{1,0:T(8,128)(2,1)S(1)}, bf16[128,768]{1,0:T(8,128)(2,1)}, u32[]{:S(2)}) copy-start(bf16[128,768]{1,0:T(8,128)(2,1)} %get-tuple-element.41.normed_ref.n0) | copy-start | bytes 589828
  19.2 2.4 %copy-start.1 = (bf16[1536,768]{1,0:T(8,128)(2,1)S(1)}, bf16[1536,768]{1,0:T(8,128)(2,1)}, u32[]{:S(2)}) copy-start(bf16[1536,768]{1,0:T(8,128)(2,1)} %w_in_ref.1) | copy-start | bytes 7077892
  19.2 2.4 %copy-start.2 = (bf16[768,768]{1,0:T(8,128)(2,1)S(1)}, bf16[768,768]{1,0:T(8,128)(2,1)}, u32[]{:S(2)}) copy-start(bf16[768,768]{1,0:T(8,128)(2,1)} %w_out_ref.1) | copy-start | bytes 3538948
  19.2 2.4 %copy-start.11 = (bf16[128,768]{1,0:T(8,128)(2,1)S(1)}, bf16[128,768]{1,0:T(8,128)(2,1)}, u32[]{:S(2)}) copy-start(bf16[128,768]{1,0:T(8,128)(2,1)} %get-tuple-element.51.hidden_ref) | copy-start | bytes 589828
  21.7 1.7 %copy-start.6 = (bf16[768,768]{1,0:T(8,128)(2,1)S(1)}, bf16[768,768]{1,0:T(8,128)(2,1)}, u32[]{:S(2)}) copy-start(bf16[768,768]{1,0:T(8,128)(2,1)} %constant.11.clone.order_ref) | copy-start | bytes 3538948
  23.4 1.5 %copy-start.8 = (bf16[384,384]{1,0:T(8,128)(2,1)S(1)}, bf16[384,384]{1,0:T(8,128)(2,1)}, u32[]{:S(2)}) copy-start(bf16[384,384]{1,0:T(8,128)(2,1)} %constant.10.clone.spread_ref) | copy-start | bytes 884740
  24.8 6.8 %collective-permute-start.6 = (bf16[384,768]{1,0:T(8,128)(2,1)S(1)}, bf16[384,768]{1,0:T(8,128)(2,1)S(1)}, u32[]{:S(2)}, u32[]{:S(2)}) collective-permute-start(bf16[384,768]{1,0:T(8,128)(2,1)S(1)} %get-tuple-element.63), channel_id=1, source_target_pairs={{0,4},{4,0},{8,12},{12,8},{16,20},{20,16},{24,28},{28,24},{32,36},... | collective-permute-start | bytes 1769480 | tf_op jit(solution)/shard_map/ppermute | solution.py:567
  27.8 20.7 %copy-start.7 = (bf16[640,576]{1,0:T(8,128)(2,1)S(1)}, bf16[640,576]{1,0:T(8,128)(2,1)}, u32[]{:S(2)}) copy-start(bf16[640,576]{1,0:T(8,128)(2,1)} %constant.13.clone.order_ref) | copy-start | bytes 2211844
  27.9 15.3 %collective-permute-start.3 = (bf16[976,128]{1,0:T(8,128)(2,1)S(1)}, bf16[976,128]{1,0:T(8,128)(2,1)S(1)}, u32[]{:S(2)}, u32[]{:S(2)}) collective-permute-start(bf16[976,128]{1,0:T(8,128)(2,1)S(1)} %get-tuple-element.57), channel_id=1, source_target_pairs={{0,1},{1,2},{2,3},{3,0},{4,5},{5,6},{6,7},{7,4},{8,9},{9,10},{10,1... | collective-permute-start | bytes 749576 | tf_op jit(solution)/shard_map/ppermute | solution.py:503
  28.1 15.4 %collective-permute-start.4 = (bf16[976,128]{1,0:T(8,128)(2,1)S(1)}, bf16[976,128]{1,0:T(8,128)(2,1)S(1)}, u32[]{:S(2)}, u32[]{:S(2)}) collective-permute-start(bf16[976,128]{1,0:T(8,128)(2,1)S(1)} %get-tuple-element.58), channel_id=1, source_target_pairs={{0,2},{1,3},{2,0},{3,1},{4,6},{5,7},{6,4},{7,5},{8,10},{9,11},{10,... | collective-permute-start | bytes 749576 | tf_op jit(solution)/shard_map/ppermute | solution.py:503
  30.3 13.5 %collective-permute-start.5 = (bf16[976,128]{1,0:T(8,128)(2,1)S(1)}, bf16[976,128]{1,0:T(8,128)(2,1)S(1)}, u32[]{:S(2)}, u32[]{:S(2)}) collective-permute-start(bf16[976,128]{1,0:T(8,128)(2,1)S(1)} %get-tuple-element.59), channel_id=1, source_target_pairs={{0,3},{1,0},{2,1},{3,2},{4,7},{5,4},{6,5},{7,6},{8,11},{9,8},{10,9... | collective-permute-start | bytes 749576 | tf_op jit(solution)/shard_map/ppermute | solution.py:503
  31.8 12.0 %collective-permute-start.7 = (bf16[96,768]{1,0:T(8,128)(2,1)S(1)}, bf16[96,768]{1,0:T(8,128)(2,1)S(1)}, u32[]{:S(2)}, u32[]{:S(2)}) collective-permute-start(bf16[96,768]{1,0:T(8,128)(2,1)S(1)} %get-tuple-element.64), channel_id=1, source_target_pairs={{0,8},{4,12},{8,16},{12,20},{16,24},{20,28},{24,0},{28,4},{32,40},... | collective-permute-start | bytes 442376 | tf_op jit(solution)/shard_map/ppermute | solution.py:503
  33.4 10.3 %collective-permute-start.8 = (bf16[96,768]{1,0:T(8,128)(2,1)S(1)}, bf16[96,768]{1,0:T(8,128)(2,1)S(1)}, u32[]{:S(2)}, u32[]{:S(2)}) collective-permute-start(bf16[96,768]{1,0:T(8,128)(2,1)S(1)} %get-tuple-element.65), channel_id=1, source_target_pairs={{0,16},{4,20},{8,24},{12,28},{16,0},{20,4},{24,8},{28,12},{32,48},... | collective-permute-start | bytes 442376 | tf_op jit(solution)/shard_map/ppermute | solution.py:503
  43.1 5.5 %collective-permute-start.9 = (bf16[96,768]{1,0:T(8,128)(2,1)S(1)}, bf16[96,768]{1,0:T(8,128)(2,1)S(1)}, u32[]{:S(2)}, u32[]{:S(2)}) collective-permute-start(bf16[96,768]{1,0:T(8,128)(2,1)S(1)} %get-tuple-element.66), channel_id=1, source_target_pairs={{0,24},{4,28},{8,0},{12,4},{16,8},{20,12},{24,16},{28,20},{32,56},... | collective-permute-start | bytes 442376 | tf_op jit(solution)/shard_map/ppermute | solution.py:503
  48.6 2.1 %copy-start.9 = (bf16[128,96]{1,0:T(8,128)(2,1)S(1)}, bf16[128,96]{1,0:T(8,128)(2,1)}, u32[]{:S(2)}) copy-start(bf16[128,96]{1,0:T(8,128)(2,1)} %constant.12.clone.order_ref) | copy-start | bytes 73732
  50.5 2.0 %collective-permute-start.10 = (bf16[320,768]{1,0:T(8,128)(2,1)S(1)}, bf16[320,768]{1,0:T(8,128)(2,1)S(1)}, u32[]{:S(2)}, u32[]{:S(2)}) collective-permute-start(bf16[320,768]{1,0:T(8,128)(2,1)S(1)} %get-tuple-element.68), channel_id=1, source_target_pairs={{0,4},{4,0},{8,12},{12,8},{16,20},{20,16},{24,28},{28,24},{32,36},... | collective-permute-start | bytes 1474568 | tf_op jit(solution)/shard_map/ppermute | solution.py:581
  50.9 17.9 %copy-start.10 = (bf16[96,80]{1,0:T(8,128)(2,1)S(1)}, bf16[96,80]{1,0:T(8,128)(2,1)}, u32[]{:S(2)}) copy-start(bf16[96,80]{1,0:T(8,128)(2,1)} %constant.14.clone.order_ref) | copy-start | bytes 46084
  52.7 16.1 %collective-permute-start.11 = (bf16[80,768]{1,0:T(8,128)(2,1)S(1)}, bf16[80,768]{1,0:T(8,128)(2,1)S(1)}, u32[]{:S(2)}, u32[]{:S(2)}) collective-permute-start(bf16[80,768]{1,0:T(8,128)(2,1)S(1)} %get-tuple-element.72), channel_id=1, source_target_pairs={{0,8},{4,12},{8,16},{12,20},{16,24},{20,28},{24,0},{28,4},{32,40},... | collective-permute-start | bytes 368648 | tf_op jit(solution)/shard_map/ppermute | solution.py:503
  54.3 14.5 %collective-permute-start.12 = (bf16[80,768]{1,0:T(8,128)(2,1)S(1)}, bf16[80,768]{1,0:T(8,128)(2,1)S(1)}, u32[]{:S(2)}, u32[]{:S(2)}) collective-permute-start(bf16[80,768]{1,0:T(8,128)(2,1)S(1)} %get-tuple-element.73), channel_id=1, source_target_pairs={{0,16},{4,20},{8,24},{12,28},{16,0},{20,4},{24,8},{28,12},{32,48},... | collective-permute-start | bytes 368648 | tf_op jit(solution)/shard_map/ppermute | solution.py:503
  56.4 12.5 %collective-permute-start.13 = (bf16[80,768]{1,0:T(8,128)(2,1)S(1)}, bf16[80,768]{1,0:T(8,128)(2,1)S(1)}, u32[]{:S(2)}, u32[]{:S(2)}) collective-permute-start(bf16[80,768]{1,0:T(8,128)(2,1)S(1)} %get-tuple-element.74), channel_id=1, source_target_pairs={{0,24},{4,28},{8,0},{12,4},{16,8},{20,12},{24,16},{28,20},{32,56},... | collective-permute-start | bytes 368648 | tf_op jit(solution)/shard_map/ppermute | solution.py:503
  58.9 5.8 %collective-permute-start.14 = (bf16[32,768]{1,0:T(8,128)(2,1)S(1)}, bf16[32,768]{1,0:T(8,128)(2,1)S(1)}, u32[]{:S(2)}, u32[]{:S(2)}) collective-permute-start(bf16[32,768]{1,0:T(8,128)(2,1)S(1)} %get-tuple-element.75), channel_id=1, source_target_pairs={{0,1},{1,2},{2,3},{3,0},{4,5},{5,6},{6,7},{7,4},{8,9},{9,10},{10,1... | collective-permute-start | bytes 147464 | tf_op jit(solution)/shard_map/ppermute | solution.py:503
  58.9 5.8 %collective-permute-start.15 = (bf16[32,768]{1,0:T(8,128)(2,1)S(1)}, bf16[32,768]{1,0:T(8,128)(2,1)S(1)}, u32[]{:S(2)}, u32[]{:S(2)}) collective-permute-start(bf16[32,768]{1,0:T(8,128)(2,1)S(1)} %get-tuple-element.76), channel_id=1, source_target_pairs={{0,2},{1,3},{2,0},{3,1},{4,6},{5,7},{6,4},{7,5},{8,10},{9,11},{10,... | collective-permute-start | bytes 147464 | tf_op jit(solution)/shard_map/ppermute | solution.py:503
  64.7 4.1 %collective-permute-start.16 = (bf16[32,768]{1,0:T(8,128)(2,1)S(1)}, bf16[32,768]{1,0:T(8,128)(2,1)S(1)}, u32[]{:S(2)}, u32[]{:S(2)}) collective-permute-start(bf16[32,768]{1,0:T(8,128)(2,1)S(1)} %get-tuple-element.77), channel_id=1, source_target_pairs={{0,3},{1,0},{2,1},{3,2},{4,7},{5,4},{6,5},{7,6},{8,11},{9,8},{10,9... | collective-permute-start | bytes 147464 | tf_op jit(solution)/shard_map/ppermute | solution.py:503

commit v6 on v5

--- a/solution.py
+++ b/solution.py
@@ -26,7 +26,9 @@
 SUB = 96
 SECTIONS = 10
 YROWS = 80
-XROWS = SECTIONS * SUB + 16
+ALLROWS = 112
+MAINROWS = SECTIONS * SUB + 16
+XROWS = MAINROWS + 6 * SUB
 NZ, NY, NC = 8, 4, 2
 
 
@@ -258,11 +260,10 @@
 
 
 def backward_kernel(
-    proj_ref, fk_ref, fv_ref, pnear_ref, pfar_ref, ga_ref, loss_ref, spread_ref,
-    x0, x1, x2, x3,
-    gq, gk, gv, gkf, gvf, turned,
+    proj_ref, fk_ref, fv_ref, pnear_ref, pfar_ref, ga_ref, spread_ref,
+    turned,
+    gq, gk, gv, gkf, gvf,
 ):
-    seq = lax.axis_index("seq")
     own_class = iota((1, TOK), 1) >> 5
     for ref in (gq, gk, gv, gkf, gvf):
         ref[...] = jnp.zeros_like(ref)
@@ -306,18 +307,25 @@
             piece = value[:, half * HALF : (half + 1) * HALF].astype(BF)
             turned[section] = nt(place, piece).astype(BF)
             section += 1
+
+def pack_kernel(turned_ref, loss_ref, mine_ref, other_ref, x0, x1, x2, x3):
+    seq = lax.axis_index("seq")
     for turn, ref in enumerate((x0, x1, x2, x3)):
-        first = pl.multiple_of(((seq + turn) & 3) * SUB, 16)
+        rows = pl.ds(pl.multiple_of(((seq + turn) & 3) * SUB, 16), SUB)
         for section in range(SECTIONS):
-            ref[section * SUB : (section + 1) * SUB] = turned[section, pl.ds(first, SUB)]
-        ref[SECTIONS * SUB :] = loss_ref[...]
-
-
-def product_kernel(x0, x1, x2, x3, pn_ref, order_ref, wait0, wait1, wait2, mine_ref, other_ref, got, left):
+            ref[section * SUB : (section + 1) * SUB] = turned_ref[section, rows]
+        ref[SECTIONS * SUB : MAINROWS] = loss_ref[...]
+        for block in range(6):
+            cols = slice(128 * block, 128 * (block + 1))
+            total = mine_ref[rows, cols].astype(F32) + other_ref[rows, cols].astype(F32)
+            ref[MAINROWS + SUB * block : MAINROWS + SUB * (block + 1)] = total.astype(BF)
+
+
+def product_kernel(x0, x1, x2, x3, pn_ref, order_ref, mine_ref, other_ref, out_ref, got, left):
     seq = lax.axis_index("seq")
     core = lax.axis_index("slide") & 1
     for turn, x_ref in enumerate((x0, x1, x2, x3)):
-        got[(seq - turn) & 3] = x_ref[...]
+        got[(seq - turn) & 3] = x_ref[0:MAINROWS]
     for src in range(N_SEQ):
         left[0 : 2 * SUB, src * TOK : (src + 1) * TOK] = got[src, 0 : 2 * SUB]
     shape = (SUB, TOK)
@@ -340,10 +348,14 @@
                 for r in range(RATE):
                     total = total + jnp.where(spots[r], turns[(r - src) & 3], 0.0)
                 left[near_at : near_at + SUB, src * TOK : (src + 1) * TOK] = total.astype(BF)
+    for block in range(6):
+        rows = slice(MAINROWS + SUB * block, MAINROWS + SUB * (block + 1))
+        out = x0[rows].astype(F32) + x1[rows].astype(F32) + x2[rows].astype(F32) + x3[rows].astype(F32)
+        out_ref[:, 128 * block : 128 * (block + 1)] = out.astype(BF)
     whole = nn(left[...], pn_ref[...].reshape(N_SEQ * TOK, D)).astype(BF)
-    loss = got[0, SECTIONS * SUB :].astype(F32)
+    loss = got[0, SECTIONS * SUB : MAINROWS].astype(F32)
     for src in range(1, N_SEQ):
-        loss = loss + got[src, SECTIONS * SUB :].astype(F32)
+        loss = loss + got[src, SECTIONS * SUB : MAINROWS].astype(F32)
     loss = jnp.sum(loss, axis=0, keepdims=True)[:, 0:1]
     tail = split_rows(jnp.broadcast_to(loss, (YROWS, D)), (YROWS, D), 72)
     for turn, ref in enumerate((mine_ref, other_ref)):
@@ -358,40 +370,23 @@
     row = iota(total.shape, 0)
     loss = jnp.sum(jnp.where(row >= 72, total, 0.0), axis=0, keepdims=True)
     pieces = split_rows(jnp.broadcast_to(loss, total.shape), total.shape, 72)
-    return jnp.where(row >= 72, pieces, total), loss
-
-
-def core_kernel(mine_ref, other_ref, wait_ref, y0, y1, y2, y3):
+    return jnp.where(row >= 72, pieces, total)
+
+
+def core_kernel(mine_ref, other_ref, out_ref, order_ref, y0, y1, y2, y3):
     y = (lax.axis_index("slide") >> 1) & 3
     for turn, ref in enumerate((y0, y1, y2, y3)):
-        rows = pl.ds(pl.multiple_of(((y + turn) & 3) * YROWS, 16), YROWS)
-        ref[...] = resplit(mine_ref[rows].astype(F32) + other_ref[rows].astype(F32))[0].astype(BF)
-
-
-def y_kernel(y0, y1, y2, y3, o0, o1, o2, o3, order_ref, out_ref):
+        place = (y + turn) & 3
+        rows = pl.ds(pl.multiple_of(place * YROWS, 16), YROWS)
+        total = resplit(mine_ref[rows].astype(F32) + other_ref[rows].astype(F32))
+        ref[0:YROWS] = total.astype(BF)
+        ref[YROWS:] = nn(order_ref[pl.ds(pl.multiple_of(place * 32, 32), 32)], out_ref[...]).astype(BF)
+
+
+def y_kernel(y0, y1, y2, y3, order_ref, out_ref):
     total = y0[...].astype(F32) + y1[...].astype(F32) + y2[...].astype(F32) + y3[...].astype(F32)
-    total, loss = resplit(total)
-    out_ref[0:6] = nn(order_ref[...], total.astype(BF)).astype(BF).reshape(6, 16, D)
-    out = o0[...].astype(F32) + o1[...].astype(F32) + o2[...].astype(F32) + o3[...].astype(F32)
-    tail = split_rows(jnp.broadcast_to(loss, (16, D)), (16, D), 12)
-    for half in range(2):
-        out_ref[6 + half] = (out[16 * half : 16 * (half + 1)] + tail).astype(BF)
-
-
-def out_core_kernel(mine_ref, other_ref, wait_ref, y0, y1, y2, y3):
-    y = (lax.axis_index("slide") >> 1) & 3
-    for turn, ref in enumerate((y0, y1, y2, y3)):
-        rows = pl.ds(pl.multiple_of(((y + turn) & 3) * SUB, 16), SUB)
-        ref[...] = (mine_ref[rows].astype(F32) + other_ref[rows].astype(F32)).astype(BF)
-
-
-def out_y_kernel(y0, y1, y2, y3, order_ref, x0, x1, x2, x3):
-    seq = lax.axis_index("seq")
-    total = y0[...].astype(F32) + y1[...].astype(F32) + y2[...].astype(F32) + y3[...].astype(F32)
-    total = total.astype(BF)
-    for turn, ref in enumerate((x0, x1, x2, x3)):
-        rows = pl.ds(pl.multiple_of(((seq + turn) & 3) * 32, 32), 32)
-        ref[...] = nn(order_ref[rows], total).astype(BF)
+    total = jnp.concatenate([resplit(total[:YROWS]), total[YROWS:]], 0)
+    out_ref[...] = nn(order_ref[...], total.astype(BF)).astype(BF).reshape(NZ, 16, D)
 
 
 def z_kernel(in_ref, out_ref, loss_ref):
@@ -426,8 +421,8 @@
     place = np.zeros((D, D), np.float32)
     row = 0
     for c in range(NC):
-        for y in range(NY):
-            for j in range(N_SEQ):
+        for j in range(N_SEQ):
+            for y in range(NY):
                 for half in range(2):
                     for r in range(12):
                         place[row, (half * 8 + y * NC + c) * HD + j * 12 + r] = 1.0
@@ -436,19 +431,19 @@
 
 
 def out_pad_order():
-    place = np.zeros((N_SEQ * 32, SUB), np.float32)
-    for j in range(N_SEQ):
-        for half in range(2):
-            for r in range(12):
-                place[j * 32 + half * 16 + r, j * 24 + half * 12 + r] = 1.0
+    place = np.zeros((NY * 32, SUB), np.float32)
+    for y in range(NY):
+        for r in range(24):
+            place[y * 32 + r, y * 24 + r] = 1.0
     return jnp.asarray(place, BF)
 
 
 def pad_order():
-    place = np.zeros((SUB, YROWS), np.float32)
-    for z in range(6):
+    place = np.zeros((NZ * 16, ALLROWS), np.float32)
+    for z in range(NZ):
         for r in range(12):
-            place[z * 16 + r, z * 12 + r] = 1.0
+            first = z * 12 if z < 6 else YROWS + (z - 6) * 12
+            place[z * 16 + r, first + r] = 1.0
         for r in range(3):
             place[z * 16 + 12 + r, 72 + r] = 1.0
     return jnp.asarray(place, BF)
@@ -553,35 +548,30 @@
         (),
         3.0,
     )
-    sent = call(
-        backward_kernel,
-        [shape(XROWS, TOK)] * N_SEQ,
-        (projected, fk, fv, pnear, pfar, grad_attended, loss, spread_order()),
-        [pltpu.VMEM((TOK, D), F32)] * 5 + [pltpu.VMEM((SECTIONS, HALF, TOK), BF)],
-        4.0,
-    )
-    got = swap(sent, "seq", SEQ_TURNS)
     out_mine, out_other = call(
         out_kernel, [shape(HALF, D)] * 2, (grad_mixed, attended, out_order())
     )
     out_other = lax.ppermute(out_other, "slide", CORE_PAIRS)
-    out = call(out_core_kernel, [shape(SUB, D)] * NY, (out_mine, out_other, sent[0]), unread=1)
-    out = swap(out, "slide", Y_TURNS)
-    out_rows = out
-    out_sums = call(out_y_kernel, [shape(32, D)] * N_SEQ, (*out, out_pad_order()))
-    out = swap(out_sums, "seq", SEQ_TURNS)
-    mine, other = call(
+    (turned,) = call(
+        backward_kernel,
+        [shape(SECTIONS, HALF, TOK)],
+        (projected, fk, fv, pnear, pfar, grad_attended, spread_order()),
+        [pltpu.VMEM((TOK, D), F32)] * 5,
+        4.0,
+    )
+    sent = call(pack_kernel, [shape(XROWS, TOK)] * N_SEQ, (turned, loss, out_mine, out_other))
+    got = swap(sent, "seq", SEQ_TURNS)
+    mine, other, out = call(
         product_kernel,
-        [shape(NY * YROWS, D)] * 2,
-        (*got, pn, product_order(), *out_rows[1:]),
-        [pltpu.VMEM((N_SEQ, XROWS, TOK), BF), pltpu.VMEM((6 * SUB, N_SEQ * TOK), BF)],
+        [shape(NY * YROWS, D), shape(NY * YROWS, D), shape(SUB, D)],
+        (*got, pn, product_order()),
+        [pltpu.VMEM((N_SEQ, MAINROWS, TOK), BF), pltpu.VMEM((6 * SUB, N_SEQ * TOK), BF)],
         3.0,
-        unread=3,
     )
     other = lax.ppermute(other, "slide", CORE_PAIRS)
-    by_y = call(core_kernel, [shape(YROWS, D)] * NY, (mine, other, out_sums[0]), unread=1)
+    by_y = call(core_kernel, [shape(ALLROWS, D)] * NY, (mine, other, out, out_pad_order()))
     by_y = swap(by_y, "slide", Y_TURNS)
-    (by_z,) = call(y_kernel, [shape(NZ, 16, D)], (*by_y, *out, pad_order()))
+    (by_z,) = call(y_kernel, [shape(NZ, 16, D)], (*by_y, pad_order()))
     by_z = lax.all_to_all(by_z, "slide", 0, 0, tiled=True, axis_index_groups=Z_GROUPS)
     gradients, loss = call(z_kernel, [shape(12, D, dtype=F32), shape(1, 1, dtype=F32)], (by_z,))
     return (gradients, loss[0, 0])

time: 88 us -> 86 us (0.977)
  the two profiles are of different devices: /device:TPU:8 before, /device:TPU:2 now
where the time goes in v6:
time: 86 us; the launch traced here: 84.9 us
  waiting for transfers between devices  32 us (37%)
  blocking collectives  18.2 us (21%)
  Pallas kernels  16.3 us (19%)
  starting transfers between devices  16 us (19%)
  between operations  1.5 us (2%)
  local copies, waits for them, and re-layouts  0.97 us (1%)
    ppermute x9, waiting for transfers between devices, swap(): got = {t: lax.ppermute(arrays[t], axis, turns[t]) for t in (2, 1, 3)}  30.2 us
    all_to_all x1, blocking collectives, per_device(): lax.all_to_all(by_z, 'slide', 0, 0, tiled=True, axis_index_groups=Z_GROUPS)  18.2 us
    pallas_call x11, Pallas kernels, call(): pl.pallas_call(kernel, out_shape=out_shapes, in_specs=specs, out_specs=[V...  16.3 us
    ppermute x9, starting transfers between devices, swap(): got = {t: lax.ppermute(arrays[t], axis, turns[t]) for t in (2, 1, 3)}  15.8 us
    ppermute x1, waiting for transfers between devices, per_device(): other = lax.ppermute(other, 'slide', CORE_PAIRS)  1.84 us
  transfers between devices with their start and end apart: 11, of which 8 were waited for; matrix products, arithmetic and copies ran while one was open for 0% of the time, Pallas kernels for 5%

profile of v6, /device:TPU:2, one launch (start us, length us, event | category | flops | bytes accessed | tf_op | source)
XLA Modules:
  0.0 84.9 jit_solution(16641678507903157032)
XLA Ops:
  0.6 0.0 copy-start.5
  0.6 0.0 copy-start.3
  0.7 0.0 copy-start
  0.7 3.4 %shard_map.131 = (bf16[128,768]{1,0:T(8,128)(2,1)}, bf16[128,768]{1,0:T(8,128)(2,1)}) custom-call(bf16[1,128,1536]{2,1,0:T(8,128)(2,1)} %tiles_ref.1, s32[1,128]{1,0:T(1,128)} %masked_ref.1, f32[768]{0:T(1024)} %gain_hbm.1, bf16[1536,768]{1,0:T(8,128)(2,1)} %w_in_ref.1), custom_call_target="tpu_custom_call" | custom-call | flops 2000000000 | bytes 2000000 | tf_op jit(solution)/shard_map/pallas_call | solution.py:462
  4.1 2.3 %collective-permute-start.2 = (bf16[128,768]{1,0:T(8,128)(2,1)}, bf16[128,768]{1,0:T(8,128)(2,1)S(1)}, u32[]{:S(2)}, u32[]{:S(2)}) collective-permute-start(bf16[128,768]{1,0:T(8,128)(2,1)} %get-tuple-element.34.normed_ref.n0), channel_id=1, source_target_pairs={{0,3},{1,0},{2,1},{3,2},{4,7},{5,4},{6,5},{7,6},{8,11},{9,8},{10,9... | collective-permute-start | bytes 589832 | tf_op jit(solution)/shard_map/ppermute | solution.py:498
  6.4 0.7 collective-permute-start.1
  7.1 1.8 %collective-permute-start = (bf16[128,768]{1,0:T(8,128)(2,1)}, bf16[128,768]{1,0:T(8,128)(2,1)S(1)}, u32[]{:S(2)}, u32[]{:S(2)}) collective-permute-start(bf16[128,768]{1,0:T(8,128)(2,1)} %get-tuple-element.34.normed_ref.n0), channel_id=1, source_target_pairs={{0,1},{1,2},{2,3},{3,0},{4,5},{5,6},{6,7},{7,4},{8,9},{9,10},{10,1... | collective-permute-start | bytes 589832 | tf_op jit(solution)/shard_map/ppermute | solution.py:498
  9.6 0.0 copy-done.5
  9.6 0.0 copy-done.3
  9.6 0.0 copy-done
  9.6 0.0 copy-start.4
  9.6 0.9 %copy-done.4 = bf16[128,768]{1,0:T(8,128)(2,1)S(1)} copy-done((bf16[128,768]{1,0:T(8,128)(2,1)S(1)}, bf16[128,768]{1,0:T(8,128)(2,1)}, u32[]{:S(2)}) %copy-start.4) | copy-done | bytes 196632
  10.5 1.2 %shard_map.132 = (bf16[128,2304]{1,0:T(8,128)(2,1)S(1)}, f32[4,128,512]{2,1,0:T(8,128)S(1)}, f32[16,128]{1,0:T(8,128)S(1)}, f32[16,128]{1,0:T(8,128)S(1)}, bf16[...) custom-call(s32[1]{0:T(128)S(6)} %copy.14.count_ref, bf16[128,768]{1,0:T(8,128)(2,1)S(1)} %copy-done.4, ...), custom_call_target="tpu_custom_call" | custom-call | flops 5000000000 | bytes 5000000 | tf_op jit(solution)/shard_map/pallas_call | solution.py:462
  11.7 0.0 collective-permute-done.2.n3
  11.7 4.5 %collective-permute-done.1.n2 = bf16[128,768]{1,0:T(8,128)(2,1)S(1)} collective-permute-done((bf16[128,768]{1,0:T(8,128)(2,1)}, bf16[128,768]{1,0:T(8,128)(2,1)S(1)}, u32[]{:S(2)}, u32[]{:S(2)}) %collective-permute-start.1) | collective-permute-done | bytes 196640 | tf_op jit(solution)/shard_map/ppermute | solution.py:498
  16.2 0.9 %collective-permute-done.n1 = bf16[128,768]{1,0:T(8,128)(2,1)S(1)} collective-permute-done((bf16[128,768]{1,0:T(8,128)(2,1)}, bf16[128,768]{1,0:T(8,128)(2,1)S(1)}, u32[]{:S(2)}, u32[]{:S(2)}) %collective-permute-start) | collective-permute-done | bytes 196640 | tf_op jit(solution)/shard_map/ppermute | solution.py:498
  17.1 2.4 %shard_map.133 = (bf16[4,128,768]{2,1,0:T(8,128)(2,1)S(1)}, bf16[128,768]{1,0:T(8,128)(2,1)S(1)}, bf16[128,768]{1,0:T(8,128)(2,1)S(1)}, f32[4,128,512]{2,1,0:T(8...) custom-call(s32[1]{0:T(128)S(6)} %copy.14.count_ref, bf16[128,768]{1,0:T(8,128)(2,1)S(1)} %copy-done.4, ...), custom_call_target="tpu_custom_call" | custom-call | flops 4000000000 | bytes 4000000 | tf_op jit(solution)/shard_map/pallas_call | solution.py:462
  19.5 0.0 copy-start.6
  19.5 1.7 %shard_map.134 = (bf16[128,768]{1,0:T(8,128)(2,1)S(1)}, bf16[16,128]{1,0:T(8,128)(2,1)S(1)}, bf16[128,768]{1,0:T(8,128)(2,1)S(1)}) custom-call(bf16[128,768]{1,0:T(8,128)(2,1)S(1)} %get-tuple-element.43.att_ref, bf16[128,768]{1,0:T(8,128)(2,1)S(1)} %copy-done.11, bf16[128,1536]{1,0:T(8,128)(2,1)S(1)} %get-tuple-element.45.tiles_ref, ...), custom_call_target="tpu_custom_call" | custom-call | flops 3000000000 | bytes 3000000 | tf_op jit(solution)/shard_map/pallas_call | solution.py:462
  21.2 0.0 copy-start.8
  21.2 0.0 copy-done.6
  21.2 1.4 %shard_map.136 = (bf16[384,768]{1,0:T(8,128)(2,1)S(1)}, bf16[384,768]{1,0:T(8,128)(2,1)S(1)}) custom-call(bf16[128,768]{1,0:T(8,128)(2,1)S(1)} %get-tuple-element.49.gm_ref, bf16[128,768]{1,0:T(8,128)(2,1)S(1)} %get-tuple-element.43.att_ref, bf16[768,768]{1,0:T(8,128)(2,1)S(1)} %copy-done.6), custom_call_target="tpu_custom_call" | custom-call | flops 1000000000 | bytes 1000000 | tf_op jit(solution)/shard_map/pallas_call | solution.py:462
  22.6 0.1 collective-permute-start.3
  22.7 0.0 copy-done.8
  22.7 2.9 %shard_map.135.turned_ref = bf16[10,384,128]{2,1,0:T(8,128)(2,1)S(1)} custom-call(bf16[128,2304]{1,0:T(8,128)(2,1)S(1)} %get-tuple-element.35.proj_ref, bf16[128,768]{1,0:T(8,128)(2,1)S(1)} %get-tuple-element.39.fk_ref, bf16[128,768]{1,0:T(8,128)(2,1)S(1)} %get-tuple-element.40.fv_ref, f32[4,128,512]{2,1,0:T(8,128)S(1)} %get-tuple-element.41.pnear_ref, ...), custom_call_target="tpu_custom_call" | custom-call | flops 4000000000 | bytes 4000000 | tf_op jit(solution)/shard_map/pallas_call | solution.py:462
  25.6 0.0 copy-start.7
  25.6 0.0 collective-permute-done.3.other_ref
  25.6 0.2 shard_map.137
  25.8 1.7 %collective-permute-start.4 = (bf16[1552,128]{1,0:T(8,128)(2,1)S(1)}, bf16[1552,128]{1,0:T(8,128)(2,1)S(1)}, u32[]{:S(2)}, u32[]{:S(2)}) collective-permute-start(bf16[1552,128]{1,0:T(8,128)(2,1)S(1)} %get-tuple-element.53), channel_id=1, source_target_pairs={{0,1},{1,2},{2,3},{3,0},{4,5},{5,6},{6,7},{7,4},{8,9},{9,10},{10,1... | collective-permute-start | bytes 1191944 | tf_op jit(solution)/shard_map/ppermute | solution.py:498
  27.5 3.3 %collective-permute-start.5 = (bf16[1552,128]{1,0:T(8,128)(2,1)S(1)}, bf16[1552,128]{1,0:T(8,128)(2,1)S(1)}, u32[]{:S(2)}, u32[]{:S(2)}) collective-permute-start(bf16[1552,128]{1,0:T(8,128)(2,1)S(1)} %get-tuple-element.54), channel_id=1, source_target_pairs={{0,2},{1,3},{2,0},{3,1},{4,6},{5,7},{6,4},{7,5},{8,10},{9,11},{10,... | collective-permute-start | bytes 1191944 | tf_op jit(solution)/shard_map/ppermute | solution.py:498
  30.8 0.0 collective-permute-start.6
  30.9 8.0 %collective-permute-done.4.x1 = bf16[1552,128]{1,0:T(8,128)(2,1)S(1)} collective-permute-done((bf16[1552,128]{1,0:T(8,128)(2,1)S(1)}, bf16[1552,128]{1,0:T(8,128)(2,1)S(1)}, u32[]{:S(2)}, u32[]{:S(2)}) %collective-permute-start.4) | collective-permute-done | bytes 397344 | tf_op jit(solution)/shard_map/ppermute | solution.py:498
  38.8 2.2 %collective-permute-done.5.x2 = bf16[1552,128]{1,0:T(8,128)(2,1)S(1)} collective-permute-done((bf16[1552,128]{1,0:T(8,128)(2,1)S(1)}, bf16[1552,128]{1,0:T(8,128)(2,1)S(1)}, u32[]{:S(2)}, u32[]{:S(2)}) %collective-permute-start.5) | collective-permute-done | bytes 397344 | tf_op jit(solution)/shard_map/ppermute | solution.py:498
  41.1 7.8 %collective-permute-done.6.x3 = bf16[1552,128]{1,0:T(8,128)(2,1)S(1)} collective-permute-done((bf16[1552,128]{1,0:T(8,128)(2,1)S(1)}, bf16[1552,128]{1,0:T(8,128)(2,1)S(1)}, u32[]{:S(2)}, u32[]{:S(2)}) %collective-permute-start.6) | collective-permute-done | bytes 397344 | tf_op jit(solution)/shard_map/ppermute | solution.py:498
  48.9 2.0 %shard_map.138 = (bf16[320,768]{1,0:T(8,128)(2,1)S(1)}, bf16[320,768]{1,0:T(8,128)(2,1)S(1)}, bf16[96,768]{1,0:T(8,128)(2,1)S(1)}) custom-call(bf16[1552,128]{1,0:T(8,128)(2,1)S(1)} %get-tuple-element.52.x0, bf16[1552,128]{1,0:T(8,128)(2,1)S(1)} %collective-permute-done.4.x1, bf16[1552,128]{1,0:T(8,128)(2,1)S(1)} %collective-permute-done.5.x2, ...), custom_call_target="tpu_custom_call" | custom-call | flops 3000000000 | bytes 3000000 | tf_op jit(solution)/shard_map/pallas_call | solution.py:462
  50.9 0.0 copy-start.9
  50.9 0.1 collective-permute-start.7
  51.0 1.8 %collective-permute-done.7.other_ref = bf16[320,768]{1,0:T(8,128)(2,1)S(1)} collective-permute-done((bf16[320,768]{1,0:T(8,128)(2,1)S(1)}, bf16[320,768]{1,0:T(8,128)(2,1)S(1)}, u32[]{:S(2)}, u32[]{:S(2)}) %collective-permute-start.7) | collective-permute-done | bytes 491552 | tf_op jit(solution)/shard_map/ppermute | solution.py:571
  52.9 0.3 shard_map.139
  53.2 1.7 %collective-permute-start.8 = (bf16[112,768]{1,0:T(8,128)(2,1)S(1)}, bf16[112,768]{1,0:T(8,128)(2,1)S(1)}, u32[]{:S(2)}, u32[]{:S(2)}) collective-permute-start(bf16[112,768]{1,0:T(8,128)(2,1)S(1)} %get-tuple-element.61), channel_id=1, source_target_pairs={{0,8},{4,12},{8,16},{12,20},{16,24},{20,28},{24,0},{28,4},{32,40},... | collective-permute-start | bytes 516104 | tf_op jit(solution)/shard_map/ppermute | solution.py:498
  54.8 2.9 %collective-permute-start.9 = (bf16[112,768]{1,0:T(8,128)(2,1)S(1)}, bf16[112,768]{1,0:T(8,128)(2,1)S(1)}, u32[]{:S(2)}, u32[]{:S(2)}) collective-permute-start(bf16[112,768]{1,0:T(8,128)(2,1)S(1)} %get-tuple-element.62), channel_id=1, source_target_pairs={{0,16},{4,20},{8,24},{12,28},{16,0},{20,4},{24,8},{28,12},{32,48},... | collective-permute-start | bytes 516104 | tf_op jit(solution)/shard_map/ppermute | solution.py:498
  57.7 1.4 %collective-permute-start.10 = (bf16[112,768]{1,0:T(8,128)(2,1)S(1)}, bf16[112,768]{1,0:T(8,128)(2,1)S(1)}, u32[]{:S(2)}, u32[]{:S(2)}) collective-permute-start(bf16[112,768]{1,0:T(8,128)(2,1)S(1)} %get-tuple-element.63), channel_id=1, source_target_pairs={{0,24},{4,28},{8,0},{12,4},{16,8},{20,12},{24,16},{28,20},{32,56},... | collective-permute-start | bytes 516104 | tf_op jit(solution)/shard_map/ppermute | solution.py:498
  59.1 1.9 %collective-permute-done.8.y1 = bf16[112,768]{1,0:T(8,128)(2,1)S(1)} collective-permute-done((bf16[112,768]{1,0:T(8,128)(2,1)S(1)}, bf16[112,768]{1,0:T(8,128)(2,1)S(1)}, u32[]{:S(2)}, u32[]{:S(2)}) %collective-permute-start.8) | collective-permute-done | bytes 172064 | tf_op jit(solution)/shard_map/ppermute | solution.py:498
  60.9 4.9 %collective-permute-done.9.y2 = bf16[112,768]{1,0:T(8,128)(2,1)S(1)} collective-permute-done((bf16[112,768]{1,0:T(8,128)(2,1)S(1)}, bf16[112,768]{1,0:T(8,128)(2,1)S(1)}, u32[]{:S(2)}, u32[]{:S(2)}) %collective-permute-start.9) | collective-permute-done | bytes 172064 | tf_op jit(solution)/shard_map/ppermute | solution.py:498
  65.8 0.0 collective-permute-done.10.y3
  65.8 0.3 shard_map.140
  66.1 18.2 %all_to_all.5.in_ref = bf16[8,16,768]{2,1,0:T(8,128)(2,1)S(1)} all-to-all(bf16[8,16,768]{2,1,0:T(8,128)(2,1)S(1)} %shard_map.140), channel_id=1, replica_groups={{0,32,64,96,128,160,192,224},{4,36,68,100,132,164,196,228},{8,40,72,104..., dimensions={0} | all-to-all | bytes 393216 | tf_op jit(solution)/shard_map/all_to_all | solution.py:575
  84.3 0.7 shard_map.141
  (10 shorter events, 0.0 us)
Async XLA Ops:
  0.6 8.9 %copy-start.5 = (s32[1,128]{1,0:T(1,128)S(1)}, s32[1,128]{1,0:T(1,128)}, u32[]{:S(2)}) copy-start(s32[1,128]{1,0:T(1,128)} %masked_ref.1) | copy-start | bytes 1540
  0.6 8.9 %copy-start.3 = (bf16[1,128,1536]{2,1,0:T(8,128)(2,1)S(1)}, bf16[1,128,1536]{2,1,0:T(8,128)(2,1)}, u32[]{:S(2)}) copy-start(bf16[1,128,1536]{2,1,0:T(8,128)(2,1)} %tiles_ref.1) | copy-start | bytes 1179652
  0.7 8.9 %copy-start = (bf16[768,2304]{1,0:T(8,128)(2,1)S(1)}, bf16[768,2304]{1,0:T(8,128)(2,1)}, u32[]{:S(2)}) copy-start(bf16[768,2304]{1,0:T(8,128)(2,1)} %w_qkv_ref.3) | copy-start | bytes 10616836
  4.1 7.6 %collective-permute-start.2 = (bf16[128,768]{1,0:T(8,128)(2,1)}, bf16[128,768]{1,0:T(8,128)(2,1)S(1)}, u32[]{:S(2)}, u32[]{:S(2)}) collective-permute-start(bf16[128,768]{1,0:T(8,128)(2,1)} %get-tuple-element.34.normed_ref.n0), channel_id=1, source_target_pairs={{0,3},{1,0},{2,1},{3,2},{4,7},{5,4},{6,5},{7,6},{8,11},{9,8},{10,9... | collective-permute-start | bytes 589832 | tf_op jit(solution)/shard_map/ppermute | solution.py:498
  6.4 9.7 %collective-permute-start.1 = (bf16[128,768]{1,0:T(8,128)(2,1)}, bf16[128,768]{1,0:T(8,128)(2,1)S(1)}, u32[]{:S(2)}, u32[]{:S(2)}) collective-permute-start(bf16[128,768]{1,0:T(8,128)(2,1)} %get-tuple-element.34.normed_ref.n0), channel_id=1, source_target_pairs={{0,2},{1,3},{2,0},{3,1},{4,6},{5,7},{6,4},{7,5},{8,10},{9,11},{10,... | collective-permute-start | bytes 589832 | tf_op jit(solution)/shard_map/ppermute | solution.py:498
  7.1 9.9 %collective-permute-start = (bf16[128,768]{1,0:T(8,128)(2,1)}, bf16[128,768]{1,0:T(8,128)(2,1)S(1)}, u32[]{:S(2)}, u32[]{:S(2)}) collective-permute-start(bf16[128,768]{1,0:T(8,128)(2,1)} %get-tuple-element.34.normed_ref.n0), channel_id=1, source_target_pairs={{0,1},{1,2},{2,3},{3,0},{4,5},{5,6},{6,7},{7,4},{8,9},{9,10},{10,1... | collective-permute-start | bytes 589832 | tf_op jit(solution)/shard_map/ppermute | solution.py:498
  9.6 0.9 %copy-start.4 = (bf16[128,768]{1,0:T(8,128)(2,1)S(1)}, bf16[128,768]{1,0:T(8,128)(2,1)}, u32[]{:S(2)}) copy-start(bf16[128,768]{1,0:T(8,128)(2,1)} %get-tuple-element.34.normed_ref.n0) | copy-start | bytes 589828
  17.0 2.4 %copy-start.1 = (bf16[1536,768]{1,0:T(8,128)(2,1)S(1)}, bf16[1536,768]{1,0:T(8,128)(2,1)}, u32[]{:S(2)}) copy-start(bf16[1536,768]{1,0:T(8,128)(2,1)} %w_in_ref.1) | copy-start | bytes 7077892
  17.1 2.4 %copy-start.2 = (bf16[768,768]{1,0:T(8,128)(2,1)S(1)}, bf16[768,768]{1,0:T(8,128)(2,1)}, u32[]{:S(2)}) copy-start(bf16[768,768]{1,0:T(8,128)(2,1)} %w_out_ref.1) | copy-start | bytes 3538948
  17.1 2.4 %copy-start.11 = (bf16[128,768]{1,0:T(8,128)(2,1)S(1)}, bf16[128,768]{1,0:T(8,128)(2,1)}, u32[]{:S(2)}) copy-start(bf16[128,768]{1,0:T(8,128)(2,1)} %get-tuple-element.44.hidden_ref) | copy-start | bytes 589828
  19.5 1.7 %copy-start.6 = (bf16[768,768]{1,0:T(8,128)(2,1)S(1)}, bf16[768,768]{1,0:T(8,128)(2,1)}, u32[]{:S(2)}) copy-start(bf16[768,768]{1,0:T(8,128)(2,1)} %constant.10.clone.order_ref) | copy-start | bytes 3538948
  21.2 1.5 %copy-start.8 = (bf16[384,384]{1,0:T(8,128)(2,1)S(1)}, bf16[384,384]{1,0:T(8,128)(2,1)}, u32[]{:S(2)}) copy-start(bf16[384,384]{1,0:T(8,128)(2,1)} %constant.11.clone.spread_ref) | copy-start | bytes 884740
  22.6 3.0 %collective-permute-start.3 = (bf16[384,768]{1,0:T(8,128)(2,1)S(1)}, bf16[384,768]{1,0:T(8,128)(2,1)S(1)}, u32[]{:S(2)}, u32[]{:S(2)}) collective-permute-start(bf16[384,768]{1,0:T(8,128)(2,1)S(1)} %get-tuple-element.51), channel_id=1, source_target_pairs={{0,4},{4,0},{8,12},{12,8},{16,20},{20,16},{24,28},{28,24},{32,36},... | collective-permute-start | bytes 1769480 | tf_op jit(solution)/shard_map/ppermute | solution.py:554
  25.6 23.3 %copy-start.7 = (bf16[640,576]{1,0:T(8,128)(2,1)S(1)}, bf16[640,576]{1,0:T(8,128)(2,1)}, u32[]{:S(2)}) copy-start(bf16[640,576]{1,0:T(8,128)(2,1)} %constant.12.clone.order_ref) | copy-start | bytes 2211844
  25.8 13.0 %collective-permute-start.4 = (bf16[1552,128]{1,0:T(8,128)(2,1)S(1)}, bf16[1552,128]{1,0:T(8,128)(2,1)S(1)}, u32[]{:S(2)}, u32[]{:S(2)}) collective-permute-start(bf16[1552,128]{1,0:T(8,128)(2,1)S(1)} %get-tuple-element.53), channel_id=1, source_target_pairs={{0,1},{1,2},{2,3},{3,0},{4,5},{5,6},{6,7},{7,4},{8,9},{9,10},{10,1... | collective-permute-start | bytes 1191944 | tf_op jit(solution)/shard_map/ppermute | solution.py:498
  27.5 13.6 %collective-permute-start.5 = (bf16[1552,128]{1,0:T(8,128)(2,1)S(1)}, bf16[1552,128]{1,0:T(8,128)(2,1)S(1)}, u32[]{:S(2)}, u32[]{:S(2)}) collective-permute-start(bf16[1552,128]{1,0:T(8,128)(2,1)S(1)} %get-tuple-element.54), channel_id=1, source_target_pairs={{0,2},{1,3},{2,0},{3,1},{4,6},{5,7},{6,4},{7,5},{8,10},{9,11},{10,... | collective-permute-start | bytes 1191944 | tf_op jit(solution)/shard_map/ppermute | solution.py:498
  30.8 18.1 %collective-permute-start.6 = (bf16[1552,128]{1,0:T(8,128)(2,1)S(1)}, bf16[1552,128]{1,0:T(8,128)(2,1)S(1)}, u32[]{:S(2)}, u32[]{:S(2)}) collective-permute-start(bf16[1552,128]{1,0:T(8,128)(2,1)S(1)} %get-tuple-element.55), channel_id=1, source_target_pairs={{0,3},{1,0},{2,1},{3,2},{4,7},{5,4},{6,5},{7,6},{8,11},{9,8},{10,9... | collective-permute-start | bytes 1191944 | tf_op jit(solution)/shard_map/ppermute | solution.py:498
  48.9 4.0 %copy-start.10 = (bf16[128,96]{1,0:T(8,128)(2,1)S(1)}, bf16[128,96]{1,0:T(8,128)(2,1)}, u32[]{:S(2)}) copy-start(bf16[128,96]{1,0:T(8,128)(2,1)} %constant.13.clone.order_ref) | copy-start | bytes 73732
  50.9 14.9 %copy-start.9 = (bf16[128,112]{1,0:T(8,128)(2,1)S(1)}, bf16[128,112]{1,0:T(8,128)(2,1)}, u32[]{:S(2)}) copy-start(bf16[128,112]{1,0:T(8,128)(2,1)} %constant.14.clone.order_ref) | copy-start | bytes 86020
  50.9 2.0 %collective-permute-start.7 = (bf16[320,768]{1,0:T(8,128)(2,1)S(1)}, bf16[320,768]{1,0:T(8,128)(2,1)S(1)}, u32[]{:S(2)}, u32[]{:S(2)}) collective-permute-start(bf16[320,768]{1,0:T(8,128)(2,1)S(1)} %get-tuple-element.58), channel_id=1, source_target_pairs={{0,4},{4,0},{8,12},{12,8},{16,20},{20,16},{24,28},{28,24},{32,36},... | collective-permute-start | bytes 1474568 | tf_op jit(solution)/shard_map/ppermute | solution.py:571
  53.2 7.8 %collective-permute-start.8 = (bf16[112,768]{1,0:T(8,128)(2,1)S(1)}, bf16[112,768]{1,0:T(8,128)(2,1)S(1)}, u32[]{:S(2)}, u32[]{:S(2)}) collective-permute-start(bf16[112,768]{1,0:T(8,128)(2,1)S(1)} %get-tuple-element.61), channel_id=1, source_target_pairs={{0,8},{4,12},{8,16},{12,20},{16,24},{20,28},{24,0},{28,4},{32,40},... | collective-permute-start | bytes 516104 | tf_op jit(solution)/shard_map/ppermute | solution.py:498
  54.8 11.0 %collective-permute-start.9 = (bf16[112,768]{1,0:T(8,128)(2,1)S(1)}, bf16[112,768]{1,0:T(8,128)(2,1)S(1)}, u32[]{:S(2)}, u32[]{:S(2)}) collective-permute-start(bf16[112,768]{1,0:T(8,128)(2,1)S(1)} %get-tuple-element.62), channel_id=1, source_target_pairs={{0,16},{4,20},{8,24},{12,28},{16,0},{20,4},{24,8},{28,12},{32,48},... | collective-permute-start | bytes 516104 | tf_op jit(solution)/shard_map/ppermute | solution.py:498
  57.7 8.1 %collective-permute-start.10 = (bf16[112,768]{1,0:T(8,128)(2,1)S(1)}, bf16[112,768]{1,0:T(8,128)(2,1)S(1)}, u32[]{:S(2)}, u32[]{:S(2)}) collective-permute-start(bf16[112,768]{1,0:T(8,128)(2,1)S(1)} %get-tuple-element.63), channel_id=1, source_target_pairs={{0,24},{4,28},{8,0},{12,4},{16,8},{20,12},{24,16},{28,20},{32,56},... | collective-permute-start | bytes 516104 | tf_op jit(solution)/shard_map/ppermute | solution.py:498

commit v7 on v4

--- a/solution.py
+++ b/solution.py
@@ -78,7 +78,9 @@
 
 
 def prep_kernel(
-    tiles_hbm, masked_hbm, gain_hbm, w_in_hbm, hidden_out, normed_out, tiles, masked, gain, w_in, sems
+    tiles_hbm, masked_hbm, gain_hbm, w_in_hbm, w_qkv_hbm,
+    hidden_out, normed_out, proj_out, dilated_out,
+    tiles, masked, gain, w_in, w_qkv, sems,
 ):
     blocks = w_in_hbm.shape[0] // 256
     loads = [
@@ -88,11 +90,17 @@
     ]
     chunks = [
         pltpu.make_async_copy(
-            w_in_hbm.at[256 * i : 256 * (i + 1)], w_in.at[256 * i : 256 * (i + 1)], sems.at[3 + i]
+            w_in_hbm.at[256 * i : 256 * (i + 1)], w_in.at[256 * i : 256 * (i + 1)], sems.at[6 + i]
         )
         for i in range(blocks)
     ]
-    for copy in loads + chunks:
+    parts = [
+        pltpu.make_async_copy(
+            w_qkv_hbm.at[:, D * i : D * (i + 1)], w_qkv.at[:, D * i : D * (i + 1)], sems.at[3 + i]
+        )
+        for i in range(3)
+    ]
+    for copy in loads + chunks + parts[1:] + parts[:1]:
         copy.start()
     order = class_order()
     positions = lax.axis_index("seq") * TOK + iota((TOK, TOK), 0)
@@ -109,7 +117,18 @@
     hidden_out[...] = hidden_f.astype(BF)
     scale_rows = lax.rsqrt(jnp.mean(hidden_f * hidden_f, axis=1, keepdims=True) + NORM_EPS)
     loads[2].wait()
-    normed_out[...] = (hidden_f * scale_rows * gain[...].reshape(1, D)).astype(BF)
+    normed = (hidden_f * scale_rows * gain[...].reshape(1, D)).astype(BF)
+    normed_out[...] = normed
+    for part in (1, 2, 0):
+        parts[part].wait()
+        for block in range(D // 256):
+            first = part * D + block * 256
+            rows = nn(normed, w_qkv[:, first : first + 256]).astype(BF)
+            proj_out[:, first : first + 256] = rows
+            if part > 0:
+                lane_class = ((iota((FAR, 256), 1) + block * 256) // HD) & 3
+                pieces = [rows[FAR * r : FAR * (r + 1)] for r in range(RATE)]
+                dilated_out[:, first - D : first - D + 256] = by_class(lane_class, pieces)
 
 
 def window(group):
@@ -141,17 +160,14 @@
 
 
 def near_kernel(
-    count_ref, normed_ref, w_qkv_ref, tiles_ref, masked_ref,
-    proj_ref, exp_ref, top_ref, sum_ref, tiles_out, flag_ref,
+    count_ref, normed_ref, proj_ref, tiles_ref, masked_ref,
+    exp_ref, top_ref, sum_ref, tiles_out, flag_ref, late_ref,
 ):
     count = count_ref[0]
     pos0 = lax.axis_index("seq") * TOK
     flag_ref[...] = masked_rows(pos0 + class_major(iota((TOK, TOK), 0)), masked_ref[...])
     tiles_out[...] = nn(class_order(), tiles_ref[0]).astype(BF)
-    normed = normed_ref[...]
-    for block in range(3 * D // 256):
-        cols = slice(block * 256, (block + 1) * 256)
-        proj_ref[:, cols] = nn(normed, w_qkv_ref[:, cols]).astype(BF)
+    late_ref[...] = normed_ref[...]
     square = (TOK, TOK)
     key_pos = pos0 + class_major(iota(square, 0))
     query_pos = pos0 + class_major(iota(square, 1))
@@ -173,26 +189,16 @@
 
 
 def far_kernel(
-    count_ref, n0, n1, n2, n3, proj_ref, exp_ref, top_ref, sum_ref, w_qkv_ref,
-    pn_ref, fk_ref, fv_ref, pnear_ref, pfar_ref, att_ref,
+    count_ref, f0, f1, f2, f3, proj_ref, exp_ref, top_ref, sum_ref,
+    fk_ref, fv_ref, pnear_ref, pfar_ref, att_ref,
     att_acc,
 ):
     count = count_ref[0]
     seq = lax.axis_index("seq")
-    for turn, ref in enumerate((n0, n1, n2, n3)):
-        pn_ref[(seq - turn) & 3] = ref[...]
-    pn_all = pn_ref[...].reshape(N_SEQ * TOK, D)
-    for part, far_ref in enumerate((fk_ref, fv_ref)):
-        for block in range(D // 256):
-            first = (1 + part) * D + block * 256
-            every = nn(pn_all, w_qkv_ref[:, first : first + 256])
-            lane_class = ((iota((FAR, 256), 1) + block * 256) // HD) & 3
-            for src in range(N_SEQ):
-                base = src * TOK
-                pieces = [every[base + FAR * r : base + FAR * (r + 1)] for r in range(RATE)]
-                far_ref[src * FAR : (src + 1) * FAR, block * 256 : (block + 1) * 256] = by_class(
-                    lane_class, pieces
-                ).astype(BF)
+    for turn, ref in enumerate((f0, f1, f2, f3)):
+        rows = pl.ds(pl.multiple_of(((seq - turn) & 3) * FAR, FAR), FAR)
+        fk_ref[rows] = ref[:, 0:D]
+        fv_ref[rows] = ref[:, D:]
 
     square = (TOK, TOK)
     far_row = iota(square, 0)
@@ -251,7 +257,7 @@
 
 
 def backward_kernel(
-    proj_ref, fk_ref, fv_ref, pnear_ref, pfar_ref, ga_ref, loss_ref, spread_ref,
+    proj_ref, fk_ref, fv_ref, pnear_ref, pfar_ref, ga_ref, loss_ref, spread_ref, wait1, wait2, wait3,
     x0, x1, x2, x3,
     gq, gk, gv, gkf, gvf, turned,
 ):
@@ -306,11 +312,15 @@
         ref[SECTIONS * SUB :] = loss_ref[...]
 
 
-def product_kernel(x0, x1, x2, x3, pn_ref, order_ref, wait_ref, mine_ref, other_ref, got, left):
+def product_kernel(
+    x0, x1, x2, x3, n0, n1, n2, n3, order_ref, wait_ref, mine_ref, other_ref, got, left, right
+):
     seq = lax.axis_index("seq")
     core = lax.axis_index("slide") & 1
-    for turn, x_ref in enumerate((x0, x1, x2, x3)):
-        got[(seq - turn) & 3] = x_ref[...]
+    for turn, (x_ref, n_ref) in enumerate(zip((x0, x1, x2, x3), (n0, n1, n2, n3))):
+        src = (seq - turn) & 3
+        got[src] = x_ref[...]
+        right[pl.ds(pl.multiple_of(src * TOK, TOK), TOK)] = n_ref[...]
     for src in range(N_SEQ):
         left[0 : 2 * SUB, src * TOK : (src + 1) * TOK] = got[src, 0 : 2 * SUB]
     shape = (SUB, TOK)
@@ -333,7 +343,7 @@
                 for r in range(RATE):
                     total = total + jnp.where(spots[r], turns[(r - src) & 3], 0.0)
                 left[near_at : near_at + SUB, src * TOK : (src + 1) * TOK] = total.astype(BF)
-    whole = nn(left[...], pn_ref[...].reshape(N_SEQ * TOK, D)).astype(BF)
+    whole = nn(left[...], right[...]).astype(BF)
     loss = got[0, SECTIONS * SUB :].astype(F32)
     for src in range(1, N_SEQ):
         loss = loss + got[src, SECTIONS * SUB :].astype(F32)
@@ -498,60 +508,56 @@
 
 def per_device(embeddings, tile_counts, masked_tiles, w_in, norm_gain, w_qkv, w_out):
     inv_count = 1.0 / (lax.axis_size("slide") * masked_tiles.shape[1])
-    hidden, normed = call(
+    hidden, normed, projected, dilated = call(
         prep_kernel,
-        [shape(TOK, D), shape(TOK, D)],
-        (embeddings, masked_tiles, norm_gain, w_in),
+        [shape(TOK, D), shape(TOK, D), shape(TOK, 3 * D), shape(FAR, 2 * D)],
+        (embeddings, masked_tiles, norm_gain, w_in, w_qkv),
         [
             pltpu.VMEM((TOK, 2 * D), BF),
             pltpu.VMEM((1, TOK), jnp.int32),
             pltpu.VMEM((D,), F32),
             pltpu.VMEM((2 * D, D), BF),
-            pltpu.SemaphoreType.DMA((3 + 2 * D // 256,)),
+            pltpu.VMEM((D, 3 * D), BF),
+            pltpu.SemaphoreType.DMA((6 + 2 * D // 256,)),
         ],
-        2.0,
-        [HBM] * 4,
+        4.0,
+        [HBM] * 5,
         60,
     )
-    norms = swap([normed] * N_SEQ, "seq", SEQ_TURNS)
+    fars = swap([dilated] * N_SEQ, "seq", SEQ_TURNS)
     scores = shape(GROUPS, TOK, RATE * TOK, dtype=F32)
     rows = shape(HEADS, TOK, dtype=F32)
-    projected, exps, tops, sums, tiles, flag = call(
+    exps, tops, sums, tiles, flag, late = call(
         near_kernel,
-        [shape(TOK, 3 * D), scores, rows, rows, shape(TOK, 2 * D), shape(TOK, TOK, dtype=F32)],
-        (tile_counts, normed, w_qkv, embeddings, masked_tiles),
+        [scores, rows, rows, shape(TOK, 2 * D), shape(TOK, TOK, dtype=F32), shape(TOK, D)],
+        (tile_counts, normed, projected, embeddings, masked_tiles),
         (),
         5.0,
         [SMEM] + [VMEM] * 4,
     )
-    pn, fk, fv, pnear, pfar, attended = call(
+    norms = swap([late] * N_SEQ, "seq", SEQ_TURNS)
+    fk, fv, pnear, pfar, attended = call(
         far_kernel,
-        [
-            shape(N_SEQ, TOK, D),
-            shape(TOK, D),
-            shape(TOK, D),
-            scores,
-            shape(GROUPS, TOK, TOK, dtype=F32),
-            shape(TOK, D),
-        ],
-        (tile_counts, *norms, projected, exps, tops, sums, w_qkv),
+        [shape(TOK, D), shape(TOK, D), scores, shape(GROUPS, TOK, TOK, dtype=F32), shape(TOK, D)],
+        (tile_counts, *fars, projected, exps, tops, sums),
         [pltpu.VMEM((TOK, D), F32)],
-        4.0,
+        10.0,
     )
     grad_attended, loss, out_mine, out_other = call(
         functools.partial(chain_kernel, inv_count),
         [shape(TOK, D), shape(16, 128), shape(HALF, D), shape(HALF, D)],
         (attended, hidden, tiles, flag, w_in, w_out, out_order()),
         (),
-        3.0,
+        15.0,
     )
     out_other = lax.ppermute(out_other, "slide", CORE_PAIRS)
     sent = call(
         backward_kernel,
         [shape(XROWS, TOK)] * N_SEQ,
-        (projected, fk, fv, pnear, pfar, grad_attended, loss, spread_order()),
+        (projected, fk, fv, pnear, pfar, grad_attended, loss, spread_order(), *norms[1:]),
         [pltpu.VMEM((TOK, D), F32)] * 5 + [pltpu.VMEM((SECTIONS, HALF, TOK), BF)],
-        4.0,
+        8.0,
+        unread=3,
     )
     got = swap(sent, "seq", SEQ_TURNS)
     out = call(out_core_kernel, [shape(SUB, D)] * NY, (out_mine, out_other, sent[0]), unread=1)
@@ -561,8 +567,12 @@
     mine, other = call(
         product_kernel,
         [shape(NY * YROWS, D)] * 2,
-        (*got, pn, product_order(), out_sums[0]),
-        [pltpu.VMEM((N_SEQ, XROWS, TOK), BF), pltpu.VMEM((6 * SUB, N_SEQ * TOK), BF)],
+        (*got, *norms, product_order(), out_sums[0]),
+        [
+            pltpu.VMEM((N_SEQ, XROWS, TOK), BF),
+            pltpu.VMEM((6 * SUB, N_SEQ * TOK), BF),
+            pltpu.VMEM((N_SEQ * TOK, D), BF),
+        ],
         3.0,
         unread=1,
     )

time: 83.4 us -> 84.2 us (level)
  waiting for transfers between devices: 17.6 us -> 14.7 us
  starting transfers between devices: 27.2 us -> 29.8 us
  local copies, waits for them, and re-layouts: 0.97 us -> 2.99 us
    ppermute x15 -> x18, waiting for transfers between devices: 17.6 us -> 14.7 us  [swap(): lax.ppermute(arrays[t], axis, turns[t])]
    ppermute x15 -> x18, starting transfers between devices: 27 us -> 29.4 us  [swap(): lax.ppermute(arrays[t], axis, turns[t])]
    unnamed x24 -> x28, local copies, waits for them, and re-layouts: 0.97 us -> 2.99 us
  transfers between devices with their start and end apart: 17 -> 20, of which waited for: 10 -> 10; matrix products, arithmetic and copies ran while one was open for 0% -> 0% of each run, Pallas kernels for 5% -> 10%
where the time goes in v7:
time: 84.2 us; the launch traced here: 82.7 us
  starting transfers between devices  29.8 us (35%)
  blocking collectives  18 us (21%)
  Pallas kernels  15.7 us (19%)
  waiting for transfers between devices  14.7 us (17%)
  local copies, waits for them, and re-layouts  2.99 us (4%)
  between operations  1.5 us (2%)
    ppermute x18, starting transfers between devices, swap(): lax.ppermute(arrays[t], axis, turns[t])  29.4 us
    all_to_all x1, blocking collectives, per_device(): lax.all_to_all(by_z, 'slide', 0, 0, tiled=True, axis_index_groups=Z_GROUPS)  18 us
    pallas_call x11, Pallas kernels, call(): pl.pallas_call(kernel, out_shape=out_shapes, in_specs=specs, out_specs=[V...  15.7 us
    ppermute x18, waiting for transfers between devices, swap(): lax.ppermute(arrays[t], axis, turns[t])  14.7 us
    unnamed x28, local copies, waits for them, and re-layouts  2.99 us
  transfers between devices with their start and end apart: 20, of which 10 were waited for; matrix products, arithmetic and copies ran while one was open for 0% of the time, Pallas kernels for 10%

profile of v7, /device:TPU:2, one launch (start us, length us, event | category | flops | bytes accessed | tf_op | source)
XLA Modules:
  0.0 82.7 jit_solution(6106637411076862170)
XLA Ops:
  0.7 4.4 %shard_map.131 = (bf16[128,768]{1,0:T(8,128)(2,1)}, bf16[128,768]{1,0:T(8,128)(2,1)}, bf16[128,2304]{1,0:T(8,128)(2,1)}, bf16[32,1536]{1,0:T(8,128)(2,1)}) custom-call(bf16[1,128,1536]{2,1,0:T(8,128)(2,1)} %tiles_ref.1, s32[1,128]{1,0:T(1,128)} %masked_ref.1, f32[768]{0:T(1024)} %gain_hbm.1, bf16[1536,768]{1,0:T(8,128)(2,1)} %w_in_ref.1, ...), custom_call_target="tpu_custom_call" | custom-call | flops 4000000000 | bytes 4000000 | tf_op jit(solution)/shard_map/pallas_call | solution.py:470
  5.1 2.3 %collective-permute-start.2 = (bf16[32,1536]{1,0:T(8,128)(2,1)}, bf16[32,1536]{1,0:T(8,128)(2,1)S(1)}, u32[]{:S(2)}, u32[]{:S(2)}) collective-permute-start(bf16[32,1536]{1,0:T(8,128)(2,1)} %get-tuple-element.42.f0), channel_id=1, source_target_pairs={{0,3},{1,0},{2,1},{3,2},{4,7},{5,4},{6,5},{7,6},{8,11},{9,8},{10,9... | collective-permute-start | bytes 294920 | tf_op jit(solution)/shard_map/ppermute | solution.py:506
  7.5 0.7 collective-permute-start.1
  8.1 1.8 %collective-permute-start = (bf16[32,1536]{1,0:T(8,128)(2,1)}, bf16[32,1536]{1,0:T(8,128)(2,1)S(1)}, u32[]{:S(2)}, u32[]{:S(2)}) collective-permute-start(bf16[32,1536]{1,0:T(8,128)(2,1)} %get-tuple-element.42.f0), channel_id=1, source_target_pairs={{0,1},{1,2},{2,3},{3,0},{4,5},{5,6},{6,7},{7,4},{8,9},{9,10},{10,1... | collective-permute-start | bytes 294920 | tf_op jit(solution)/shard_map/ppermute | solution.py:506
  10.6 1.1 %copy-done.10 = bf16[128,2304]{1,0:T(8,128)(2,1)S(1)} copy-done((bf16[128,2304]{1,0:T(8,128)(2,1)S(1)}, bf16[128,2304]{1,0:T(8,128)(2,1)}, u32[]{:S(2)}) %copy-start.10) | copy-done | bytes 589848
  11.7 0.9 %copy-done.13 = bf16[128,768]{1,0:T(8,128)(2,1)S(1)} copy-done((bf16[128,768]{1,0:T(8,128)(2,1)S(1)}, bf16[128,768]{1,0:T(8,128)(2,1)}, u32[]{:S(2)}) %copy-start.13) | copy-done | bytes 196632
  12.6 0.7 shard_map.132
  13.3 0.3 collective-permute-start.5
  13.6 2.9 %collective-permute-start.4 = (bf16[128,768]{1,0:T(8,128)(2,1)S(1)}, bf16[128,768]{1,0:T(8,128)(2,1)S(1)}, u32[]{:S(2)}, u32[]{:S(2)}) collective-permute-start(bf16[128,768]{1,0:T(8,128)(2,1)S(1)} %get-tuple-element.57.n0), channel_id=1, source_target_pairs={{0,2},{1,3},{2,0},{3,1},{4,6},{5,7},{6,4},{7,5},{8,10},{9,11},{10,... | collective-permute-start | bytes 589832 | tf_op jit(solution)/shard_map/ppermute | solution.py:506
  16.5 1.0 %collective-permute-start.3 = (bf16[128,768]{1,0:T(8,128)(2,1)S(1)}, bf16[128,768]{1,0:T(8,128)(2,1)S(1)}, u32[]{:S(2)}, u32[]{:S(2)}) collective-permute-start(bf16[128,768]{1,0:T(8,128)(2,1)S(1)} %get-tuple-element.57.n0), channel_id=1, source_target_pairs={{0,1},{1,2},{2,3},{3,0},{4,5},{5,6},{6,7},{7,4},{8,9},{9,10},{10,1... | collective-permute-start | bytes 589832 | tf_op jit(solution)/shard_map/ppermute | solution.py:506
  17.5 1.3 %shard_map.133 = (bf16[128,768]{1,0:T(8,128)(2,1)S(1)}, bf16[128,768]{1,0:T(8,128)(2,1)S(1)}, f32[4,128,512]{2,1,0:T(8,128)S(1)}, f32[4,128,128]{2,1,0:T(8,128)S(1)}, bf16[128,768]{1,0:T(8,128)(2,1)S(1)}) custom-call(s32[1]{0:T(128)S(6)} %copy.14.count_ref, bf16[32,1536]{1,0:T(8,128)(2,1)S(1)} %copy-done.3, bf16[32,1536]{1,0:T(8,128)(2,1)S(1)} %collective-permute-done.f1, ...), custom_call_target="tpu_custom_call" | custom-call | flops 10000000000 | bytes 10000000 | tf_op jit(solution)/shard_map/pallas_call | solution.py:470
  18.8 0.3 copy-done
  19.1 0.3 copy-done.1
  19.4 0.4 copy-done.5
  19.8 0.0 copy-done.12
  19.8 2.7 %shard_map.134 = (bf16[128,768]{1,0:T(8,128)(2,1)S(1)}, bf16[16,128]{1,0:T(8,128)(2,1)S(1)}, bf16[384,768]{1,0:T(8,128)(2,1)S(1)}, bf16[384,768]{1,0:T(8,128)(2,1)S(1)}) custom-call(bf16[128,768]{1,0:T(8,128)(2,1)S(1)} %get-tuple-element.51.att_ref, bf16[128,768]{1,0:T(8,128)(2,1)S(1)} %copy-done.12, bf16[128,1536]{1,0:T(8,128)(2,1)S(1)} %get-tuple-element.53.tiles_ref, ...), custom_call_target="tpu_custom_call" | custom-call | flops 15000000512 | bytes 15000000 | tf_op jit(solution)/shard_map/pallas_call | solution.py:470
  22.5 0.3 collective-permute-start.9
  22.8 0.6 collective-permute-done.5.wait3.n3
  23.4 1.8 %collective-permute-done.3.wait1.n1 = bf16[128,768]{1,0:T(8,128)(2,1)S(1)} collective-permute-done((bf16[128,768]{1,0:T(8,128)(2,1)S(1)}, bf16[128,768]{1,0:T(8,128)(2,1)S(1)}, u32[]{:S(2)}, u32[]{:S(2)}) %collective-permute-start.3) | collective-permute-done | bytes 196640 | tf_op jit(solution)/shard_map/ppermute | solution.py:506
  25.2 3.0 %shard_map.135 = (bf16[976,128]{1,0:T(8,128)(2,1)S(1)}, bf16[976,128]{1,0:T(8,128)(2,1)S(1)}, bf16[976,128]{1,0:T(8,128)(2,1)S(1)}, bf16[976,128]{1,0:T(8,128)(2,1)S(1)}) custom-call(bf16[128,2304]{1,0:T(8,128)(2,1)S(1)} %copy-done.11, bf16[128,768]{1,0:T(8,128)(2,1)S(1)} %get-tuple-element.47.fk_ref, bf16[128,768]{1,0:T(8,128)(2,1)S(1)} %get-tuple-element.48.fv_ref, ...), custom_call_target="tpu_custom_call" | custom-call | flops 8000000000 | bytes 8000000 | tf_op jit(solution)/shard_map/pallas_call | solution.py:470
  28.3 0.2 shard_map.136
  28.4 1.7 %collective-permute-start.10 = (bf16[96,768]{1,0:T(8,128)(2,1)S(1)}, bf16[96,768]{1,0:T(8,128)(2,1)S(1)}, u32[]{:S(2)}, u32[]{:S(2)}) collective-permute-start(bf16[96,768]{1,0:T(8,128)(2,1)S(1)} %get-tuple-element.65), channel_id=1, source_target_pairs={{0,8},{4,12},{8,16},{12,20},{16,24},{20,28},{24,0},{28,4},{32,40},... | collective-permute-start | bytes 442376 | tf_op jit(solution)/shard_map/ppermute | solution.py:506
  30.1 1.5 %collective-permute-start.6 = (bf16[976,128]{1,0:T(8,128)(2,1)S(1)}, bf16[976,128]{1,0:T(8,128)(2,1)S(1)}, u32[]{:S(2)}, u32[]{:S(2)}) collective-permute-start(bf16[976,128]{1,0:T(8,128)(2,1)S(1)} %get-tuple-element.59), channel_id=1, source_target_pairs={{0,1},{1,2},{2,3},{3,0},{4,5},{5,6},{6,7},{7,4},{8,9},{9,10},{10,1... | collective-permute-start | bytes 749576 | tf_op jit(solution)/shard_map/ppermute | solution.py:506
  31.6 2.6 %collective-permute-start.7 = (bf16[976,128]{1,0:T(8,128)(2,1)S(1)}, bf16[976,128]{1,0:T(8,128)(2,1)S(1)}, u32[]{:S(2)}, u32[]{:S(2)}) collective-permute-start(bf16[976,128]{1,0:T(8,128)(2,1)S(1)} %get-tuple-element.60), channel_id=1, source_target_pairs={{0,2},{1,3},{2,0},{3,1},{4,6},{5,7},{6,4},{7,5},{8,10},{9,11},{10,... | collective-permute-start | bytes 749576 | tf_op jit(solution)/shard_map/ppermute | solution.py:506
  34.1 0.1 collective-permute-start.8
  34.2 2.9 %collective-permute-start.11 = (bf16[96,768]{1,0:T(8,128)(2,1)S(1)}, bf16[96,768]{1,0:T(8,128)(2,1)S(1)}, u32[]{:S(2)}, u32[]{:S(2)}) collective-permute-start(bf16[96,768]{1,0:T(8,128)(2,1)S(1)} %get-tuple-element.66), channel_id=1, source_target_pairs={{0,16},{4,20},{8,24},{12,28},{16,0},{20,4},{24,8},{28,12},{32,48},... | collective-permute-start | bytes 442376 | tf_op jit(solution)/shard_map/ppermute | solution.py:506
  37.1 1.3 %collective-permute-start.12 = (bf16[96,768]{1,0:T(8,128)(2,1)S(1)}, bf16[96,768]{1,0:T(8,128)(2,1)S(1)}, u32[]{:S(2)}, u32[]{:S(2)}) collective-permute-start(bf16[96,768]{1,0:T(8,128)(2,1)S(1)} %get-tuple-element.67), channel_id=1, source_target_pairs={{0,24},{4,28},{8,0},{12,4},{16,8},{20,12},{24,16},{28,20},{32,56},... | collective-permute-start | bytes 442376 | tf_op jit(solution)/shard_map/ppermute | solution.py:506
  38.4 2.4 %collective-permute-done.11.y2 = bf16[96,768]{1,0:T(8,128)(2,1)S(1)} collective-permute-done((bf16[96,768]{1,0:T(8,128)(2,1)S(1)}, bf16[96,768]{1,0:T(8,128)(2,1)S(1)}, u32[]{:S(2)}, u32[]{:S(2)}) %collective-permute-start.11) | collective-permute-done | bytes 147488 | tf_op jit(solution)/shard_map/ppermute | solution.py:506
  40.8 1.7 %collective-permute-done.12.y3 = bf16[96,768]{1,0:T(8,128)(2,1)S(1)} collective-permute-done((bf16[96,768]{1,0:T(8,128)(2,1)S(1)}, bf16[96,768]{1,0:T(8,128)(2,1)S(1)}, u32[]{:S(2)}, u32[]{:S(2)}) %collective-permute-start.12) | collective-permute-done | bytes 147488 | tf_op jit(solution)/shard_map/ppermute | solution.py:506
  42.5 0.3 shard_map.137
  42.8 2.6 %collective-permute-done.8.x3 = bf16[976,128]{1,0:T(8,128)(2,1)S(1)} collective-permute-done((bf16[976,128]{1,0:T(8,128)(2,1)S(1)}, bf16[976,128]{1,0:T(8,128)(2,1)S(1)}, u32[]{:S(2)}, u32[]{:S(2)}) %collective-permute-start.8) | collective-permute-done | bytes 249888 | tf_op jit(solution)/shard_map/ppermute | solution.py:506
  45.4 2.0 %shard_map.138 = (bf16[320,768]{1,0:T(8,128)(2,1)S(1)}, bf16[320,768]{1,0:T(8,128)(2,1)S(1)}) custom-call(bf16[976,128]{1,0:T(8,128)(2,1)S(1)} %get-tuple-element.58.wait_ref.x0, bf16[976,128]{1,0:T(8,128)(2,1)S(1)} %collective-permute-done.6.x1, bf16[976,128]{1,0:T(8,128)(2,1)S(1)} %collective-permute-done.7.x2, ...), custom_call_target="tpu_custom_call" | custom-call | flops 3000000000 | bytes 3000000 | tf_op jit(solution)/shard_map/pallas_call | solution.py:470
  47.4 0.1 collective-permute-start.13
  47.5 0.7 collective-permute-start.14
  48.2 2.2 %collective-permute-start.15 = (bf16[32,768]{1,0:T(8,128)(2,1)S(1)}, bf16[32,768]{1,0:T(8,128)(2,1)S(1)}, u32[]{:S(2)}, u32[]{:S(2)}) collective-permute-start(bf16[32,768]{1,0:T(8,128)(2,1)S(1)} %get-tuple-element.72), channel_id=1, source_target_pairs={{0,2},{1,3},{2,0},{3,1},{4,6},{5,7},{6,4},{7,5},{8,10},{9,11},{10,... | collective-permute-start | bytes 147464 | tf_op jit(solution)/shard_map/ppermute | solution.py:506
  50.4 2.0 %collective-permute-start.16 = (bf16[32,768]{1,0:T(8,128)(2,1)S(1)}, bf16[32,768]{1,0:T(8,128)(2,1)S(1)}, u32[]{:S(2)}, u32[]{:S(2)}) collective-permute-start(bf16[32,768]{1,0:T(8,128)(2,1)S(1)} %get-tuple-element.73), channel_id=1, source_target_pairs={{0,3},{1,0},{2,1},{3,2},{4,7},{5,4},{6,5},{7,6},{8,11},{9,8},{10,9... | collective-permute-start | bytes 147464 | tf_op jit(solution)/shard_map/ppermute | solution.py:506
  52.4 1.6 %collective-permute-done.15.wait2.o2 = bf16[32,768]{1,0:T(8,128)(2,1)S(1)} collective-permute-done((bf16[32,768]{1,0:T(8,128)(2,1)S(1)}, bf16[32,768]{1,0:T(8,128)(2,1)S(1)}, u32[]{:S(2)}, u32[]{:S(2)}) %collective-permute-start.15) | collective-permute-done | bytes 49184 | tf_op jit(solution)/shard_map/ppermute | solution.py:506
  54.0 0.5 collective-permute-done.16.wait3.o3
  54.5 0.2 shard_map.139
  54.7 1.6 %collective-permute-start.17 = (bf16[80,768]{1,0:T(8,128)(2,1)S(1)}, bf16[80,768]{1,0:T(8,128)(2,1)S(1)}, u32[]{:S(2)}, u32[]{:S(2)}) collective-permute-start(bf16[80,768]{1,0:T(8,128)(2,1)S(1)} %get-tuple-element.75), channel_id=1, source_target_pairs={{0,8},{4,12},{8,16},{12,20},{16,24},{20,28},{24,0},{28,4},{32,40},... | collective-permute-start | bytes 368648 | tf_op jit(solution)/shard_map/ppermute | solution.py:506
  56.4 1.7 %collective-permute-start.18 = (bf16[80,768]{1,0:T(8,128)(2,1)S(1)}, bf16[80,768]{1,0:T(8,128)(2,1)S(1)}, u32[]{:S(2)}, u32[]{:S(2)}) collective-permute-start(bf16[80,768]{1,0:T(8,128)(2,1)S(1)} %get-tuple-element.76), channel_id=1, source_target_pairs={{0,16},{4,20},{8,24},{12,28},{16,0},{20,4},{24,8},{28,12},{32,48},... | collective-permute-start | bytes 368648 | tf_op jit(solution)/shard_map/ppermute | solution.py:506
  58.1 2.3 %collective-permute-start.19 = (bf16[80,768]{1,0:T(8,128)(2,1)S(1)}, bf16[80,768]{1,0:T(8,128)(2,1)S(1)}, u32[]{:S(2)}, u32[]{:S(2)}) collective-permute-start(bf16[80,768]{1,0:T(8,128)(2,1)S(1)} %get-tuple-element.77), channel_id=1, source_target_pairs={{0,24},{4,28},{8,0},{12,4},{16,8},{20,12},{24,16},{28,20},{32,56},... | collective-permute-start | bytes 368648 | tf_op jit(solution)/shard_map/ppermute | solution.py:506
  60.3 1.8 %collective-permute-done.17.y1 = bf16[80,768]{1,0:T(8,128)(2,1)S(1)} collective-permute-done((bf16[80,768]{1,0:T(8,128)(2,1)S(1)}, bf16[80,768]{1,0:T(8,128)(2,1)S(1)}, u32[]{:S(2)}, u32[]{:S(2)}) %collective-permute-start.17) | collective-permute-done | bytes 122912 | tf_op jit(solution)/shard_map/ppermute | solution.py:506
  62.1 1.3 %collective-permute-done.18.y2 = bf16[80,768]{1,0:T(8,128)(2,1)S(1)} collective-permute-done((bf16[80,768]{1,0:T(8,128)(2,1)S(1)}, bf16[80,768]{1,0:T(8,128)(2,1)S(1)}, u32[]{:S(2)}, u32[]{:S(2)}) %collective-permute-start.18) | collective-permute-done | bytes 122912 | tf_op jit(solution)/shard_map/ppermute | solution.py:506
  63.4 0.3 collective-permute-done.19.y3
  63.7 0.3 shard_map.140
  64.0 18.0 %all_to_all.5.in_ref = bf16[8,16,768]{2,1,0:T(8,128)(2,1)S(1)} all-to-all(bf16[8,16,768]{2,1,0:T(8,128)(2,1)S(1)} %shard_map.140), channel_id=1, replica_groups={{0,32,64,96,128,160,192,224},{4,36,68,100,132,164,196,228},{8,40,72,104..., dimensions={0} | all-to-all | bytes 393216 | tf_op jit(solution)/shard_map/all_to_all | solution.py:583
  82.0 0.7 shard_map.141
  (32 shorter events, 0.1 us)
Async XLA Ops:
  0.6 10.0 %copy-start.4 = (s32[1,128]{1,0:T(1,128)S(1)}, s32[1,128]{1,0:T(1,128)}, u32[]{:S(2)}) copy-start(s32[1,128]{1,0:T(1,128)} %masked_ref.1) | copy-start | bytes 1540
  0.6 10.0 %copy-start.2 = (bf16[1,128,1536]{2,1,0:T(8,128)(2,1)S(1)}, bf16[1,128,1536]{2,1,0:T(8,128)(2,1)}, u32[]{:S(2)}) copy-start(bf16[1,128,1536]{2,1,0:T(8,128)(2,1)} %tiles_ref.1) | copy-start | bytes 1179652
  5.1 11.4 %collective-permute-start.2 = (bf16[32,1536]{1,0:T(8,128)(2,1)}, bf16[32,1536]{1,0:T(8,128)(2,1)S(1)}, u32[]{:S(2)}, u32[]{:S(2)}) collective-permute-start(bf16[32,1536]{1,0:T(8,128)(2,1)} %get-tuple-element.42.f0), channel_id=1, source_target_pairs={{0,3},{1,0},{2,1},{3,2},{4,7},{5,4},{6,5},{7,6},{8,11},{9,8},{10,9... | collective-permute-start | bytes 294920 | tf_op jit(solution)/shard_map/ppermute | solution.py:506
  7.5 10.0 %collective-permute-start.1 = (bf16[32,1536]{1,0:T(8,128)(2,1)}, bf16[32,1536]{1,0:T(8,128)(2,1)S(1)}, u32[]{:S(2)}, u32[]{:S(2)}) collective-permute-start(bf16[32,1536]{1,0:T(8,128)(2,1)} %get-tuple-element.42.f0), channel_id=1, source_target_pairs={{0,2},{1,3},{2,0},{3,1},{4,6},{5,7},{6,4},{7,5},{8,10},{9,11},{10,... | collective-permute-start | bytes 294920 | tf_op jit(solution)/shard_map/ppermute | solution.py:506
  8.1 9.3 %collective-permute-start = (bf16[32,1536]{1,0:T(8,128)(2,1)}, bf16[32,1536]{1,0:T(8,128)(2,1)S(1)}, u32[]{:S(2)}, u32[]{:S(2)}) collective-permute-start(bf16[32,1536]{1,0:T(8,128)(2,1)} %get-tuple-element.42.f0), channel_id=1, source_target_pairs={{0,1},{1,2},{2,3},{3,0},{4,5},{5,6},{6,7},{7,4},{8,9},{9,10},{10,1... | collective-permute-start | bytes 294920 | tf_op jit(solution)/shard_map/ppermute | solution.py:506
  10.6 1.1 %copy-start.10 = (bf16[128,2304]{1,0:T(8,128)(2,1)S(1)}, bf16[128,2304]{1,0:T(8,128)(2,1)}, u32[]{:S(2)}) copy-start(bf16[128,2304]{1,0:T(8,128)(2,1)} %get-tuple-element.41.proj_ref) | copy-start | bytes 1769476
  11.7 0.9 %copy-start.13 = (bf16[128,768]{1,0:T(8,128)(2,1)S(1)}, bf16[128,768]{1,0:T(8,128)(2,1)}, u32[]{:S(2)}) copy-start(bf16[128,768]{1,0:T(8,128)(2,1)} %get-tuple-element.43.normed_ref) | copy-start | bytes 589828
  12.6 4.8 %copy-start.3 = (bf16[32,1536]{1,0:T(8,128)(2,1)S(1)}, bf16[32,1536]{1,0:T(8,128)(2,1)}, u32[]{:S(2)}) copy-start(bf16[32,1536]{1,0:T(8,128)(2,1)} %get-tuple-element.42.f0) | copy-start | bytes 294916
  12.6 4.8 %copy-start.11 = (bf16[128,2304]{1,0:T(8,128)(2,1)S(1)}, bf16[128,2304]{1,0:T(8,128)(2,1)}, u32[]{:S(2)}) copy-start(bf16[128,2304]{1,0:T(8,128)(2,1)} %get-tuple-element.41.proj_ref) | copy-start | bytes 1769476
  13.3 10.1 %collective-permute-start.5 = (bf16[128,768]{1,0:T(8,128)(2,1)S(1)}, bf16[128,768]{1,0:T(8,128)(2,1)S(1)}, u32[]{:S(2)}, u32[]{:S(2)}) collective-permute-start(bf16[128,768]{1,0:T(8,128)(2,1)S(1)} %get-tuple-element.57.n0), channel_id=1, source_target_pairs={{0,3},{1,0},{2,1},{3,2},{4,7},{5,4},{6,5},{7,6},{8,11},{9,8},{10,9... | collective-permute-start | bytes 589832 | tf_op jit(solution)/shard_map/ppermute | solution.py:506
  13.6 9.8 %collective-permute-start.4 = (bf16[128,768]{1,0:T(8,128)(2,1)S(1)}, bf16[128,768]{1,0:T(8,128)(2,1)S(1)}, u32[]{:S(2)}, u32[]{:S(2)}) collective-permute-start(bf16[128,768]{1,0:T(8,128)(2,1)S(1)} %get-tuple-element.57.n0), channel_id=1, source_target_pairs={{0,2},{1,3},{2,0},{3,1},{4,6},{5,7},{6,4},{7,5},{8,10},{9,11},{10,... | collective-permute-start | bytes 589832 | tf_op jit(solution)/shard_map/ppermute | solution.py:506
  16.5 8.8 %collective-permute-start.3 = (bf16[128,768]{1,0:T(8,128)(2,1)S(1)}, bf16[128,768]{1,0:T(8,128)(2,1)S(1)}, u32[]{:S(2)}, u32[]{:S(2)}) collective-permute-start(bf16[128,768]{1,0:T(8,128)(2,1)S(1)} %get-tuple-element.57.n0), channel_id=1, source_target_pairs={{0,1},{1,2},{2,3},{3,0},{4,5},{5,6},{6,7},{7,4},{8,9},{9,10},{10,1... | collective-permute-start | bytes 589832 | tf_op jit(solution)/shard_map/ppermute | solution.py:506
  17.4 1.7 %copy-start = (bf16[1536,768]{1,0:T(8,128)(2,1)S(1)}, bf16[1536,768]{1,0:T(8,128)(2,1)}, u32[]{:S(2)}) copy-start(bf16[1536,768]{1,0:T(8,128)(2,1)} %w_in_ref.1) | copy-start | bytes 7077892
  17.5 2.0 %copy-start.1 = (bf16[768,768]{1,0:T(8,128)(2,1)S(1)}, bf16[768,768]{1,0:T(8,128)(2,1)}, u32[]{:S(2)}) copy-start(bf16[768,768]{1,0:T(8,128)(2,1)} %w_out_ref.1) | copy-start | bytes 3538948
  17.5 2.3 %copy-start.5 = (bf16[768,768]{1,0:T(8,128)(2,1)S(1)}, bf16[768,768]{1,0:T(8,128)(2,1)}, u32[]{:S(2)}) copy-start(bf16[768,768]{1,0:T(8,128)(2,1)} %constant.10.clone.order_ref) | copy-start | bytes 3538948
  17.5 2.3 %copy-start.12 = (bf16[128,768]{1,0:T(8,128)(2,1)S(1)}, bf16[128,768]{1,0:T(8,128)(2,1)}, u32[]{:S(2)}) copy-start(bf16[128,768]{1,0:T(8,128)(2,1)} %get-tuple-element.52.hidden_ref) | copy-start | bytes 589828
  19.8 5.4 %copy-start.7 = (bf16[384,384]{1,0:T(8,128)(2,1)S(1)}, bf16[384,384]{1,0:T(8,128)(2,1)}, u32[]{:S(2)}) copy-start(bf16[384,384]{1,0:T(8,128)(2,1)} %constant.11.clone.spread_ref) | copy-start | bytes 884740
  22.5 5.7 %collective-permute-start.9 = (bf16[384,768]{1,0:T(8,128)(2,1)S(1)}, bf16[384,768]{1,0:T(8,128)(2,1)S(1)}, u32[]{:S(2)}, u32[]{:S(2)}) collective-permute-start(bf16[384,768]{1,0:T(8,128)(2,1)S(1)} %get-tuple-element.63), channel_id=1, source_target_pairs={{0,4},{4,0},{8,12},{12,8},{16,20},{20,16},{24,28},{28,24},{32,36},... | collective-permute-start | bytes 1769480 | tf_op jit(solution)/shard_map/ppermute | solution.py:553
  28.3 14.2 %copy-start.8 = (bf16[128,96]{1,0:T(8,128)(2,1)S(1)}, bf16[128,96]{1,0:T(8,128)(2,1)}, u32[]{:S(2)}) copy-start(bf16[128,96]{1,0:T(8,128)(2,1)} %constant.12.clone.order_ref) | copy-start | bytes 73732
  28.4 17.0 %copy-start.6 = (bf16[640,576]{1,0:T(8,128)(2,1)S(1)}, bf16[640,576]{1,0:T(8,128)(2,1)}, u32[]{:S(2)}) copy-start(bf16[640,576]{1,0:T(8,128)(2,1)} %constant.13.clone.order_ref) | copy-start | bytes 2211844
  28.4 8.6 %collective-permute-start.10 = (bf16[96,768]{1,0:T(8,128)(2,1)S(1)}, bf16[96,768]{1,0:T(8,128)(2,1)S(1)}, u32[]{:S(2)}, u32[]{:S(2)}) collective-permute-start(bf16[96,768]{1,0:T(8,128)(2,1)S(1)} %get-tuple-element.65), channel_id=1, source_target_pairs={{0,8},{4,12},{8,16},{12,20},{16,24},{20,28},{24,0},{28,4},{32,40},... | collective-permute-start | bytes 442376 | tf_op jit(solution)/shard_map/ppermute | solution.py:506
  30.1 12.7 %collective-permute-start.6 = (bf16[976,128]{1,0:T(8,128)(2,1)S(1)}, bf16[976,128]{1,0:T(8,128)(2,1)S(1)}, u32[]{:S(2)}, u32[]{:S(2)}) collective-permute-start(bf16[976,128]{1,0:T(8,128)(2,1)S(1)} %get-tuple-element.59), channel_id=1, source_target_pairs={{0,1},{1,2},{2,3},{3,0},{4,5},{5,6},{6,7},{7,4},{8,9},{9,10},{10,1... | collective-permute-start | bytes 749576 | tf_op jit(solution)/shard_map/ppermute | solution.py:506
  31.6 11.2 %collective-permute-start.7 = (bf16[976,128]{1,0:T(8,128)(2,1)S(1)}, bf16[976,128]{1,0:T(8,128)(2,1)S(1)}, u32[]{:S(2)}, u32[]{:S(2)}) collective-permute-start(bf16[976,128]{1,0:T(8,128)(2,1)S(1)} %get-tuple-element.60), channel_id=1, source_target_pairs={{0,2},{1,3},{2,0},{3,1},{4,6},{5,7},{6,4},{7,5},{8,10},{9,11},{10,... | collective-permute-start | bytes 749576 | tf_op jit(solution)/shard_map/ppermute | solution.py:506
  34.1 11.3 %collective-permute-start.8 = (bf16[976,128]{1,0:T(8,128)(2,1)S(1)}, bf16[976,128]{1,0:T(8,128)(2,1)S(1)}, u32[]{:S(2)}, u32[]{:S(2)}) collective-permute-start(bf16[976,128]{1,0:T(8,128)(2,1)S(1)} %get-tuple-element.61), channel_id=1, source_target_pairs={{0,3},{1,0},{2,1},{3,2},{4,7},{5,4},{6,5},{7,6},{8,11},{9,8},{10,9... | collective-permute-start | bytes 749576 | tf_op jit(solution)/shard_map/ppermute | solution.py:506
  34.2 6.6 %collective-permute-start.11 = (bf16[96,768]{1,0:T(8,128)(2,1)S(1)}, bf16[96,768]{1,0:T(8,128)(2,1)S(1)}, u32[]{:S(2)}, u32[]{:S(2)}) collective-permute-start(bf16[96,768]{1,0:T(8,128)(2,1)S(1)} %get-tuple-element.66), channel_id=1, source_target_pairs={{0,16},{4,20},{8,24},{12,28},{16,0},{20,4},{24,8},{28,12},{32,48},... | collective-permute-start | bytes 442376 | tf_op jit(solution)/shard_map/ppermute | solution.py:506
  37.1 5.4 %collective-permute-start.12 = (bf16[96,768]{1,0:T(8,128)(2,1)S(1)}, bf16[96,768]{1,0:T(8,128)(2,1)S(1)}, u32[]{:S(2)}, u32[]{:S(2)}) collective-permute-start(bf16[96,768]{1,0:T(8,128)(2,1)S(1)} %get-tuple-element.67), channel_id=1, source_target_pairs={{0,24},{4,28},{8,0},{12,4},{16,8},{20,12},{24,16},{28,20},{32,56},... | collective-permute-start | bytes 442376 | tf_op jit(solution)/shard_map/ppermute | solution.py:506
  47.4 16.4 %copy-start.9 = (bf16[96,80]{1,0:T(8,128)(2,1)S(1)}, bf16[96,80]{1,0:T(8,128)(2,1)}, u32[]{:S(2)}) copy-start(bf16[96,80]{1,0:T(8,128)(2,1)} %constant.14.clone.order_ref) | copy-start | bytes 46084
  47.4 7.2 %collective-permute-start.13 = (bf16[320,768]{1,0:T(8,128)(2,1)S(1)}, bf16[320,768]{1,0:T(8,128)(2,1)S(1)}, u32[]{:S(2)}, u32[]{:S(2)}) collective-permute-start(bf16[320,768]{1,0:T(8,128)(2,1)S(1)} %get-tuple-element.70), channel_id=1, source_target_pairs={{0,4},{4,0},{8,12},{12,8},{16,20},{20,16},{24,28},{28,24},{32,36},... | collective-permute-start | bytes 1474568 | tf_op jit(solution)/shard_map/ppermute | solution.py:579
  47.5 4.9 %collective-permute-start.14 = (bf16[32,768]{1,0:T(8,128)(2,1)S(1)}, bf16[32,768]{1,0:T(8,128)(2,1)S(1)}, u32[]{:S(2)}, u32[]{:S(2)}) collective-permute-start(bf16[32,768]{1,0:T(8,128)(2,1)S(1)} %get-tuple-element.71), channel_id=1, source_target_pairs={{0,1},{1,2},{2,3},{3,0},{4,5},{5,6},{6,7},{7,4},{8,9},{9,10},{10,1... | collective-permute-start | bytes 147464 | tf_op jit(solution)/shard_map/ppermute | solution.py:506
  48.2 5.8 %collective-permute-start.15 = (bf16[32,768]{1,0:T(8,128)(2,1)S(1)}, bf16[32,768]{1,0:T(8,128)(2,1)S(1)}, u32[]{:S(2)}, u32[]{:S(2)}) collective-permute-start(bf16[32,768]{1,0:T(8,128)(2,1)S(1)} %get-tuple-element.72), channel_id=1, source_target_pairs={{0,2},{1,3},{2,0},{3,1},{4,6},{5,7},{6,4},{7,5},{8,10},{9,11},{10,... | collective-permute-start | bytes 147464 | tf_op jit(solution)/shard_map/ppermute | solution.py:506
  50.4 4.2 %collective-permute-start.16 = (bf16[32,768]{1,0:T(8,128)(2,1)S(1)}, bf16[32,768]{1,0:T(8,128)(2,1)S(1)}, u32[]{:S(2)}, u32[]{:S(2)}) collective-permute-start(bf16[32,768]{1,0:T(8,128)(2,1)S(1)} %get-tuple-element.73), channel_id=1, source_target_pairs={{0,3},{1,0},{2,1},{3,2},{4,7},{5,4},{6,5},{7,6},{8,11},{9,8},{10,9... | collective-permute-start | bytes 147464 | tf_op jit(solution)/shard_map/ppermute | solution.py:506
  54.7 7.4 %collective-permute-start.17 = (bf16[80,768]{1,0:T(8,128)(2,1)S(1)}, bf16[80,768]{1,0:T(8,128)(2,1)S(1)}, u32[]{:S(2)}, u32[]{:S(2)}) collective-permute-start(bf16[80,768]{1,0:T(8,128)(2,1)S(1)} %get-tuple-element.75), channel_id=1, source_target_pairs={{0,8},{4,12},{8,16},{12,20},{16,24},{20,28},{24,0},{28,4},{32,40},... | collective-permute-start | bytes 368648 | tf_op jit(solution)/shard_map/ppermute | solution.py:506
  56.4 7.1 %collective-permute-start.18 = (bf16[80,768]{1,0:T(8,128)(2,1)S(1)}, bf16[80,768]{1,0:T(8,128)(2,1)S(1)}, u32[]{:S(2)}, u32[]{:S(2)}) collective-permute-start(bf16[80,768]{1,0:T(8,128)(2,1)S(1)} %get-tuple-element.76), channel_id=1, source_target_pairs={{0,16},{4,20},{8,24},{12,28},{16,0},{20,4},{24,8},{28,12},{32,48},... | collective-permute-start | bytes 368648 | tf_op jit(solution)/shard_map/ppermute | solution.py:506
  58.1 5.7 %collective-permute-start.19 = (bf16[80,768]{1,0:T(8,128)(2,1)S(1)}, bf16[80,768]{1,0:T(8,128)(2,1)S(1)}, u32[]{:S(2)}, u32[]{:S(2)}) collective-permute-start(bf16[80,768]{1,0:T(8,128)(2,1)S(1)} %get-tuple-element.77), channel_id=1, source_target_pairs={{0,24},{4,28},{8,0},{12,4},{16,8},{20,12},{24,16},{28,20},{32,56},... | collective-permute-start | bytes 368648 | tf_op jit(solution)/shard_map/ppermute | solution.py:506

commit v8 on v7

--- a/solution.py
+++ b/solution.py
@@ -160,14 +160,13 @@
 
 
 def near_kernel(
-    count_ref, normed_ref, proj_ref, tiles_ref, masked_ref,
-    exp_ref, top_ref, sum_ref, tiles_out, flag_ref, late_ref,
+    count_ref, proj_ref, tiles_ref, masked_ref,
+    exp_ref, top_ref, sum_ref, tiles_out, flag_ref,
 ):
     count = count_ref[0]
     pos0 = lax.axis_index("seq") * TOK
     flag_ref[...] = masked_rows(pos0 + class_major(iota((TOK, TOK), 0)), masked_ref[...])
     tiles_out[...] = nn(class_order(), tiles_ref[0]).astype(BF)
-    late_ref[...] = normed_ref[...]
     square = (TOK, TOK)
     key_pos = pos0 + class_major(iota(square, 0))
     query_pos = pos0 + class_major(iota(square, 1))
@@ -257,7 +256,7 @@
 
 
 def backward_kernel(
-    proj_ref, fk_ref, fv_ref, pnear_ref, pfar_ref, ga_ref, loss_ref, spread_ref, wait1, wait2, wait3,
+    proj_ref, fk_ref, fv_ref, pnear_ref, pfar_ref, ga_ref, loss_ref, spread_ref,
     x0, x1, x2, x3,
     gq, gk, gv, gkf, gvf, turned,
 ):
@@ -313,10 +312,9 @@
 
 
 def product_kernel(
-    x0, x1, x2, x3, n0, n1, n2, n3, order_ref, wait_ref, mine_ref, other_ref, got, left, right
+    x0, x1, x2, x3, n0, n1, n2, n3, wait_ref, whole_ref, tail_ref, got, left, right
 ):
     seq = lax.axis_index("seq")
-    core = lax.axis_index("slide") & 1
     for turn, (x_ref, n_ref) in enumerate(zip((x0, x1, x2, x3), (n0, n1, n2, n3))):
         src = (seq - turn) & 3
         got[src] = x_ref[...]
@@ -343,18 +341,23 @@
                 for r in range(RATE):
                     total = total + jnp.where(spots[r], turns[(r - src) & 3], 0.0)
                 left[near_at : near_at + SUB, src * TOK : (src + 1) * TOK] = total.astype(BF)
-    whole = nn(left[...], right[...]).astype(BF)
+    whole_ref[...] = nn(left[...], right[...]).astype(BF)
     loss = got[0, SECTIONS * SUB :].astype(F32)
     for src in range(1, N_SEQ):
         loss = loss + got[src, SECTIONS * SUB :].astype(F32)
     loss = jnp.sum(loss, axis=0, keepdims=True)[:, 0:1]
-    tail = split_rows(jnp.broadcast_to(loss, (YROWS, D)), (YROWS, D), 72)
+    tail_ref[...] = split_rows(jnp.broadcast_to(loss, (YROWS, D)), (YROWS, D), 72)
+
+
+def place_kernel(whole_ref, tail_ref, order_ref, wait1, wait2, wait3, mine_ref, other_ref):
+    core = lax.axis_index("slide") & 1
+    whole = whole_ref[...]
     for turn, ref in enumerate((mine_ref, other_ref)):
         first = pl.multiple_of(((core + turn) & 1) * NY * YROWS, NY * YROWS)
         half = nn(order_ref[pl.ds(first, NY * YROWS)], whole)
         for y in range(NY):
             rows = slice(y * YROWS, (y + 1) * YROWS)
-            ref[rows] = (half[rows] + tail).astype(BF)
+            ref[rows] = (half[rows] + tail_ref[...]).astype(BF)
 
 
 def resplit(total):
@@ -364,7 +367,7 @@
     return jnp.where(row >= 72, pieces, total), loss
 
 
-def core_kernel(mine_ref, other_ref, wait1, wait2, wait3, y0, y1, y2, y3):
+def core_kernel(mine_ref, other_ref, y0, y1, y2, y3):
     y = (lax.axis_index("slide") >> 1) & 3
     for turn, ref in enumerate((y0, y1, y2, y3)):
         rows = pl.ds(pl.multiple_of(((y + turn) & 3) * YROWS, 16), YROWS)
@@ -381,7 +384,7 @@
         out_ref[6 + half] = (out[16 * half : 16 * (half + 1)] + tail).astype(BF)
 
 
-def out_core_kernel(mine_ref, other_ref, wait_ref, y0, y1, y2, y3):
+def out_core_kernel(mine_ref, other_ref, wait0, wait1, wait2, wait3, y0, y1, y2, y3):
     y = (lax.axis_index("slide") >> 1) & 3
     for turn, ref in enumerate((y0, y1, y2, y3)):
         rows = pl.ds(pl.multiple_of(((y + turn) & 3) * SUB, 16), SUB)
@@ -527,57 +530,62 @@
     fars = swap([dilated] * N_SEQ, "seq", SEQ_TURNS)
     scores = shape(GROUPS, TOK, RATE * TOK, dtype=F32)
     rows = shape(HEADS, TOK, dtype=F32)
-    exps, tops, sums, tiles, flag, late = call(
+    exps, tops, sums, tiles, flag = call(
         near_kernel,
-        [scores, rows, rows, shape(TOK, 2 * D), shape(TOK, TOK, dtype=F32), shape(TOK, D)],
-        (tile_counts, normed, projected, embeddings, masked_tiles),
+        [scores, rows, rows, shape(TOK, 2 * D), shape(TOK, TOK, dtype=F32)],
+        (tile_counts, projected, embeddings, masked_tiles),
         (),
-        5.0,
-        [SMEM] + [VMEM] * 4,
-    )
-    norms = swap([late] * N_SEQ, "seq", SEQ_TURNS)
+        1.0,
+        [SMEM] + [VMEM] * 3,
+    )
+    norms = swap([normed] * N_SEQ, "seq", SEQ_TURNS)
     fk, fv, pnear, pfar, attended = call(
         far_kernel,
         [shape(TOK, D), shape(TOK, D), scores, shape(GROUPS, TOK, TOK, dtype=F32), shape(TOK, D)],
         (tile_counts, *fars, projected, exps, tops, sums),
         [pltpu.VMEM((TOK, D), F32)],
-        10.0,
+        2.0,
     )
     grad_attended, loss, out_mine, out_other = call(
         functools.partial(chain_kernel, inv_count),
         [shape(TOK, D), shape(16, 128), shape(HALF, D), shape(HALF, D)],
         (attended, hidden, tiles, flag, w_in, w_out, out_order()),
         (),
-        15.0,
+        3.0,
     )
     out_other = lax.ppermute(out_other, "slide", CORE_PAIRS)
     sent = call(
         backward_kernel,
         [shape(XROWS, TOK)] * N_SEQ,
-        (projected, fk, fv, pnear, pfar, grad_attended, loss, spread_order(), *norms[1:]),
+        (projected, fk, fv, pnear, pfar, grad_attended, loss, spread_order()),
         [pltpu.VMEM((TOK, D), F32)] * 5 + [pltpu.VMEM((SECTIONS, HALF, TOK), BF)],
         8.0,
-        unread=3,
     )
     got = swap(sent, "seq", SEQ_TURNS)
-    out = call(out_core_kernel, [shape(SUB, D)] * NY, (out_mine, out_other, sent[0]), unread=1)
+    out = call(out_core_kernel, [shape(SUB, D)] * NY, (out_mine, out_other, sent[0], *norms[1:]), unread=4)
     out = swap(out, "slide", Y_TURNS)
     out_sums = call(out_y_kernel, [shape(32, D)] * N_SEQ, (*out, out_pad_order()))
     out = swap(out_sums, "seq", SEQ_TURNS)
-    mine, other = call(
+    whole, tail = call(
         product_kernel,
-        [shape(NY * YROWS, D)] * 2,
-        (*got, *norms, product_order(), out_sums[0]),
+        [shape(6 * SUB, D), shape(YROWS, D, dtype=F32)],
+        (*got, *norms, out_sums[0]),
         [
             pltpu.VMEM((N_SEQ, XROWS, TOK), BF),
             pltpu.VMEM((6 * SUB, N_SEQ * TOK), BF),
             pltpu.VMEM((N_SEQ * TOK, D), BF),
         ],
-        3.0,
+        15.0,
         unread=1,
     )
+    mine, other = call(
+        place_kernel,
+        [shape(NY * YROWS, D)] * 2,
+        (whole, tail, product_order(), *out[1:]),
+        unread=3,
+    )
     other = lax.ppermute(other, "slide", CORE_PAIRS)
-    by_y = call(core_kernel, [shape(YROWS, D)] * NY, (mine, other, *out[1:]), unread=3)
+    by_y = call(core_kernel, [shape(YROWS, D)] * NY, (mine, other))
     by_y = swap(by_y, "slide", Y_TURNS)
     (by_z,) = call(y_kernel, [shape(NZ, 16, D)], (*by_y, *out, pad_order()))
     by_z = lax.all_to_all(by_z, "slide", 0, 0, tiled=True, axis_index_groups=Z_GROUPS)

time: 84.2 us -> 81.1 us (0.963); the launches traced: 82.7 us -> 80.9 us
  starting transfers between devices: 29.8 us -> 28.5 us
    ppermute x18, waiting for transfers between devices: 14.7 us -> 12.8 us  [swap(): lax.ppermute(arrays[t], axis, turns[t])]
    ppermute x1, waiting for transfers between devices: 0.01 us -> 1.85 us  [per_device(): other = lax.ppermute(other, 'slide', CORE_PAIRS)]
    ppermute x18, starting transfers between devices: 29.4 us -> 28.2 us  [swap(): lax.ppermute(arrays[t], axis, turns[t])]
    pallas_call x11 -> x12, Pallas kernels: 15.7 us -> 15.8 us  [call(): pl.pallas_call(kernel, out_shape=out_shapes, in_specs=specs, out_specs=[V...]
  transfers between devices with their start and end apart: 20 -> 20, of which waited for: 10 -> 7; matrix products, arithmetic and copies ran while one was open for 0% -> 0% of each run, Pallas kernels for 10% -> 11%
where the time goes in v8:
time: 81.1 us; the launch traced here: 80.9 us
  starting transfers between devices  28.5 us (35%)
  blocking collectives  18.2 us (22%)
  Pallas kernels  15.8 us (19%)
  waiting for transfers between devices  14.7 us (18%)
  local copies, waits for them, and re-layouts  2.17 us (3%)
  between operations  1.53 us (2%)
    ppermute x18, starting transfers between devices, swap(): lax.ppermute(arrays[t], axis, turns[t])  28.2 us
    all_to_all x1, blocking collectives, per_device(): lax.all_to_all(by_z, 'slide', 0, 0, tiled=True, axis_index_groups=Z_GROUPS)  18.2 us
    pallas_call x12, Pallas kernels, call(): pl.pallas_call(kernel, out_shape=out_shapes, in_specs=specs, out_specs=[V...  15.8 us
    ppermute x18, waiting for transfers between devices, swap(): lax.ppermute(arrays[t], axis, turns[t])  12.8 us
    unnamed x28, local copies, waits for them, and re-layouts  2.17 us
    ppermute x1, waiting for transfers between devices, per_device(): other = lax.ppermute(other, 'slide', CORE_PAIRS)  1.85 us
  transfers between devices with their start and end apart: 20, of which 7 were waited for; matrix products, arithmetic and copies ran while one was open for 0% of the time, Pallas kernels for 11%

profile of v8, /device:TPU:2, one launch (start us, length us, event | category | flops | bytes accessed | tf_op | source)
XLA Modules:
  0.0 80.9 jit_solution(187977470394682347)
XLA Ops:
  0.7 4.4 %shard_map.131 = (bf16[128,768]{1,0:T(8,128)(2,1)}, bf16[128,768]{1,0:T(8,128)(2,1)}, bf16[128,2304]{1,0:T(8,128)(2,1)}, bf16[32,1536]{1,0:T(8,128)(2,1)}) custom-call(bf16[1,128,1536]{2,1,0:T(8,128)(2,1)} %tiles_ref.1, s32[1,128]{1,0:T(1,128)} %masked_ref.1, f32[768]{0:T(1024)} %gain_hbm.1, bf16[1536,768]{1,0:T(8,128)(2,1)} %w_in_ref.1, ...), custom_call_target="tpu_custom_call" | custom-call | flops 4000000000 | bytes 4000000 | tf_op jit(solution)/shard_map/pallas_call | solution.py:473
  5.1 1.6 %collective-permute-start = (bf16[32,1536]{1,0:T(8,128)(2,1)}, bf16[32,1536]{1,0:T(8,128)(2,1)S(1)}, u32[]{:S(2)}, u32[]{:S(2)}) collective-permute-start(bf16[32,1536]{1,0:T(8,128)(2,1)} %get-tuple-element.43.f0), channel_id=1, source_target_pairs={{0,1},{1,2},{2,3},{3,0},{4,5},{5,6},{6,7},{7,4},{8,9},{9,10},{10,1... | collective-permute-start | bytes 294920 | tf_op jit(solution)/shard_map/ppermute | solution.py:509
  6.7 2.8 %collective-permute-start.1 = (bf16[32,1536]{1,0:T(8,128)(2,1)}, bf16[32,1536]{1,0:T(8,128)(2,1)S(1)}, u32[]{:S(2)}, u32[]{:S(2)}) collective-permute-start(bf16[32,1536]{1,0:T(8,128)(2,1)} %get-tuple-element.43.f0), channel_id=1, source_target_pairs={{0,2},{1,3},{2,0},{3,1},{4,6},{5,7},{6,4},{7,5},{8,10},{9,11},{10,... | collective-permute-start | bytes 294920 | tf_op jit(solution)/shard_map/ppermute | solution.py:509
  9.5 0.4 collective-permute-start.2
  10.0 1.6 %collective-permute-start.6 = (bf16[128,768]{1,0:T(8,128)(2,1)}, bf16[128,768]{1,0:T(8,128)(2,1)S(1)}, u32[]{:S(2)}, u32[]{:S(2)}) collective-permute-start(bf16[128,768]{1,0:T(8,128)(2,1)} %get-tuple-element.61.n0), channel_id=1, source_target_pairs={{0,1},{1,2},{2,3},{3,0},{4,5},{5,6},{6,7},{7,4},{8,9},{9,10},{10,1... | collective-permute-start | bytes 589832 | tf_op jit(solution)/shard_map/ppermute | solution.py:509
  11.6 1.9 %collective-permute-start.7 = (bf16[128,768]{1,0:T(8,128)(2,1)}, bf16[128,768]{1,0:T(8,128)(2,1)S(1)}, u32[]{:S(2)}, u32[]{:S(2)}) collective-permute-start(bf16[128,768]{1,0:T(8,128)(2,1)} %get-tuple-element.61.n0), channel_id=1, source_target_pairs={{0,2},{1,3},{2,0},{3,1},{4,6},{5,7},{6,4},{7,5},{8,10},{9,11},{10,... | collective-permute-start | bytes 589832 | tf_op jit(solution)/shard_map/ppermute | solution.py:509
  14.1 1.1 %copy-done.11 = bf16[128,2304]{1,0:T(8,128)(2,1)S(1)} copy-done((bf16[128,2304]{1,0:T(8,128)(2,1)S(1)}, bf16[128,2304]{1,0:T(8,128)(2,1)}, u32[]{:S(2)}) %copy-start.11) | copy-done | bytes 589848
  15.2 0.7 shard_map.132
  15.9 0.2 collective-permute-start.8
  16.2 0.1 copy-done.12
  16.3 1.3 %shard_map.133 = (bf16[128,768]{1,0:T(8,128)(2,1)S(1)}, bf16[128,768]{1,0:T(8,128)(2,1)S(1)}, f32[4,128,512]{2,1,0:T(8,128)S(1)}, f32[4,128,128]{2,1,0:T(8,128)S(1)}, bf16[128,768]{1,0:T(8,128)(2,1)S(1)}) custom-call(s32[1]{0:T(128)S(6)} %copy.14.count_ref, bf16[32,1536]{1,0:T(8,128)(2,1)S(1)} %copy-done.4, bf16[32,1536]{1,0:T(8,128)(2,1)S(1)} %collective-permute-done.f1, ...), custom_call_target="tpu_custom_call" | custom-call | flops 2000000000 | bytes 2000000 | tf_op jit(solution)/shard_map/pallas_call | solution.py:473
  17.6 0.3 copy-done
  17.9 0.3 copy-done.1
  18.2 0.4 copy-done.6
  18.6 0.0 copy-done.13
  18.6 2.7 %shard_map.134 = (bf16[128,768]{1,0:T(8,128)(2,1)S(1)}, bf16[16,128]{1,0:T(8,128)(2,1)S(1)}, bf16[384,768]{1,0:T(8,128)(2,1)S(1)}, bf16[384,768]{1,0:T(8,128)(2,1)S(1)}) custom-call(bf16[128,768]{1,0:T(8,128)(2,1)S(1)} %get-tuple-element.51.att_ref, bf16[128,768]{1,0:T(8,128)(2,1)S(1)} %copy-done.13, bf16[128,1536]{1,0:T(8,128)(2,1)S(1)} %get-tuple-element.53.tiles_ref, ...), custom_call_target="tpu_custom_call" | custom-call | flops 3000000000 | bytes 3000000 | tf_op jit(solution)/shard_map/pallas_call | solution.py:473
  21.4 0.3 collective-permute-start.9
  21.6 3.0 %shard_map.135 = (bf16[976,128]{1,0:T(8,128)(2,1)S(1)}, bf16[976,128]{1,0:T(8,128)(2,1)S(1)}, bf16[976,128]{1,0:T(8,128)(2,1)S(1)}, bf16[976,128]{1,0:T(8,128)(2,1)S(1)}) custom-call(bf16[128,2304]{1,0:T(8,128)(2,1)S(1)} %copy-done.12, bf16[128,768]{1,0:T(8,128)(2,1)S(1)} %get-tuple-element.47.fk_ref, bf16[128,768]{1,0:T(8,128)(2,1)S(1)} %get-tuple-element.48.fv_ref, ...), custom_call_target="tpu_custom_call" | custom-call | flops 8000000000 | bytes 8000000 | tf_op jit(solution)/shard_map/pallas_call | solution.py:473
  24.7 0.0 copy-start.9
  24.7 0.2 shard_map.136
  24.9 1.6 %collective-permute-start.10 = (bf16[96,768]{1,0:T(8,128)(2,1)S(1)}, bf16[96,768]{1,0:T(8,128)(2,1)S(1)}, u32[]{:S(2)}, u32[]{:S(2)}) collective-permute-start(bf16[96,768]{1,0:T(8,128)(2,1)S(1)} %get-tuple-element.65), channel_id=1, source_target_pairs={{0,8},{4,12},{8,16},{12,20},{16,24},{20,28},{24,0},{28,4},{32,40},... | collective-permute-start | bytes 442376 | tf_op jit(solution)/shard_map/ppermute | solution.py:509
  26.5 1.8 %collective-permute-start.3 = (bf16[976,128]{1,0:T(8,128)(2,1)S(1)}, bf16[976,128]{1,0:T(8,128)(2,1)S(1)}, u32[]{:S(2)}, u32[]{:S(2)}) collective-permute-start(bf16[976,128]{1,0:T(8,128)(2,1)S(1)} %get-tuple-element.58), channel_id=1, source_target_pairs={{0,1},{1,2},{2,3},{3,0},{4,5},{5,6},{6,7},{7,4},{8,9},{9,10},{10,1... | collective-permute-start | bytes 749576 | tf_op jit(solution)/shard_map/ppermute | solution.py:509
  28.3 1.3 %collective-permute-start.4 = (bf16[976,128]{1,0:T(8,128)(2,1)S(1)}, bf16[976,128]{1,0:T(8,128)(2,1)S(1)}, u32[]{:S(2)}, u32[]{:S(2)}) collective-permute-start(bf16[976,128]{1,0:T(8,128)(2,1)S(1)} %get-tuple-element.59), channel_id=1, source_target_pairs={{0,2},{1,3},{2,0},{3,1},{4,6},{5,7},{6,4},{7,5},{8,10},{9,11},{10,... | collective-permute-start | bytes 749576 | tf_op jit(solution)/shard_map/ppermute | solution.py:509
  29.6 0.8 collective-permute-start.5
  30.4 2.9 %collective-permute-start.11 = (bf16[96,768]{1,0:T(8,128)(2,1)S(1)}, bf16[96,768]{1,0:T(8,128)(2,1)S(1)}, u32[]{:S(2)}, u32[]{:S(2)}) collective-permute-start(bf16[96,768]{1,0:T(8,128)(2,1)S(1)} %get-tuple-element.66), channel_id=1, source_target_pairs={{0,16},{4,20},{8,24},{12,28},{16,0},{20,4},{24,8},{28,12},{32,48},... | collective-permute-start | bytes 442376 | tf_op jit(solution)/shard_map/ppermute | solution.py:509
  33.3 1.3 %collective-permute-start.12 = (bf16[96,768]{1,0:T(8,128)(2,1)S(1)}, bf16[96,768]{1,0:T(8,128)(2,1)S(1)}, u32[]{:S(2)}, u32[]{:S(2)}) collective-permute-start(bf16[96,768]{1,0:T(8,128)(2,1)S(1)} %get-tuple-element.67), channel_id=1, source_target_pairs={{0,24},{4,28},{8,0},{12,4},{16,8},{20,12},{24,16},{28,20},{32,56},... | collective-permute-start | bytes 442376 | tf_op jit(solution)/shard_map/ppermute | solution.py:509
  34.7 2.6 %collective-permute-done.11.y2 = bf16[96,768]{1,0:T(8,128)(2,1)S(1)} collective-permute-done((bf16[96,768]{1,0:T(8,128)(2,1)S(1)}, bf16[96,768]{1,0:T(8,128)(2,1)S(1)}, u32[]{:S(2)}, u32[]{:S(2)}) %collective-permute-start.11) | collective-permute-done | bytes 147488 | tf_op jit(solution)/shard_map/ppermute | solution.py:509
  37.3 2.9 %collective-permute-done.12.y3 = bf16[96,768]{1,0:T(8,128)(2,1)S(1)} collective-permute-done((bf16[96,768]{1,0:T(8,128)(2,1)S(1)}, bf16[96,768]{1,0:T(8,128)(2,1)S(1)}, u32[]{:S(2)}, u32[]{:S(2)}) %collective-permute-start.12) | collective-permute-done | bytes 147488 | tf_op jit(solution)/shard_map/ppermute | solution.py:509
  40.2 0.3 shard_map.137
  40.4 1.8 %collective-permute-start.13 = (bf16[32,768]{1,0:T(8,128)(2,1)S(1)}, bf16[32,768]{1,0:T(8,128)(2,1)S(1)}, u32[]{:S(2)}, u32[]{:S(2)}) collective-permute-start(bf16[32,768]{1,0:T(8,128)(2,1)S(1)} %get-tuple-element.71), channel_id=1, source_target_pairs={{0,1},{1,2},{2,3},{3,0},{4,5},{5,6},{6,7},{7,4},{8,9},{9,10},{10,1... | collective-permute-start | bytes 147464 | tf_op jit(solution)/shard_map/ppermute | solution.py:509
  42.3 2.1 %collective-permute-start.14 = (bf16[32,768]{1,0:T(8,128)(2,1)S(1)}, bf16[32,768]{1,0:T(8,128)(2,1)S(1)}, u32[]{:S(2)}, u32[]{:S(2)}) collective-permute-start(bf16[32,768]{1,0:T(8,128)(2,1)S(1)} %get-tuple-element.72), channel_id=1, source_target_pairs={{0,2},{1,3},{2,0},{3,1},{4,6},{5,7},{6,4},{7,5},{8,10},{9,11},{10,... | collective-permute-start | bytes 147464 | tf_op jit(solution)/shard_map/ppermute | solution.py:509
  44.4 0.1 collective-permute-start.15
  44.5 1.1 %shard_map.138 = (bf16[576,768]{1,0:T(8,128)(2,1)S(1)}, f32[80,768]{1,0:T(8,128)S(1)}) custom-call(bf16[976,128]{1,0:T(8,128)(2,1)S(1)} %get-tuple-element.57.wait0.x0, bf16[976,128]{1,0:T(8,128)(2,1)S(1)} %collective-permute-done.3.x1, bf16[976,128]{1,0:T(8,128)(2,1)S(1)} %collective-permute-done.4.x2, bf16[976,128]{1,0:T(8,128)(2,1)S(1)} %collective-permute-done.5.x3, ...), custom_call_target="tpu_custom_call" | custom-call | flops 15000000512 | bytes 15000000 | tf_op jit(solution)/shard_map/pallas_call | solution.py:473
  45.6 2.3 %collective-permute-done.14.wait2.o2 = bf16[32,768]{1,0:T(8,128)(2,1)S(1)} collective-permute-done((bf16[32,768]{1,0:T(8,128)(2,1)S(1)}, bf16[32,768]{1,0:T(8,128)(2,1)S(1)}, u32[]{:S(2)}, u32[]{:S(2)}) %collective-permute-start.14) | collective-permute-done | bytes 49184 | tf_op jit(solution)/shard_map/ppermute | solution.py:509
  47.9 0.6 collective-permute-done.15.wait3.o3
  48.5 0.9 %shard_map.139 = (bf16[320,768]{1,0:T(8,128)(2,1)S(1)}, bf16[320,768]{1,0:T(8,128)(2,1)S(1)}) custom-call(bf16[576,768]{1,0:T(8,128)(2,1)S(1)} %get-tuple-element.69.whole_ref, f32[80,768]{1,0:T(8,128)S(1)} %get-tuple-element.70.tail_ref, bf16[640,576]{1,0:T(8,128)(2,1)S(1)} %copy-done.7, bf16[32,768]{1,0:T(8,128)(2,1)S(1)} %collective-permute-done.13.wait1.o1, ...), custom_call_target="tpu_custom_call" | custom-call | flops 1000000000 | bytes 1000000 | tf_op jit(solution)/shard_map/pallas_call | solution.py:473
  49.4 0.0 copy-start.10
  49.4 0.1 collective-permute-start.16
  49.5 1.9 %collective-permute-done.16.other_ref = bf16[320,768]{1,0:T(8,128)(2,1)S(1)} collective-permute-done((bf16[320,768]{1,0:T(8,128)(2,1)S(1)}, bf16[320,768]{1,0:T(8,128)(2,1)S(1)}, u32[]{:S(2)}, u32[]{:S(2)}) %collective-permute-start.16) | collective-permute-done | bytes 491552 | tf_op jit(solution)/shard_map/ppermute | solution.py:587
  51.4 0.2 shard_map.140
  51.6 1.8 %collective-permute-start.17 = (bf16[80,768]{1,0:T(8,128)(2,1)S(1)}, bf16[80,768]{1,0:T(8,128)(2,1)S(1)}, u32[]{:S(2)}, u32[]{:S(2)}) collective-permute-start(bf16[80,768]{1,0:T(8,128)(2,1)S(1)} %get-tuple-element.77), channel_id=1, source_target_pairs={{0,8},{4,12},{8,16},{12,20},{16,24},{20,28},{24,0},{28,4},{32,40},... | collective-permute-start | bytes 368648 | tf_op jit(solution)/shard_map/ppermute | solution.py:509
  53.4 2.4 %collective-permute-start.18 = (bf16[80,768]{1,0:T(8,128)(2,1)S(1)}, bf16[80,768]{1,0:T(8,128)(2,1)S(1)}, u32[]{:S(2)}, u32[]{:S(2)}) collective-permute-start(bf16[80,768]{1,0:T(8,128)(2,1)S(1)} %get-tuple-element.78), channel_id=1, source_target_pairs={{0,16},{4,20},{8,24},{12,28},{16,0},{20,4},{24,8},{28,12},{32,48},... | collective-permute-start | bytes 368648 | tf_op jit(solution)/shard_map/ppermute | solution.py:509
  55.8 1.6 %collective-permute-start.19 = (bf16[80,768]{1,0:T(8,128)(2,1)S(1)}, bf16[80,768]{1,0:T(8,128)(2,1)S(1)}, u32[]{:S(2)}, u32[]{:S(2)}) collective-permute-start(bf16[80,768]{1,0:T(8,128)(2,1)S(1)} %get-tuple-element.79), channel_id=1, source_target_pairs={{0,24},{4,28},{8,0},{12,4},{16,8},{20,12},{24,16},{28,20},{32,56},... | collective-permute-start | bytes 368648 | tf_op jit(solution)/shard_map/ppermute | solution.py:509
  57.4 0.9 %collective-permute-done.17.y1 = bf16[80,768]{1,0:T(8,128)(2,1)S(1)} collective-permute-done((bf16[80,768]{1,0:T(8,128)(2,1)S(1)}, bf16[80,768]{1,0:T(8,128)(2,1)S(1)}, u32[]{:S(2)}, u32[]{:S(2)}) %collective-permute-start.17) | collective-permute-done | bytes 122912 | tf_op jit(solution)/shard_map/ppermute | solution.py:509
  58.2 3.5 %collective-permute-done.18.y2 = bf16[80,768]{1,0:T(8,128)(2,1)S(1)} collective-permute-done((bf16[80,768]{1,0:T(8,128)(2,1)S(1)}, bf16[80,768]{1,0:T(8,128)(2,1)S(1)}, u32[]{:S(2)}, u32[]{:S(2)}) %collective-permute-start.18) | collective-permute-done | bytes 122912 | tf_op jit(solution)/shard_map/ppermute | solution.py:509
  61.8 0.3 shard_map.141
  62.0 18.2 %all_to_all.5.in_ref = bf16[8,16,768]{2,1,0:T(8,128)(2,1)S(1)} all-to-all(bf16[8,16,768]{2,1,0:T(8,128)(2,1)S(1)} %shard_map.141), channel_id=1, replica_groups={{0,32,64,96,128,160,192,224},{4,36,68,100,132,164,196,228},{8,40,72,104..., dimensions={0} | all-to-all | bytes 393216 | tf_op jit(solution)/shard_map/all_to_all | solution.py:591
  80.2 0.7 shard_map.142
  (33 shorter events, 0.1 us)
Async XLA Ops:
  0.6 13.5 %copy-start.2 = (bf16[1,128,1536]{2,1,0:T(8,128)(2,1)S(1)}, bf16[1,128,1536]{2,1,0:T(8,128)(2,1)}, u32[]{:S(2)}) copy-start(bf16[1,128,1536]{2,1,0:T(8,128)(2,1)} %tiles_ref.1) | copy-start | bytes 1179652
  0.6 13.5 %copy-start.5 = (s32[1,128]{1,0:T(1,128)S(1)}, s32[1,128]{1,0:T(1,128)}, u32[]{:S(2)}) copy-start(s32[1,128]{1,0:T(1,128)} %masked_ref.1) | copy-start | bytes 1540
  5.1 10.8 %copy-start.3 = (bf16[128,768]{1,0:T(8,128)(2,1)S(1)}, bf16[128,768]{1,0:T(8,128)(2,1)}, u32[]{:S(2)}) copy-start(bf16[128,768]{1,0:T(8,128)(2,1)} %get-tuple-element.61.n0) | copy-start | bytes 589828
  5.1 11.1 %copy-start.4 = (bf16[32,1536]{1,0:T(8,128)(2,1)S(1)}, bf16[32,1536]{1,0:T(8,128)(2,1)}, u32[]{:S(2)}) copy-start(bf16[32,1536]{1,0:T(8,128)(2,1)} %get-tuple-element.43.f0) | copy-start | bytes 294916
  5.1 10.8 %collective-permute-start = (bf16[32,1536]{1,0:T(8,128)(2,1)}, bf16[32,1536]{1,0:T(8,128)(2,1)S(1)}, u32[]{:S(2)}, u32[]{:S(2)}) collective-permute-start(bf16[32,1536]{1,0:T(8,128)(2,1)} %get-tuple-element.43.f0), channel_id=1, source_target_pairs={{0,1},{1,2},{2,3},{3,0},{4,5},{5,6},{6,7},{7,4},{8,9},{9,10},{10,1... | collective-permute-start | bytes 294920 | tf_op jit(solution)/shard_map/ppermute | solution.py:509
  6.7 9.5 %collective-permute-start.1 = (bf16[32,1536]{1,0:T(8,128)(2,1)}, bf16[32,1536]{1,0:T(8,128)(2,1)S(1)}, u32[]{:S(2)}, u32[]{:S(2)}) collective-permute-start(bf16[32,1536]{1,0:T(8,128)(2,1)} %get-tuple-element.43.f0), channel_id=1, source_target_pairs={{0,2},{1,3},{2,0},{3,1},{4,6},{5,7},{6,4},{7,5},{8,10},{9,11},{10,... | collective-permute-start | bytes 294920 | tf_op jit(solution)/shard_map/ppermute | solution.py:509
  9.5 6.6 %collective-permute-start.2 = (bf16[32,1536]{1,0:T(8,128)(2,1)}, bf16[32,1536]{1,0:T(8,128)(2,1)S(1)}, u32[]{:S(2)}, u32[]{:S(2)}) collective-permute-start(bf16[32,1536]{1,0:T(8,128)(2,1)} %get-tuple-element.43.f0), channel_id=1, source_target_pairs={{0,3},{1,0},{2,1},{3,2},{4,7},{5,4},{6,5},{7,6},{8,11},{9,8},{10,9... | collective-permute-start | bytes 294920 | tf_op jit(solution)/shard_map/ppermute | solution.py:509
  10.0 14.7 %collective-permute-start.6 = (bf16[128,768]{1,0:T(8,128)(2,1)}, bf16[128,768]{1,0:T(8,128)(2,1)S(1)}, u32[]{:S(2)}, u32[]{:S(2)}) collective-permute-start(bf16[128,768]{1,0:T(8,128)(2,1)} %get-tuple-element.61.n0), channel_id=1, source_target_pairs={{0,1},{1,2},{2,3},{3,0},{4,5},{5,6},{6,7},{7,4},{8,9},{9,10},{10,1... | collective-permute-start | bytes 589832 | tf_op jit(solution)/shard_map/ppermute | solution.py:509
  11.6 13.1 %collective-permute-start.7 = (bf16[128,768]{1,0:T(8,128)(2,1)}, bf16[128,768]{1,0:T(8,128)(2,1)S(1)}, u32[]{:S(2)}, u32[]{:S(2)}) collective-permute-start(bf16[128,768]{1,0:T(8,128)(2,1)} %get-tuple-element.61.n0), channel_id=1, source_target_pairs={{0,2},{1,3},{2,0},{3,1},{4,6},{5,7},{6,4},{7,5},{8,10},{9,11},{10,... | collective-permute-start | bytes 589832 | tf_op jit(solution)/shard_map/ppermute | solution.py:509
  14.1 1.1 %copy-start.11 = (bf16[128,2304]{1,0:T(8,128)(2,1)S(1)}, bf16[128,2304]{1,0:T(8,128)(2,1)}, u32[]{:S(2)}) copy-start(bf16[128,2304]{1,0:T(8,128)(2,1)} %get-tuple-element.42.proj_ref) | copy-start | bytes 1769476
  15.2 1.1 %copy-start.12 = (bf16[128,2304]{1,0:T(8,128)(2,1)S(1)}, bf16[128,2304]{1,0:T(8,128)(2,1)}, u32[]{:S(2)}) copy-start(bf16[128,2304]{1,0:T(8,128)(2,1)} %get-tuple-element.42.proj_ref) | copy-start | bytes 1769476
  15.9 8.8 %collective-permute-start.8 = (bf16[128,768]{1,0:T(8,128)(2,1)S(1)}, bf16[128,768]{1,0:T(8,128)(2,1)S(1)}, u32[]{:S(2)}, u32[]{:S(2)}) collective-permute-start(bf16[128,768]{1,0:T(8,128)(2,1)S(1)} %copy-done.3), channel_id=1, source_target_pairs={{0,3},{1,0},{2,1},{3,2},{4,7},{5,4},{6,5},{7,6},{8,11},{9,8},{10,9... | collective-permute-start | bytes 589832 | tf_op jit(solution)/shard_map/ppermute | solution.py:509
  16.3 1.7 %copy-start = (bf16[1536,768]{1,0:T(8,128)(2,1)S(1)}, bf16[1536,768]{1,0:T(8,128)(2,1)}, u32[]{:S(2)}) copy-start(bf16[1536,768]{1,0:T(8,128)(2,1)} %w_in_ref.1) | copy-start | bytes 7077892
  16.3 2.0 %copy-start.1 = (bf16[768,768]{1,0:T(8,128)(2,1)S(1)}, bf16[768,768]{1,0:T(8,128)(2,1)}, u32[]{:S(2)}) copy-start(bf16[768,768]{1,0:T(8,128)(2,1)} %w_out_ref.1) | copy-start | bytes 3538948
  16.3 2.3 %copy-start.6 = (bf16[768,768]{1,0:T(8,128)(2,1)S(1)}, bf16[768,768]{1,0:T(8,128)(2,1)}, u32[]{:S(2)}) copy-start(bf16[768,768]{1,0:T(8,128)(2,1)} %constant.10.clone.order_ref) | copy-start | bytes 3538948
  16.3 2.3 %copy-start.13 = (bf16[128,768]{1,0:T(8,128)(2,1)S(1)}, bf16[128,768]{1,0:T(8,128)(2,1)}, u32[]{:S(2)}) copy-start(bf16[128,768]{1,0:T(8,128)(2,1)} %get-tuple-element.52.hidden_ref) | copy-start | bytes 589828
  18.6 3.0 %copy-start.8 = (bf16[384,384]{1,0:T(8,128)(2,1)S(1)}, bf16[384,384]{1,0:T(8,128)(2,1)}, u32[]{:S(2)}) copy-start(bf16[384,384]{1,0:T(8,128)(2,1)} %constant.11.clone.spread_ref) | copy-start | bytes 884740
  21.4 3.4 %collective-permute-start.9 = (bf16[384,768]{1,0:T(8,128)(2,1)S(1)}, bf16[384,768]{1,0:T(8,128)(2,1)S(1)}, u32[]{:S(2)}, u32[]{:S(2)}) collective-permute-start(bf16[384,768]{1,0:T(8,128)(2,1)S(1)} %get-tuple-element.63), channel_id=1, source_target_pairs={{0,4},{4,0},{8,12},{12,8},{16,20},{20,16},{24,28},{28,24},{32,36},... | collective-permute-start | bytes 1769480 | tf_op jit(solution)/shard_map/ppermute | solution.py:556
  24.7 15.5 %copy-start.9 = (bf16[128,96]{1,0:T(8,128)(2,1)S(1)}, bf16[128,96]{1,0:T(8,128)(2,1)}, u32[]{:S(2)}) copy-start(bf16[128,96]{1,0:T(8,128)(2,1)} %constant.12.clone.order_ref) | copy-start | bytes 73732
  24.9 8.5 %collective-permute-start.10 = (bf16[96,768]{1,0:T(8,128)(2,1)S(1)}, bf16[96,768]{1,0:T(8,128)(2,1)S(1)}, u32[]{:S(2)}, u32[]{:S(2)}) collective-permute-start(bf16[96,768]{1,0:T(8,128)(2,1)S(1)} %get-tuple-element.65), channel_id=1, source_target_pairs={{0,8},{4,12},{8,16},{12,20},{16,24},{20,28},{24,0},{28,4},{32,40},... | collective-permute-start | bytes 442376 | tf_op jit(solution)/shard_map/ppermute | solution.py:509
  26.5 17.9 %collective-permute-start.3 = (bf16[976,128]{1,0:T(8,128)(2,1)S(1)}, bf16[976,128]{1,0:T(8,128)(2,1)S(1)}, u32[]{:S(2)}, u32[]{:S(2)}) collective-permute-start(bf16[976,128]{1,0:T(8,128)(2,1)S(1)} %get-tuple-element.58), channel_id=1, source_target_pairs={{0,1},{1,2},{2,3},{3,0},{4,5},{5,6},{6,7},{7,4},{8,9},{9,10},{10,1... | collective-permute-start | bytes 749576 | tf_op jit(solution)/shard_map/ppermute | solution.py:509
  28.3 16.1 %collective-permute-start.4 = (bf16[976,128]{1,0:T(8,128)(2,1)S(1)}, bf16[976,128]{1,0:T(8,128)(2,1)S(1)}, u32[]{:S(2)}, u32[]{:S(2)}) collective-permute-start(bf16[976,128]{1,0:T(8,128)(2,1)S(1)} %get-tuple-element.59), channel_id=1, source_target_pairs={{0,2},{1,3},{2,0},{3,1},{4,6},{5,7},{6,4},{7,5},{8,10},{9,11},{10,... | collective-permute-start | bytes 749576 | tf_op jit(solution)/shard_map/ppermute | solution.py:509
  29.6 14.8 %collective-permute-start.5 = (bf16[976,128]{1,0:T(8,128)(2,1)S(1)}, bf16[976,128]{1,0:T(8,128)(2,1)S(1)}, u32[]{:S(2)}, u32[]{:S(2)}) collective-permute-start(bf16[976,128]{1,0:T(8,128)(2,1)S(1)} %get-tuple-element.60), channel_id=1, source_target_pairs={{0,3},{1,0},{2,1},{3,2},{4,7},{5,4},{6,5},{7,6},{8,11},{9,8},{10,9... | collective-permute-start | bytes 749576 | tf_op jit(solution)/shard_map/ppermute | solution.py:509
  30.4 6.9 %collective-permute-start.11 = (bf16[96,768]{1,0:T(8,128)(2,1)S(1)}, bf16[96,768]{1,0:T(8,128)(2,1)S(1)}, u32[]{:S(2)}, u32[]{:S(2)}) collective-permute-start(bf16[96,768]{1,0:T(8,128)(2,1)S(1)} %get-tuple-element.66), channel_id=1, source_target_pairs={{0,16},{4,20},{8,24},{12,28},{16,0},{20,4},{24,8},{28,12},{32,48},... | collective-permute-start | bytes 442376 | tf_op jit(solution)/shard_map/ppermute | solution.py:509
  33.3 6.8 %collective-permute-start.12 = (bf16[96,768]{1,0:T(8,128)(2,1)S(1)}, bf16[96,768]{1,0:T(8,128)(2,1)S(1)}, u32[]{:S(2)}, u32[]{:S(2)}) collective-permute-start(bf16[96,768]{1,0:T(8,128)(2,1)S(1)} %get-tuple-element.67), channel_id=1, source_target_pairs={{0,24},{4,28},{8,0},{12,4},{16,8},{20,12},{24,16},{28,20},{32,56},... | collective-permute-start | bytes 442376 | tf_op jit(solution)/shard_map/ppermute | solution.py:509
  40.4 5.1 %collective-permute-start.13 = (bf16[32,768]{1,0:T(8,128)(2,1)S(1)}, bf16[32,768]{1,0:T(8,128)(2,1)S(1)}, u32[]{:S(2)}, u32[]{:S(2)}) collective-permute-start(bf16[32,768]{1,0:T(8,128)(2,1)S(1)} %get-tuple-element.71), channel_id=1, source_target_pairs={{0,1},{1,2},{2,3},{3,0},{4,5},{5,6},{6,7},{7,4},{8,9},{9,10},{10,1... | collective-permute-start | bytes 147464 | tf_op jit(solution)/shard_map/ppermute | solution.py:509
  42.3 5.6 %collective-permute-start.14 = (bf16[32,768]{1,0:T(8,128)(2,1)S(1)}, bf16[32,768]{1,0:T(8,128)(2,1)S(1)}, u32[]{:S(2)}, u32[]{:S(2)}) collective-permute-start(bf16[32,768]{1,0:T(8,128)(2,1)S(1)} %get-tuple-element.72), channel_id=1, source_target_pairs={{0,2},{1,3},{2,0},{3,1},{4,6},{5,7},{6,4},{7,5},{8,10},{9,11},{10,... | collective-permute-start | bytes 147464 | tf_op jit(solution)/shard_map/ppermute | solution.py:509
  44.4 4.1 %collective-permute-start.15 = (bf16[32,768]{1,0:T(8,128)(2,1)S(1)}, bf16[32,768]{1,0:T(8,128)(2,1)S(1)}, u32[]{:S(2)}, u32[]{:S(2)}) collective-permute-start(bf16[32,768]{1,0:T(8,128)(2,1)S(1)} %get-tuple-element.73), channel_id=1, source_target_pairs={{0,3},{1,0},{2,1},{3,2},{4,7},{5,4},{6,5},{7,6},{8,11},{9,8},{10,9... | collective-permute-start | bytes 147464 | tf_op jit(solution)/shard_map/ppermute | solution.py:509
  44.4 4.0 %copy-start.7 = (bf16[640,576]{1,0:T(8,128)(2,1)S(1)}, bf16[640,576]{1,0:T(8,128)(2,1)}, u32[]{:S(2)}) copy-start(bf16[640,576]{1,0:T(8,128)(2,1)} %constant.13.clone.order_ref) | copy-start | bytes 2211844
  49.4 12.3 %copy-start.10 = (bf16[96,80]{1,0:T(8,128)(2,1)S(1)}, bf16[96,80]{1,0:T(8,128)(2,1)}, u32[]{:S(2)}) copy-start(bf16[96,80]{1,0:T(8,128)(2,1)} %constant.14.clone.order_ref) | copy-start | bytes 46084
  49.4 2.0 %collective-permute-start.16 = (bf16[320,768]{1,0:T(8,128)(2,1)S(1)}, bf16[320,768]{1,0:T(8,128)(2,1)S(1)}, u32[]{:S(2)}, u32[]{:S(2)}) collective-permute-start(bf16[320,768]{1,0:T(8,128)(2,1)S(1)} %get-tuple-element.75), channel_id=1, source_target_pairs={{0,4},{4,0},{8,12},{12,8},{16,20},{20,16},{24,28},{28,24},{32,36},... | collective-permute-start | bytes 1474568 | tf_op jit(solution)/shard_map/ppermute | solution.py:587
  51.6 6.7 %collective-permute-start.17 = (bf16[80,768]{1,0:T(8,128)(2,1)S(1)}, bf16[80,768]{1,0:T(8,128)(2,1)S(1)}, u32[]{:S(2)}, u32[]{:S(2)}) collective-permute-start(bf16[80,768]{1,0:T(8,128)(2,1)S(1)} %get-tuple-element.77), channel_id=1, source_target_pairs={{0,8},{4,12},{8,16},{12,20},{16,24},{20,28},{24,0},{28,4},{32,40},... | collective-permute-start | bytes 368648 | tf_op jit(solution)/shard_map/ppermute | solution.py:509
  53.4 8.4 %collective-permute-start.18 = (bf16[80,768]{1,0:T(8,128)(2,1)S(1)}, bf16[80,768]{1,0:T(8,128)(2,1)S(1)}, u32[]{:S(2)}, u32[]{:S(2)}) collective-permute-start(bf16[80,768]{1,0:T(8,128)(2,1)S(1)} %get-tuple-element.78), channel_id=1, source_target_pairs={{0,16},{4,20},{8,24},{12,28},{16,0},{20,4},{24,8},{28,12},{32,48},... | collective-permute-start | bytes 368648 | tf_op jit(solution)/shard_map/ppermute | solution.py:509
  55.8 6.0 %collective-permute-start.19 = (bf16[80,768]{1,0:T(8,128)(2,1)S(1)}, bf16[80,768]{1,0:T(8,128)(2,1)S(1)}, u32[]{:S(2)}, u32[]{:S(2)}) collective-permute-start(bf16[80,768]{1,0:T(8,128)(2,1)S(1)} %get-tuple-element.79), channel_id=1, source_target_pairs={{0,24},{4,28},{8,0},{12,4},{16,8},{20,12},{24,16},{28,20},{32,56},... | collective-permute-start | bytes 368648 | tf_op jit(solution)/shard_map/ppermute | solution.py:509

commit v9 on v8

--- a/solution.py
+++ b/solution.py
@@ -159,47 +159,25 @@
     return out
 
 
-def near_kernel(
-    count_ref, proj_ref, tiles_ref, masked_ref,
-    exp_ref, top_ref, sum_ref, tiles_out, flag_ref,
+def forward_kernel(
+    count_ref, f0, f1, f2, f3, proj_ref, tiles_ref, masked_ref,
+    fk_ref, fv_ref, pnear_ref, pfar_ref, att_ref, tiles_out, flag_ref,
+    att_acc,
 ):
-    count = count_ref[0]
-    pos0 = lax.axis_index("seq") * TOK
+    count = count_ref[...]
+    seq = lax.axis_index("seq")
+    pos0 = seq * TOK
+    for turn, ref in enumerate((f0, f1, f2, f3)):
+        rows = pl.ds(pl.multiple_of(((seq - turn) & 3) * FAR, FAR), FAR)
+        fk_ref[rows] = ref[:, 0:D]
+        fv_ref[rows] = ref[:, D:]
     flag_ref[...] = masked_rows(pos0 + class_major(iota((TOK, TOK), 0)), masked_ref[...])
     tiles_out[...] = nn(class_order(), tiles_ref[0]).astype(BF)
+
     square = (TOK, TOK)
     key_pos = pos0 + class_major(iota(square, 0))
     query_pos = pos0 + class_major(iota(square, 1))
     near_ok = (key_pos < count) | (key_pos == query_pos)
-    for g in range(GROUPS):
-        lo = window(g)
-        masks, _ = head_masks(g)
-        q = proj_ref[:, lo : lo + 256]
-        k = proj_ref[:, D + lo : D + lo + 256]
-        near = nt(k, jnp.concatenate([keep(m, q) for m in masks], 0))
-        for r in range(RATE):
-            head = g * RATE + r
-            scores = jnp.where(near_ok, near[:, TOK * r : TOK * (r + 1)] * SCALE, NEG_FILL)
-            top = jnp.max(scores, axis=0, keepdims=True)
-            exps = jnp.exp(scores - top)
-            exp_ref[g, :, TOK * r : TOK * (r + 1)] = exps
-            top_ref[head : head + 1] = top
-            sum_ref[head : head + 1] = jnp.sum(exps, axis=0, keepdims=True)
-
-
-def far_kernel(
-    count_ref, f0, f1, f2, f3, proj_ref, exp_ref, top_ref, sum_ref,
-    fk_ref, fv_ref, pnear_ref, pfar_ref, att_ref,
-    att_acc,
-):
-    count = count_ref[0]
-    seq = lax.axis_index("seq")
-    for turn, ref in enumerate((f0, f1, f2, f3)):
-        rows = pl.ds(pl.multiple_of(((seq - turn) & 3) * FAR, FAR), FAR)
-        fk_ref[rows] = ref[:, 0:D]
-        fv_ref[rows] = ref[:, D:]
-
-    square = (TOK, TOK)
     far_row = iota(square, 0)
     far_ok = (far_row >> 5) * TOK + (far_row & (FAR - 1)) * RATE + (iota(square, 1) >> 5) < count
     own_class = iota((1, TOK), 1) >> 5
@@ -210,20 +188,28 @@
         win = slice(lo, lo + 256)
         masks, picked = head_masks(g)
         q = proj_ref[:, lo : lo + 256]
+        k = proj_ref[:, D + lo : D + lo + 256]
         v = proj_ref[:, 2 * D + lo : 2 * D + lo + 256]
+        near = nt(k, jnp.concatenate([keep(m, q) for m in masks], 0))
         far = jnp.where(far_ok, nt(fk_ref[:, win], keep(picked, q)) * SCALE, NEG_FILL)
-        heads = range(g * RATE, (g + 1) * RATE)
-        near_tops = [top_ref[h : h + 1] for h in heads]
-        near_sums = [sum_ref[h : h + 1] for h in heads]
-        top = jnp.maximum(jnp.max(far, axis=0, keepdims=True), by_class(own_class, near_tops))
-        shrink = jnp.exp(by_class(own_class, near_tops) - top)
-        far_exp = jnp.exp(far - top)
-        total = by_class(own_class, near_sums) * shrink + jnp.sum(far_exp, axis=0, keepdims=True)
-        far_probs = far_exp / total
-        probs = []
+        far_max = jnp.max(far, axis=0, keepdims=True)
+        scores = [
+            jnp.where(near_ok, near[:, TOK * r : TOK * (r + 1)] * SCALE, NEG_FILL) for r in range(RATE)
+        ]
+        tops = []
         for r in range(RATE):
-            factor = jnp.where(own_class == r, shrink / total, 1.0 / near_sums[r])
-            probs.append(exp_ref[g, :, TOK * r : TOK * (r + 1)] * factor)
+            top = jnp.max(scores[r], axis=0, keepdims=True)
+            tops.append(jnp.where(own_class == r, jnp.maximum(top, far_max), top))
+        exps = [jnp.exp(scores[r] - tops[r]) for r in range(RATE)]
+        far_exp = jnp.exp(far - by_class(own_class, tops))
+        far_sum = jnp.sum(far_exp, axis=0, keepdims=True)
+        inverse = []
+        for r in range(RATE):
+            total = jnp.sum(exps[r], axis=0, keepdims=True)
+            inverse.append(1.0 / jnp.where(own_class == r, total + far_sum, total))
+        probs = [exps[r] * inverse[r] for r in range(RATE)]
+        far_probs = far_exp * by_class(own_class, inverse)
+        for r in range(RATE):
             pnear_ref[g, :, TOK * r : TOK * (r + 1)] = probs[r]
         pfar_ref[g] = far_probs
         att = tn(
@@ -528,23 +514,22 @@
         60,
     )
     fars = swap([dilated] * N_SEQ, "seq", SEQ_TURNS)
-    scores = shape(GROUPS, TOK, RATE * TOK, dtype=F32)
-    rows = shape(HEADS, TOK, dtype=F32)
-    exps, tops, sums, tiles, flag = call(
-        near_kernel,
-        [scores, rows, rows, shape(TOK, 2 * D), shape(TOK, TOK, dtype=F32)],
-        (tile_counts, projected, embeddings, masked_tiles),
-        (),
-        1.0,
-        [SMEM] + [VMEM] * 3,
-    )
     norms = swap([normed] * N_SEQ, "seq", SEQ_TURNS)
-    fk, fv, pnear, pfar, attended = call(
-        far_kernel,
-        [shape(TOK, D), shape(TOK, D), scores, shape(GROUPS, TOK, TOK, dtype=F32), shape(TOK, D)],
-        (tile_counts, *fars, projected, exps, tops, sums),
+    fk, fv, pnear, pfar, attended, tiles, flag = call(
+        forward_kernel,
+        [
+            shape(TOK, D),
+            shape(TOK, D),
+            shape(GROUPS, TOK, RATE * TOK, dtype=F32),
+            shape(GROUPS, TOK, TOK, dtype=F32),
+            shape(TOK, D),
+            shape(TOK, 2 * D),
+            shape(TOK, TOK, dtype=F32),
+        ],
+        (tile_counts.reshape(1, 1), *fars, projected, embeddings, masked_tiles),
         [pltpu.VMEM((TOK, D), F32)],
         2.0,
+        [VMEM] * 8,
     )
     grad_attended, loss, out_mine, out_other = call(
         functools.partial(chain_kernel, inv_count),

time: 81.1 us -> 81.8 us (level)
  waiting for transfers between devices: 14.7 us -> 20 us
  starting transfers between devices: 28.5 us -> 25.2 us
  blocking collectives: 18.2 us -> 16.8 us
    ppermute x18, waiting for transfers between devices: 12.8 us -> 18.2 us  [swap(): lax.ppermute(arrays[t], axis, turns[t])]
    ppermute x18, starting transfers between devices: 28.2 us -> 24.8 us  [swap(): lax.ppermute(arrays[t], axis, turns[t])]
    all_to_all x1, blocking collectives: 18.2 us -> 16.8 us  [per_device(): lax.all_to_all(by_z, 'slide', 0, 0, tiled=True, axis_index_groups=Z_GROUPS)]
    pallas_call x12 -> x11, Pallas kernels: 15.8 us -> 15.8 us  [call(): pl.pallas_call(kernel, out_shape=out_shapes, in_specs=specs, out_specs=[V...]
  transfers between devices with their start and end apart: 20 -> 20, of which waited for: 7 -> 8; matrix products, arithmetic and copies ran while one was open for 0% -> 0% of each run, Pallas kernels for 11% -> 11%
where the time goes in v9:
time: 81.8 us; the launch traced here: 81.6 us
  starting transfers between devices  25.2 us (31%)
  waiting for transfers between devices  20 us (24%)
  blocking collectives  16.8 us (21%)
  Pallas kernels  15.8 us (19%)
  local copies, waits for them, and re-layouts  2.21 us (3%)
  between operations  1.54 us (2%)
    ppermute x18, starting transfers between devices, swap(): lax.ppermute(arrays[t], axis, turns[t])  24.8 us
    ppermute x18, waiting for transfers between devices, swap(): lax.ppermute(arrays[t], axis, turns[t])  18.2 us
    all_to_all x1, blocking collectives, per_device(): lax.all_to_all(by_z, 'slide', 0, 0, tiled=True, axis_index_groups=Z_GROUPS)  16.8 us
    pallas_call x11, Pallas kernels, call(): pl.pallas_call(kernel, out_shape=out_shapes, in_specs=specs, out_specs=[V...  15.8 us
    unnamed x28, local copies, waits for them, and re-layouts  2.21 us
    ppermute x1, waiting for transfers between devices, per_device(): other = lax.ppermute(other, 'slide', CORE_PAIRS)  1.85 us
  transfers between devices with their start and end apart: 20, of which 8 were waited for; matrix products, arithmetic and copies ran while one was open for 0% of the time, Pallas kernels for 11%

profile of v9, /device:TPU:2, one launch (start us, length us, event | category | flops | bytes accessed | tf_op | source)
XLA Modules:
  0.0 81.6 jit_solution(16318932302859966072)
XLA Ops:
  0.7 4.4 %shard_map.131 = (bf16[128,768]{1,0:T(8,128)(2,1)}, bf16[128,768]{1,0:T(8,128)(2,1)}, bf16[128,2304]{1,0:T(8,128)(2,1)}, bf16[32,1536]{1,0:T(8,128)(2,1)}) custom-call(bf16[1,128,1536]{2,1,0:T(8,128)(2,1)} %tiles_ref.1, s32[1,128]{1,0:T(1,128)} %masked_ref.1, f32[768]{0:T(1024)} %gain_hbm.1, bf16[1536,768]{1,0:T(8,128)(2,1)} %w_in_ref.1, ...), custom_call_target="tpu_custom_call" | custom-call | flops 4000000000 | bytes 4000000 | tf_op jit(solution)/shard_map/pallas_call | solution.py:459
  5.1 1.6 %collective-permute-start = (bf16[32,1536]{1,0:T(8,128)(2,1)}, bf16[32,1536]{1,0:T(8,128)(2,1)S(1)}, u32[]{:S(2)}, u32[]{:S(2)}) collective-permute-start(bf16[32,1536]{1,0:T(8,128)(2,1)} %get-tuple-element.40.f0), channel_id=1, source_target_pairs={{0,1},{1,2},{2,3},{3,0},{4,5},{5,6},{6,7},{7,4},{8,9},{9,10},{10,1... | collective-permute-start | bytes 294920 | tf_op jit(solution)/shard_map/ppermute | solution.py:495
  6.7 2.8 %collective-permute-start.1 = (bf16[32,1536]{1,0:T(8,128)(2,1)}, bf16[32,1536]{1,0:T(8,128)(2,1)S(1)}, u32[]{:S(2)}, u32[]{:S(2)}) collective-permute-start(bf16[32,1536]{1,0:T(8,128)(2,1)} %get-tuple-element.40.f0), channel_id=1, source_target_pairs={{0,2},{1,3},{2,0},{3,1},{4,6},{5,7},{6,4},{7,5},{8,10},{9,11},{10,... | collective-permute-start | bytes 294920 | tf_op jit(solution)/shard_map/ppermute | solution.py:495
  9.5 0.4 collective-permute-start.2
  9.9 1.6 %collective-permute-start.6 = (bf16[128,768]{1,0:T(8,128)(2,1)}, bf16[128,768]{1,0:T(8,128)(2,1)S(1)}, u32[]{:S(2)}, u32[]{:S(2)}) collective-permute-start(bf16[128,768]{1,0:T(8,128)(2,1)} %get-tuple-element.55.n0), channel_id=1, source_target_pairs={{0,1},{1,2},{2,3},{3,0},{4,5},{5,6},{6,7},{7,4},{8,9},{9,10},{10,1... | collective-permute-start | bytes 589832 | tf_op jit(solution)/shard_map/ppermute | solution.py:495
  11.5 1.9 %collective-permute-start.7 = (bf16[128,768]{1,0:T(8,128)(2,1)}, bf16[128,768]{1,0:T(8,128)(2,1)S(1)}, u32[]{:S(2)}, u32[]{:S(2)}) collective-permute-start(bf16[128,768]{1,0:T(8,128)(2,1)} %get-tuple-element.55.n0), channel_id=1, source_target_pairs={{0,2},{1,3},{2,0},{3,1},{4,6},{5,7},{6,4},{7,5},{8,10},{9,11},{10,... | collective-permute-start | bytes 589832 | tf_op jit(solution)/shard_map/ppermute | solution.py:495
  14.1 0.3 collective-permute-start.8
  14.4 0.0 collective-permute-done.1.f2
  14.4 3.1 %collective-permute-done.2.f3 = bf16[32,1536]{1,0:T(8,128)(2,1)S(1)} collective-permute-done((bf16[32,1536]{1,0:T(8,128)(2,1)}, bf16[32,1536]{1,0:T(8,128)(2,1)S(1)}, u32[]{:S(2)}, u32[]{:S(2)}) %collective-permute-start.2) | collective-permute-done | bytes 98336 | tf_op jit(solution)/shard_map/ppermute | solution.py:495
  17.4 0.9 %copy-done.4 = bf16[32,1536]{1,0:T(8,128)(2,1)S(1)} copy-done((bf16[32,1536]{1,0:T(8,128)(2,1)S(1)}, bf16[32,1536]{1,0:T(8,128)(2,1)}, u32[]{:S(2)}) %copy-start.4) | copy-done | bytes 98328
  18.3 1.1 %copy-done.11 = bf16[128,2304]{1,0:T(8,128)(2,1)S(1)} copy-done((bf16[128,2304]{1,0:T(8,128)(2,1)S(1)}, bf16[128,2304]{1,0:T(8,128)(2,1)}, u32[]{:S(2)}) %copy-start.11) | copy-done | bytes 589848
  19.4 2.1 %shard_map.132 = (bf16[128,768]{1,0:T(8,128)(2,1)S(1)}, bf16[128,768]{1,0:T(8,128)(2,1)S(1)}, f32[4,128,512]{2,1,0:T(8,128)S(1)}, f32[4,128,128]{2,1,0:T(8,128)S...) custom-call(s32[1,1]{1,0:T(1,128)} %bitcast.2.count_ref, ...), custom_call_target="tpu_custom_call" | custom-call | flops 2000000000 | bytes 2000000 | tf_op jit(solution)/shard_map/pallas_call | solution.py:459
  21.5 0.2 copy-done.6
  21.7 0.0 copy-done.13
  21.8 2.7 %shard_map.133 = (bf16[128,768]{1,0:T(8,128)(2,1)S(1)}, bf16[16,128]{1,0:T(8,128)(2,1)S(1)}, bf16[384,768]{1,0:T(8,128)(2,1)S(1)}, bf16[384,768]{1,0:T(8,128)(2,1)S(1)}) custom-call(bf16[128,768]{1,0:T(8,128)(2,1)S(1)} %get-tuple-element.45.att_ref, bf16[128,768]{1,0:T(8,128)(2,1)S(1)} %copy-done.13, bf16[128,1536]{1,0:T(8,128)(2,1)S(1)} %get-tuple-element.47.tiles_ref, ...), custom_call_target="tpu_custom_call" | custom-call | flops 3000000000 | bytes 3000000 | tf_op jit(solution)/shard_map/pallas_call | solution.py:459
  24.5 0.3 collective-permute-start.9
  24.8 3.0 %shard_map.134 = (bf16[976,128]{1,0:T(8,128)(2,1)S(1)}, bf16[976,128]{1,0:T(8,128)(2,1)S(1)}, bf16[976,128]{1,0:T(8,128)(2,1)S(1)}, bf16[976,128]{1,0:T(8,128)(2,1)S(1)}) custom-call(bf16[128,2304]{1,0:T(8,128)(2,1)S(1)} %copy-done.12, bf16[128,768]{1,0:T(8,128)(2,1)S(1)} %get-tuple-element.41.fk_ref, bf16[128,768]{1,0:T(8,128)(2,1)S(1)} %get-tuple-element.42.fv_ref, ...), custom_call_target="tpu_custom_call" | custom-call | flops 8000000000 | bytes 8000000 | tf_op jit(solution)/shard_map/pallas_call | solution.py:459
  27.8 0.0 copy-start.9
  27.8 0.2 shard_map.135
  28.0 0.1 collective-permute-start.10
  28.1 0.9 %collective-permute-start.3 = (bf16[976,128]{1,0:T(8,128)(2,1)S(1)}, bf16[976,128]{1,0:T(8,128)(2,1)S(1)}, u32[]{:S(2)}, u32[]{:S(2)}) collective-permute-start(bf16[976,128]{1,0:T(8,128)(2,1)S(1)} %get-tuple-element.52), channel_id=1, source_target_pairs={{0,1},{1,2},{2,3},{3,0},{4,5},{5,6},{6,7},{7,4},{8,9},{9,10},{10,1... | collective-permute-start | bytes 749576 | tf_op jit(solution)/shard_map/ppermute | solution.py:495
  29.0 1.3 %collective-permute-start.4 = (bf16[976,128]{1,0:T(8,128)(2,1)S(1)}, bf16[976,128]{1,0:T(8,128)(2,1)S(1)}, u32[]{:S(2)}, u32[]{:S(2)}) collective-permute-start(bf16[976,128]{1,0:T(8,128)(2,1)S(1)} %get-tuple-element.53), channel_id=1, source_target_pairs={{0,2},{1,3},{2,0},{3,1},{4,6},{5,7},{6,4},{7,5},{8,10},{9,11},{10,... | collective-permute-start | bytes 749576 | tf_op jit(solution)/shard_map/ppermute | solution.py:495
  30.3 2.5 %collective-permute-start.5 = (bf16[976,128]{1,0:T(8,128)(2,1)S(1)}, bf16[976,128]{1,0:T(8,128)(2,1)S(1)}, u32[]{:S(2)}, u32[]{:S(2)}) collective-permute-start(bf16[976,128]{1,0:T(8,128)(2,1)S(1)} %get-tuple-element.54), channel_id=1, source_target_pairs={{0,3},{1,0},{2,1},{3,2},{4,7},{5,4},{6,5},{7,6},{8,11},{9,8},{10,9... | collective-permute-start | bytes 749576 | tf_op jit(solution)/shard_map/ppermute | solution.py:495
  32.9 1.2 %collective-permute-start.11 = (bf16[96,768]{1,0:T(8,128)(2,1)S(1)}, bf16[96,768]{1,0:T(8,128)(2,1)S(1)}, u32[]{:S(2)}, u32[]{:S(2)}) collective-permute-start(bf16[96,768]{1,0:T(8,128)(2,1)S(1)} %get-tuple-element.60), channel_id=1, source_target_pairs={{0,16},{4,20},{8,24},{12,28},{16,0},{20,4},{24,8},{28,12},{32,48},... | collective-permute-start | bytes 442376 | tf_op jit(solution)/shard_map/ppermute | solution.py:495
  34.1 1.5 %collective-permute-done.10.y1 = bf16[96,768]{1,0:T(8,128)(2,1)S(1)} collective-permute-done((bf16[96,768]{1,0:T(8,128)(2,1)S(1)}, bf16[96,768]{1,0:T(8,128)(2,1)S(1)}, u32[]{:S(2)}, u32[]{:S(2)}) %collective-permute-start.10) | collective-permute-done | bytes 147488 | tf_op jit(solution)/shard_map/ppermute | solution.py:495
  35.5 0.5 collective-permute-start.12
  36.0 3.7 %collective-permute-done.11.y2 = bf16[96,768]{1,0:T(8,128)(2,1)S(1)} collective-permute-done((bf16[96,768]{1,0:T(8,128)(2,1)S(1)}, bf16[96,768]{1,0:T(8,128)(2,1)S(1)}, u32[]{:S(2)}, u32[]{:S(2)}) %collective-permute-start.11) | collective-permute-done | bytes 147488 | tf_op jit(solution)/shard_map/ppermute | solution.py:495
  39.8 3.4 %collective-permute-done.12.y3 = bf16[96,768]{1,0:T(8,128)(2,1)S(1)} collective-permute-done((bf16[96,768]{1,0:T(8,128)(2,1)S(1)}, bf16[96,768]{1,0:T(8,128)(2,1)S(1)}, u32[]{:S(2)}, u32[]{:S(2)}) %collective-permute-start.12) | collective-permute-done | bytes 147488 | tf_op jit(solution)/shard_map/ppermute | solution.py:495
  43.2 0.3 shard_map.136
  43.4 0.1 collective-permute-start.13
  43.5 3.1 %collective-permute-start.14 = (bf16[32,768]{1,0:T(8,128)(2,1)S(1)}, bf16[32,768]{1,0:T(8,128)(2,1)S(1)}, u32[]{:S(2)}, u32[]{:S(2)}) collective-permute-start(bf16[32,768]{1,0:T(8,128)(2,1)S(1)} %get-tuple-element.66), channel_id=1, source_target_pairs={{0,2},{1,3},{2,0},{3,1},{4,6},{5,7},{6,4},{7,5},{8,10},{9,11},{10,... | collective-permute-start | bytes 147464 | tf_op jit(solution)/shard_map/ppermute | solution.py:495
  46.6 2.5 %collective-permute-start.15 = (bf16[32,768]{1,0:T(8,128)(2,1)S(1)}, bf16[32,768]{1,0:T(8,128)(2,1)S(1)}, u32[]{:S(2)}, u32[]{:S(2)}) collective-permute-start(bf16[32,768]{1,0:T(8,128)(2,1)S(1)} %get-tuple-element.67), channel_id=1, source_target_pairs={{0,3},{1,0},{2,1},{3,2},{4,7},{5,4},{6,5},{7,6},{8,11},{9,8},{10,9... | collective-permute-start | bytes 147464 | tf_op jit(solution)/shard_map/ppermute | solution.py:495
  49.2 0.0 copy-start.7
  49.2 1.1 %shard_map.137 = (bf16[576,768]{1,0:T(8,128)(2,1)S(1)}, f32[80,768]{1,0:T(8,128)S(1)}) custom-call(bf16[976,128]{1,0:T(8,128)(2,1)S(1)} %get-tuple-element.51.wait0.x0, bf16[976,128]{1,0:T(8,128)(2,1)S(1)} %collective-permute-done.3.x1, bf16[976,128]{1,0:T(8,128)(2,1)S(1)} %collective-permute-done.4.x2, bf16[976,128]{1,0:T(8,128)(2,1)S(1)} %collective-permute-done.5.x3, ...), custom_call_target="tpu_custom_call" | custom-call | flops 15000000512 | bytes 15000000 | tf_op jit(solution)/shard_map/pallas_call | solution.py:459
  50.3 0.6 collective-permute-done.15.wait3.o3
  50.9 0.9 %shard_map.138 = (bf16[320,768]{1,0:T(8,128)(2,1)S(1)}, bf16[320,768]{1,0:T(8,128)(2,1)S(1)}) custom-call(bf16[576,768]{1,0:T(8,128)(2,1)S(1)} %get-tuple-element.63.whole_ref, f32[80,768]{1,0:T(8,128)S(1)} %get-tuple-element.64.tail_ref, bf16[640,576]{1,0:T(8,128)(2,1)S(1)} %copy-done.7, bf16[32,768]{1,0:T(8,128)(2,1)S(1)} %collective-permute-done.13.wait1.o1, ...), custom_call_target="tpu_custom_call" | custom-call | flops 1000000000 | bytes 1000000 | tf_op jit(solution)/shard_map/pallas_call | solution.py:459
  51.9 0.0 copy-start.10
  51.9 0.1 collective-permute-start.16
  52.0 1.9 %collective-permute-done.16.other_ref = bf16[320,768]{1,0:T(8,128)(2,1)S(1)} collective-permute-done((bf16[320,768]{1,0:T(8,128)(2,1)S(1)}, bf16[320,768]{1,0:T(8,128)(2,1)S(1)}, u32[]{:S(2)}, u32[]{:S(2)}) %collective-permute-start.16) | collective-permute-done | bytes 491552 | tf_op jit(solution)/shard_map/ppermute | solution.py:572
  53.8 0.2 shard_map.139
  54.0 0.7 collective-permute-start.17
  54.8 2.5 %collective-permute-start.18 = (bf16[80,768]{1,0:T(8,128)(2,1)S(1)}, bf16[80,768]{1,0:T(8,128)(2,1)S(1)}, u32[]{:S(2)}, u32[]{:S(2)}) collective-permute-start(bf16[80,768]{1,0:T(8,128)(2,1)S(1)} %get-tuple-element.72), channel_id=1, source_target_pairs={{0,16},{4,20},{8,24},{12,28},{16,0},{20,4},{24,8},{28,12},{32,48},... | collective-permute-start | bytes 368648 | tf_op jit(solution)/shard_map/ppermute | solution.py:495
  57.2 0.8 collective-permute-start.19
  58.0 5.3 %collective-permute-done.17.y1 = bf16[80,768]{1,0:T(8,128)(2,1)S(1)} collective-permute-done((bf16[80,768]{1,0:T(8,128)(2,1)S(1)}, bf16[80,768]{1,0:T(8,128)(2,1)S(1)}, u32[]{:S(2)}, u32[]{:S(2)}) %collective-permute-start.17) | collective-permute-done | bytes 122912 | tf_op jit(solution)/shard_map/ppermute | solution.py:495
  63.3 0.6 collective-permute-done.19.y3
  63.9 0.3 shard_map.140
  64.2 16.8 %all_to_all.5.in_ref = bf16[8,16,768]{2,1,0:T(8,128)(2,1)S(1)} all-to-all(bf16[8,16,768]{2,1,0:T(8,128)(2,1)S(1)} %shard_map.140), channel_id=1, replica_groups={{0,32,64,96,128,160,192,224},{4,36,68,100,132,164,196,228},{8,40,72,104..., dimensions={0} | all-to-all | bytes 393216 | tf_op jit(solution)/shard_map/all_to_all | solution.py:576
  80.9 0.7 shard_map.141
  (32 shorter events, 0.1 us)
Async XLA Ops:
  0.6 16.8 %copy-start.2 = (bf16[1,128,1536]{2,1,0:T(8,128)(2,1)S(1)}, bf16[1,128,1536]{2,1,0:T(8,128)(2,1)}, u32[]{:S(2)}) copy-start(bf16[1,128,1536]{2,1,0:T(8,128)(2,1)} %tiles_ref.1) | copy-start | bytes 1179652
  0.6 16.8 %copy-start.5 = (s32[1,128]{1,0:T(1,128)S(1)}, s32[1,128]{1,0:T(1,128)}, u32[]{:S(2)}) copy-start(s32[1,128]{1,0:T(1,128)} %masked_ref.1) | copy-start | bytes 1540
  5.1 9.0 %collective-permute-start = (bf16[32,1536]{1,0:T(8,128)(2,1)}, bf16[32,1536]{1,0:T(8,128)(2,1)S(1)}, u32[]{:S(2)}, u32[]{:S(2)}) collective-permute-start(bf16[32,1536]{1,0:T(8,128)(2,1)} %get-tuple-element.40.f0), channel_id=1, source_target_pairs={{0,1},{1,2},{2,3},{3,0},{4,5},{5,6},{6,7},{7,4},{8,9},{9,10},{10,1... | collective-permute-start | bytes 294920 | tf_op jit(solution)/shard_map/ppermute | solution.py:495
  6.7 7.7 %collective-permute-start.1 = (bf16[32,1536]{1,0:T(8,128)(2,1)}, bf16[32,1536]{1,0:T(8,128)(2,1)S(1)}, u32[]{:S(2)}, u32[]{:S(2)}) collective-permute-start(bf16[32,1536]{1,0:T(8,128)(2,1)} %get-tuple-element.40.f0), channel_id=1, source_target_pairs={{0,2},{1,3},{2,0},{3,1},{4,6},{5,7},{6,4},{7,5},{8,10},{9,11},{10,... | collective-permute-start | bytes 294920 | tf_op jit(solution)/shard_map/ppermute | solution.py:495
  9.5 7.9 %collective-permute-start.2 = (bf16[32,1536]{1,0:T(8,128)(2,1)}, bf16[32,1536]{1,0:T(8,128)(2,1)S(1)}, u32[]{:S(2)}, u32[]{:S(2)}) collective-permute-start(bf16[32,1536]{1,0:T(8,128)(2,1)} %get-tuple-element.40.f0), channel_id=1, source_target_pairs={{0,3},{1,0},{2,1},{3,2},{4,7},{5,4},{6,5},{7,6},{8,11},{9,8},{10,9... | collective-permute-start | bytes 294920 | tf_op jit(solution)/shard_map/ppermute | solution.py:495
  9.9 17.9 %collective-permute-start.6 = (bf16[128,768]{1,0:T(8,128)(2,1)}, bf16[128,768]{1,0:T(8,128)(2,1)S(1)}, u32[]{:S(2)}, u32[]{:S(2)}) collective-permute-start(bf16[128,768]{1,0:T(8,128)(2,1)} %get-tuple-element.55.n0), channel_id=1, source_target_pairs={{0,1},{1,2},{2,3},{3,0},{4,5},{5,6},{6,7},{7,4},{8,9},{9,10},{10,1... | collective-permute-start | bytes 589832 | tf_op jit(solution)/shard_map/ppermute | solution.py:495
  11.5 16.3 %collective-permute-start.7 = (bf16[128,768]{1,0:T(8,128)(2,1)}, bf16[128,768]{1,0:T(8,128)(2,1)S(1)}, u32[]{:S(2)}, u32[]{:S(2)}) collective-permute-start(bf16[128,768]{1,0:T(8,128)(2,1)} %get-tuple-element.55.n0), channel_id=1, source_target_pairs={{0,2},{1,3},{2,0},{3,1},{4,6},{5,7},{6,4},{7,5},{8,10},{9,11},{10,... | collective-permute-start | bytes 589832 | tf_op jit(solution)/shard_map/ppermute | solution.py:495
  14.1 13.7 %collective-permute-start.8 = (bf16[128,768]{1,0:T(8,128)(2,1)}, bf16[128,768]{1,0:T(8,128)(2,1)S(1)}, u32[]{:S(2)}, u32[]{:S(2)}) collective-permute-start(bf16[128,768]{1,0:T(8,128)(2,1)} %get-tuple-element.55.n0), channel_id=1, source_target_pairs={{0,3},{1,0},{2,1},{3,2},{4,7},{5,4},{6,5},{7,6},{8,11},{9,8},{10,9... | collective-permute-start | bytes 589832 | tf_op jit(solution)/shard_map/ppermute | solution.py:495
  17.4 0.9 %copy-start.4 = (bf16[32,1536]{1,0:T(8,128)(2,1)S(1)}, bf16[32,1536]{1,0:T(8,128)(2,1)}, u32[]{:S(2)}) copy-start(bf16[32,1536]{1,0:T(8,128)(2,1)} %get-tuple-element.40.f0) | copy-start | bytes 294916
  18.3 1.1 %copy-start.11 = (bf16[128,2304]{1,0:T(8,128)(2,1)S(1)}, bf16[128,2304]{1,0:T(8,128)(2,1)}, u32[]{:S(2)}) copy-start(bf16[128,2304]{1,0:T(8,128)(2,1)} %get-tuple-element.39.proj_ref) | copy-start | bytes 1769476
  19.4 2.1 %copy-start = (bf16[1536,768]{1,0:T(8,128)(2,1)S(1)}, bf16[1536,768]{1,0:T(8,128)(2,1)}, u32[]{:S(2)}) copy-start(bf16[1536,768]{1,0:T(8,128)(2,1)} %w_in_ref.1) | copy-start | bytes 7077892
  19.4 2.1 %copy-start.1 = (bf16[768,768]{1,0:T(8,128)(2,1)S(1)}, bf16[768,768]{1,0:T(8,128)(2,1)}, u32[]{:S(2)}) copy-start(bf16[768,768]{1,0:T(8,128)(2,1)} %w_out_ref.1) | copy-start | bytes 3538948
  19.4 2.3 %copy-start.6 = (bf16[768,768]{1,0:T(8,128)(2,1)S(1)}, bf16[768,768]{1,0:T(8,128)(2,1)}, u32[]{:S(2)}) copy-start(bf16[768,768]{1,0:T(8,128)(2,1)} %constant.10.clone.order_ref) | copy-start | bytes 3538948
  19.4 2.3 %copy-start.13 = (bf16[128,768]{1,0:T(8,128)(2,1)S(1)}, bf16[128,768]{1,0:T(8,128)(2,1)}, u32[]{:S(2)}) copy-start(bf16[128,768]{1,0:T(8,128)(2,1)} %get-tuple-element.46.hidden_ref) | copy-start | bytes 589828
  21.7 3.0 %copy-start.8 = (bf16[384,384]{1,0:T(8,128)(2,1)S(1)}, bf16[384,384]{1,0:T(8,128)(2,1)}, u32[]{:S(2)}) copy-start(bf16[384,384]{1,0:T(8,128)(2,1)} %constant.11.clone.spread_ref) | copy-start | bytes 884740
  21.8 3.0 %copy-start.12 = (bf16[128,2304]{1,0:T(8,128)(2,1)S(1)}, bf16[128,2304]{1,0:T(8,128)(2,1)}, u32[]{:S(2)}) copy-start(bf16[128,2304]{1,0:T(8,128)(2,1)} %get-tuple-element.39.proj_ref) | copy-start | bytes 1769476
  24.5 3.4 %collective-permute-start.9 = (bf16[384,768]{1,0:T(8,128)(2,1)S(1)}, bf16[384,768]{1,0:T(8,128)(2,1)S(1)}, u32[]{:S(2)}, u32[]{:S(2)}) collective-permute-start(bf16[384,768]{1,0:T(8,128)(2,1)S(1)} %get-tuple-element.57), channel_id=1, source_target_pairs={{0,4},{4,0},{8,12},{12,8},{16,20},{20,16},{24,28},{28,24},{32,36},... | collective-permute-start | bytes 1769480 | tf_op jit(solution)/shard_map/ppermute | solution.py:541
  27.8 15.4 %copy-start.9 = (bf16[128,96]{1,0:T(8,128)(2,1)S(1)}, bf16[128,96]{1,0:T(8,128)(2,1)}, u32[]{:S(2)}) copy-start(bf16[128,96]{1,0:T(8,128)(2,1)} %constant.12.clone.order_ref) | copy-start | bytes 73732
  28.0 21.2 %copy-start.3 = (bf16[128,768]{1,0:T(8,128)(2,1)S(1)}, bf16[128,768]{1,0:T(8,128)(2,1)}, u32[]{:S(2)}) copy-start(bf16[128,768]{1,0:T(8,128)(2,1)} %get-tuple-element.55.n0) | copy-start | bytes 589828
  28.0 7.5 %collective-permute-start.10 = (bf16[96,768]{1,0:T(8,128)(2,1)S(1)}, bf16[96,768]{1,0:T(8,128)(2,1)S(1)}, u32[]{:S(2)}, u32[]{:S(2)}) collective-permute-start(bf16[96,768]{1,0:T(8,128)(2,1)S(1)} %get-tuple-element.59), channel_id=1, source_target_pairs={{0,8},{4,12},{8,16},{12,20},{16,24},{20,28},{24,0},{28,4},{32,40},... | collective-permute-start | bytes 442376 | tf_op jit(solution)/shard_map/ppermute | solution.py:495
  28.1 18.5 %collective-permute-start.3 = (bf16[976,128]{1,0:T(8,128)(2,1)S(1)}, bf16[976,128]{1,0:T(8,128)(2,1)S(1)}, u32[]{:S(2)}, u32[]{:S(2)}) collective-permute-start(bf16[976,128]{1,0:T(8,128)(2,1)S(1)} %get-tuple-element.52), channel_id=1, source_target_pairs={{0,1},{1,2},{2,3},{3,0},{4,5},{5,6},{6,7},{7,4},{8,9},{9,10},{10,1... | collective-permute-start | bytes 749576 | tf_op jit(solution)/shard_map/ppermute | solution.py:495
  29.0 20.1 %collective-permute-start.4 = (bf16[976,128]{1,0:T(8,128)(2,1)S(1)}, bf16[976,128]{1,0:T(8,128)(2,1)S(1)}, u32[]{:S(2)}, u32[]{:S(2)}) collective-permute-start(bf16[976,128]{1,0:T(8,128)(2,1)S(1)} %get-tuple-element.53), channel_id=1, source_target_pairs={{0,2},{1,3},{2,0},{3,1},{4,6},{5,7},{6,4},{7,5},{8,10},{9,11},{10,... | collective-permute-start | bytes 749576 | tf_op jit(solution)/shard_map/ppermute | solution.py:495
  30.3 18.8 %collective-permute-start.5 = (bf16[976,128]{1,0:T(8,128)(2,1)S(1)}, bf16[976,128]{1,0:T(8,128)(2,1)S(1)}, u32[]{:S(2)}, u32[]{:S(2)}) collective-permute-start(bf16[976,128]{1,0:T(8,128)(2,1)S(1)} %get-tuple-element.54), channel_id=1, source_target_pairs={{0,3},{1,0},{2,1},{3,2},{4,7},{5,4},{6,5},{7,6},{8,11},{9,8},{10,9... | collective-permute-start | bytes 749576 | tf_op jit(solution)/shard_map/ppermute | solution.py:495
  32.9 6.9 %collective-permute-start.11 = (bf16[96,768]{1,0:T(8,128)(2,1)S(1)}, bf16[96,768]{1,0:T(8,128)(2,1)S(1)}, u32[]{:S(2)}, u32[]{:S(2)}) collective-permute-start(bf16[96,768]{1,0:T(8,128)(2,1)S(1)} %get-tuple-element.60), channel_id=1, source_target_pairs={{0,16},{4,20},{8,24},{12,28},{16,0},{20,4},{24,8},{28,12},{32,48},... | collective-permute-start | bytes 442376 | tf_op jit(solution)/shard_map/ppermute | solution.py:495
  35.5 7.6 %collective-permute-start.12 = (bf16[96,768]{1,0:T(8,128)(2,1)S(1)}, bf16[96,768]{1,0:T(8,128)(2,1)S(1)}, u32[]{:S(2)}, u32[]{:S(2)}) collective-permute-start(bf16[96,768]{1,0:T(8,128)(2,1)S(1)} %get-tuple-element.61), channel_id=1, source_target_pairs={{0,24},{4,28},{8,0},{12,4},{16,8},{20,12},{24,16},{28,20},{32,56},... | collective-permute-start | bytes 442376 | tf_op jit(solution)/shard_map/ppermute | solution.py:495
  43.4 6.9 %collective-permute-start.13 = (bf16[32,768]{1,0:T(8,128)(2,1)S(1)}, bf16[32,768]{1,0:T(8,128)(2,1)S(1)}, u32[]{:S(2)}, u32[]{:S(2)}) collective-permute-start(bf16[32,768]{1,0:T(8,128)(2,1)S(1)} %get-tuple-element.65), channel_id=1, source_target_pairs={{0,1},{1,2},{2,3},{3,0},{4,5},{5,6},{6,7},{7,4},{8,9},{9,10},{10,1... | collective-permute-start | bytes 147464 | tf_op jit(solution)/shard_map/ppermute | solution.py:495
  43.5 6.8 %collective-permute-start.14 = (bf16[32,768]{1,0:T(8,128)(2,1)S(1)}, bf16[32,768]{1,0:T(8,128)(2,1)S(1)}, u32[]{:S(2)}, u32[]{:S(2)}) collective-permute-start(bf16[32,768]{1,0:T(8,128)(2,1)S(1)} %get-tuple-element.66), channel_id=1, source_target_pairs={{0,2},{1,3},{2,0},{3,1},{4,6},{5,7},{6,4},{7,5},{8,10},{9,11},{10,... | collective-permute-start | bytes 147464 | tf_op jit(solution)/shard_map/ppermute | solution.py:495
  46.6 4.3 %collective-permute-start.15 = (bf16[32,768]{1,0:T(8,128)(2,1)S(1)}, bf16[32,768]{1,0:T(8,128)(2,1)S(1)}, u32[]{:S(2)}, u32[]{:S(2)}) collective-permute-start(bf16[32,768]{1,0:T(8,128)(2,1)S(1)} %get-tuple-element.67), channel_id=1, source_target_pairs={{0,3},{1,0},{2,1},{3,2},{4,7},{5,4},{6,5},{7,6},{8,11},{9,8},{10,9... | collective-permute-start | bytes 147464 | tf_op jit(solution)/shard_map/ppermute | solution.py:495
  49.2 1.7 %copy-start.7 = (bf16[640,576]{1,0:T(8,128)(2,1)S(1)}, bf16[640,576]{1,0:T(8,128)(2,1)}, u32[]{:S(2)}) copy-start(bf16[640,576]{1,0:T(8,128)(2,1)} %constant.13.clone.order_ref) | copy-start | bytes 2211844
  51.9 12.0 %copy-start.10 = (bf16[96,80]{1,0:T(8,128)(2,1)S(1)}, bf16[96,80]{1,0:T(8,128)(2,1)}, u32[]{:S(2)}) copy-start(bf16[96,80]{1,0:T(8,128)(2,1)} %constant.14.clone.order_ref) | copy-start | bytes 46084
  51.9 2.0 %collective-permute-start.16 = (bf16[320,768]{1,0:T(8,128)(2,1)S(1)}, bf16[320,768]{1,0:T(8,128)(2,1)S(1)}, u32[]{:S(2)}, u32[]{:S(2)}) collective-permute-start(bf16[320,768]{1,0:T(8,128)(2,1)S(1)} %get-tuple-element.69), channel_id=1, source_target_pairs={{0,4},{4,0},{8,12},{12,8},{16,20},{20,16},{24,28},{28,24},{32,36},... | collective-permute-start | bytes 1474568 | tf_op jit(solution)/shard_map/ppermute | solution.py:572
  54.0 9.3 %collective-permute-start.17 = (bf16[80,768]{1,0:T(8,128)(2,1)S(1)}, bf16[80,768]{1,0:T(8,128)(2,1)S(1)}, u32[]{:S(2)}, u32[]{:S(2)}) collective-permute-start(bf16[80,768]{1,0:T(8,128)(2,1)S(1)} %get-tuple-element.71), channel_id=1, source_target_pairs={{0,8},{4,12},{8,16},{12,20},{16,24},{20,28},{24,0},{28,4},{32,40},... | collective-permute-start | bytes 368648 | tf_op jit(solution)/shard_map/ppermute | solution.py:495
  54.8 8.6 %collective-permute-start.18 = (bf16[80,768]{1,0:T(8,128)(2,1)S(1)}, bf16[80,768]{1,0:T(8,128)(2,1)S(1)}, u32[]{:S(2)}, u32[]{:S(2)}) collective-permute-start(bf16[80,768]{1,0:T(8,128)(2,1)S(1)} %get-tuple-element.72), channel_id=1, source_target_pairs={{0,16},{4,20},{8,24},{12,28},{16,0},{20,4},{24,8},{28,12},{32,48},... | collective-permute-start | bytes 368648 | tf_op jit(solution)/shard_map/ppermute | solution.py:495
  57.2 6.7 %collective-permute-start.19 = (bf16[80,768]{1,0:T(8,128)(2,1)S(1)}, bf16[80,768]{1,0:T(8,128)(2,1)S(1)}, u32[]{:S(2)}, u32[]{:S(2)}) collective-permute-start(bf16[80,768]{1,0:T(8,128)(2,1)S(1)} %get-tuple-element.73), channel_id=1, source_target_pairs={{0,24},{4,28},{8,0},{12,4},{16,8},{20,12},{24,16},{28,20},{32,56},... | collective-permute-start | bytes 368648 | tf_op jit(solution)/shard_map/ppermute | solution.py:495

commit v10 on v9

--- a/solution.py
+++ b/solution.py
@@ -126,9 +126,12 @@
             rows = nn(normed, w_qkv[:, first : first + 256]).astype(BF)
             proj_out[:, first : first + 256] = rows
             if part > 0:
-                lane_class = ((iota((FAR, 256), 1) + block * 256) // HD) & 3
-                pieces = [rows[FAR * r : FAR * (r + 1)] for r in range(RATE)]
-                dilated_out[:, first - D : first - D + 256] = by_class(lane_class, pieces)
+                dilated_out[:, first - D : first - D + 256] = dilate(rows, block * 256)
+
+
+def dilate(rows, lane0):
+    lane_class = ((iota((FAR, 256), 1) + lane0) // HD) & 3
+    return by_class(lane_class, [rows[FAR * r : FAR * (r + 1)] for r in range(RATE)])
 
 
 def window(group):
@@ -160,17 +163,24 @@
 
 
 def forward_kernel(
-    count_ref, f0, f1, f2, f3, proj_ref, tiles_ref, masked_ref,
+    count_ref, f2, f1, f3, proj_ref, tiles_ref, masked_ref,
     fk_ref, fv_ref, pnear_ref, pfar_ref, att_ref, tiles_out, flag_ref,
     att_acc,
 ):
     count = count_ref[...]
     seq = lax.axis_index("seq")
     pos0 = seq * TOK
-    for turn, ref in enumerate((f0, f1, f2, f3)):
-        rows = pl.ds(pl.multiple_of(((seq - turn) & 3) * FAR, FAR), FAR)
+    for turn, ref in enumerate((f1, f2, f3)):
+        rows = pl.ds(pl.multiple_of(((seq - turn - 1) & 3) * FAR, FAR), FAR)
         fk_ref[rows] = ref[:, 0:D]
         fv_ref[rows] = ref[:, D:]
+    own_rows = pl.ds(pl.multiple_of(seq * FAR, FAR), FAR)
+    for part, far_ref in enumerate((fk_ref, fv_ref)):
+        for block in range(D // 256):
+            first = (1 + part) * D + block * 256
+            far_ref[own_rows, block * 256 : (block + 1) * 256] = dilate(
+                proj_ref[:, first : first + 256], block * 256
+            )
     flag_ref[...] = masked_rows(pos0 + class_major(iota((TOK, TOK), 0)), masked_ref[...])
     tiles_out[...] = nn(class_order(), tiles_ref[0]).astype(BF)
 
@@ -284,12 +294,11 @@
         gkf[:, win] += nn(far_scores, keep(picked, q))
         gvf[:, win] += nn(far_probs.astype(BF), ga_picked)
     place = spread_ref[...]
-    section = 0
-    for value in (gq, gk, gv, gkf, gvf):
-        for half in range(2):
-            piece = value[:, half * HALF : (half + 1) * HALF].astype(BF)
-            turned[section] = nt(place, piece).astype(BF)
-            section += 1
+    for section, value in enumerate((gq, gk, gv, gkf, gvf)):
+        halves = jnp.concatenate([value[:, 0:HALF], value[:, HALF:]], 0).astype(BF)
+        both = nt(place, halves).astype(BF)
+        turned[2 * section] = both[:, 0:TOK]
+        turned[2 * section + 1] = both[:, TOK:]
     for turn, ref in enumerate((x0, x1, x2, x3)):
         first = pl.multiple_of(((seq + turn) & 3) * SUB, 16)
         for section in range(SECTIONS):
@@ -298,7 +307,7 @@
 
 
 def product_kernel(
-    x0, x1, x2, x3, n0, n1, n2, n3, wait_ref, whole_ref, tail_ref, got, left, right
+    x0, x2, x1, x3, n0, n1, n3, n2, wait_ref, whole_ref, tail_ref, got, left, right
 ):
     seq = lax.axis_index("seq")
     for turn, (x_ref, n_ref) in enumerate(zip((x0, x1, x2, x3), (n0, n1, n2, n3))):
@@ -491,8 +500,9 @@
 ]
 
 
-def swap(arrays, axis, turns):
-    return [arrays[0]] + [lax.ppermute(arrays[t], axis, turns[t]) for t in range(1, len(arrays))]
+def swap(arrays, axis, turns, order=(1, 2, 3)):
+    got = {t: lax.ppermute(arrays[t], axis, turns[t]) for t in order}
+    return [arrays[0], got[1], got[2], got[3]]
 
 
 def per_device(embeddings, tile_counts, masked_tiles, w_in, norm_gain, w_qkv, w_out):
@@ -513,8 +523,8 @@
         [HBM] * 5,
         60,
     )
-    fars = swap([dilated] * N_SEQ, "seq", SEQ_TURNS)
-    norms = swap([normed] * N_SEQ, "seq", SEQ_TURNS)
+    fars = swap([dilated] * N_SEQ, "seq", SEQ_TURNS, (2, 1, 3))
+    norms = swap([normed] * N_SEQ, "seq", SEQ_TURNS, (1, 3, 2))
     fk, fv, pnear, pfar, attended, tiles, flag = call(
         forward_kernel,
         [
@@ -526,10 +536,10 @@
             shape(TOK, 2 * D),
             shape(TOK, TOK, dtype=F32),
         ],
-        (tile_counts.reshape(1, 1), *fars, projected, embeddings, masked_tiles),
+        (tile_counts.reshape(1, 1), fars[2], fars[1], fars[3], projected, embeddings, masked_tiles),
         [pltpu.VMEM((TOK, D), F32)],
         2.0,
-        [VMEM] * 8,
+        [VMEM] * 7,
     )
     grad_attended, loss, out_mine, out_other = call(
         functools.partial(chain_kernel, inv_count),
@@ -547,14 +557,16 @@
         8.0,
     )
     got = swap(sent, "seq", SEQ_TURNS)
-    out = call(out_core_kernel, [shape(SUB, D)] * NY, (out_mine, out_other, sent[0], *norms[1:]), unread=4)
+    out = call(out_core_kernel, [shape(SUB, D)] * NY, (out_mine, out_other, sent[0], norms[1], norms[3], norms[2]), unread=4)
     out = swap(out, "slide", Y_TURNS)
-    out_sums = call(out_y_kernel, [shape(32, D)] * N_SEQ, (*out, out_pad_order()))
+    out_sums = call(
+        out_y_kernel, [shape(32, D)] * N_SEQ, (out[0], out[2], out[1], out[3], out_pad_order())
+    )
     out = swap(out_sums, "seq", SEQ_TURNS)
     whole, tail = call(
         product_kernel,
         [shape(6 * SUB, D), shape(YROWS, D, dtype=F32)],
-        (*got, *norms, out_sums[0]),
+        (got[0], got[2], got[1], got[3], norms[0], norms[1], norms[3], norms[2], out_sums[0]),
         [
             pltpu.VMEM((N_SEQ, XROWS, TOK), BF),
             pltpu.VMEM((6 * SUB, N_SEQ * TOK), BF),
@@ -572,7 +584,11 @@
     other = lax.ppermute(other, "slide", CORE_PAIRS)
     by_y = call(core_kernel, [shape(YROWS, D)] * NY, (mine, other))
     by_y = swap(by_y, "slide", Y_TURNS)
-    (by_z,) = call(y_kernel, [shape(NZ, 16, D)], (*by_y, *out, pad_order()))
+    (by_z,) = call(
+        y_kernel,
+        [shape(NZ, 16, D)],
+        (by_y[0], by_y[2], by_y[1], by_y[3], *out, pad_order()),
+    )
     by_z = lax.all_to_all(by_z, "slide", 0, 0, tiled=True, axis_index_groups=Z_GROUPS)
     gradients, loss = call(z_kernel, [shape(12, D, dtype=F32), shape(1, 1, dtype=F32)], (by_z,))
     return (gradients, loss[0, 0])

time: 81.8 us -> 81.4 us (level)
  waiting for transfers between devices: 20 us -> 13.4 us
  starting transfers between devices: 25.2 us -> 30.7 us
  blocking collectives: 16.8 us -> 18.3 us
  local copies, waits for them, and re-layouts: 2.21 us -> 1.31 us
    ppermute x18, waiting for transfers between devices: 18.2 us -> 11.6 us  [swap(): got = {t: lax.ppermute(arrays[t], axis, turns[t]) for t in order}]
    ppermute x18, starting transfers between devices: 24.8 us -> 30.3 us  [swap(): got = {t: lax.ppermute(arrays[t], axis, turns[t]) for t in order}]
    all_to_all x1, blocking collectives: 16.8 us -> 18.3 us  [per_device(): lax.all_to_all(by_z, 'slide', 0, 0, tiled=True, axis_index_groups=Z_GROUPS)]
    unnamed x28 -> x26, local copies, waits for them, and re-layouts: 2.21 us -> 1.31 us
  transfers between devices with their start and end apart: 20 -> 20, of which waited for: 8 -> 9; matrix products, arithmetic and copies ran while one was open for 0% -> 0% of each run, Pallas kernels for 11% -> 11%
where the time goes in v10:
time: 81.4 us; the launch traced here: 80.9 us
  starting transfers between devices  30.7 us (38%)
  blocking collectives  18.3 us (22%)
  Pallas kernels  15.7 us (19%)
  waiting for transfers between devices  13.4 us (16%)
  between operations  1.52 us (2%)
  local copies, waits for them, and re-layouts  1.31 us (2%)
    ppermute x18, starting transfers between devices, swap(): got = {t: lax.ppermute(arrays[t], axis, turns[t]) for t in order}  30.3 us
    all_to_all x1, blocking collectives, per_device(): lax.all_to_all(by_z, 'slide', 0, 0, tiled=True, axis_index_groups=Z_GROUPS)  18.3 us
    pallas_call x11, Pallas kernels, call(): pl.pallas_call(kernel, out_shape=out_shapes, in_specs=specs, out_specs=[V...  15.7 us
    ppermute x18, waiting for transfers between devices, swap(): got = {t: lax.ppermute(arrays[t], axis, turns[t]) for t in order}  11.6 us
    ppermute x1, waiting for transfers between devices, per_device(): other = lax.ppermute(other, 'slide', CORE_PAIRS)  1.85 us
  transfers between devices with their start and end apart: 20, of which 9 were waited for; matrix products, arithmetic and copies ran while one was open for 0% of the time, Pallas kernels for 11%

profile of v10, /device:TPU:2, one launch (start us, length us, event | category | flops | bytes accessed | tf_op | source)
XLA Modules:
  0.0 80.9 jit_solution(781164946019455450)
XLA Ops:
  0.7 4.5 %shard_map.131 = (bf16[128,768]{1,0:T(8,128)(2,1)}, bf16[128,768]{1,0:T(8,128)(2,1)}, bf16[128,2304]{1,0:T(8,128)(2,1)}, bf16[32,1536]{1,0:T(8,128)(2,1)}) custom-call(bf16[1,128,1536]{2,1,0:T(8,128)(2,1)} %tiles_ref.1, s32[1,128]{1,0:T(1,128)} %masked_ref.1, f32[768]{0:T(1024)} %gain_hbm.1, bf16[1536,768]{1,0:T(8,128)(2,1)} %w_in_ref.1, ...), custom_call_target="tpu_custom_call" | custom-call | flops 4000000000 | bytes 4000000 | tf_op jit(solution)/shard_map/pallas_call | solution.py:468
  5.1 2.2 %collective-permute-start = (bf16[32,1536]{1,0:T(8,128)(2,1)}, bf16[32,1536]{1,0:T(8,128)(2,1)S(1)}, u32[]{:S(2)}, u32[]{:S(2)}) collective-permute-start(bf16[32,1536]{1,0:T(8,128)(2,1)} %get-tuple-element.40), channel_id=1, source_target_pairs={{0,2},{1,3},{2,0},{3,1},{4,6},{5,7},{6,4},{7,5},{8,10},{9,11},{10,... | collective-permute-start | bytes 294920 | tf_op jit(solution)/shard_map/ppermute | solution.py:504
  7.3 1.6 %collective-permute-start.1 = (bf16[32,1536]{1,0:T(8,128)(2,1)}, bf16[32,1536]{1,0:T(8,128)(2,1)S(1)}, u32[]{:S(2)}, u32[]{:S(2)}) collective-permute-start(bf16[32,1536]{1,0:T(8,128)(2,1)} %get-tuple-element.40), channel_id=1, source_target_pairs={{0,1},{1,2},{2,3},{3,0},{4,5},{5,6},{6,7},{7,4},{8,9},{9,10},{10,1... | collective-permute-start | bytes 294920 | tf_op jit(solution)/shard_map/ppermute | solution.py:504
  8.9 0.4 collective-permute-start.2
  9.4 1.6 %collective-permute-start.6 = (bf16[128,768]{1,0:T(8,128)(2,1)}, bf16[128,768]{1,0:T(8,128)(2,1)S(1)}, u32[]{:S(2)}, u32[]{:S(2)}) collective-permute-start(bf16[128,768]{1,0:T(8,128)(2,1)} %get-tuple-element.55.n0), channel_id=1, source_target_pairs={{0,1},{1,2},{2,3},{3,0},{4,5},{5,6},{6,7},{7,4},{8,9},{9,10},{10,1... | collective-permute-start | bytes 589832 | tf_op jit(solution)/shard_map/ppermute | solution.py:504
  11.0 1.0 %collective-permute-start.7 = (bf16[128,768]{1,0:T(8,128)(2,1)}, bf16[128,768]{1,0:T(8,128)(2,1)S(1)}, u32[]{:S(2)}, u32[]{:S(2)}) collective-permute-start(bf16[128,768]{1,0:T(8,128)(2,1)} %get-tuple-element.55.n0), channel_id=1, source_target_pairs={{0,3},{1,0},{2,1},{3,2},{4,7},{5,4},{6,5},{7,6},{8,11},{9,8},{10,9... | collective-permute-start | bytes 589832 | tf_op jit(solution)/shard_map/ppermute | solution.py:504
  12.7 0.0 collective-permute-done.f2
  12.7 2.2 %collective-permute-start.8 = (bf16[128,768]{1,0:T(8,128)(2,1)}, bf16[128,768]{1,0:T(8,128)(2,1)S(1)}, u32[]{:S(2)}, u32[]{:S(2)}) collective-permute-start(bf16[128,768]{1,0:T(8,128)(2,1)} %get-tuple-element.55.n0), channel_id=1, source_target_pairs={{0,2},{1,3},{2,0},{3,1},{4,6},{5,7},{6,4},{7,5},{8,10},{9,11},{10,... | collective-permute-start | bytes 589832 | tf_op jit(solution)/shard_map/ppermute | solution.py:504
  14.8 0.0 collective-permute-done.1.f1
  14.8 0.1 collective-permute-done.2.f3
  14.9 1.1 %copy-done.10 = bf16[128,2304]{1,0:T(8,128)(2,1)S(1)} copy-done((bf16[128,2304]{1,0:T(8,128)(2,1)S(1)}, bf16[128,2304]{1,0:T(8,128)(2,1)}, u32[]{:S(2)}) %copy-start.10) | copy-done | bytes 589848
  16.0 2.1 %shard_map.132 = (bf16[128,768]{1,0:T(8,128)(2,1)S(1)}, bf16[128,768]{1,0:T(8,128)(2,1)S(1)}, f32[4,128,512]{2,1,0:T(8,128)S(1)}, f32[4,128,128]{2,1,0:T(8,128)S...) custom-call(s32[1,1]{1,0:T(1,128)} %bitcast.2.count_ref, ...), custom_call_target="tpu_custom_call" | custom-call | flops 2000000000 | bytes 2000000 | tf_op jit(solution)/shard_map/pallas_call | solution.py:468
  18.1 0.2 copy-done.5
  18.3 0.0 copy-done.12
  18.3 2.7 %shard_map.133 = (bf16[128,768]{1,0:T(8,128)(2,1)S(1)}, bf16[16,128]{1,0:T(8,128)(2,1)S(1)}, bf16[384,768]{1,0:T(8,128)(2,1)S(1)}, bf16[384,768]{1,0:T(8,128)(2,1)S(1)}) custom-call(bf16[128,768]{1,0:T(8,128)(2,1)S(1)} %get-tuple-element.45.att_ref, bf16[128,768]{1,0:T(8,128)(2,1)S(1)} %copy-done.12, bf16[128,1536]{1,0:T(8,128)(2,1)S(1)} %get-tuple-element.47.tiles_ref, ...), custom_call_target="tpu_custom_call" | custom-call | flops 3000000000 | bytes 3000000 | tf_op jit(solution)/shard_map/pallas_call | solution.py:468
  21.0 0.3 collective-permute-start.9
  21.3 2.9 %shard_map.134 = (bf16[976,128]{1,0:T(8,128)(2,1)S(1)}, bf16[976,128]{1,0:T(8,128)(2,1)S(1)}, bf16[976,128]{1,0:T(8,128)(2,1)S(1)}, bf16[976,128]{1,0:T(8,128)(2,1)S(1)}) custom-call(bf16[128,2304]{1,0:T(8,128)(2,1)S(1)} %copy-done.11, bf16[128,768]{1,0:T(8,128)(2,1)S(1)} %get-tuple-element.41.fk_ref, bf16[128,768]{1,0:T(8,128)(2,1)S(1)} %get-tuple-element.42.fv_ref, ...), custom_call_target="tpu_custom_call" | custom-call | flops 8000000000 | bytes 8000000 | tf_op jit(solution)/shard_map/pallas_call | solution.py:468
  24.2 0.0 copy-start.8
  24.2 0.0 collective-permute-done.8.wait3.n2
  24.3 0.2 shard_map.135
  24.4 3.2 %collective-permute-start.10 = (bf16[96,768]{1,0:T(8,128)(2,1)S(1)}, bf16[96,768]{1,0:T(8,128)(2,1)S(1)}, u32[]{:S(2)}, u32[]{:S(2)}) collective-permute-start(bf16[96,768]{1,0:T(8,128)(2,1)S(1)} %get-tuple-element.59), channel_id=1, source_target_pairs={{0,16},{4,20},{8,24},{12,28},{16,0},{20,4},{24,8},{28,12},{32,48},... | collective-permute-start | bytes 442376 | tf_op jit(solution)/shard_map/ppermute | solution.py:504
  27.7 2.1 %collective-permute-start.3 = (bf16[976,128]{1,0:T(8,128)(2,1)S(1)}, bf16[976,128]{1,0:T(8,128)(2,1)S(1)}, u32[]{:S(2)}, u32[]{:S(2)}) collective-permute-start(bf16[976,128]{1,0:T(8,128)(2,1)S(1)} %get-tuple-element.52), channel_id=1, source_target_pairs={{0,2},{1,3},{2,0},{3,1},{4,6},{5,7},{6,4},{7,5},{8,10},{9,11},{10,... | collective-permute-start | bytes 749576 | tf_op jit(solution)/shard_map/ppermute | solution.py:504
  29.8 0.7 collective-permute-start.4
  30.5 1.9 %collective-permute-start.5 = (bf16[976,128]{1,0:T(8,128)(2,1)S(1)}, bf16[976,128]{1,0:T(8,128)(2,1)S(1)}, u32[]{:S(2)}, u32[]{:S(2)}) collective-permute-start(bf16[976,128]{1,0:T(8,128)(2,1)S(1)} %get-tuple-element.54), channel_id=1, source_target_pairs={{0,3},{1,0},{2,1},{3,2},{4,7},{5,4},{6,5},{7,6},{8,11},{9,8},{10,9... | collective-permute-start | bytes 749576 | tf_op jit(solution)/shard_map/ppermute | solution.py:504
  32.4 0.7 collective-permute-start.11
  33.1 2.6 %collective-permute-start.12 = (bf16[96,768]{1,0:T(8,128)(2,1)S(1)}, bf16[96,768]{1,0:T(8,128)(2,1)S(1)}, u32[]{:S(2)}, u32[]{:S(2)}) collective-permute-start(bf16[96,768]{1,0:T(8,128)(2,1)S(1)} %get-tuple-element.61), channel_id=1, source_target_pairs={{0,24},{4,28},{8,0},{12,4},{16,8},{20,12},{24,16},{28,20},{32,56},... | collective-permute-start | bytes 442376 | tf_op jit(solution)/shard_map/ppermute | solution.py:504
  35.6 3.4 %collective-permute-done.11.y2 = bf16[96,768]{1,0:T(8,128)(2,1)S(1)} collective-permute-done((bf16[96,768]{1,0:T(8,128)(2,1)S(1)}, bf16[96,768]{1,0:T(8,128)(2,1)S(1)}, u32[]{:S(2)}, u32[]{:S(2)}) %collective-permute-start.11) | collective-permute-done | bytes 147488 | tf_op jit(solution)/shard_map/ppermute | solution.py:504
  39.0 0.3 shard_map.136
  39.2 1.9 %collective-permute-start.13 = (bf16[32,768]{1,0:T(8,128)(2,1)S(1)}, bf16[32,768]{1,0:T(8,128)(2,1)S(1)}, u32[]{:S(2)}, u32[]{:S(2)}) collective-permute-start(bf16[32,768]{1,0:T(8,128)(2,1)S(1)} %get-tuple-element.65), channel_id=1, source_target_pairs={{0,1},{1,2},{2,3},{3,0},{4,5},{5,6},{6,7},{7,4},{8,9},{9,10},{10,1... | collective-permute-start | bytes 147464 | tf_op jit(solution)/shard_map/ppermute | solution.py:504
  41.2 3.2 %collective-permute-start.14 = (bf16[32,768]{1,0:T(8,128)(2,1)S(1)}, bf16[32,768]{1,0:T(8,128)(2,1)S(1)}, u32[]{:S(2)}, u32[]{:S(2)}) collective-permute-start(bf16[32,768]{1,0:T(8,128)(2,1)S(1)} %get-tuple-element.66), channel_id=1, source_target_pairs={{0,2},{1,3},{2,0},{3,1},{4,6},{5,7},{6,4},{7,5},{8,10},{9,11},{10,... | collective-permute-start | bytes 147464 | tf_op jit(solution)/shard_map/ppermute | solution.py:504
  44.4 0.2 collective-permute-done.4.x1
  44.6 1.1 %shard_map.137 = (bf16[576,768]{1,0:T(8,128)(2,1)S(1)}, f32[80,768]{1,0:T(8,128)S(1)}) custom-call(bf16[976,128]{1,0:T(8,128)(2,1)S(1)} %get-tuple-element.51.wait0.x0, bf16[976,128]{1,0:T(8,128)(2,1)S(1)} %collective-permute-done.3.x2, bf16[976,128]{1,0:T(8,128)(2,1)S(1)} %collective-permute-done.4.x1, bf16[976,128]{1,0:T(8,128)(2,1)S(1)} %collective-permute-done.5.x3, ...), custom_call_target="tpu_custom_call" | custom-call | flops 15000000512 | bytes 15000000 | tf_op jit(solution)/shard_map/pallas_call | solution.py:468
  45.8 1.0 %collective-permute-done.14.wait2.o2 = bf16[32,768]{1,0:T(8,128)(2,1)S(1)} collective-permute-done((bf16[32,768]{1,0:T(8,128)(2,1)S(1)}, bf16[32,768]{1,0:T(8,128)(2,1)S(1)}, u32[]{:S(2)}, u32[]{:S(2)}) %collective-permute-start.14) | collective-permute-done | bytes 49184 | tf_op jit(solution)/shard_map/ppermute | solution.py:504
  46.8 1.7 %collective-permute-done.15.wait3.o3 = bf16[32,768]{1,0:T(8,128)(2,1)S(1)} collective-permute-done((bf16[32,768]{1,0:T(8,128)(2,1)S(1)}, bf16[32,768]{1,0:T(8,128)(2,1)S(1)}, u32[]{:S(2)}, u32[]{:S(2)}) %collective-permute-start.15) | collective-permute-done | bytes 49184 | tf_op jit(solution)/shard_map/ppermute | solution.py:504
  48.5 0.9 %shard_map.138 = (bf16[320,768]{1,0:T(8,128)(2,1)S(1)}, bf16[320,768]{1,0:T(8,128)(2,1)S(1)}) custom-call(bf16[576,768]{1,0:T(8,128)(2,1)S(1)} %get-tuple-element.63.whole_ref, f32[80,768]{1,0:T(8,128)S(1)} %get-tuple-element.64.tail_ref, bf16[640,576]{1,0:T(8,128)(2,1)S(1)} %copy-done.6, bf16[32,768]{1,0:T(8,128)(2,1)S(1)} %collective-permute-done.13.wait1.o1, ...), custom_call_target="tpu_custom_call" | custom-call | flops 1000000000 | bytes 1000000 | tf_op jit(solution)/shard_map/pallas_call | solution.py:468
  49.4 0.0 copy-start.9
  49.4 0.1 collective-permute-start.16
  49.5 1.9 %collective-permute-done.16.other_ref = bf16[320,768]{1,0:T(8,128)(2,1)S(1)} collective-permute-done((bf16[320,768]{1,0:T(8,128)(2,1)S(1)}, bf16[320,768]{1,0:T(8,128)(2,1)S(1)}, u32[]{:S(2)}, u32[]{:S(2)}) %collective-permute-start.16) | collective-permute-done | bytes 491552 | tf_op jit(solution)/shard_map/ppermute | solution.py:584
  51.4 0.2 shard_map.139
  51.6 1.7 %collective-permute-start.17 = (bf16[80,768]{1,0:T(8,128)(2,1)S(1)}, bf16[80,768]{1,0:T(8,128)(2,1)S(1)}, u32[]{:S(2)}, u32[]{:S(2)}) collective-permute-start(bf16[80,768]{1,0:T(8,128)(2,1)S(1)} %get-tuple-element.71), channel_id=1, source_target_pairs={{0,16},{4,20},{8,24},{12,28},{16,0},{20,4},{24,8},{28,12},{32,48},... | collective-permute-start | bytes 368648 | tf_op jit(solution)/shard_map/ppermute | solution.py:504
  53.3 2.5 %collective-permute-start.18 = (bf16[80,768]{1,0:T(8,128)(2,1)S(1)}, bf16[80,768]{1,0:T(8,128)(2,1)S(1)}, u32[]{:S(2)}, u32[]{:S(2)}) collective-permute-start(bf16[80,768]{1,0:T(8,128)(2,1)S(1)} %get-tuple-element.72), channel_id=1, source_target_pairs={{0,8},{4,12},{8,16},{12,20},{16,24},{20,28},{24,0},{28,4},{32,40},... | collective-permute-start | bytes 368648 | tf_op jit(solution)/shard_map/ppermute | solution.py:504
  55.7 0.8 collective-permute-start.19
  56.5 2.8 %collective-permute-done.17.y1 = bf16[80,768]{1,0:T(8,128)(2,1)S(1)} collective-permute-done((bf16[80,768]{1,0:T(8,128)(2,1)S(1)}, bf16[80,768]{1,0:T(8,128)(2,1)S(1)}, u32[]{:S(2)}, u32[]{:S(2)}) %collective-permute-start.17) | collective-permute-done | bytes 122912 | tf_op jit(solution)/shard_map/ppermute | solution.py:504
  59.3 1.8 %collective-permute-done.18.y2 = bf16[80,768]{1,0:T(8,128)(2,1)S(1)} collective-permute-done((bf16[80,768]{1,0:T(8,128)(2,1)S(1)}, bf16[80,768]{1,0:T(8,128)(2,1)S(1)}, u32[]{:S(2)}, u32[]{:S(2)}) %collective-permute-start.18) | collective-permute-done | bytes 122912 | tf_op jit(solution)/shard_map/ppermute | solution.py:504
  61.1 0.6 collective-permute-done.19.y3
  61.7 0.3 shard_map.140
  62.0 18.3 %all_to_all.5.in_ref = bf16[8,16,768]{2,1,0:T(8,128)(2,1)S(1)} all-to-all(bf16[8,16,768]{2,1,0:T(8,128)(2,1)S(1)} %shard_map.140), channel_id=1, replica_groups={{0,32,64,96,128,160,192,224},{4,36,68,100,132,164,196,228},{8,40,72,104..., dimensions={0} | all-to-all | bytes 393216 | tf_op jit(solution)/shard_map/all_to_all | solution.py:592
  80.3 0.7 shard_map.141
  (30 shorter events, 0.1 us)
Async XLA Ops:
  0.6 14.3 %copy-start.2 = (bf16[1,128,1536]{2,1,0:T(8,128)(2,1)S(1)}, bf16[1,128,1536]{2,1,0:T(8,128)(2,1)}, u32[]{:S(2)}) copy-start(bf16[1,128,1536]{2,1,0:T(8,128)(2,1)} %tiles_ref.1) | copy-start | bytes 1179652
  0.6 14.2 %copy-start.4 = (s32[1,128]{1,0:T(1,128)S(1)}, s32[1,128]{1,0:T(1,128)}, u32[]{:S(2)}) copy-start(s32[1,128]{1,0:T(1,128)} %masked_ref.1) | copy-start | bytes 1540
  5.1 7.5 %collective-permute-start = (bf16[32,1536]{1,0:T(8,128)(2,1)}, bf16[32,1536]{1,0:T(8,128)(2,1)S(1)}, u32[]{:S(2)}, u32[]{:S(2)}) collective-permute-start(bf16[32,1536]{1,0:T(8,128)(2,1)} %get-tuple-element.40), channel_id=1, source_target_pairs={{0,2},{1,3},{2,0},{3,1},{4,6},{5,7},{6,4},{7,5},{8,10},{9,11},{10,... | collective-permute-start | bytes 294920 | tf_op jit(solution)/shard_map/ppermute | solution.py:504
  7.3 7.5 %collective-permute-start.1 = (bf16[32,1536]{1,0:T(8,128)(2,1)}, bf16[32,1536]{1,0:T(8,128)(2,1)S(1)}, u32[]{:S(2)}, u32[]{:S(2)}) collective-permute-start(bf16[32,1536]{1,0:T(8,128)(2,1)} %get-tuple-element.40), channel_id=1, source_target_pairs={{0,1},{1,2},{2,3},{3,0},{4,5},{5,6},{6,7},{7,4},{8,9},{9,10},{10,1... | collective-permute-start | bytes 294920 | tf_op jit(solution)/shard_map/ppermute | solution.py:504
  8.9 5.9 %collective-permute-start.2 = (bf16[32,1536]{1,0:T(8,128)(2,1)}, bf16[32,1536]{1,0:T(8,128)(2,1)S(1)}, u32[]{:S(2)}, u32[]{:S(2)}) collective-permute-start(bf16[32,1536]{1,0:T(8,128)(2,1)} %get-tuple-element.40), channel_id=1, source_target_pairs={{0,3},{1,0},{2,1},{3,2},{4,7},{5,4},{6,5},{7,6},{8,11},{9,8},{10,9... | collective-permute-start | bytes 294920 | tf_op jit(solution)/shard_map/ppermute | solution.py:504
  9.4 14.9 %collective-permute-start.6 = (bf16[128,768]{1,0:T(8,128)(2,1)}, bf16[128,768]{1,0:T(8,128)(2,1)S(1)}, u32[]{:S(2)}, u32[]{:S(2)}) collective-permute-start(bf16[128,768]{1,0:T(8,128)(2,1)} %get-tuple-element.55.n0), channel_id=1, source_target_pairs={{0,1},{1,2},{2,3},{3,0},{4,5},{5,6},{6,7},{7,4},{8,9},{9,10},{10,1... | collective-permute-start | bytes 589832 | tf_op jit(solution)/shard_map/ppermute | solution.py:504
  11.0 13.3 %collective-permute-start.7 = (bf16[128,768]{1,0:T(8,128)(2,1)}, bf16[128,768]{1,0:T(8,128)(2,1)S(1)}, u32[]{:S(2)}, u32[]{:S(2)}) collective-permute-start(bf16[128,768]{1,0:T(8,128)(2,1)} %get-tuple-element.55.n0), channel_id=1, source_target_pairs={{0,3},{1,0},{2,1},{3,2},{4,7},{5,4},{6,5},{7,6},{8,11},{9,8},{10,9... | collective-permute-start | bytes 589832 | tf_op jit(solution)/shard_map/ppermute | solution.py:504
  12.7 11.6 %collective-permute-start.8 = (bf16[128,768]{1,0:T(8,128)(2,1)}, bf16[128,768]{1,0:T(8,128)(2,1)S(1)}, u32[]{:S(2)}, u32[]{:S(2)}) collective-permute-start(bf16[128,768]{1,0:T(8,128)(2,1)} %get-tuple-element.55.n0), channel_id=1, source_target_pairs={{0,2},{1,3},{2,0},{3,1},{4,6},{5,7},{6,4},{7,5},{8,10},{9,11},{10,... | collective-permute-start | bytes 589832 | tf_op jit(solution)/shard_map/ppermute | solution.py:504
  14.9 1.1 %copy-start.10 = (bf16[128,2304]{1,0:T(8,128)(2,1)S(1)}, bf16[128,2304]{1,0:T(8,128)(2,1)}, u32[]{:S(2)}) copy-start(bf16[128,2304]{1,0:T(8,128)(2,1)} %get-tuple-element.39.proj_ref) | copy-start | bytes 1769476
  15.9 2.1 %copy-start = (bf16[1536,768]{1,0:T(8,128)(2,1)S(1)}, bf16[1536,768]{1,0:T(8,128)(2,1)}, u32[]{:S(2)}) copy-start(bf16[1536,768]{1,0:T(8,128)(2,1)} %w_in_ref.1) | copy-start | bytes 7077892
  16.0 2.1 %copy-start.1 = (bf16[768,768]{1,0:T(8,128)(2,1)S(1)}, bf16[768,768]{1,0:T(8,128)(2,1)}, u32[]{:S(2)}) copy-start(bf16[768,768]{1,0:T(8,128)(2,1)} %w_out_ref.1) | copy-start | bytes 3538948
  16.0 2.3 %copy-start.5 = (bf16[768,768]{1,0:T(8,128)(2,1)S(1)}, bf16[768,768]{1,0:T(8,128)(2,1)}, u32[]{:S(2)}) copy-start(bf16[768,768]{1,0:T(8,128)(2,1)} %constant.10.clone.order_ref) | copy-start | bytes 3538948
  16.0 2.3 %copy-start.12 = (bf16[128,768]{1,0:T(8,128)(2,1)S(1)}, bf16[128,768]{1,0:T(8,128)(2,1)}, u32[]{:S(2)}) copy-start(bf16[128,768]{1,0:T(8,128)(2,1)} %get-tuple-element.46.hidden_ref) | copy-start | bytes 589828
  18.3 3.0 %copy-start.7 = (bf16[384,384]{1,0:T(8,128)(2,1)S(1)}, bf16[384,384]{1,0:T(8,128)(2,1)}, u32[]{:S(2)}) copy-start(bf16[384,384]{1,0:T(8,128)(2,1)} %constant.11.clone.spread_ref) | copy-start | bytes 884740
  18.3 3.0 %copy-start.11 = (bf16[128,2304]{1,0:T(8,128)(2,1)S(1)}, bf16[128,2304]{1,0:T(8,128)(2,1)}, u32[]{:S(2)}) copy-start(bf16[128,2304]{1,0:T(8,128)(2,1)} %get-tuple-element.39.proj_ref) | copy-start | bytes 1769476
  21.0 3.2 %collective-permute-start.9 = (bf16[384,768]{1,0:T(8,128)(2,1)S(1)}, bf16[384,768]{1,0:T(8,128)(2,1)S(1)}, u32[]{:S(2)}, u32[]{:S(2)}) collective-permute-start(bf16[384,768]{1,0:T(8,128)(2,1)S(1)} %get-tuple-element.57), channel_id=1, source_target_pairs={{0,4},{4,0},{8,12},{12,8},{16,20},{20,16},{24,28},{28,24},{32,36},... | collective-permute-start | bytes 1769480 | tf_op jit(solution)/shard_map/ppermute | solution.py:551
  24.2 14.8 %copy-start.8 = (bf16[128,96]{1,0:T(8,128)(2,1)S(1)}, bf16[128,96]{1,0:T(8,128)(2,1)}, u32[]{:S(2)}) copy-start(bf16[128,96]{1,0:T(8,128)(2,1)} %constant.12.clone.order_ref) | copy-start | bytes 73732
  24.4 20.2 %copy-start.3 = (bf16[128,768]{1,0:T(8,128)(2,1)S(1)}, bf16[128,768]{1,0:T(8,128)(2,1)}, u32[]{:S(2)}) copy-start(bf16[128,768]{1,0:T(8,128)(2,1)} %get-tuple-element.55.n0) | copy-start | bytes 589828
  24.4 8.6 %collective-permute-start.10 = (bf16[96,768]{1,0:T(8,128)(2,1)S(1)}, bf16[96,768]{1,0:T(8,128)(2,1)S(1)}, u32[]{:S(2)}, u32[]{:S(2)}) collective-permute-start(bf16[96,768]{1,0:T(8,128)(2,1)S(1)} %get-tuple-element.59), channel_id=1, source_target_pairs={{0,16},{4,20},{8,24},{12,28},{16,0},{20,4},{24,8},{28,12},{32,48},... | collective-permute-start | bytes 442376 | tf_op jit(solution)/shard_map/ppermute | solution.py:504
  27.7 16.7 %collective-permute-start.3 = (bf16[976,128]{1,0:T(8,128)(2,1)S(1)}, bf16[976,128]{1,0:T(8,128)(2,1)S(1)}, u32[]{:S(2)}, u32[]{:S(2)}) collective-permute-start(bf16[976,128]{1,0:T(8,128)(2,1)S(1)} %get-tuple-element.52), channel_id=1, source_target_pairs={{0,2},{1,3},{2,0},{3,1},{4,6},{5,7},{6,4},{7,5},{8,10},{9,11},{10,... | collective-permute-start | bytes 749576 | tf_op jit(solution)/shard_map/ppermute | solution.py:504
  29.8 14.9 %collective-permute-start.4 = (bf16[976,128]{1,0:T(8,128)(2,1)S(1)}, bf16[976,128]{1,0:T(8,128)(2,1)S(1)}, u32[]{:S(2)}, u32[]{:S(2)}) collective-permute-start(bf16[976,128]{1,0:T(8,128)(2,1)S(1)} %get-tuple-element.53), channel_id=1, source_target_pairs={{0,1},{1,2},{2,3},{3,0},{4,5},{5,6},{6,7},{7,4},{8,9},{9,10},{10,1... | collective-permute-start | bytes 749576 | tf_op jit(solution)/shard_map/ppermute | solution.py:504
  30.5 14.2 %collective-permute-start.5 = (bf16[976,128]{1,0:T(8,128)(2,1)S(1)}, bf16[976,128]{1,0:T(8,128)(2,1)S(1)}, u32[]{:S(2)}, u32[]{:S(2)}) collective-permute-start(bf16[976,128]{1,0:T(8,128)(2,1)S(1)} %get-tuple-element.54), channel_id=1, source_target_pairs={{0,3},{1,0},{2,1},{3,2},{4,7},{5,4},{6,5},{7,6},{8,11},{9,8},{10,9... | collective-permute-start | bytes 749576 | tf_op jit(solution)/shard_map/ppermute | solution.py:504
  32.4 6.6 %collective-permute-start.11 = (bf16[96,768]{1,0:T(8,128)(2,1)S(1)}, bf16[96,768]{1,0:T(8,128)(2,1)S(1)}, u32[]{:S(2)}, u32[]{:S(2)}) collective-permute-start(bf16[96,768]{1,0:T(8,128)(2,1)S(1)} %get-tuple-element.60), channel_id=1, source_target_pairs={{0,8},{4,12},{8,16},{12,20},{16,24},{20,28},{24,0},{28,4},{32,40},... | collective-permute-start | bytes 442376 | tf_op jit(solution)/shard_map/ppermute | solution.py:504
  33.1 5.9 %collective-permute-start.12 = (bf16[96,768]{1,0:T(8,128)(2,1)S(1)}, bf16[96,768]{1,0:T(8,128)(2,1)S(1)}, u32[]{:S(2)}, u32[]{:S(2)}) collective-permute-start(bf16[96,768]{1,0:T(8,128)(2,1)S(1)} %get-tuple-element.61), channel_id=1, source_target_pairs={{0,24},{4,28},{8,0},{12,4},{16,8},{20,12},{24,16},{28,20},{32,56},... | collective-permute-start | bytes 442376 | tf_op jit(solution)/shard_map/ppermute | solution.py:504
  39.2 6.5 %collective-permute-start.13 = (bf16[32,768]{1,0:T(8,128)(2,1)S(1)}, bf16[32,768]{1,0:T(8,128)(2,1)S(1)}, u32[]{:S(2)}, u32[]{:S(2)}) collective-permute-start(bf16[32,768]{1,0:T(8,128)(2,1)S(1)} %get-tuple-element.65), channel_id=1, source_target_pairs={{0,1},{1,2},{2,3},{3,0},{4,5},{5,6},{6,7},{7,4},{8,9},{9,10},{10,1... | collective-permute-start | bytes 147464 | tf_op jit(solution)/shard_map/ppermute | solution.py:504
  41.2 5.6 %collective-permute-start.14 = (bf16[32,768]{1,0:T(8,128)(2,1)S(1)}, bf16[32,768]{1,0:T(8,128)(2,1)S(1)}, u32[]{:S(2)}, u32[]{:S(2)}) collective-permute-start(bf16[32,768]{1,0:T(8,128)(2,1)S(1)} %get-tuple-element.66), channel_id=1, source_target_pairs={{0,2},{1,3},{2,0},{3,1},{4,6},{5,7},{6,4},{7,5},{8,10},{9,11},{10,... | collective-permute-start | bytes 147464 | tf_op jit(solution)/shard_map/ppermute | solution.py:504
  44.4 4.1 %collective-permute-start.15 = (bf16[32,768]{1,0:T(8,128)(2,1)S(1)}, bf16[32,768]{1,0:T(8,128)(2,1)S(1)}, u32[]{:S(2)}, u32[]{:S(2)}) collective-permute-start(bf16[32,768]{1,0:T(8,128)(2,1)S(1)} %get-tuple-element.67), channel_id=1, source_target_pairs={{0,3},{1,0},{2,1},{3,2},{4,7},{5,4},{6,5},{7,6},{8,11},{9,8},{10,9... | collective-permute-start | bytes 147464 | tf_op jit(solution)/shard_map/ppermute | solution.py:504
  44.6 3.8 %copy-start.6 = (bf16[640,576]{1,0:T(8,128)(2,1)S(1)}, bf16[640,576]{1,0:T(8,128)(2,1)}, u32[]{:S(2)}) copy-start(bf16[640,576]{1,0:T(8,128)(2,1)} %constant.13.clone.order_ref) | copy-start | bytes 2211844
  49.4 12.3 %copy-start.9 = (bf16[96,80]{1,0:T(8,128)(2,1)S(1)}, bf16[96,80]{1,0:T(8,128)(2,1)}, u32[]{:S(2)}) copy-start(bf16[96,80]{1,0:T(8,128)(2,1)} %constant.14.clone.order_ref) | copy-start | bytes 46084
  49.4 2.0 %collective-permute-start.16 = (bf16[320,768]{1,0:T(8,128)(2,1)S(1)}, bf16[320,768]{1,0:T(8,128)(2,1)S(1)}, u32[]{:S(2)}, u32[]{:S(2)}) collective-permute-start(bf16[320,768]{1,0:T(8,128)(2,1)S(1)} %get-tuple-element.69), channel_id=1, source_target_pairs={{0,4},{4,0},{8,12},{12,8},{16,20},{20,16},{24,28},{28,24},{32,36},... | collective-permute-start | bytes 1474568 | tf_op jit(solution)/shard_map/ppermute | solution.py:584
  51.6 7.8 %collective-permute-start.17 = (bf16[80,768]{1,0:T(8,128)(2,1)S(1)}, bf16[80,768]{1,0:T(8,128)(2,1)S(1)}, u32[]{:S(2)}, u32[]{:S(2)}) collective-permute-start(bf16[80,768]{1,0:T(8,128)(2,1)S(1)} %get-tuple-element.71), channel_id=1, source_target_pairs={{0,16},{4,20},{8,24},{12,28},{16,0},{20,4},{24,8},{28,12},{32,48},... | collective-permute-start | bytes 368648 | tf_op jit(solution)/shard_map/ppermute | solution.py:504
  53.3 7.9 %collective-permute-start.18 = (bf16[80,768]{1,0:T(8,128)(2,1)S(1)}, bf16[80,768]{1,0:T(8,128)(2,1)S(1)}, u32[]{:S(2)}, u32[]{:S(2)}) collective-permute-start(bf16[80,768]{1,0:T(8,128)(2,1)S(1)} %get-tuple-element.72), channel_id=1, source_target_pairs={{0,8},{4,12},{8,16},{12,20},{16,24},{20,28},{24,0},{28,4},{32,40},... | collective-permute-start | bytes 368648 | tf_op jit(solution)/shard_map/ppermute | solution.py:504
  55.7 6.0 %collective-permute-start.19 = (bf16[80,768]{1,0:T(8,128)(2,1)S(1)}, bf16[80,768]{1,0:T(8,128)(2,1)S(1)}, u32[]{:S(2)}, u32[]{:S(2)}) collective-permute-start(bf16[80,768]{1,0:T(8,128)(2,1)S(1)} %get-tuple-element.73), channel_id=1, source_target_pairs={{0,24},{4,28},{8,0},{12,4},{16,8},{20,12},{24,16},{28,20},{32,56},... | collective-permute-start | bytes 368648 | tf_op jit(solution)/shard_map/ppermute | solution.py:504

commit v11 on v10

--- a/solution.py
+++ b/solution.py
@@ -336,7 +336,7 @@
                 for r in range(RATE):
                     total = total + jnp.where(spots[r], turns[(r - src) & 3], 0.0)
                 left[near_at : near_at + SUB, src * TOK : (src + 1) * TOK] = total.astype(BF)
-    whole_ref[...] = nn(left[...], right[...]).astype(BF)
+    whole_ref[...] = nn(left[...], right[...])
     loss = got[0, SECTIONS * SUB :].astype(F32)
     for src in range(1, N_SEQ):
         loss = loss + got[src, SECTIONS * SUB :].astype(F32)
@@ -344,15 +344,15 @@
     tail_ref[...] = split_rows(jnp.broadcast_to(loss, (YROWS, D)), (YROWS, D), 72)
 
 
-def place_kernel(whole_ref, tail_ref, order_ref, wait1, wait2, wait3, mine_ref, other_ref):
+def place_kernel(whole_ref, tail_ref, wait1, wait2, wait3, mine_ref, other_ref):
     core = lax.axis_index("slide") & 1
-    whole = whole_ref[...]
+    tail = tail_ref[72:]
     for turn, ref in enumerate((mine_ref, other_ref)):
-        first = pl.multiple_of(((core + turn) & 1) * NY * YROWS, NY * YROWS)
-        half = nn(order_ref[pl.ds(first, NY * YROWS)], whole)
+        side = ((core + turn) & 1) * 48
+        blocks = [whole_ref[pl.ds(pl.multiple_of(z * SUB + side, 16), 48)] for z in range(6)]
         for y in range(NY):
-            rows = slice(y * YROWS, (y + 1) * YROWS)
-            ref[rows] = (half[rows] + tail_ref[...]).astype(BF)
+            rows = [block[12 * y : 12 * (y + 1)] for block in blocks]
+            ref[y * YROWS : (y + 1) * YROWS] = jnp.concatenate(rows + [tail], 0).astype(BF)
 
 
 def resplit(total):
@@ -410,16 +410,6 @@
         c, rest = divmod(rest, 48)
         y, r = divmod(rest, 12)
         place[row, (y * NC + c) * HD + j * 12 + r] = 1.0
-    return jnp.asarray(place, BF)
-
-
-def product_order():
-    place = np.zeros((NC * NY * YROWS, 6 * SUB), np.float32)
-    for c in range(NC):
-        for y in range(NY):
-            for z in range(6):
-                for r in range(12):
-                    place[(c * NY + y) * YROWS + z * 12 + r, z * SUB + c * 48 + y * 12 + r] = 1.0
     return jnp.asarray(place, BF)
 
 
@@ -560,12 +550,12 @@
     out = call(out_core_kernel, [shape(SUB, D)] * NY, (out_mine, out_other, sent[0], norms[1], norms[3], norms[2]), unread=4)
     out = swap(out, "slide", Y_TURNS)
     out_sums = call(
-        out_y_kernel, [shape(32, D)] * N_SEQ, (out[0], out[2], out[1], out[3], out_pad_order())
+        out_y_kernel, [shape(32, D)] * N_SEQ, (out[0], out[2], out[1], out[3], out_pad_order()), (), 20.0
     )
     out = swap(out_sums, "seq", SEQ_TURNS)
     whole, tail = call(
         product_kernel,
-        [shape(6 * SUB, D), shape(YROWS, D, dtype=F32)],
+        [shape(6 * SUB, D, dtype=F32), shape(YROWS, D, dtype=F32)],
         (got[0], got[2], got[1], got[3], norms[0], norms[1], norms[3], norms[2], out_sums[0]),
         [
             pltpu.VMEM((N_SEQ, XROWS, TOK), BF),
@@ -578,7 +568,7 @@
     mine, other = call(
         place_kernel,
         [shape(NY * YROWS, D)] * 2,
-        (whole, tail, product_order(), *out[1:]),
+        (whole, tail, *out[1:]),
         unread=3,
     )
     other = lax.ppermute(other, "slide", CORE_PAIRS)

time: 81.4 us -> 80.2 us (0.985)
    pallas_call x11, Pallas kernels: 15.7 us -> 14.9 us  [call(): pl.pallas_call(kernel, out_shape=out_shapes, in_specs=specs, out_specs=[V...]
  transfers between devices with their start and end apart: 20 -> 20, of which waited for: 9 -> 7; matrix products, arithmetic and copies ran while one was open for 0% -> 0% of each run, Pallas kernels for 11% -> 11%
where the time goes in v11:
time: 80.2 us; the launch traced here: 80 us
  starting transfers between devices  30.6 us (38%)
  blocking collectives  18.7 us (23%)
  Pallas kernels  14.9 us (19%)
  waiting for transfers between devices  13.1 us (16%)
  between operations  1.52 us (2%)
  local copies, waits for them, and re-layouts  1.29 us (2%)
    ppermute x18, starting transfers between devices, swap(): got = {t: lax.ppermute(arrays[t], axis, turns[t]) for t in order}  30.2 us
    all_to_all x1, blocking collectives, per_device(): lax.all_to_all(by_z, 'slide', 0, 0, tiled=True, axis_index_groups=Z_GROUPS)  18.7 us
    pallas_call x11, Pallas kernels, call(): pl.pallas_call(kernel, out_shape=out_shapes, in_specs=specs, out_specs=[V...  14.9 us
    ppermute x18, waiting for transfers between devices, swap(): got = {t: lax.ppermute(arrays[t], axis, turns[t]) for t in order}  11.2 us
    ppermute x1, waiting for transfers between devices, per_device(): other = lax.ppermute(other, 'slide', CORE_PAIRS)  1.85 us
  transfers between devices with their start and end apart: 20, of which 7 were waited for; matrix products, arithmetic and copies ran while one was open for 0% of the time, Pallas kernels for 11%

profile of v11, /device:TPU:2, one launch (start us, length us, event | category | flops | bytes accessed | tf_op | source)
XLA Modules:
  0.0 80.0 jit_solution(7009657724793974727)
XLA Ops:
  0.7 4.4 %shard_map.122 = (bf16[128,768]{1,0:T(8,128)(2,1)}, bf16[128,768]{1,0:T(8,128)(2,1)}, bf16[128,2304]{1,0:T(8,128)(2,1)}, bf16[32,1536]{1,0:T(8,128)(2,1)}) custom-call(bf16[1,128,1536]{2,1,0:T(8,128)(2,1)} %tiles_ref.1, s32[1,128]{1,0:T(1,128)} %masked_ref.1, f32[768]{0:T(1024)} %gain_hbm.1, bf16[1536,768]{1,0:T(8,128)(2,1)} %w_in_ref.1, ...), custom_call_target="tpu_custom_call" | custom-call | flops 4000000000 | bytes 4000000 | tf_op jit(solution)/shard_map/pallas_call | solution.py:458
  5.1 2.2 %collective-permute-start = (bf16[32,1536]{1,0:T(8,128)(2,1)}, bf16[32,1536]{1,0:T(8,128)(2,1)S(1)}, u32[]{:S(2)}, u32[]{:S(2)}) collective-permute-start(bf16[32,1536]{1,0:T(8,128)(2,1)} %get-tuple-element.40), channel_id=1, source_target_pairs={{0,2},{1,3},{2,0},{3,1},{4,6},{5,7},{6,4},{7,5},{8,10},{9,11},{10,... | collective-permute-start | bytes 294920 | tf_op jit(solution)/shard_map/ppermute | solution.py:494
  7.3 1.6 %collective-permute-start.1 = (bf16[32,1536]{1,0:T(8,128)(2,1)}, bf16[32,1536]{1,0:T(8,128)(2,1)S(1)}, u32[]{:S(2)}, u32[]{:S(2)}) collective-permute-start(bf16[32,1536]{1,0:T(8,128)(2,1)} %get-tuple-element.40), channel_id=1, source_target_pairs={{0,1},{1,2},{2,3},{3,0},{4,5},{5,6},{6,7},{7,4},{8,9},{9,10},{10,1... | collective-permute-start | bytes 294920 | tf_op jit(solution)/shard_map/ppermute | solution.py:494
  8.9 0.4 collective-permute-start.2
  9.3 1.6 %collective-permute-start.6 = (bf16[128,768]{1,0:T(8,128)(2,1)}, bf16[128,768]{1,0:T(8,128)(2,1)S(1)}, u32[]{:S(2)}, u32[]{:S(2)}) collective-permute-start(bf16[128,768]{1,0:T(8,128)(2,1)} %get-tuple-element.55.n0), channel_id=1, source_target_pairs={{0,1},{1,2},{2,3},{3,0},{4,5},{5,6},{6,7},{7,4},{8,9},{9,10},{10,1... | collective-permute-start | bytes 589832 | tf_op jit(solution)/shard_map/ppermute | solution.py:494
  10.9 1.0 %collective-permute-start.7 = (bf16[128,768]{1,0:T(8,128)(2,1)}, bf16[128,768]{1,0:T(8,128)(2,1)S(1)}, u32[]{:S(2)}, u32[]{:S(2)}) collective-permute-start(bf16[128,768]{1,0:T(8,128)(2,1)} %get-tuple-element.55.n0), channel_id=1, source_target_pairs={{0,3},{1,0},{2,1},{3,2},{4,7},{5,4},{6,5},{7,6},{8,11},{9,8},{10,9... | collective-permute-start | bytes 589832 | tf_op jit(solution)/shard_map/ppermute | solution.py:494
  12.6 2.2 %collective-permute-start.8 = (bf16[128,768]{1,0:T(8,128)(2,1)}, bf16[128,768]{1,0:T(8,128)(2,1)S(1)}, u32[]{:S(2)}, u32[]{:S(2)}) collective-permute-start(bf16[128,768]{1,0:T(8,128)(2,1)} %get-tuple-element.55.n0), channel_id=1, source_target_pairs={{0,2},{1,3},{2,0},{3,1},{4,6},{5,7},{6,4},{7,5},{8,10},{9,11},{10,... | collective-permute-start | bytes 589832 | tf_op jit(solution)/shard_map/ppermute | solution.py:494
  14.8 0.1 collective-permute-done.2.f3
  14.9 1.1 %copy-done.9 = bf16[128,2304]{1,0:T(8,128)(2,1)S(1)} copy-done((bf16[128,2304]{1,0:T(8,128)(2,1)S(1)}, bf16[128,2304]{1,0:T(8,128)(2,1)}, u32[]{:S(2)}) %copy-start.9) | copy-done | bytes 589848
  15.9 2.1 %shard_map.123 = (bf16[128,768]{1,0:T(8,128)(2,1)S(1)}, bf16[128,768]{1,0:T(8,128)(2,1)S(1)}, f32[4,128,512]{2,1,0:T(8,128)S(1)}, f32[4,128,128]{2,1,0:T(8,128)S...) custom-call(s32[1,1]{1,0:T(1,128)} %bitcast.2.count_ref, ...), custom_call_target="tpu_custom_call" | custom-call | flops 2000000000 | bytes 2000000 | tf_op jit(solution)/shard_map/pallas_call | solution.py:458
  18.1 0.2 copy-done.5
  18.3 0.0 copy-done.11
  18.3 2.7 %shard_map.124 = (bf16[128,768]{1,0:T(8,128)(2,1)S(1)}, bf16[16,128]{1,0:T(8,128)(2,1)S(1)}, bf16[384,768]{1,0:T(8,128)(2,1)S(1)}, bf16[384,768]{1,0:T(8,128)(2,1)S(1)}) custom-call(bf16[128,768]{1,0:T(8,128)(2,1)S(1)} %get-tuple-element.45.att_ref, bf16[128,768]{1,0:T(8,128)(2,1)S(1)} %copy-done.11, bf16[128,1536]{1,0:T(8,128)(2,1)S(1)} %get-tuple-element.47.tiles_ref, ...), custom_call_target="tpu_custom_call" | custom-call | flops 3000000000 | bytes 3000000 | tf_op jit(solution)/shard_map/pallas_call | solution.py:458
  21.0 0.3 collective-permute-start.9
  21.3 2.9 %shard_map.125 = (bf16[976,128]{1,0:T(8,128)(2,1)S(1)}, bf16[976,128]{1,0:T(8,128)(2,1)S(1)}, bf16[976,128]{1,0:T(8,128)(2,1)S(1)}, bf16[976,128]{1,0:T(8,128)(2,1)S(1)}) custom-call(bf16[128,2304]{1,0:T(8,128)(2,1)S(1)} %copy-done.10, bf16[128,768]{1,0:T(8,128)(2,1)S(1)} %get-tuple-element.41.fk_ref, bf16[128,768]{1,0:T(8,128)(2,1)S(1)} %get-tuple-element.42.fv_ref, ...), custom_call_target="tpu_custom_call" | custom-call | flops 8000000000 | bytes 8000000 | tf_op jit(solution)/shard_map/pallas_call | solution.py:458
  24.2 0.0 collective-permute-done.7.wait2.n3
  24.2 0.0 collective-permute-done.8.wait3.n2
  24.2 0.0 copy-start.7
  24.2 0.2 shard_map.126
  24.4 3.2 %collective-permute-start.10 = (bf16[96,768]{1,0:T(8,128)(2,1)S(1)}, bf16[96,768]{1,0:T(8,128)(2,1)S(1)}, u32[]{:S(2)}, u32[]{:S(2)}) collective-permute-start(bf16[96,768]{1,0:T(8,128)(2,1)S(1)} %get-tuple-element.59), channel_id=1, source_target_pairs={{0,16},{4,20},{8,24},{12,28},{16,0},{20,4},{24,8},{28,12},{32,48},... | collective-permute-start | bytes 442376 | tf_op jit(solution)/shard_map/ppermute | solution.py:494
  27.6 0.7 collective-permute-start.11
  28.3 2.6 %collective-permute-start.12 = (bf16[96,768]{1,0:T(8,128)(2,1)S(1)}, bf16[96,768]{1,0:T(8,128)(2,1)S(1)}, u32[]{:S(2)}, u32[]{:S(2)}) collective-permute-start(bf16[96,768]{1,0:T(8,128)(2,1)S(1)} %get-tuple-element.61), channel_id=1, source_target_pairs={{0,24},{4,28},{8,0},{12,4},{16,8},{20,12},{24,16},{28,20},{32,56},... | collective-permute-start | bytes 442376 | tf_op jit(solution)/shard_map/ppermute | solution.py:494
  30.9 2.1 %collective-permute-start.3 = (bf16[976,128]{1,0:T(8,128)(2,1)S(1)}, bf16[976,128]{1,0:T(8,128)(2,1)S(1)}, u32[]{:S(2)}, u32[]{:S(2)}) collective-permute-start(bf16[976,128]{1,0:T(8,128)(2,1)S(1)} %get-tuple-element.52), channel_id=1, source_target_pairs={{0,2},{1,3},{2,0},{3,1},{4,6},{5,7},{6,4},{7,5},{8,10},{9,11},{10,... | collective-permute-start | bytes 749576 | tf_op jit(solution)/shard_map/ppermute | solution.py:494
  33.0 0.7 collective-permute-start.4
  33.7 0.0 collective-permute-done.10.y1
  33.7 1.9 %collective-permute-start.5 = (bf16[976,128]{1,0:T(8,128)(2,1)S(1)}, bf16[976,128]{1,0:T(8,128)(2,1)S(1)}, u32[]{:S(2)}, u32[]{:S(2)}) collective-permute-start(bf16[976,128]{1,0:T(8,128)(2,1)S(1)} %get-tuple-element.54), channel_id=1, source_target_pairs={{0,3},{1,0},{2,1},{3,2},{4,7},{5,4},{6,5},{7,6},{8,11},{9,8},{10,9... | collective-permute-start | bytes 749576 | tf_op jit(solution)/shard_map/ppermute | solution.py:494
  35.6 0.1 collective-permute-done.12.y3
  35.7 0.3 shard_map.127
  36.0 2.7 %collective-permute-start.13 = (bf16[32,768]{1,0:T(8,128)(2,1)S(1)}, bf16[32,768]{1,0:T(8,128)(2,1)S(1)}, u32[]{:S(2)}, u32[]{:S(2)}) collective-permute-start(bf16[32,768]{1,0:T(8,128)(2,1)S(1)} %get-tuple-element.65), channel_id=1, source_target_pairs={{0,1},{1,2},{2,3},{3,0},{4,5},{5,6},{6,7},{7,4},{8,9},{9,10},{10,1... | collective-permute-start | bytes 147464 | tf_op jit(solution)/shard_map/ppermute | solution.py:494
  38.7 2.6 %collective-permute-start.14 = (bf16[32,768]{1,0:T(8,128)(2,1)S(1)}, bf16[32,768]{1,0:T(8,128)(2,1)S(1)}, u32[]{:S(2)}, u32[]{:S(2)}) collective-permute-start(bf16[32,768]{1,0:T(8,128)(2,1)S(1)} %get-tuple-element.66), channel_id=1, source_target_pairs={{0,2},{1,3},{2,0},{3,1},{4,6},{5,7},{6,4},{7,5},{8,10},{9,11},{10,... | collective-permute-start | bytes 147464 | tf_op jit(solution)/shard_map/ppermute | solution.py:494
  41.2 0.1 collective-permute-done.3.x2
  41.4 1.3 %collective-permute-start.15 = (bf16[32,768]{1,0:T(8,128)(2,1)S(1)}, bf16[32,768]{1,0:T(8,128)(2,1)S(1)}, u32[]{:S(2)}, u32[]{:S(2)}) collective-permute-start(bf16[32,768]{1,0:T(8,128)(2,1)S(1)} %get-tuple-element.67), channel_id=1, source_target_pairs={{0,3},{1,0},{2,1},{3,2},{4,7},{5,4},{6,5},{7,6},{8,11},{9,8},{10,9... | collective-permute-start | bytes 147464 | tf_op jit(solution)/shard_map/ppermute | solution.py:494
  42.7 4.9 %collective-permute-done.4.x1 = bf16[976,128]{1,0:T(8,128)(2,1)S(1)} collective-permute-done((bf16[976,128]{1,0:T(8,128)(2,1)S(1)}, bf16[976,128]{1,0:T(8,128)(2,1)S(1)}, u32[]{:S(2)}, u32[]{:S(2)}) %collective-permute-start.4) | collective-permute-done | bytes 249888 | tf_op jit(solution)/shard_map/ppermute | solution.py:494
  47.6 1.1 %shard_map.128 = (f32[576,768]{1,0:T(8,128)S(1)}, f32[80,768]{1,0:T(8,128)S(1)}) custom-call(bf16[976,128]{1,0:T(8,128)(2,1)S(1)} %get-tuple-element.51.wait0.x0, bf16[976,128]{1,0:T(8,128)(2,1)S(1)} %collective-permute-done.3.x2, bf16[976,128]{1,0:T(8,128)(2,1)S(1)} %collective-permute-done.4.x1, bf16[976,128]{1,0:T(8,128)(2,1)S(1)} %collective-permute-done.5.x3, ...), custom_call_target="tpu_custom_call" | custom-call | flops 15000000512 | bytes 15000000 | tf_op jit(solution)/shard_map/pallas_call | solution.py:458
  48.7 0.0 collective-permute-done.13.wait1.o1
  48.7 0.0 collective-permute-done.14.wait2.o2
  48.7 0.1 shard_map.129
  48.9 0.1 collective-permute-start.16
  49.0 1.9 %collective-permute-done.16.other_ref = bf16[320,768]{1,0:T(8,128)(2,1)S(1)} collective-permute-done((bf16[320,768]{1,0:T(8,128)(2,1)S(1)}, bf16[320,768]{1,0:T(8,128)(2,1)S(1)}, u32[]{:S(2)}, u32[]{:S(2)}) %collective-permute-start.16) | collective-permute-done | bytes 491552 | tf_op jit(solution)/shard_map/ppermute | solution.py:574
  50.8 0.2 shard_map.130
  51.0 0.1 collective-permute-start.17
  51.1 1.1 %collective-permute-start.18 = (bf16[80,768]{1,0:T(8,128)(2,1)S(1)}, bf16[80,768]{1,0:T(8,128)(2,1)S(1)}, u32[]{:S(2)}, u32[]{:S(2)}) collective-permute-start(bf16[80,768]{1,0:T(8,128)(2,1)S(1)} %get-tuple-element.72), channel_id=1, source_target_pairs={{0,8},{4,12},{8,16},{12,20},{16,24},{20,28},{24,0},{28,4},{32,40},... | collective-permute-start | bytes 368648 | tf_op jit(solution)/shard_map/ppermute | solution.py:494
  52.2 2.2 %collective-permute-start.19 = (bf16[80,768]{1,0:T(8,128)(2,1)S(1)}, bf16[80,768]{1,0:T(8,128)(2,1)S(1)}, u32[]{:S(2)}, u32[]{:S(2)}) collective-permute-start(bf16[80,768]{1,0:T(8,128)(2,1)S(1)} %get-tuple-element.73), channel_id=1, source_target_pairs={{0,24},{4,28},{8,0},{12,4},{16,8},{20,12},{24,16},{28,20},{32,56},... | collective-permute-start | bytes 368648 | tf_op jit(solution)/shard_map/ppermute | solution.py:494
  54.4 4.4 %collective-permute-done.17.y1 = bf16[80,768]{1,0:T(8,128)(2,1)S(1)} collective-permute-done((bf16[80,768]{1,0:T(8,128)(2,1)S(1)}, bf16[80,768]{1,0:T(8,128)(2,1)S(1)}, u32[]{:S(2)}, u32[]{:S(2)}) %collective-permute-start.17) | collective-permute-done | bytes 122912 | tf_op jit(solution)/shard_map/ppermute | solution.py:494
  58.8 1.6 %collective-permute-done.18.y2 = bf16[80,768]{1,0:T(8,128)(2,1)S(1)} collective-permute-done((bf16[80,768]{1,0:T(8,128)(2,1)S(1)}, bf16[80,768]{1,0:T(8,128)(2,1)S(1)}, u32[]{:S(2)}, u32[]{:S(2)}) %collective-permute-start.18) | collective-permute-done | bytes 122912 | tf_op jit(solution)/shard_map/ppermute | solution.py:494
  60.4 0.3 shard_map.131
  60.7 18.7 %all_to_all.5.in_ref = bf16[8,16,768]{2,1,0:T(8,128)(2,1)S(1)} all-to-all(bf16[8,16,768]{2,1,0:T(8,128)(2,1)S(1)} %shard_map.131), channel_id=1, replica_groups={{0,32,64,96,128,160,192,224},{4,36,68,100,132,164,196,228},{8,40,72,104..., dimensions={0} | all-to-all | bytes 393216 | tf_op jit(solution)/shard_map/all_to_all | solution.py:582
  79.4 0.7 shard_map.132
  (28 shorter events, 0.1 us)
Async XLA Ops:
  0.6 14.2 %copy-start.2 = (bf16[1,128,1536]{2,1,0:T(8,128)(2,1)S(1)}, bf16[1,128,1536]{2,1,0:T(8,128)(2,1)}, u32[]{:S(2)}) copy-start(bf16[1,128,1536]{2,1,0:T(8,128)(2,1)} %tiles_ref.1) | copy-start | bytes 1179652
  0.6 14.2 %copy-start.4 = (s32[1,128]{1,0:T(1,128)S(1)}, s32[1,128]{1,0:T(1,128)}, u32[]{:S(2)}) copy-start(s32[1,128]{1,0:T(1,128)} %masked_ref.1) | copy-start | bytes 1540
  5.1 7.5 %collective-permute-start = (bf16[32,1536]{1,0:T(8,128)(2,1)}, bf16[32,1536]{1,0:T(8,128)(2,1)S(1)}, u32[]{:S(2)}, u32[]{:S(2)}) collective-permute-start(bf16[32,1536]{1,0:T(8,128)(2,1)} %get-tuple-element.40), channel_id=1, source_target_pairs={{0,2},{1,3},{2,0},{3,1},{4,6},{5,7},{6,4},{7,5},{8,10},{9,11},{10,... | collective-permute-start | bytes 294920 | tf_op jit(solution)/shard_map/ppermute | solution.py:494
  7.3 7.5 %collective-permute-start.1 = (bf16[32,1536]{1,0:T(8,128)(2,1)}, bf16[32,1536]{1,0:T(8,128)(2,1)S(1)}, u32[]{:S(2)}, u32[]{:S(2)}) collective-permute-start(bf16[32,1536]{1,0:T(8,128)(2,1)} %get-tuple-element.40), channel_id=1, source_target_pairs={{0,1},{1,2},{2,3},{3,0},{4,5},{5,6},{6,7},{7,4},{8,9},{9,10},{10,1... | collective-permute-start | bytes 294920 | tf_op jit(solution)/shard_map/ppermute | solution.py:494
  8.9 5.9 %collective-permute-start.2 = (bf16[32,1536]{1,0:T(8,128)(2,1)}, bf16[32,1536]{1,0:T(8,128)(2,1)S(1)}, u32[]{:S(2)}, u32[]{:S(2)}) collective-permute-start(bf16[32,1536]{1,0:T(8,128)(2,1)} %get-tuple-element.40), channel_id=1, source_target_pairs={{0,3},{1,0},{2,1},{3,2},{4,7},{5,4},{6,5},{7,6},{8,11},{9,8},{10,9... | collective-permute-start | bytes 294920 | tf_op jit(solution)/shard_map/ppermute | solution.py:494
  9.3 14.9 %collective-permute-start.6 = (bf16[128,768]{1,0:T(8,128)(2,1)}, bf16[128,768]{1,0:T(8,128)(2,1)S(1)}, u32[]{:S(2)}, u32[]{:S(2)}) collective-permute-start(bf16[128,768]{1,0:T(8,128)(2,1)} %get-tuple-element.55.n0), channel_id=1, source_target_pairs={{0,1},{1,2},{2,3},{3,0},{4,5},{5,6},{6,7},{7,4},{8,9},{9,10},{10,1... | collective-permute-start | bytes 589832 | tf_op jit(solution)/shard_map/ppermute | solution.py:494
  10.9 13.3 %collective-permute-start.7 = (bf16[128,768]{1,0:T(8,128)(2,1)}, bf16[128,768]{1,0:T(8,128)(2,1)S(1)}, u32[]{:S(2)}, u32[]{:S(2)}) collective-permute-start(bf16[128,768]{1,0:T(8,128)(2,1)} %get-tuple-element.55.n0), channel_id=1, source_target_pairs={{0,3},{1,0},{2,1},{3,2},{4,7},{5,4},{6,5},{7,6},{8,11},{9,8},{10,9... | collective-permute-start | bytes 589832 | tf_op jit(solution)/shard_map/ppermute | solution.py:494
  12.6 11.6 %collective-permute-start.8 = (bf16[128,768]{1,0:T(8,128)(2,1)}, bf16[128,768]{1,0:T(8,128)(2,1)S(1)}, u32[]{:S(2)}, u32[]{:S(2)}) collective-permute-start(bf16[128,768]{1,0:T(8,128)(2,1)} %get-tuple-element.55.n0), channel_id=1, source_target_pairs={{0,2},{1,3},{2,0},{3,1},{4,6},{5,7},{6,4},{7,5},{8,10},{9,11},{10,... | collective-permute-start | bytes 589832 | tf_op jit(solution)/shard_map/ppermute | solution.py:494
  14.9 1.1 %copy-start.9 = (bf16[128,2304]{1,0:T(8,128)(2,1)S(1)}, bf16[128,2304]{1,0:T(8,128)(2,1)}, u32[]{:S(2)}) copy-start(bf16[128,2304]{1,0:T(8,128)(2,1)} %get-tuple-element.39.proj_ref) | copy-start | bytes 1769476
  15.9 2.1 %copy-start = (bf16[1536,768]{1,0:T(8,128)(2,1)S(1)}, bf16[1536,768]{1,0:T(8,128)(2,1)}, u32[]{:S(2)}) copy-start(bf16[1536,768]{1,0:T(8,128)(2,1)} %w_in_ref.1) | copy-start | bytes 7077892
  15.9 2.1 %copy-start.1 = (bf16[768,768]{1,0:T(8,128)(2,1)S(1)}, bf16[768,768]{1,0:T(8,128)(2,1)}, u32[]{:S(2)}) copy-start(bf16[768,768]{1,0:T(8,128)(2,1)} %w_out_ref.1) | copy-start | bytes 3538948
  15.9 2.3 %copy-start.5 = (bf16[768,768]{1,0:T(8,128)(2,1)S(1)}, bf16[768,768]{1,0:T(8,128)(2,1)}, u32[]{:S(2)}) copy-start(bf16[768,768]{1,0:T(8,128)(2,1)} %constant.8.clone.order_ref) | copy-start | bytes 3538948
  15.9 2.3 %copy-start.11 = (bf16[128,768]{1,0:T(8,128)(2,1)S(1)}, bf16[128,768]{1,0:T(8,128)(2,1)}, u32[]{:S(2)}) copy-start(bf16[128,768]{1,0:T(8,128)(2,1)} %get-tuple-element.46.hidden_ref) | copy-start | bytes 589828
  18.3 3.0 %copy-start.6 = (bf16[384,384]{1,0:T(8,128)(2,1)S(1)}, bf16[384,384]{1,0:T(8,128)(2,1)}, u32[]{:S(2)}) copy-start(bf16[384,384]{1,0:T(8,128)(2,1)} %constant.9.clone.spread_ref) | copy-start | bytes 884740
  18.3 3.0 %copy-start.10 = (bf16[128,2304]{1,0:T(8,128)(2,1)S(1)}, bf16[128,2304]{1,0:T(8,128)(2,1)}, u32[]{:S(2)}) copy-start(bf16[128,2304]{1,0:T(8,128)(2,1)} %get-tuple-element.39.proj_ref) | copy-start | bytes 1769476
  21.0 3.2 %collective-permute-start.9 = (bf16[384,768]{1,0:T(8,128)(2,1)S(1)}, bf16[384,768]{1,0:T(8,128)(2,1)S(1)}, u32[]{:S(2)}, u32[]{:S(2)}) collective-permute-start(bf16[384,768]{1,0:T(8,128)(2,1)S(1)} %get-tuple-element.57), channel_id=1, source_target_pairs={{0,4},{4,0},{8,12},{12,8},{16,20},{20,16},{24,28},{28,24},{32,36},... | collective-permute-start | bytes 1769480 | tf_op jit(solution)/shard_map/ppermute | solution.py:541
  24.2 11.5 %copy-start.7 = (bf16[128,96]{1,0:T(8,128)(2,1)S(1)}, bf16[128,96]{1,0:T(8,128)(2,1)}, u32[]{:S(2)}) copy-start(bf16[128,96]{1,0:T(8,128)(2,1)} %constant.10.clone.order_ref) | copy-start | bytes 73732
  24.4 9.3 %collective-permute-start.10 = (bf16[96,768]{1,0:T(8,128)(2,1)S(1)}, bf16[96,768]{1,0:T(8,128)(2,1)S(1)}, u32[]{:S(2)}, u32[]{:S(2)}) collective-permute-start(bf16[96,768]{1,0:T(8,128)(2,1)S(1)} %get-tuple-element.59), channel_id=1, source_target_pairs={{0,16},{4,20},{8,24},{12,28},{16,0},{20,4},{24,8},{28,12},{32,48},... | collective-permute-start | bytes 442376 | tf_op jit(solution)/shard_map/ppermute | solution.py:494
  27.6 7.9 %collective-permute-start.11 = (bf16[96,768]{1,0:T(8,128)(2,1)S(1)}, bf16[96,768]{1,0:T(8,128)(2,1)S(1)}, u32[]{:S(2)}, u32[]{:S(2)}) collective-permute-start(bf16[96,768]{1,0:T(8,128)(2,1)S(1)} %get-tuple-element.60), channel_id=1, source_target_pairs={{0,8},{4,12},{8,16},{12,20},{16,24},{20,28},{24,0},{28,4},{32,40},... | collective-permute-start | bytes 442376 | tf_op jit(solution)/shard_map/ppermute | solution.py:494
  28.3 7.4 %collective-permute-start.12 = (bf16[96,768]{1,0:T(8,128)(2,1)S(1)}, bf16[96,768]{1,0:T(8,128)(2,1)S(1)}, u32[]{:S(2)}, u32[]{:S(2)}) collective-permute-start(bf16[96,768]{1,0:T(8,128)(2,1)S(1)} %get-tuple-element.61), channel_id=1, source_target_pairs={{0,24},{4,28},{8,0},{12,4},{16,8},{20,12},{24,16},{28,20},{32,56},... | collective-permute-start | bytes 442376 | tf_op jit(solution)/shard_map/ppermute | solution.py:494
  30.9 10.5 %collective-permute-start.3 = (bf16[976,128]{1,0:T(8,128)(2,1)S(1)}, bf16[976,128]{1,0:T(8,128)(2,1)S(1)}, u32[]{:S(2)}, u32[]{:S(2)}) collective-permute-start(bf16[976,128]{1,0:T(8,128)(2,1)S(1)} %get-tuple-element.52), channel_id=1, source_target_pairs={{0,2},{1,3},{2,0},{3,1},{4,6},{5,7},{6,4},{7,5},{8,10},{9,11},{10,... | collective-permute-start | bytes 749576 | tf_op jit(solution)/shard_map/ppermute | solution.py:494
  33.0 14.6 %collective-permute-start.4 = (bf16[976,128]{1,0:T(8,128)(2,1)S(1)}, bf16[976,128]{1,0:T(8,128)(2,1)S(1)}, u32[]{:S(2)}, u32[]{:S(2)}) collective-permute-start(bf16[976,128]{1,0:T(8,128)(2,1)S(1)} %get-tuple-element.53), channel_id=1, source_target_pairs={{0,1},{1,2},{2,3},{3,0},{4,5},{5,6},{6,7},{7,4},{8,9},{9,10},{10,1... | collective-permute-start | bytes 749576 | tf_op jit(solution)/shard_map/ppermute | solution.py:494
  33.7 13.9 %collective-permute-start.5 = (bf16[976,128]{1,0:T(8,128)(2,1)S(1)}, bf16[976,128]{1,0:T(8,128)(2,1)S(1)}, u32[]{:S(2)}, u32[]{:S(2)}) collective-permute-start(bf16[976,128]{1,0:T(8,128)(2,1)S(1)} %get-tuple-element.54), channel_id=1, source_target_pairs={{0,3},{1,0},{2,1},{3,2},{4,7},{5,4},{6,5},{7,6},{8,11},{9,8},{10,9... | collective-permute-start | bytes 749576 | tf_op jit(solution)/shard_map/ppermute | solution.py:494
  35.7 11.9 %copy-start.3 = (bf16[128,768]{1,0:T(8,128)(2,1)S(1)}, bf16[128,768]{1,0:T(8,128)(2,1)}, u32[]{:S(2)}) copy-start(bf16[128,768]{1,0:T(8,128)(2,1)} %get-tuple-element.55.n0) | copy-start | bytes 589828
  36.0 12.8 %collective-permute-start.13 = (bf16[32,768]{1,0:T(8,128)(2,1)S(1)}, bf16[32,768]{1,0:T(8,128)(2,1)S(1)}, u32[]{:S(2)}, u32[]{:S(2)}) collective-permute-start(bf16[32,768]{1,0:T(8,128)(2,1)S(1)} %get-tuple-element.65), channel_id=1, source_target_pairs={{0,1},{1,2},{2,3},{3,0},{4,5},{5,6},{6,7},{7,4},{8,9},{9,10},{10,1... | collective-permute-start | bytes 147464 | tf_op jit(solution)/shard_map/ppermute | solution.py:494
  38.7 10.1 %collective-permute-start.14 = (bf16[32,768]{1,0:T(8,128)(2,1)S(1)}, bf16[32,768]{1,0:T(8,128)(2,1)S(1)}, u32[]{:S(2)}, u32[]{:S(2)}) collective-permute-start(bf16[32,768]{1,0:T(8,128)(2,1)S(1)} %get-tuple-element.66), channel_id=1, source_target_pairs={{0,2},{1,3},{2,0},{3,1},{4,6},{5,7},{6,4},{7,5},{8,10},{9,11},{10,... | collective-permute-start | bytes 147464 | tf_op jit(solution)/shard_map/ppermute | solution.py:494
  41.4 7.3 %collective-permute-start.15 = (bf16[32,768]{1,0:T(8,128)(2,1)S(1)}, bf16[32,768]{1,0:T(8,128)(2,1)S(1)}, u32[]{:S(2)}, u32[]{:S(2)}) collective-permute-start(bf16[32,768]{1,0:T(8,128)(2,1)S(1)} %get-tuple-element.67), channel_id=1, source_target_pairs={{0,3},{1,0},{2,1},{3,2},{4,7},{5,4},{6,5},{7,6},{8,11},{9,8},{10,9... | collective-permute-start | bytes 147464 | tf_op jit(solution)/shard_map/ppermute | solution.py:494
  48.9 2.0 %collective-permute-start.16 = (bf16[320,768]{1,0:T(8,128)(2,1)S(1)}, bf16[320,768]{1,0:T(8,128)(2,1)S(1)}, u32[]{:S(2)}, u32[]{:S(2)}) collective-permute-start(bf16[320,768]{1,0:T(8,128)(2,1)S(1)} %get-tuple-element.69), channel_id=1, source_target_pairs={{0,4},{4,0},{8,12},{12,8},{16,20},{20,16},{24,28},{28,24},{32,36},... | collective-permute-start | bytes 1474568 | tf_op jit(solution)/shard_map/ppermute | solution.py:574
  50.8 9.6 %copy-start.8 = (bf16[96,80]{1,0:T(8,128)(2,1)S(1)}, bf16[96,80]{1,0:T(8,128)(2,1)}, u32[]{:S(2)}) copy-start(bf16[96,80]{1,0:T(8,128)(2,1)} %constant.11.clone.order_ref) | copy-start | bytes 46084
  51.0 7.8 %collective-permute-start.17 = (bf16[80,768]{1,0:T(8,128)(2,1)S(1)}, bf16[80,768]{1,0:T(8,128)(2,1)S(1)}, u32[]{:S(2)}, u32[]{:S(2)}) collective-permute-start(bf16[80,768]{1,0:T(8,128)(2,1)S(1)} %get-tuple-element.71), channel_id=1, source_target_pairs={{0,16},{4,20},{8,24},{12,28},{16,0},{20,4},{24,8},{28,12},{32,48},... | collective-permute-start | bytes 368648 | tf_op jit(solution)/shard_map/ppermute | solution.py:494
  51.1 9.3 %collective-permute-start.18 = (bf16[80,768]{1,0:T(8,128)(2,1)S(1)}, bf16[80,768]{1,0:T(8,128)(2,1)S(1)}, u32[]{:S(2)}, u32[]{:S(2)}) collective-permute-start(bf16[80,768]{1,0:T(8,128)(2,1)S(1)} %get-tuple-element.72), channel_id=1, source_target_pairs={{0,8},{4,12},{8,16},{12,20},{16,24},{20,28},{24,0},{28,4},{32,40},... | collective-permute-start | bytes 368648 | tf_op jit(solution)/shard_map/ppermute | solution.py:494
  52.2 8.2 %collective-permute-start.19 = (bf16[80,768]{1,0:T(8,128)(2,1)S(1)}, bf16[80,768]{1,0:T(8,128)(2,1)S(1)}, u32[]{:S(2)}, u32[]{:S(2)}) collective-permute-start(bf16[80,768]{1,0:T(8,128)(2,1)S(1)} %get-tuple-element.73), channel_id=1, source_target_pairs={{0,24},{4,28},{8,0},{12,4},{16,8},{20,12},{24,16},{28,20},{32,56},... | collective-permute-start | bytes 368648 | tf_op jit(solution)/shard_map/ppermute | solution.py:494

commit v12 on v11

--- a/solution.py
+++ b/solution.py
@@ -163,7 +163,7 @@
 
 
 def forward_kernel(
-    count_ref, f2, f1, f3, proj_ref, tiles_ref, masked_ref,
+    count_ref, f1, f2, f3, proj_ref, tiles_ref, masked_ref,
     fk_ref, fv_ref, pnear_ref, pfar_ref, att_ref, tiles_out, flag_ref,
     att_acc,
 ):
@@ -307,7 +307,7 @@
 
 
 def product_kernel(
-    x0, x2, x1, x3, n0, n1, n3, n2, wait_ref, whole_ref, tail_ref, got, left, right
+    x0, x1, x2, x3, n0, n1, n3, n2, wait_ref, whole_ref, tail_ref, got, left, right
 ):
     seq = lax.axis_index("seq")
     for turn, (x_ref, n_ref) in enumerate(zip((x0, x1, x2, x3), (n0, n1, n2, n3))):
@@ -526,7 +526,7 @@
             shape(TOK, 2 * D),
             shape(TOK, TOK, dtype=F32),
         ],
-        (tile_counts.reshape(1, 1), fars[2], fars[1], fars[3], projected, embeddings, masked_tiles),
+        (tile_counts.reshape(1, 1), *fars[1:], projected, embeddings, masked_tiles),
         [pltpu.VMEM((TOK, D), F32)],
         2.0,
         [VMEM] * 7,
@@ -550,13 +550,13 @@
     out = call(out_core_kernel, [shape(SUB, D)] * NY, (out_mine, out_other, sent[0], norms[1], norms[3], norms[2]), unread=4)
     out = swap(out, "slide", Y_TURNS)
     out_sums = call(
-        out_y_kernel, [shape(32, D)] * N_SEQ, (out[0], out[2], out[1], out[3], out_pad_order()), (), 20.0
+        out_y_kernel, [shape(32, D)] * N_SEQ, (*out, out_pad_order()), (), 20.0
     )
     out = swap(out_sums, "seq", SEQ_TURNS)
     whole, tail = call(
         product_kernel,
         [shape(6 * SUB, D, dtype=F32), shape(YROWS, D, dtype=F32)],
-        (got[0], got[2], got[1], got[3], norms[0], norms[1], norms[3], norms[2], out_sums[0]),
+        (*got, norms[0], norms[1], norms[3], norms[2], out_sums[0]),
         [
             pltpu.VMEM((N_SEQ, XROWS, TOK), BF),
             pltpu.VMEM((6 * SUB, N_SEQ * TOK), BF),

time: 80.2 us -> 80.4 us (level)
  starting transfers between devices: 30.6 us -> 27.4 us
  waiting for transfers between devices: 13.1 us -> 16.1 us
    ppermute x18, starting transfers between devices: 30.2 us -> 27.1 us  [swap(): got = {t: lax.ppermute(arrays[t], axis, turns[t]) for t in order}]
    ppermute x18, waiting for transfers between devices: 11.2 us -> 14.3 us  [swap(): got = {t: lax.ppermute(arrays[t], axis, turns[t]) for t in order}]
  transfers between devices with their start and end apart: 20 -> 20, of which waited for: 7 -> 8; matrix products, arithmetic and copies ran while one was open for 0% -> 0% of each run, Pallas kernels for 11% -> 11%
where the time goes in v12:
time: 80.4 us; the launch traced here: 80.1 us
  starting transfers between devices  27.4 us (34%)
  blocking collectives  18.9 us (24%)
  waiting for transfers between devices  16.1 us (20%)
  Pallas kernels  14.9 us (19%)
  between operations  1.51 us (2%)
  local copies, waits for them, and re-layouts  1.3 us (2%)
    ppermute x18, starting transfers between devices, swap(): got = {t: lax.ppermute(arrays[t], axis, turns[t]) for t in order}  27.1 us
    all_to_all x1, blocking collectives, per_device(): lax.all_to_all(by_z, 'slide', 0, 0, tiled=True, axis_index_groups=Z_GROUPS)  18.9 us
    pallas_call x11, Pallas kernels, call(): pl.pallas_call(kernel, out_shape=out_shapes, in_specs=specs, out_specs=[V...  14.9 us
    ppermute x18, waiting for transfers between devices, swap(): got = {t: lax.ppermute(arrays[t], axis, turns[t]) for t in order}  14.3 us
    ppermute x1, waiting for transfers between devices, per_device(): other = lax.ppermute(other, 'slide', CORE_PAIRS)  1.85 us
  transfers between devices with their start and end apart: 20, of which 8 were waited for; matrix products, arithmetic and copies ran while one was open for 0% of the time, Pallas kernels for 11%

profile of v12, /device:TPU:2, one launch (start us, length us, event | category | flops | bytes accessed | tf_op | source)
XLA Modules:
  0.0 80.1 jit_solution(13095700718837904616)
XLA Ops:
  0.7 4.4 %shard_map.122 = (bf16[128,768]{1,0:T(8,128)(2,1)}, bf16[128,768]{1,0:T(8,128)(2,1)}, bf16[128,2304]{1,0:T(8,128)(2,1)}, bf16[32,1536]{1,0:T(8,128)(2,1)}) custom-call(bf16[1,128,1536]{2,1,0:T(8,128)(2,1)} %tiles_ref.1, s32[1,128]{1,0:T(1,128)} %masked_ref.1, f32[768]{0:T(1024)} %gain_hbm.1, bf16[1536,768]{1,0:T(8,128)(2,1)} %w_in_ref.1, ...), custom_call_target="tpu_custom_call" | custom-call | flops 4000000000 | bytes 4000000 | tf_op jit(solution)/shard_map/pallas_call | solution.py:458
  5.1 1.6 %collective-permute-start = (bf16[32,1536]{1,0:T(8,128)(2,1)}, bf16[32,1536]{1,0:T(8,128)(2,1)S(1)}, u32[]{:S(2)}, u32[]{:S(2)}) collective-permute-start(bf16[32,1536]{1,0:T(8,128)(2,1)} %get-tuple-element.40), channel_id=1, source_target_pairs={{0,1},{1,2},{2,3},{3,0},{4,5},{5,6},{6,7},{7,4},{8,9},{9,10},{10,1... | collective-permute-start | bytes 294920 | tf_op jit(solution)/shard_map/ppermute | solution.py:494
  6.7 2.8 %collective-permute-start.1 = (bf16[32,1536]{1,0:T(8,128)(2,1)}, bf16[32,1536]{1,0:T(8,128)(2,1)S(1)}, u32[]{:S(2)}, u32[]{:S(2)}) collective-permute-start(bf16[32,1536]{1,0:T(8,128)(2,1)} %get-tuple-element.40), channel_id=1, source_target_pairs={{0,2},{1,3},{2,0},{3,1},{4,6},{5,7},{6,4},{7,5},{8,10},{9,11},{10,... | collective-permute-start | bytes 294920 | tf_op jit(solution)/shard_map/ppermute | solution.py:494
  9.5 0.4 collective-permute-start.2
  9.9 1.6 %collective-permute-start.6 = (bf16[128,768]{1,0:T(8,128)(2,1)}, bf16[128,768]{1,0:T(8,128)(2,1)S(1)}, u32[]{:S(2)}, u32[]{:S(2)}) collective-permute-start(bf16[128,768]{1,0:T(8,128)(2,1)} %get-tuple-element.55.n0), channel_id=1, source_target_pairs={{0,1},{1,2},{2,3},{3,0},{4,5},{5,6},{6,7},{7,4},{8,9},{9,10},{10,1... | collective-permute-start | bytes 589832 | tf_op jit(solution)/shard_map/ppermute | solution.py:494
  11.5 0.4 collective-permute-start.7
  12.6 0.0 collective-permute-done.f1
  12.6 1.6 %collective-permute-start.8 = (bf16[128,768]{1,0:T(8,128)(2,1)}, bf16[128,768]{1,0:T(8,128)(2,1)S(1)}, u32[]{:S(2)}, u32[]{:S(2)}) collective-permute-start(bf16[128,768]{1,0:T(8,128)(2,1)} %get-tuple-element.55.n0), channel_id=1, source_target_pairs={{0,2},{1,3},{2,0},{3,1},{4,6},{5,7},{6,4},{7,5},{8,10},{9,11},{10,... | collective-permute-start | bytes 589832 | tf_op jit(solution)/shard_map/ppermute | solution.py:494
  14.2 1.7 %collective-permute-done.2.f3 = bf16[32,1536]{1,0:T(8,128)(2,1)S(1)} collective-permute-done((bf16[32,1536]{1,0:T(8,128)(2,1)}, bf16[32,1536]{1,0:T(8,128)(2,1)S(1)}, u32[]{:S(2)}, u32[]{:S(2)}) %collective-permute-start.2) | collective-permute-done | bytes 98336 | tf_op jit(solution)/shard_map/ppermute | solution.py:494
  15.9 1.1 %copy-done.9 = bf16[128,2304]{1,0:T(8,128)(2,1)S(1)} copy-done((bf16[128,2304]{1,0:T(8,128)(2,1)S(1)}, bf16[128,2304]{1,0:T(8,128)(2,1)}, u32[]{:S(2)}) %copy-start.9) | copy-done | bytes 589848
  16.9 2.1 %shard_map.123 = (bf16[128,768]{1,0:T(8,128)(2,1)S(1)}, bf16[128,768]{1,0:T(8,128)(2,1)S(1)}, f32[4,128,512]{2,1,0:T(8,128)S(1)}, f32[4,128,128]{2,1,0:T(8,128)S...) custom-call(s32[1,1]{1,0:T(1,128)} %bitcast.2.count_ref, ...), custom_call_target="tpu_custom_call" | custom-call | flops 2000000000 | bytes 2000000 | tf_op jit(solution)/shard_map/pallas_call | solution.py:458
  19.1 0.2 copy-done.5
  19.3 0.0 copy-done.11
  19.3 2.7 %shard_map.124 = (bf16[128,768]{1,0:T(8,128)(2,1)S(1)}, bf16[16,128]{1,0:T(8,128)(2,1)S(1)}, bf16[384,768]{1,0:T(8,128)(2,1)S(1)}, bf16[384,768]{1,0:T(8,128)(2,1)S(1)}) custom-call(bf16[128,768]{1,0:T(8,128)(2,1)S(1)} %get-tuple-element.45.att_ref, bf16[128,768]{1,0:T(8,128)(2,1)S(1)} %copy-done.11, bf16[128,1536]{1,0:T(8,128)(2,1)S(1)} %get-tuple-element.47.tiles_ref, ...), custom_call_target="tpu_custom_call" | custom-call | flops 3000000000 | bytes 3000000 | tf_op jit(solution)/shard_map/pallas_call | solution.py:458
  22.0 0.3 collective-permute-start.9
  22.3 2.9 %shard_map.125 = (bf16[976,128]{1,0:T(8,128)(2,1)S(1)}, bf16[976,128]{1,0:T(8,128)(2,1)S(1)}, bf16[976,128]{1,0:T(8,128)(2,1)S(1)}, bf16[976,128]{1,0:T(8,128)(2,1)S(1)}) custom-call(bf16[128,2304]{1,0:T(8,128)(2,1)S(1)} %copy-done.10, bf16[128,768]{1,0:T(8,128)(2,1)S(1)} %get-tuple-element.41.fk_ref, bf16[128,768]{1,0:T(8,128)(2,1)S(1)} %get-tuple-element.42.fv_ref, ...), custom_call_target="tpu_custom_call" | custom-call | flops 8000000000 | bytes 8000000 | tf_op jit(solution)/shard_map/pallas_call | solution.py:458
  25.2 0.0 collective-permute-done.6.wait1.n1
  25.2 0.0 collective-permute-done.7.wait2.n3
  25.2 0.0 collective-permute-done.9.other_ref
  25.2 0.0 copy-start.7
  25.2 0.2 shard_map.126
  25.4 0.7 collective-permute-start.10
  26.1 2.9 %collective-permute-start.11 = (bf16[96,768]{1,0:T(8,128)(2,1)S(1)}, bf16[96,768]{1,0:T(8,128)(2,1)S(1)}, u32[]{:S(2)}, u32[]{:S(2)}) collective-permute-start(bf16[96,768]{1,0:T(8,128)(2,1)S(1)} %get-tuple-element.60), channel_id=1, source_target_pairs={{0,16},{4,20},{8,24},{12,28},{16,0},{20,4},{24,8},{28,12},{32,48},... | collective-permute-start | bytes 442376 | tf_op jit(solution)/shard_map/ppermute | solution.py:494
  29.0 1.3 %collective-permute-start.12 = (bf16[96,768]{1,0:T(8,128)(2,1)S(1)}, bf16[96,768]{1,0:T(8,128)(2,1)S(1)}, u32[]{:S(2)}, u32[]{:S(2)}) collective-permute-start(bf16[96,768]{1,0:T(8,128)(2,1)S(1)} %get-tuple-element.61), channel_id=1, source_target_pairs={{0,24},{4,28},{8,0},{12,4},{16,8},{20,12},{24,16},{28,20},{32,56},... | collective-permute-start | bytes 442376 | tf_op jit(solution)/shard_map/ppermute | solution.py:494
  30.4 1.9 %collective-permute-start.3 = (bf16[976,128]{1,0:T(8,128)(2,1)S(1)}, bf16[976,128]{1,0:T(8,128)(2,1)S(1)}, u32[]{:S(2)}, u32[]{:S(2)}) collective-permute-start(bf16[976,128]{1,0:T(8,128)(2,1)S(1)} %get-tuple-element.52), channel_id=1, source_target_pairs={{0,1},{1,2},{2,3},{3,0},{4,5},{5,6},{6,7},{7,4},{8,9},{9,10},{10,1... | collective-permute-start | bytes 749576 | tf_op jit(solution)/shard_map/ppermute | solution.py:494
  32.3 1.2 %collective-permute-start.4 = (bf16[976,128]{1,0:T(8,128)(2,1)S(1)}, bf16[976,128]{1,0:T(8,128)(2,1)S(1)}, u32[]{:S(2)}, u32[]{:S(2)}) collective-permute-start(bf16[976,128]{1,0:T(8,128)(2,1)S(1)} %get-tuple-element.53), channel_id=1, source_target_pairs={{0,2},{1,3},{2,0},{3,1},{4,6},{5,7},{6,4},{7,5},{8,10},{9,11},{10,... | collective-permute-start | bytes 749576 | tf_op jit(solution)/shard_map/ppermute | solution.py:494
  33.4 4.1 %collective-permute-start.5 = (bf16[976,128]{1,0:T(8,128)(2,1)S(1)}, bf16[976,128]{1,0:T(8,128)(2,1)S(1)}, u32[]{:S(2)}, u32[]{:S(2)}) collective-permute-start(bf16[976,128]{1,0:T(8,128)(2,1)S(1)} %get-tuple-element.54), channel_id=1, source_target_pairs={{0,3},{1,0},{2,1},{3,2},{4,7},{5,4},{6,5},{7,6},{8,11},{9,8},{10,9... | collective-permute-start | bytes 749576 | tf_op jit(solution)/shard_map/ppermute | solution.py:494
  37.6 0.3 shard_map.127
  37.8 0.8 %collective-permute-start.13 = (bf16[32,768]{1,0:T(8,128)(2,1)S(1)}, bf16[32,768]{1,0:T(8,128)(2,1)S(1)}, u32[]{:S(2)}, u32[]{:S(2)}) collective-permute-start(bf16[32,768]{1,0:T(8,128)(2,1)S(1)} %get-tuple-element.65), channel_id=1, source_target_pairs={{0,1},{1,2},{2,3},{3,0},{4,5},{5,6},{6,7},{7,4},{8,9},{9,10},{10,1... | collective-permute-start | bytes 147464 | tf_op jit(solution)/shard_map/ppermute | solution.py:494
  38.6 1.9 %collective-permute-start.14 = (bf16[32,768]{1,0:T(8,128)(2,1)S(1)}, bf16[32,768]{1,0:T(8,128)(2,1)S(1)}, u32[]{:S(2)}, u32[]{:S(2)}) collective-permute-start(bf16[32,768]{1,0:T(8,128)(2,1)S(1)} %get-tuple-element.66), channel_id=1, source_target_pairs={{0,2},{1,3},{2,0},{3,1},{4,6},{5,7},{6,4},{7,5},{8,10},{9,11},{10,... | collective-permute-start | bytes 147464 | tf_op jit(solution)/shard_map/ppermute | solution.py:494
  40.6 1.3 %collective-permute-done.3.x1 = bf16[976,128]{1,0:T(8,128)(2,1)S(1)} collective-permute-done((bf16[976,128]{1,0:T(8,128)(2,1)S(1)}, bf16[976,128]{1,0:T(8,128)(2,1)S(1)}, u32[]{:S(2)}, u32[]{:S(2)}) %collective-permute-start.3) | collective-permute-done | bytes 249888 | tf_op jit(solution)/shard_map/ppermute | solution.py:494
  41.9 0.9 %collective-permute-done.4.x2 = bf16[976,128]{1,0:T(8,128)(2,1)S(1)} collective-permute-done((bf16[976,128]{1,0:T(8,128)(2,1)S(1)}, bf16[976,128]{1,0:T(8,128)(2,1)S(1)}, u32[]{:S(2)}, u32[]{:S(2)}) %collective-permute-start.4) | collective-permute-done | bytes 249888 | tf_op jit(solution)/shard_map/ppermute | solution.py:494
  42.8 4.2 %collective-permute-done.5.x3 = bf16[976,128]{1,0:T(8,128)(2,1)S(1)} collective-permute-done((bf16[976,128]{1,0:T(8,128)(2,1)S(1)}, bf16[976,128]{1,0:T(8,128)(2,1)S(1)}, u32[]{:S(2)}, u32[]{:S(2)}) %collective-permute-start.5) | collective-permute-done | bytes 249888 | tf_op jit(solution)/shard_map/ppermute | solution.py:494
  47.0 1.1 %shard_map.128 = (f32[576,768]{1,0:T(8,128)S(1)}, f32[80,768]{1,0:T(8,128)S(1)}) custom-call(bf16[976,128]{1,0:T(8,128)(2,1)S(1)} %get-tuple-element.51.wait0.x0, bf16[976,128]{1,0:T(8,128)(2,1)S(1)} %collective-permute-done.3.x1, bf16[976,128]{1,0:T(8,128)(2,1)S(1)} %collective-permute-done.4.x2, bf16[976,128]{1,0:T(8,128)(2,1)S(1)} %collective-permute-done.5.x3, ...), custom_call_target="tpu_custom_call" | custom-call | flops 15000000512 | bytes 15000000 | tf_op jit(solution)/shard_map/pallas_call | solution.py:458
  48.1 0.0 collective-permute-done.14.wait2.o2
  48.1 0.5 collective-permute-done.15.wait3.o3
  48.6 0.1 shard_map.129
  48.7 0.1 collective-permute-start.16
  48.8 1.9 %collective-permute-done.16.other_ref = bf16[320,768]{1,0:T(8,128)(2,1)S(1)} collective-permute-done((bf16[320,768]{1,0:T(8,128)(2,1)S(1)}, bf16[320,768]{1,0:T(8,128)(2,1)S(1)}, u32[]{:S(2)}, u32[]{:S(2)}) %collective-permute-start.16) | collective-permute-done | bytes 491552 | tf_op jit(solution)/shard_map/ppermute | solution.py:574
  50.7 0.2 shard_map.130
  50.8 0.5 collective-permute-start.17
  51.4 0.6 collective-permute-start.18
  52.0 2.6 %collective-permute-start.19 = (bf16[80,768]{1,0:T(8,128)(2,1)S(1)}, bf16[80,768]{1,0:T(8,128)(2,1)S(1)}, u32[]{:S(2)}, u32[]{:S(2)}) collective-permute-start(bf16[80,768]{1,0:T(8,128)(2,1)S(1)} %get-tuple-element.73), channel_id=1, source_target_pairs={{0,24},{4,28},{8,0},{12,4},{16,8},{20,12},{24,16},{28,20},{32,56},... | collective-permute-start | bytes 368648 | tf_op jit(solution)/shard_map/ppermute | solution.py:494
  54.6 4.0 %collective-permute-done.17.y1 = bf16[80,768]{1,0:T(8,128)(2,1)S(1)} collective-permute-done((bf16[80,768]{1,0:T(8,128)(2,1)S(1)}, bf16[80,768]{1,0:T(8,128)(2,1)S(1)}, u32[]{:S(2)}, u32[]{:S(2)}) %collective-permute-start.17) | collective-permute-done | bytes 122912 | tf_op jit(solution)/shard_map/ppermute | solution.py:494
  58.6 1.7 %collective-permute-done.18.y2 = bf16[80,768]{1,0:T(8,128)(2,1)S(1)} collective-permute-done((bf16[80,768]{1,0:T(8,128)(2,1)S(1)}, bf16[80,768]{1,0:T(8,128)(2,1)S(1)}, u32[]{:S(2)}, u32[]{:S(2)}) %collective-permute-start.18) | collective-permute-done | bytes 122912 | tf_op jit(solution)/shard_map/ppermute | solution.py:494
  60.3 0.3 shard_map.131
  60.6 18.9 %all_to_all.5.in_ref = bf16[8,16,768]{2,1,0:T(8,128)(2,1)S(1)} all-to-all(bf16[8,16,768]{2,1,0:T(8,128)(2,1)S(1)} %shard_map.131), channel_id=1, replica_groups={{0,32,64,96,128,160,192,224},{4,36,68,100,132,164,196,228},{8,40,72,104..., dimensions={0} | all-to-all | bytes 393216 | tf_op jit(solution)/shard_map/all_to_all | solution.py:582
  79.5 0.7 shard_map.132
  (28 shorter events, 0.1 us)
Async XLA Ops:
  0.6 15.2 %copy-start.2 = (bf16[1,128,1536]{2,1,0:T(8,128)(2,1)S(1)}, bf16[1,128,1536]{2,1,0:T(8,128)(2,1)}, u32[]{:S(2)}) copy-start(bf16[1,128,1536]{2,1,0:T(8,128)(2,1)} %tiles_ref.1) | copy-start | bytes 1179652
  0.6 15.2 %copy-start.4 = (s32[1,128]{1,0:T(1,128)S(1)}, s32[1,128]{1,0:T(1,128)}, u32[]{:S(2)}) copy-start(s32[1,128]{1,0:T(1,128)} %masked_ref.1) | copy-start | bytes 1540
  5.1 7.5 %collective-permute-start = (bf16[32,1536]{1,0:T(8,128)(2,1)}, bf16[32,1536]{1,0:T(8,128)(2,1)S(1)}, u32[]{:S(2)}, u32[]{:S(2)}) collective-permute-start(bf16[32,1536]{1,0:T(8,128)(2,1)} %get-tuple-element.40), channel_id=1, source_target_pairs={{0,1},{1,2},{2,3},{3,0},{4,5},{5,6},{6,7},{7,4},{8,9},{9,10},{10,1... | collective-permute-start | bytes 294920 | tf_op jit(solution)/shard_map/ppermute | solution.py:494
  6.7 7.5 %collective-permute-start.1 = (bf16[32,1536]{1,0:T(8,128)(2,1)}, bf16[32,1536]{1,0:T(8,128)(2,1)S(1)}, u32[]{:S(2)}, u32[]{:S(2)}) collective-permute-start(bf16[32,1536]{1,0:T(8,128)(2,1)} %get-tuple-element.40), channel_id=1, source_target_pairs={{0,2},{1,3},{2,0},{3,1},{4,6},{5,7},{6,4},{7,5},{8,10},{9,11},{10,... | collective-permute-start | bytes 294920 | tf_op jit(solution)/shard_map/ppermute | solution.py:494
  9.5 6.4 %collective-permute-start.2 = (bf16[32,1536]{1,0:T(8,128)(2,1)}, bf16[32,1536]{1,0:T(8,128)(2,1)S(1)}, u32[]{:S(2)}, u32[]{:S(2)}) collective-permute-start(bf16[32,1536]{1,0:T(8,128)(2,1)} %get-tuple-element.40), channel_id=1, source_target_pairs={{0,3},{1,0},{2,1},{3,2},{4,7},{5,4},{6,5},{7,6},{8,11},{9,8},{10,9... | collective-permute-start | bytes 294920 | tf_op jit(solution)/shard_map/ppermute | solution.py:494
  9.9 15.3 %collective-permute-start.6 = (bf16[128,768]{1,0:T(8,128)(2,1)}, bf16[128,768]{1,0:T(8,128)(2,1)S(1)}, u32[]{:S(2)}, u32[]{:S(2)}) collective-permute-start(bf16[128,768]{1,0:T(8,128)(2,1)} %get-tuple-element.55.n0), channel_id=1, source_target_pairs={{0,1},{1,2},{2,3},{3,0},{4,5},{5,6},{6,7},{7,4},{8,9},{9,10},{10,1... | collective-permute-start | bytes 589832 | tf_op jit(solution)/shard_map/ppermute | solution.py:494
  11.5 13.7 %collective-permute-start.7 = (bf16[128,768]{1,0:T(8,128)(2,1)}, bf16[128,768]{1,0:T(8,128)(2,1)S(1)}, u32[]{:S(2)}, u32[]{:S(2)}) collective-permute-start(bf16[128,768]{1,0:T(8,128)(2,1)} %get-tuple-element.55.n0), channel_id=1, source_target_pairs={{0,3},{1,0},{2,1},{3,2},{4,7},{5,4},{6,5},{7,6},{8,11},{9,8},{10,9... | collective-permute-start | bytes 589832 | tf_op jit(solution)/shard_map/ppermute | solution.py:494
  12.6 12.6 %collective-permute-start.8 = (bf16[128,768]{1,0:T(8,128)(2,1)}, bf16[128,768]{1,0:T(8,128)(2,1)S(1)}, u32[]{:S(2)}, u32[]{:S(2)}) collective-permute-start(bf16[128,768]{1,0:T(8,128)(2,1)} %get-tuple-element.55.n0), channel_id=1, source_target_pairs={{0,2},{1,3},{2,0},{3,1},{4,6},{5,7},{6,4},{7,5},{8,10},{9,11},{10,... | collective-permute-start | bytes 589832 | tf_op jit(solution)/shard_map/ppermute | solution.py:494
  15.9 1.1 %copy-start.9 = (bf16[128,2304]{1,0:T(8,128)(2,1)S(1)}, bf16[128,2304]{1,0:T(8,128)(2,1)}, u32[]{:S(2)}) copy-start(bf16[128,2304]{1,0:T(8,128)(2,1)} %get-tuple-element.39.proj_ref) | copy-start | bytes 1769476
  16.9 2.1 %copy-start = (bf16[1536,768]{1,0:T(8,128)(2,1)S(1)}, bf16[1536,768]{1,0:T(8,128)(2,1)}, u32[]{:S(2)}) copy-start(bf16[1536,768]{1,0:T(8,128)(2,1)} %w_in_ref.1) | copy-start | bytes 7077892
  16.9 2.1 %copy-start.1 = (bf16[768,768]{1,0:T(8,128)(2,1)S(1)}, bf16[768,768]{1,0:T(8,128)(2,1)}, u32[]{:S(2)}) copy-start(bf16[768,768]{1,0:T(8,128)(2,1)} %w_out_ref.1) | copy-start | bytes 3538948
  16.9 2.3 %copy-start.5 = (bf16[768,768]{1,0:T(8,128)(2,1)S(1)}, bf16[768,768]{1,0:T(8,128)(2,1)}, u32[]{:S(2)}) copy-start(bf16[768,768]{1,0:T(8,128)(2,1)} %constant.8.clone.order_ref) | copy-start | bytes 3538948
  16.9 2.3 %copy-start.11 = (bf16[128,768]{1,0:T(8,128)(2,1)S(1)}, bf16[128,768]{1,0:T(8,128)(2,1)}, u32[]{:S(2)}) copy-start(bf16[128,768]{1,0:T(8,128)(2,1)} %get-tuple-element.46.hidden_ref) | copy-start | bytes 589828
  19.3 3.0 %copy-start.6 = (bf16[384,384]{1,0:T(8,128)(2,1)S(1)}, bf16[384,384]{1,0:T(8,128)(2,1)}, u32[]{:S(2)}) copy-start(bf16[384,384]{1,0:T(8,128)(2,1)} %constant.9.clone.spread_ref) | copy-start | bytes 884740
  19.3 3.0 %copy-start.10 = (bf16[128,2304]{1,0:T(8,128)(2,1)S(1)}, bf16[128,2304]{1,0:T(8,128)(2,1)}, u32[]{:S(2)}) copy-start(bf16[128,2304]{1,0:T(8,128)(2,1)} %get-tuple-element.39.proj_ref) | copy-start | bytes 1769476
  22.0 3.2 %collective-permute-start.9 = (bf16[384,768]{1,0:T(8,128)(2,1)S(1)}, bf16[384,768]{1,0:T(8,128)(2,1)S(1)}, u32[]{:S(2)}, u32[]{:S(2)}) collective-permute-start(bf16[384,768]{1,0:T(8,128)(2,1)S(1)} %get-tuple-element.57), channel_id=1, source_target_pairs={{0,4},{4,0},{8,12},{12,8},{16,20},{20,16},{24,28},{28,24},{32,36},... | collective-permute-start | bytes 1769480 | tf_op jit(solution)/shard_map/ppermute | solution.py:541
  25.2 12.3 %copy-start.7 = (bf16[128,96]{1,0:T(8,128)(2,1)S(1)}, bf16[128,96]{1,0:T(8,128)(2,1)}, u32[]{:S(2)}) copy-start(bf16[128,96]{1,0:T(8,128)(2,1)} %constant.10.clone.order_ref) | copy-start | bytes 73732
  25.4 8.0 %collective-permute-start.10 = (bf16[96,768]{1,0:T(8,128)(2,1)S(1)}, bf16[96,768]{1,0:T(8,128)(2,1)S(1)}, u32[]{:S(2)}, u32[]{:S(2)}) collective-permute-start(bf16[96,768]{1,0:T(8,128)(2,1)S(1)} %get-tuple-element.59), channel_id=1, source_target_pairs={{0,8},{4,12},{8,16},{12,20},{16,24},{20,28},{24,0},{28,4},{32,40},... | collective-permute-start | bytes 442376 | tf_op jit(solution)/shard_map/ppermute | solution.py:494
  26.1 11.4 %collective-permute-start.11 = (bf16[96,768]{1,0:T(8,128)(2,1)S(1)}, bf16[96,768]{1,0:T(8,128)(2,1)S(1)}, u32[]{:S(2)}, u32[]{:S(2)}) collective-permute-start(bf16[96,768]{1,0:T(8,128)(2,1)S(1)} %get-tuple-element.60), channel_id=1, source_target_pairs={{0,16},{4,20},{8,24},{12,28},{16,0},{20,4},{24,8},{28,12},{32,48},... | collective-permute-start | bytes 442376 | tf_op jit(solution)/shard_map/ppermute | solution.py:494
  29.0 8.5 %collective-permute-start.12 = (bf16[96,768]{1,0:T(8,128)(2,1)S(1)}, bf16[96,768]{1,0:T(8,128)(2,1)S(1)}, u32[]{:S(2)}, u32[]{:S(2)}) collective-permute-start(bf16[96,768]{1,0:T(8,128)(2,1)S(1)} %get-tuple-element.61), channel_id=1, source_target_pairs={{0,24},{4,28},{8,0},{12,4},{16,8},{20,12},{24,16},{28,20},{32,56},... | collective-permute-start | bytes 442376 | tf_op jit(solution)/shard_map/ppermute | solution.py:494
  30.4 11.5 %collective-permute-start.3 = (bf16[976,128]{1,0:T(8,128)(2,1)S(1)}, bf16[976,128]{1,0:T(8,128)(2,1)S(1)}, u32[]{:S(2)}, u32[]{:S(2)}) collective-permute-start(bf16[976,128]{1,0:T(8,128)(2,1)S(1)} %get-tuple-element.52), channel_id=1, source_target_pairs={{0,1},{1,2},{2,3},{3,0},{4,5},{5,6},{6,7},{7,4},{8,9},{9,10},{10,1... | collective-permute-start | bytes 749576 | tf_op jit(solution)/shard_map/ppermute | solution.py:494
  32.3 10.5 %collective-permute-start.4 = (bf16[976,128]{1,0:T(8,128)(2,1)S(1)}, bf16[976,128]{1,0:T(8,128)(2,1)S(1)}, u32[]{:S(2)}, u32[]{:S(2)}) collective-permute-start(bf16[976,128]{1,0:T(8,128)(2,1)S(1)} %get-tuple-element.53), channel_id=1, source_target_pairs={{0,2},{1,3},{2,0},{3,1},{4,6},{5,7},{6,4},{7,5},{8,10},{9,11},{10,... | collective-permute-start | bytes 749576 | tf_op jit(solution)/shard_map/ppermute | solution.py:494
  33.4 13.5 %collective-permute-start.5 = (bf16[976,128]{1,0:T(8,128)(2,1)S(1)}, bf16[976,128]{1,0:T(8,128)(2,1)S(1)}, u32[]{:S(2)}, u32[]{:S(2)}) collective-permute-start(bf16[976,128]{1,0:T(8,128)(2,1)S(1)} %get-tuple-element.54), channel_id=1, source_target_pairs={{0,3},{1,0},{2,1},{3,2},{4,7},{5,4},{6,5},{7,6},{8,11},{9,8},{10,9... | collective-permute-start | bytes 749576 | tf_op jit(solution)/shard_map/ppermute | solution.py:494
  37.5 9.4 %copy-start.3 = (bf16[128,768]{1,0:T(8,128)(2,1)S(1)}, bf16[128,768]{1,0:T(8,128)(2,1)}, u32[]{:S(2)}) copy-start(bf16[128,768]{1,0:T(8,128)(2,1)} %get-tuple-element.55.n0) | copy-start | bytes 589828
  37.8 10.3 %collective-permute-start.13 = (bf16[32,768]{1,0:T(8,128)(2,1)S(1)}, bf16[32,768]{1,0:T(8,128)(2,1)S(1)}, u32[]{:S(2)}, u32[]{:S(2)}) collective-permute-start(bf16[32,768]{1,0:T(8,128)(2,1)S(1)} %get-tuple-element.65), channel_id=1, source_target_pairs={{0,1},{1,2},{2,3},{3,0},{4,5},{5,6},{6,7},{7,4},{8,9},{9,10},{10,1... | collective-permute-start | bytes 147464 | tf_op jit(solution)/shard_map/ppermute | solution.py:494
  38.6 9.5 %collective-permute-start.14 = (bf16[32,768]{1,0:T(8,128)(2,1)S(1)}, bf16[32,768]{1,0:T(8,128)(2,1)S(1)}, u32[]{:S(2)}, u32[]{:S(2)}) collective-permute-start(bf16[32,768]{1,0:T(8,128)(2,1)S(1)} %get-tuple-element.66), channel_id=1, source_target_pairs={{0,2},{1,3},{2,0},{3,1},{4,6},{5,7},{6,4},{7,5},{8,10},{9,11},{10,... | collective-permute-start | bytes 147464 | tf_op jit(solution)/shard_map/ppermute | solution.py:494
  41.9 6.7 %collective-permute-start.15 = (bf16[32,768]{1,0:T(8,128)(2,1)S(1)}, bf16[32,768]{1,0:T(8,128)(2,1)S(1)}, u32[]{:S(2)}, u32[]{:S(2)}) collective-permute-start(bf16[32,768]{1,0:T(8,128)(2,1)S(1)} %get-tuple-element.67), channel_id=1, source_target_pairs={{0,3},{1,0},{2,1},{3,2},{4,7},{5,4},{6,5},{7,6},{8,11},{9,8},{10,9... | collective-permute-start | bytes 147464 | tf_op jit(solution)/shard_map/ppermute | solution.py:494
  48.7 2.0 %collective-permute-start.16 = (bf16[320,768]{1,0:T(8,128)(2,1)S(1)}, bf16[320,768]{1,0:T(8,128)(2,1)S(1)}, u32[]{:S(2)}, u32[]{:S(2)}) collective-permute-start(bf16[320,768]{1,0:T(8,128)(2,1)S(1)} %get-tuple-element.69), channel_id=1, source_target_pairs={{0,4},{4,0},{8,12},{12,8},{16,20},{20,16},{24,28},{28,24},{32,36},... | collective-permute-start | bytes 1474568 | tf_op jit(solution)/shard_map/ppermute | solution.py:574
  50.7 9.6 %copy-start.8 = (bf16[96,80]{1,0:T(8,128)(2,1)S(1)}, bf16[96,80]{1,0:T(8,128)(2,1)}, u32[]{:S(2)}) copy-start(bf16[96,80]{1,0:T(8,128)(2,1)} %constant.11.clone.order_ref) | copy-start | bytes 46084
  50.8 7.8 %collective-permute-start.17 = (bf16[80,768]{1,0:T(8,128)(2,1)S(1)}, bf16[80,768]{1,0:T(8,128)(2,1)S(1)}, u32[]{:S(2)}, u32[]{:S(2)}) collective-permute-start(bf16[80,768]{1,0:T(8,128)(2,1)S(1)} %get-tuple-element.71), channel_id=1, source_target_pairs={{0,16},{4,20},{8,24},{12,28},{16,0},{20,4},{24,8},{28,12},{32,48},... | collective-permute-start | bytes 368648 | tf_op jit(solution)/shard_map/ppermute | solution.py:494
  51.4 8.9 %collective-permute-start.18 = (bf16[80,768]{1,0:T(8,128)(2,1)S(1)}, bf16[80,768]{1,0:T(8,128)(2,1)S(1)}, u32[]{:S(2)}, u32[]{:S(2)}) collective-permute-start(bf16[80,768]{1,0:T(8,128)(2,1)S(1)} %get-tuple-element.72), channel_id=1, source_target_pairs={{0,8},{4,12},{8,16},{12,20},{16,24},{20,28},{24,0},{28,4},{32,40},... | collective-permute-start | bytes 368648 | tf_op jit(solution)/shard_map/ppermute | solution.py:494
  52.0 8.3 %collective-permute-start.19 = (bf16[80,768]{1,0:T(8,128)(2,1)S(1)}, bf16[80,768]{1,0:T(8,128)(2,1)S(1)}, u32[]{:S(2)}, u32[]{:S(2)}) collective-permute-start(bf16[80,768]{1,0:T(8,128)(2,1)S(1)} %get-tuple-element.73), channel_id=1, source_target_pairs={{0,24},{4,28},{8,0},{12,4},{16,8},{20,12},{24,16},{28,20},{32,56},... | collective-permute-start | bytes 368648 | tf_op jit(solution)/shard_map/ppermute | solution.py:494

commit v13 on v12

--- a/solution.py
+++ b/solution.py
@@ -24,7 +24,7 @@
 F32 = jnp.float32
 HALF = 384
 SUB = 96
-SECTIONS = 10
+SECTIONS = 9
 YROWS = 80
 XROWS = SECTIONS * SUB + 16
 NZ, NY, NC = 8, 4, 2
@@ -163,7 +163,7 @@
 
 
 def forward_kernel(
-    count_ref, f1, f2, f3, proj_ref, tiles_ref, masked_ref,
+    count_ref, f2, f1, f3, proj_ref, tiles_ref, masked_ref,
     fk_ref, fv_ref, pnear_ref, pfar_ref, att_ref, tiles_out, flag_ref,
     att_acc,
 ):
@@ -293,12 +293,24 @@
         gv[:, win] += nn(jnp.concatenate([p.astype(BF) for p in probs], 1), ga_stack)
         gkf[:, win] += nn(far_scores, keep(picked, q))
         gvf[:, win] += nn(far_probs.astype(BF), ga_picked)
+    own = pl.ds(pl.multiple_of(seq * FAR, FAR), FAR)
+    lane_class = (iota((FAR, D), 1) // HD) & 3
+    for near_ref, far_ref in ((gk, gkf), (gv, gvf)):
+        own_far = far_ref[own]
+        for r in range(RATE):
+            near_ref[FAR * r : FAR * (r + 1)] += jnp.where(lane_class == r, own_far, 0.0)
+    for turn, (ref, cols) in enumerate(
+        ((gkf, slice(0, HALF)), (gkf, slice(HALF, D)), (gvf, slice(0, HALF)))
+    ):
+        other = pl.ds(pl.multiple_of(((seq + turn + 1) & 3) * FAR, FAR), FAR)
+        ref[own, cols] = gvf[other, HALF:]
     place = spread_ref[...]
-    for section, value in enumerate((gq, gk, gv, gkf, gvf)):
+    for section, value in enumerate((gq, gk, gv, gkf)):
         halves = jnp.concatenate([value[:, 0:HALF], value[:, HALF:]], 0).astype(BF)
         both = nt(place, halves).astype(BF)
         turned[2 * section] = both[:, 0:TOK]
         turned[2 * section + 1] = both[:, TOK:]
+    turned[SECTIONS - 1] = nt(place, gvf[:, 0:HALF].astype(BF)).astype(BF)
     for turn, ref in enumerate((x0, x1, x2, x3)):
         first = pl.multiple_of(((seq + turn) & 3) * SUB, 16)
         for section in range(SECTIONS):
@@ -323,19 +335,27 @@
     row_y = (row - 48 * core_row) // 12
     row_class = ((row_y & 1) << 1) + core_row
     spots = [(row_class == r) & (lane_class == r) for r in range(RATE)]
-    for part in range(2):
-        for half in range(2):
-            near_at = (2 + 2 * part + half) * SUB
-            far_at = (6 + 2 * part + half) * SUB
-            far = got[0, far_at : far_at + SUB].astype(F32)
-            for src in range(1, N_SEQ):
-                far = far + got[src, far_at : far_at + SUB].astype(F32)
-            turns = [far] + [pltpu.roll(far, FAR * t, 1) for t in range(1, RATE)]
-            for src in range(N_SEQ):
-                total = got[src, near_at : near_at + SUB].astype(F32)
-                for r in range(RATE):
-                    total = total + jnp.where(spots[r], turns[(r - src) & 3], 0.0)
-                left[near_at : near_at + SUB, src * TOK : (src + 1) * TOK] = total.astype(BF)
+    fars = []
+    last = jnp.zeros(shape, F32)
+    for section in range(3):
+        rows = slice((6 + section) * SUB, (7 + section) * SUB)
+        far = jnp.zeros(shape, F32)
+        freed = jnp.zeros(shape, F32)
+        for src in range(N_SEQ):
+            piece = got[src, rows].astype(F32)
+            far = far + jnp.where(lane_class == src, 0.0, piece)
+            freed = freed + jnp.where(lane_class == src, piece, 0.0)
+        fars.append(far)
+        last = last + pltpu.roll(freed, FAR * (section + 1), 1)
+    fars.append(last)
+    for index, far in enumerate(fars):
+        near_at = (2 + index) * SUB
+        turns = [far] + [pltpu.roll(far, FAR * t, 1) for t in range(1, RATE)]
+        for src in range(N_SEQ):
+            total = got[src, near_at : near_at + SUB].astype(F32)
+            for r in range(RATE):
+                total = total + jnp.where(spots[r], turns[(r - src) & 3], 0.0)
+            left[near_at : near_at + SUB, src * TOK : (src + 1) * TOK] = total.astype(BF)
     whole_ref[...] = nn(left[...], right[...])
     loss = got[0, SECTIONS * SUB :].astype(F32)
     for src in range(1, N_SEQ):
@@ -526,7 +546,7 @@
             shape(TOK, 2 * D),
             shape(TOK, TOK, dtype=F32),
         ],
-        (tile_counts.reshape(1, 1), *fars[1:], projected, embeddings, masked_tiles),
+        (tile_counts.reshape(1, 1), fars[2], fars[1], fars[3], projected, embeddings, masked_tiles),
         [pltpu.VMEM((TOK, D), F32)],
         2.0,
         [VMEM] * 7,

time: 80.4 us -> 80.4 us (level)
  transfers between devices with their start and end apart: 20 -> 20, of which waited for: 8 -> 9; matrix products, arithmetic and copies ran while one was open for 0% -> 0% of each run, Pallas kernels for 11% -> 11%
where the time goes in v13:
time: 80.4 us; the launch traced here: 79.7 us
  starting transfers between devices  27.1 us (34%)
  blocking collectives  18.7 us (23%)
  waiting for transfers between devices  16.2 us (20%)
  Pallas kernels  14.9 us (19%)
  between operations  1.49 us (2%)
  local copies, waits for them, and re-layouts  1.29 us (2%)
    ppermute x18, starting transfers between devices, swap(): got = {t: lax.ppermute(arrays[t], axis, turns[t]) for t in order}  26.7 us
    all_to_all x1, blocking collectives, per_device(): lax.all_to_all(by_z, 'slide', 0, 0, tiled=True, axis_index_groups=Z_GROUPS)  18.7 us
    pallas_call x11, Pallas kernels, call(): pl.pallas_call(kernel, out_shape=out_shapes, in_specs=specs, out_specs=[V...  14.9 us
    ppermute x18, waiting for transfers between devices, swap(): got = {t: lax.ppermute(arrays[t], axis, turns[t]) for t in order}  14.4 us
    ppermute x1, waiting for transfers between devices, per_device(): other = lax.ppermute(other, 'slide', CORE_PAIRS)  1.85 us
  transfers between devices with their start and end apart: 20, of which 9 were waited for; matrix products, arithmetic and copies ran while one was open for 0% of the time, Pallas kernels for 11%

profile of v13, /device:TPU:2, one launch (start us, length us, event | category | flops | bytes accessed | tf_op | source)
XLA Modules:
  0.0 79.7 jit_solution(6954191300242106927)
XLA Ops:
  0.7 4.4 %shard_map.122 = (bf16[128,768]{1,0:T(8,128)(2,1)}, bf16[128,768]{1,0:T(8,128)(2,1)}, bf16[128,2304]{1,0:T(8,128)(2,1)}, bf16[32,1536]{1,0:T(8,128)(2,1)}) custom-call(bf16[1,128,1536]{2,1,0:T(8,128)(2,1)} %tiles_ref.1, s32[1,128]{1,0:T(1,128)} %masked_ref.1, f32[768]{0:T(1024)} %gain_hbm.1, bf16[1536,768]{1,0:T(8,128)(2,1)} %w_in_ref.1, ...), custom_call_target="tpu_custom_call" | custom-call | flops 4000000000 | bytes 4000000 | tf_op jit(solution)/shard_map/pallas_call | solution.py:478
  5.1 2.2 %collective-permute-start = (bf16[32,1536]{1,0:T(8,128)(2,1)}, bf16[32,1536]{1,0:T(8,128)(2,1)S(1)}, u32[]{:S(2)}, u32[]{:S(2)}) collective-permute-start(bf16[32,1536]{1,0:T(8,128)(2,1)} %get-tuple-element.40), channel_id=1, source_target_pairs={{0,2},{1,3},{2,0},{3,1},{4,6},{5,7},{6,4},{7,5},{8,10},{9,11},{10,... | collective-permute-start | bytes 294920 | tf_op jit(solution)/shard_map/ppermute | solution.py:514
  7.3 1.6 %collective-permute-start.1 = (bf16[32,1536]{1,0:T(8,128)(2,1)}, bf16[32,1536]{1,0:T(8,128)(2,1)S(1)}, u32[]{:S(2)}, u32[]{:S(2)}) collective-permute-start(bf16[32,1536]{1,0:T(8,128)(2,1)} %get-tuple-element.40), channel_id=1, source_target_pairs={{0,1},{1,2},{2,3},{3,0},{4,5},{5,6},{6,7},{7,4},{8,9},{9,10},{10,1... | collective-permute-start | bytes 294920 | tf_op jit(solution)/shard_map/ppermute | solution.py:514
  8.9 0.4 collective-permute-start.2
  9.3 1.6 %collective-permute-start.6 = (bf16[128,768]{1,0:T(8,128)(2,1)}, bf16[128,768]{1,0:T(8,128)(2,1)S(1)}, u32[]{:S(2)}, u32[]{:S(2)}) collective-permute-start(bf16[128,768]{1,0:T(8,128)(2,1)} %get-tuple-element.55.n0), channel_id=1, source_target_pairs={{0,1},{1,2},{2,3},{3,0},{4,5},{5,6},{6,7},{7,4},{8,9},{9,10},{10,1... | collective-permute-start | bytes 589832 | tf_op jit(solution)/shard_map/ppermute | solution.py:514
  10.9 1.0 %collective-permute-start.7 = (bf16[128,768]{1,0:T(8,128)(2,1)}, bf16[128,768]{1,0:T(8,128)(2,1)S(1)}, u32[]{:S(2)}, u32[]{:S(2)}) collective-permute-start(bf16[128,768]{1,0:T(8,128)(2,1)} %get-tuple-element.55.n0), channel_id=1, source_target_pairs={{0,3},{1,0},{2,1},{3,2},{4,7},{5,4},{6,5},{7,6},{8,11},{9,8},{10,9... | collective-permute-start | bytes 589832 | tf_op jit(solution)/shard_map/ppermute | solution.py:514
  12.6 2.2 %collective-permute-start.8 = (bf16[128,768]{1,0:T(8,128)(2,1)}, bf16[128,768]{1,0:T(8,128)(2,1)S(1)}, u32[]{:S(2)}, u32[]{:S(2)}) collective-permute-start(bf16[128,768]{1,0:T(8,128)(2,1)} %get-tuple-element.55.n0), channel_id=1, source_target_pairs={{0,2},{1,3},{2,0},{3,1},{4,6},{5,7},{6,4},{7,5},{8,10},{9,11},{10,... | collective-permute-start | bytes 589832 | tf_op jit(solution)/shard_map/ppermute | solution.py:514
  14.8 0.0 collective-permute-done.1.f1
  14.8 0.1 collective-permute-done.2.f3
  14.9 1.1 %copy-done.9 = bf16[128,2304]{1,0:T(8,128)(2,1)S(1)} copy-done((bf16[128,2304]{1,0:T(8,128)(2,1)S(1)}, bf16[128,2304]{1,0:T(8,128)(2,1)}, u32[]{:S(2)}) %copy-start.9) | copy-done | bytes 589848
  15.9 2.1 %shard_map.123 = (bf16[128,768]{1,0:T(8,128)(2,1)S(1)}, bf16[128,768]{1,0:T(8,128)(2,1)S(1)}, f32[4,128,512]{2,1,0:T(8,128)S(1)}, f32[4,128,128]{2,1,0:T(8,128)S...) custom-call(s32[1,1]{1,0:T(1,128)} %bitcast.2.count_ref, ...), custom_call_target="tpu_custom_call" | custom-call | flops 2000000000 | bytes 2000000 | tf_op jit(solution)/shard_map/pallas_call | solution.py:478
  18.1 0.2 copy-done.5
  18.3 0.0 copy-done.11
  18.3 2.7 %shard_map.124 = (bf16[128,768]{1,0:T(8,128)(2,1)S(1)}, bf16[16,128]{1,0:T(8,128)(2,1)S(1)}, bf16[384,768]{1,0:T(8,128)(2,1)S(1)}, bf16[384,768]{1,0:T(8,128)(2,1)S(1)}) custom-call(bf16[128,768]{1,0:T(8,128)(2,1)S(1)} %get-tuple-element.45.att_ref, bf16[128,768]{1,0:T(8,128)(2,1)S(1)} %copy-done.11, bf16[128,1536]{1,0:T(8,128)(2,1)S(1)} %get-tuple-element.47.tiles_ref, ...), custom_call_target="tpu_custom_call" | custom-call | flops 3000000000 | bytes 3000000 | tf_op jit(solution)/shard_map/pallas_call | solution.py:478
  21.0 0.3 collective-permute-start.9
  21.3 2.8 %shard_map.125 = (bf16[880,128]{1,0:T(8,128)(2,1)S(1)}, bf16[880,128]{1,0:T(8,128)(2,1)S(1)}, bf16[880,128]{1,0:T(8,128)(2,1)S(1)}, bf16[880,128]{1,0:T(8,128)(2,1)S(1)}) custom-call(bf16[128,2304]{1,0:T(8,128)(2,1)S(1)} %copy-done.10, bf16[128,768]{1,0:T(8,128)(2,1)S(1)} %get-tuple-element.41.fk_ref, bf16[128,768]{1,0:T(8,128)(2,1)S(1)} %get-tuple-element.42.fv_ref, ...), custom_call_target="tpu_custom_call" | custom-call | flops 8000000000 | bytes 8000000 | tf_op jit(solution)/shard_map/pallas_call | solution.py:478
  24.2 0.0 collective-permute-done.6.wait1.n1
  24.2 0.0 collective-permute-done.7.wait2.n3
  24.2 0.0 collective-permute-done.9.other_ref
  24.2 0.0 copy-start.7
  24.2 0.2 shard_map.126
  24.4 1.6 %collective-permute-start.10 = (bf16[96,768]{1,0:T(8,128)(2,1)S(1)}, bf16[96,768]{1,0:T(8,128)(2,1)S(1)}, u32[]{:S(2)}, u32[]{:S(2)}) collective-permute-start(bf16[96,768]{1,0:T(8,128)(2,1)S(1)} %get-tuple-element.59), channel_id=1, source_target_pairs={{0,8},{4,12},{8,16},{12,20},{16,24},{20,28},{24,0},{28,4},{32,40},... | collective-permute-start | bytes 442376 | tf_op jit(solution)/shard_map/ppermute | solution.py:514
  26.0 2.9 %collective-permute-start.11 = (bf16[96,768]{1,0:T(8,128)(2,1)S(1)}, bf16[96,768]{1,0:T(8,128)(2,1)S(1)}, u32[]{:S(2)}, u32[]{:S(2)}) collective-permute-start(bf16[96,768]{1,0:T(8,128)(2,1)S(1)} %get-tuple-element.60), channel_id=1, source_target_pairs={{0,16},{4,20},{8,24},{12,28},{16,0},{20,4},{24,8},{28,12},{32,48},... | collective-permute-start | bytes 442376 | tf_op jit(solution)/shard_map/ppermute | solution.py:514
  28.9 1.3 %collective-permute-start.12 = (bf16[96,768]{1,0:T(8,128)(2,1)S(1)}, bf16[96,768]{1,0:T(8,128)(2,1)S(1)}, u32[]{:S(2)}, u32[]{:S(2)}) collective-permute-start(bf16[96,768]{1,0:T(8,128)(2,1)S(1)} %get-tuple-element.61), channel_id=1, source_target_pairs={{0,24},{4,28},{8,0},{12,4},{16,8},{20,12},{24,16},{28,20},{32,56},... | collective-permute-start | bytes 442376 | tf_op jit(solution)/shard_map/ppermute | solution.py:514
  30.2 2.6 %collective-permute-start.3 = (bf16[880,128]{1,0:T(8,128)(2,1)S(1)}, bf16[880,128]{1,0:T(8,128)(2,1)S(1)}, u32[]{:S(2)}, u32[]{:S(2)}) collective-permute-start(bf16[880,128]{1,0:T(8,128)(2,1)S(1)} %get-tuple-element.52), channel_id=1, source_target_pairs={{0,1},{1,2},{2,3},{3,0},{4,5},{5,6},{6,7},{7,4},{8,9},{9,10},{10,1... | collective-permute-start | bytes 675848 | tf_op jit(solution)/shard_map/ppermute | solution.py:514
  32.9 0.8 collective-permute-start.4
  33.6 1.4 %collective-permute-start.5 = (bf16[880,128]{1,0:T(8,128)(2,1)S(1)}, bf16[880,128]{1,0:T(8,128)(2,1)S(1)}, u32[]{:S(2)}, u32[]{:S(2)}) collective-permute-start(bf16[880,128]{1,0:T(8,128)(2,1)S(1)} %get-tuple-element.54), channel_id=1, source_target_pairs={{0,3},{1,0},{2,1},{3,2},{4,7},{5,4},{6,5},{7,6},{8,11},{9,8},{10,9... | collective-permute-start | bytes 675848 | tf_op jit(solution)/shard_map/ppermute | solution.py:514
  35.0 1.3 %collective-permute-done.11.y2 = bf16[96,768]{1,0:T(8,128)(2,1)S(1)} collective-permute-done((bf16[96,768]{1,0:T(8,128)(2,1)S(1)}, bf16[96,768]{1,0:T(8,128)(2,1)S(1)}, u32[]{:S(2)}, u32[]{:S(2)}) %collective-permute-start.11) | collective-permute-done | bytes 147488 | tf_op jit(solution)/shard_map/ppermute | solution.py:514
  36.3 0.3 shard_map.127
  36.5 2.7 %collective-permute-start.13 = (bf16[32,768]{1,0:T(8,128)(2,1)S(1)}, bf16[32,768]{1,0:T(8,128)(2,1)S(1)}, u32[]{:S(2)}, u32[]{:S(2)}) collective-permute-start(bf16[32,768]{1,0:T(8,128)(2,1)S(1)} %get-tuple-element.65), channel_id=1, source_target_pairs={{0,1},{1,2},{2,3},{3,0},{4,5},{5,6},{6,7},{7,4},{8,9},{9,10},{10,1... | collective-permute-start | bytes 147464 | tf_op jit(solution)/shard_map/ppermute | solution.py:514
  39.2 0.8 collective-permute-start.14
  40.0 3.9 %collective-permute-done.3.x1 = bf16[880,128]{1,0:T(8,128)(2,1)S(1)} collective-permute-done((bf16[880,128]{1,0:T(8,128)(2,1)S(1)}, bf16[880,128]{1,0:T(8,128)(2,1)S(1)}, u32[]{:S(2)}, u32[]{:S(2)}) %collective-permute-start.3) | collective-permute-done | bytes 225312 | tf_op jit(solution)/shard_map/ppermute | solution.py:514
  43.9 2.1 %collective-permute-done.5.x3 = bf16[880,128]{1,0:T(8,128)(2,1)S(1)} collective-permute-done((bf16[880,128]{1,0:T(8,128)(2,1)S(1)}, bf16[880,128]{1,0:T(8,128)(2,1)S(1)}, u32[]{:S(2)}, u32[]{:S(2)}) %collective-permute-start.5) | collective-permute-done | bytes 225312 | tf_op jit(solution)/shard_map/ppermute | solution.py:514
  46.0 1.1 %shard_map.128 = (f32[576,768]{1,0:T(8,128)S(1)}, f32[80,768]{1,0:T(8,128)S(1)}) custom-call(bf16[880,128]{1,0:T(8,128)(2,1)S(1)} %get-tuple-element.51.wait0.x0, bf16[880,128]{1,0:T(8,128)(2,1)S(1)} %collective-permute-done.3.x1, bf16[880,128]{1,0:T(8,128)(2,1)S(1)} %collective-permute-done.4.x2, bf16[880,128]{1,0:T(8,128)(2,1)S(1)} %collective-permute-done.5.x3, ...), custom_call_target="tpu_custom_call" | custom-call | flops 15000000512 | bytes 15000000 | tf_op jit(solution)/shard_map/pallas_call | solution.py:478
  47.2 0.4 collective-permute-done.14.wait2.o2
  47.6 0.8 collective-permute-done.15.wait3.o3
  48.4 0.1 shard_map.129
  48.5 0.1 collective-permute-start.16
  48.6 1.9 %collective-permute-done.16.other_ref = bf16[320,768]{1,0:T(8,128)(2,1)S(1)} collective-permute-done((bf16[320,768]{1,0:T(8,128)(2,1)S(1)}, bf16[320,768]{1,0:T(8,128)(2,1)S(1)}, u32[]{:S(2)}, u32[]{:S(2)}) %collective-permute-start.16) | collective-permute-done | bytes 491552 | tf_op jit(solution)/shard_map/ppermute | solution.py:594
  50.5 0.2 shard_map.130
  50.6 0.4 collective-permute-start.17
  51.0 0.5 collective-permute-start.18
  51.6 2.7 %collective-permute-start.19 = (bf16[80,768]{1,0:T(8,128)(2,1)S(1)}, bf16[80,768]{1,0:T(8,128)(2,1)S(1)}, u32[]{:S(2)}, u32[]{:S(2)}) collective-permute-start(bf16[80,768]{1,0:T(8,128)(2,1)S(1)} %get-tuple-element.73), channel_id=1, source_target_pairs={{0,24},{4,28},{8,0},{12,4},{16,8},{20,12},{24,16},{28,20},{32,56},... | collective-permute-start | bytes 368648 | tf_op jit(solution)/shard_map/ppermute | solution.py:514
  54.3 4.2 %collective-permute-done.17.y1 = bf16[80,768]{1,0:T(8,128)(2,1)S(1)} collective-permute-done((bf16[80,768]{1,0:T(8,128)(2,1)S(1)}, bf16[80,768]{1,0:T(8,128)(2,1)S(1)}, u32[]{:S(2)}, u32[]{:S(2)}) %collective-permute-start.17) | collective-permute-done | bytes 122912 | tf_op jit(solution)/shard_map/ppermute | solution.py:514
  58.4 1.6 %collective-permute-done.18.y2 = bf16[80,768]{1,0:T(8,128)(2,1)S(1)} collective-permute-done((bf16[80,768]{1,0:T(8,128)(2,1)S(1)}, bf16[80,768]{1,0:T(8,128)(2,1)S(1)}, u32[]{:S(2)}, u32[]{:S(2)}) %collective-permute-start.18) | collective-permute-done | bytes 122912 | tf_op jit(solution)/shard_map/ppermute | solution.py:514
  60.1 0.3 shard_map.131
  60.3 18.7 %all_to_all.5.in_ref = bf16[8,16,768]{2,1,0:T(8,128)(2,1)S(1)} all-to-all(bf16[8,16,768]{2,1,0:T(8,128)(2,1)S(1)} %shard_map.131), channel_id=1, replica_groups={{0,32,64,96,128,160,192,224},{4,36,68,100,132,164,196,228},{8,40,72,104..., dimensions={0} | all-to-all | bytes 393216 | tf_op jit(solution)/shard_map/all_to_all | solution.py:602
  79.1 0.7 shard_map.132
  (28 shorter events, 0.1 us)
Async XLA Ops:
  0.6 14.2 %copy-start.2 = (bf16[1,128,1536]{2,1,0:T(8,128)(2,1)S(1)}, bf16[1,128,1536]{2,1,0:T(8,128)(2,1)}, u32[]{:S(2)}) copy-start(bf16[1,128,1536]{2,1,0:T(8,128)(2,1)} %tiles_ref.1) | copy-start | bytes 1179652
  0.6 14.2 %copy-start.4 = (s32[1,128]{1,0:T(1,128)S(1)}, s32[1,128]{1,0:T(1,128)}, u32[]{:S(2)}) copy-start(s32[1,128]{1,0:T(1,128)} %masked_ref.1) | copy-start | bytes 1540
  5.1 7.5 %collective-permute-start = (bf16[32,1536]{1,0:T(8,128)(2,1)}, bf16[32,1536]{1,0:T(8,128)(2,1)S(1)}, u32[]{:S(2)}, u32[]{:S(2)}) collective-permute-start(bf16[32,1536]{1,0:T(8,128)(2,1)} %get-tuple-element.40), channel_id=1, source_target_pairs={{0,2},{1,3},{2,0},{3,1},{4,6},{5,7},{6,4},{7,5},{8,10},{9,11},{10,... | collective-permute-start | bytes 294920 | tf_op jit(solution)/shard_map/ppermute | solution.py:514
  7.3 7.5 %collective-permute-start.1 = (bf16[32,1536]{1,0:T(8,128)(2,1)}, bf16[32,1536]{1,0:T(8,128)(2,1)S(1)}, u32[]{:S(2)}, u32[]{:S(2)}) collective-permute-start(bf16[32,1536]{1,0:T(8,128)(2,1)} %get-tuple-element.40), channel_id=1, source_target_pairs={{0,1},{1,2},{2,3},{3,0},{4,5},{5,6},{6,7},{7,4},{8,9},{9,10},{10,1... | collective-permute-start | bytes 294920 | tf_op jit(solution)/shard_map/ppermute | solution.py:514
  8.9 5.9 %collective-permute-start.2 = (bf16[32,1536]{1,0:T(8,128)(2,1)}, bf16[32,1536]{1,0:T(8,128)(2,1)S(1)}, u32[]{:S(2)}, u32[]{:S(2)}) collective-permute-start(bf16[32,1536]{1,0:T(8,128)(2,1)} %get-tuple-element.40), channel_id=1, source_target_pairs={{0,3},{1,0},{2,1},{3,2},{4,7},{5,4},{6,5},{7,6},{8,11},{9,8},{10,9... | collective-permute-start | bytes 294920 | tf_op jit(solution)/shard_map/ppermute | solution.py:514
  9.3 14.8 %collective-permute-start.6 = (bf16[128,768]{1,0:T(8,128)(2,1)}, bf16[128,768]{1,0:T(8,128)(2,1)S(1)}, u32[]{:S(2)}, u32[]{:S(2)}) collective-permute-start(bf16[128,768]{1,0:T(8,128)(2,1)} %get-tuple-element.55.n0), channel_id=1, source_target_pairs={{0,1},{1,2},{2,3},{3,0},{4,5},{5,6},{6,7},{7,4},{8,9},{9,10},{10,1... | collective-permute-start | bytes 589832 | tf_op jit(solution)/shard_map/ppermute | solution.py:514
  10.9 13.2 %collective-permute-start.7 = (bf16[128,768]{1,0:T(8,128)(2,1)}, bf16[128,768]{1,0:T(8,128)(2,1)S(1)}, u32[]{:S(2)}, u32[]{:S(2)}) collective-permute-start(bf16[128,768]{1,0:T(8,128)(2,1)} %get-tuple-element.55.n0), channel_id=1, source_target_pairs={{0,3},{1,0},{2,1},{3,2},{4,7},{5,4},{6,5},{7,6},{8,11},{9,8},{10,9... | collective-permute-start | bytes 589832 | tf_op jit(solution)/shard_map/ppermute | solution.py:514
  12.6 11.5 %collective-permute-start.8 = (bf16[128,768]{1,0:T(8,128)(2,1)}, bf16[128,768]{1,0:T(8,128)(2,1)S(1)}, u32[]{:S(2)}, u32[]{:S(2)}) collective-permute-start(bf16[128,768]{1,0:T(8,128)(2,1)} %get-tuple-element.55.n0), channel_id=1, source_target_pairs={{0,2},{1,3},{2,0},{3,1},{4,6},{5,7},{6,4},{7,5},{8,10},{9,11},{10,... | collective-permute-start | bytes 589832 | tf_op jit(solution)/shard_map/ppermute | solution.py:514
  14.9 1.1 %copy-start.9 = (bf16[128,2304]{1,0:T(8,128)(2,1)S(1)}, bf16[128,2304]{1,0:T(8,128)(2,1)}, u32[]{:S(2)}) copy-start(bf16[128,2304]{1,0:T(8,128)(2,1)} %get-tuple-element.39.proj_ref) | copy-start | bytes 1769476
  15.9 2.1 %copy-start = (bf16[1536,768]{1,0:T(8,128)(2,1)S(1)}, bf16[1536,768]{1,0:T(8,128)(2,1)}, u32[]{:S(2)}) copy-start(bf16[1536,768]{1,0:T(8,128)(2,1)} %w_in_ref.1) | copy-start | bytes 7077892
  15.9 2.1 %copy-start.1 = (bf16[768,768]{1,0:T(8,128)(2,1)S(1)}, bf16[768,768]{1,0:T(8,128)(2,1)}, u32[]{:S(2)}) copy-start(bf16[768,768]{1,0:T(8,128)(2,1)} %w_out_ref.1) | copy-start | bytes 3538948
  15.9 2.3 %copy-start.5 = (bf16[768,768]{1,0:T(8,128)(2,1)S(1)}, bf16[768,768]{1,0:T(8,128)(2,1)}, u32[]{:S(2)}) copy-start(bf16[768,768]{1,0:T(8,128)(2,1)} %constant.8.clone.order_ref) | copy-start | bytes 3538948
  15.9 2.3 %copy-start.11 = (bf16[128,768]{1,0:T(8,128)(2,1)S(1)}, bf16[128,768]{1,0:T(8,128)(2,1)}, u32[]{:S(2)}) copy-start(bf16[128,768]{1,0:T(8,128)(2,1)} %get-tuple-element.46.hidden_ref) | copy-start | bytes 589828
  18.3 3.0 %copy-start.6 = (bf16[384,384]{1,0:T(8,128)(2,1)S(1)}, bf16[384,384]{1,0:T(8,128)(2,1)}, u32[]{:S(2)}) copy-start(bf16[384,384]{1,0:T(8,128)(2,1)} %constant.9.clone.spread_ref) | copy-start | bytes 884740
  18.3 3.0 %copy-start.10 = (bf16[128,2304]{1,0:T(8,128)(2,1)S(1)}, bf16[128,2304]{1,0:T(8,128)(2,1)}, u32[]{:S(2)}) copy-start(bf16[128,2304]{1,0:T(8,128)(2,1)} %get-tuple-element.39.proj_ref) | copy-start | bytes 1769476
  21.0 3.2 %collective-permute-start.9 = (bf16[384,768]{1,0:T(8,128)(2,1)S(1)}, bf16[384,768]{1,0:T(8,128)(2,1)S(1)}, u32[]{:S(2)}, u32[]{:S(2)}) collective-permute-start(bf16[384,768]{1,0:T(8,128)(2,1)S(1)} %get-tuple-element.57), channel_id=1, source_target_pairs={{0,4},{4,0},{8,12},{12,8},{16,20},{20,16},{24,28},{28,24},{32,36},... | collective-permute-start | bytes 1769480 | tf_op jit(solution)/shard_map/ppermute | solution.py:561
  24.2 12.1 %copy-start.7 = (bf16[128,96]{1,0:T(8,128)(2,1)S(1)}, bf16[128,96]{1,0:T(8,128)(2,1)}, u32[]{:S(2)}) copy-start(bf16[128,96]{1,0:T(8,128)(2,1)} %constant.10.clone.order_ref) | copy-start | bytes 73732
  24.4 9.3 %collective-permute-start.10 = (bf16[96,768]{1,0:T(8,128)(2,1)S(1)}, bf16[96,768]{1,0:T(8,128)(2,1)S(1)}, u32[]{:S(2)}, u32[]{:S(2)}) collective-permute-start(bf16[96,768]{1,0:T(8,128)(2,1)S(1)} %get-tuple-element.59), channel_id=1, source_target_pairs={{0,8},{4,12},{8,16},{12,20},{16,24},{20,28},{24,0},{28,4},{32,40},... | collective-permute-start | bytes 442376 | tf_op jit(solution)/shard_map/ppermute | solution.py:514
  26.0 10.3 %collective-permute-start.11 = (bf16[96,768]{1,0:T(8,128)(2,1)S(1)}, bf16[96,768]{1,0:T(8,128)(2,1)S(1)}, u32[]{:S(2)}, u32[]{:S(2)}) collective-permute-start(bf16[96,768]{1,0:T(8,128)(2,1)S(1)} %get-tuple-element.60), channel_id=1, source_target_pairs={{0,16},{4,20},{8,24},{12,28},{16,0},{20,4},{24,8},{28,12},{32,48},... | collective-permute-start | bytes 442376 | tf_op jit(solution)/shard_map/ppermute | solution.py:514
  28.9 7.4 %collective-permute-start.12 = (bf16[96,768]{1,0:T(8,128)(2,1)S(1)}, bf16[96,768]{1,0:T(8,128)(2,1)S(1)}, u32[]{:S(2)}, u32[]{:S(2)}) collective-permute-start(bf16[96,768]{1,0:T(8,128)(2,1)S(1)} %get-tuple-element.61), channel_id=1, source_target_pairs={{0,24},{4,28},{8,0},{12,4},{16,8},{20,12},{24,16},{28,20},{32,56},... | collective-permute-start | bytes 442376 | tf_op jit(solution)/shard_map/ppermute | solution.py:514
  30.2 13.6 %collective-permute-start.3 = (bf16[880,128]{1,0:T(8,128)(2,1)S(1)}, bf16[880,128]{1,0:T(8,128)(2,1)S(1)}, u32[]{:S(2)}, u32[]{:S(2)}) collective-permute-start(bf16[880,128]{1,0:T(8,128)(2,1)S(1)} %get-tuple-element.52), channel_id=1, source_target_pairs={{0,1},{1,2},{2,3},{3,0},{4,5},{5,6},{6,7},{7,4},{8,9},{9,10},{10,1... | collective-permute-start | bytes 675848 | tf_op jit(solution)/shard_map/ppermute | solution.py:514
  32.9 11.0 %collective-permute-start.4 = (bf16[880,128]{1,0:T(8,128)(2,1)S(1)}, bf16[880,128]{1,0:T(8,128)(2,1)S(1)}, u32[]{:S(2)}, u32[]{:S(2)}) collective-permute-start(bf16[880,128]{1,0:T(8,128)(2,1)S(1)} %get-tuple-element.53), channel_id=1, source_target_pairs={{0,2},{1,3},{2,0},{3,1},{4,6},{5,7},{6,4},{7,5},{8,10},{9,11},{10,... | collective-permute-start | bytes 675848 | tf_op jit(solution)/shard_map/ppermute | solution.py:514
  33.6 12.4 %collective-permute-start.5 = (bf16[880,128]{1,0:T(8,128)(2,1)S(1)}, bf16[880,128]{1,0:T(8,128)(2,1)S(1)}, u32[]{:S(2)}, u32[]{:S(2)}) collective-permute-start(bf16[880,128]{1,0:T(8,128)(2,1)S(1)} %get-tuple-element.54), channel_id=1, source_target_pairs={{0,3},{1,0},{2,1},{3,2},{4,7},{5,4},{6,5},{7,6},{8,11},{9,8},{10,9... | collective-permute-start | bytes 675848 | tf_op jit(solution)/shard_map/ppermute | solution.py:514
  36.3 9.8 %copy-start.3 = (bf16[128,768]{1,0:T(8,128)(2,1)S(1)}, bf16[128,768]{1,0:T(8,128)(2,1)}, u32[]{:S(2)}) copy-start(bf16[128,768]{1,0:T(8,128)(2,1)} %get-tuple-element.55.n0) | copy-start | bytes 589828
  36.5 10.6 %collective-permute-start.13 = (bf16[32,768]{1,0:T(8,128)(2,1)S(1)}, bf16[32,768]{1,0:T(8,128)(2,1)S(1)}, u32[]{:S(2)}, u32[]{:S(2)}) collective-permute-start(bf16[32,768]{1,0:T(8,128)(2,1)S(1)} %get-tuple-element.65), channel_id=1, source_target_pairs={{0,1},{1,2},{2,3},{3,0},{4,5},{5,6},{6,7},{7,4},{8,9},{9,10},{10,1... | collective-permute-start | bytes 147464 | tf_op jit(solution)/shard_map/ppermute | solution.py:514
  39.2 8.4 %collective-permute-start.14 = (bf16[32,768]{1,0:T(8,128)(2,1)S(1)}, bf16[32,768]{1,0:T(8,128)(2,1)S(1)}, u32[]{:S(2)}, u32[]{:S(2)}) collective-permute-start(bf16[32,768]{1,0:T(8,128)(2,1)S(1)} %get-tuple-element.66), channel_id=1, source_target_pairs={{0,2},{1,3},{2,0},{3,1},{4,6},{5,7},{6,4},{7,5},{8,10},{9,11},{10,... | collective-permute-start | bytes 147464 | tf_op jit(solution)/shard_map/ppermute | solution.py:514
  43.9 4.5 %collective-permute-start.15 = (bf16[32,768]{1,0:T(8,128)(2,1)S(1)}, bf16[32,768]{1,0:T(8,128)(2,1)S(1)}, u32[]{:S(2)}, u32[]{:S(2)}) collective-permute-start(bf16[32,768]{1,0:T(8,128)(2,1)S(1)} %get-tuple-element.67), channel_id=1, source_target_pairs={{0,3},{1,0},{2,1},{3,2},{4,7},{5,4},{6,5},{7,6},{8,11},{9,8},{10,9... | collective-permute-start | bytes 147464 | tf_op jit(solution)/shard_map/ppermute | solution.py:514
  48.5 2.0 %collective-permute-start.16 = (bf16[320,768]{1,0:T(8,128)(2,1)S(1)}, bf16[320,768]{1,0:T(8,128)(2,1)S(1)}, u32[]{:S(2)}, u32[]{:S(2)}) collective-permute-start(bf16[320,768]{1,0:T(8,128)(2,1)S(1)} %get-tuple-element.69), channel_id=1, source_target_pairs={{0,4},{4,0},{8,12},{12,8},{16,20},{20,16},{24,28},{28,24},{32,36},... | collective-permute-start | bytes 1474568 | tf_op jit(solution)/shard_map/ppermute | solution.py:594
  50.5 9.6 %copy-start.8 = (bf16[96,80]{1,0:T(8,128)(2,1)S(1)}, bf16[96,80]{1,0:T(8,128)(2,1)}, u32[]{:S(2)}) copy-start(bf16[96,80]{1,0:T(8,128)(2,1)} %constant.11.clone.order_ref) | copy-start | bytes 46084
  50.6 7.8 %collective-permute-start.17 = (bf16[80,768]{1,0:T(8,128)(2,1)S(1)}, bf16[80,768]{1,0:T(8,128)(2,1)S(1)}, u32[]{:S(2)}, u32[]{:S(2)}) collective-permute-start(bf16[80,768]{1,0:T(8,128)(2,1)S(1)} %get-tuple-element.71), channel_id=1, source_target_pairs={{0,16},{4,20},{8,24},{12,28},{16,0},{20,4},{24,8},{28,12},{32,48},... | collective-permute-start | bytes 368648 | tf_op jit(solution)/shard_map/ppermute | solution.py:514
  51.0 9.0 %collective-permute-start.18 = (bf16[80,768]{1,0:T(8,128)(2,1)S(1)}, bf16[80,768]{1,0:T(8,128)(2,1)S(1)}, u32[]{:S(2)}, u32[]{:S(2)}) collective-permute-start(bf16[80,768]{1,0:T(8,128)(2,1)S(1)} %get-tuple-element.72), channel_id=1, source_target_pairs={{0,8},{4,12},{8,16},{12,20},{16,24},{20,28},{24,0},{28,4},{32,40},... | collective-permute-start | bytes 368648 | tf_op jit(solution)/shard_map/ppermute | solution.py:514
  51.6 8.5 %collective-permute-start.19 = (bf16[80,768]{1,0:T(8,128)(2,1)S(1)}, bf16[80,768]{1,0:T(8,128)(2,1)S(1)}, u32[]{:S(2)}, u32[]{:S(2)}) collective-permute-start(bf16[80,768]{1,0:T(8,128)(2,1)S(1)} %get-tuple-element.73), channel_id=1, source_target_pairs={{0,24},{4,28},{8,0},{12,4},{16,8},{20,12},{24,16},{28,20},{32,56},... | collective-permute-start | bytes 368648 | tf_op jit(solution)/shard_map/ppermute | solution.py:514

commit v14 on v13

--- a/solution.py
+++ b/solution.py
@@ -570,7 +570,7 @@
     out = call(out_core_kernel, [shape(SUB, D)] * NY, (out_mine, out_other, sent[0], norms[1], norms[3], norms[2]), unread=4)
     out = swap(out, "slide", Y_TURNS)
     out_sums = call(
-        out_y_kernel, [shape(32, D)] * N_SEQ, (*out, out_pad_order()), (), 20.0
+        out_y_kernel, [shape(32, D)] * N_SEQ, (*out, out_pad_order())
     )
     out = swap(out_sums, "seq", SEQ_TURNS)
     whole, tail = call(

time: 80.4 us -> 80.4 us (level)
  no operation moved by 1% of the time
where the time goes in v14:
time: 80.4 us; the launch traced here: 79.7 us
  starting transfers between devices  27.1 us (34%)
  blocking collectives  18.7 us (23%)
  waiting for transfers between devices  16.2 us (20%)
  Pallas kernels  14.9 us (19%)
  between operations  1.49 us (2%)
  local copies, waits for them, and re-layouts  1.29 us (2%)
    ppermute x18, starting transfers between devices, swap(): got = {t: lax.ppermute(arrays[t], axis, turns[t]) for t in order}  26.7 us
    all_to_all x1, blocking collectives, per_device(): lax.all_to_all(by_z, 'slide', 0, 0, tiled=True, axis_index_groups=Z_GROUPS)  18.7 us
    pallas_call x11, Pallas kernels, call(): pl.pallas_call(kernel, out_shape=out_shapes, in_specs=specs, out_specs=[V...  14.9 us
    ppermute x18, waiting for transfers between devices, swap(): got = {t: lax.ppermute(arrays[t], axis, turns[t]) for t in order}  14.4 us
    ppermute x1, waiting for transfers between devices, per_device(): other = lax.ppermute(other, 'slide', CORE_PAIRS)  1.85 us
  transfers between devices with their start and end apart: 20, of which 9 were waited for; matrix products, arithmetic and copies ran while one was open for 0% of the time, Pallas kernels for 11%

profile of v14, /device:TPU:2, one launch (start us, length us, event | category | flops | bytes accessed | tf_op | source)
XLA Modules:
  0.0 79.7 jit_solution(6954191300242106927)
XLA Ops:
  0.7 4.4 %shard_map.122 = (bf16[128,768]{1,0:T(8,128)(2,1)}, bf16[128,768]{1,0:T(8,128)(2,1)}, bf16[128,2304]{1,0:T(8,128)(2,1)}, bf16[32,1536]{1,0:T(8,128)(2,1)}) custom-call(bf16[1,128,1536]{2,1,0:T(8,128)(2,1)} %tiles_ref.1, s32[1,128]{1,0:T(1,128)} %masked_ref.1, f32[768]{0:T(1024)} %gain_hbm.1, bf16[1536,768]{1,0:T(8,128)(2,1)} %w_in_ref.1, ...), custom_call_target="tpu_custom_call" | custom-call | flops 4000000000 | bytes 4000000 | tf_op jit(solution)/shard_map/pallas_call | solution.py:478
  5.1 2.2 %collective-permute-start = (bf16[32,1536]{1,0:T(8,128)(2,1)}, bf16[32,1536]{1,0:T(8,128)(2,1)S(1)}, u32[]{:S(2)}, u32[]{:S(2)}) collective-permute-start(bf16[32,1536]{1,0:T(8,128)(2,1)} %get-tuple-element.40), channel_id=1, source_target_pairs={{0,2},{1,3},{2,0},{3,1},{4,6},{5,7},{6,4},{7,5},{8,10},{9,11},{10,... | collective-permute-start | bytes 294920 | tf_op jit(solution)/shard_map/ppermute | solution.py:514
  7.3 1.6 %collective-permute-start.1 = (bf16[32,1536]{1,0:T(8,128)(2,1)}, bf16[32,1536]{1,0:T(8,128)(2,1)S(1)}, u32[]{:S(2)}, u32[]{:S(2)}) collective-permute-start(bf16[32,1536]{1,0:T(8,128)(2,1)} %get-tuple-element.40), channel_id=1, source_target_pairs={{0,1},{1,2},{2,3},{3,0},{4,5},{5,6},{6,7},{7,4},{8,9},{9,10},{10,1... | collective-permute-start | bytes 294920 | tf_op jit(solution)/shard_map/ppermute | solution.py:514
  8.9 0.4 collective-permute-start.2
  9.3 1.6 %collective-permute-start.6 = (bf16[128,768]{1,0:T(8,128)(2,1)}, bf16[128,768]{1,0:T(8,128)(2,1)S(1)}, u32[]{:S(2)}, u32[]{:S(2)}) collective-permute-start(bf16[128,768]{1,0:T(8,128)(2,1)} %get-tuple-element.55.n0), channel_id=1, source_target_pairs={{0,1},{1,2},{2,3},{3,0},{4,5},{5,6},{6,7},{7,4},{8,9},{9,10},{10,1... | collective-permute-start | bytes 589832 | tf_op jit(solution)/shard_map/ppermute | solution.py:514
  10.9 1.0 %collective-permute-start.7 = (bf16[128,768]{1,0:T(8,128)(2,1)}, bf16[128,768]{1,0:T(8,128)(2,1)S(1)}, u32[]{:S(2)}, u32[]{:S(2)}) collective-permute-start(bf16[128,768]{1,0:T(8,128)(2,1)} %get-tuple-element.55.n0), channel_id=1, source_target_pairs={{0,3},{1,0},{2,1},{3,2},{4,7},{5,4},{6,5},{7,6},{8,11},{9,8},{10,9... | collective-permute-start | bytes 589832 | tf_op jit(solution)/shard_map/ppermute | solution.py:514
  12.6 2.2 %collective-permute-start.8 = (bf16[128,768]{1,0:T(8,128)(2,1)}, bf16[128,768]{1,0:T(8,128)(2,1)S(1)}, u32[]{:S(2)}, u32[]{:S(2)}) collective-permute-start(bf16[128,768]{1,0:T(8,128)(2,1)} %get-tuple-element.55.n0), channel_id=1, source_target_pairs={{0,2},{1,3},{2,0},{3,1},{4,6},{5,7},{6,4},{7,5},{8,10},{9,11},{10,... | collective-permute-start | bytes 589832 | tf_op jit(solution)/shard_map/ppermute | solution.py:514
  14.8 0.0 collective-permute-done.1.f1
  14.8 0.1 collective-permute-done.2.f3
  14.9 1.1 %copy-done.9 = bf16[128,2304]{1,0:T(8,128)(2,1)S(1)} copy-done((bf16[128,2304]{1,0:T(8,128)(2,1)S(1)}, bf16[128,2304]{1,0:T(8,128)(2,1)}, u32[]{:S(2)}) %copy-start.9) | copy-done | bytes 589848
  15.9 2.1 %shard_map.123 = (bf16[128,768]{1,0:T(8,128)(2,1)S(1)}, bf16[128,768]{1,0:T(8,128)(2,1)S(1)}, f32[4,128,512]{2,1,0:T(8,128)S(1)}, f32[4,128,128]{2,1,0:T(8,128)S...) custom-call(s32[1,1]{1,0:T(1,128)} %bitcast.2.count_ref, ...), custom_call_target="tpu_custom_call" | custom-call | flops 2000000000 | bytes 2000000 | tf_op jit(solution)/shard_map/pallas_call | solution.py:478
  18.1 0.2 copy-done.5
  18.3 0.0 copy-done.11
  18.3 2.7 %shard_map.124 = (bf16[128,768]{1,0:T(8,128)(2,1)S(1)}, bf16[16,128]{1,0:T(8,128)(2,1)S(1)}, bf16[384,768]{1,0:T(8,128)(2,1)S(1)}, bf16[384,768]{1,0:T(8,128)(2,1)S(1)}) custom-call(bf16[128,768]{1,0:T(8,128)(2,1)S(1)} %get-tuple-element.45.att_ref, bf16[128,768]{1,0:T(8,128)(2,1)S(1)} %copy-done.11, bf16[128,1536]{1,0:T(8,128)(2,1)S(1)} %get-tuple-element.47.tiles_ref, ...), custom_call_target="tpu_custom_call" | custom-call | flops 3000000000 | bytes 3000000 | tf_op jit(solution)/shard_map/pallas_call | solution.py:478
  21.0 0.3 collective-permute-start.9
  21.3 2.8 %shard_map.125 = (bf16[880,128]{1,0:T(8,128)(2,1)S(1)}, bf16[880,128]{1,0:T(8,128)(2,1)S(1)}, bf16[880,128]{1,0:T(8,128)(2,1)S(1)}, bf16[880,128]{1,0:T(8,128)(2,1)S(1)}) custom-call(bf16[128,2304]{1,0:T(8,128)(2,1)S(1)} %copy-done.10, bf16[128,768]{1,0:T(8,128)(2,1)S(1)} %get-tuple-element.41.fk_ref, bf16[128,768]{1,0:T(8,128)(2,1)S(1)} %get-tuple-element.42.fv_ref, ...), custom_call_target="tpu_custom_call" | custom-call | flops 8000000000 | bytes 8000000 | tf_op jit(solution)/shard_map/pallas_call | solution.py:478
  24.2 0.0 collective-permute-done.6.wait1.n1
  24.2 0.0 collective-permute-done.7.wait2.n3
  24.2 0.0 collective-permute-done.9.other_ref
  24.2 0.0 copy-start.7
  24.2 0.2 shard_map.126
  24.4 1.6 %collective-permute-start.10 = (bf16[96,768]{1,0:T(8,128)(2,1)S(1)}, bf16[96,768]{1,0:T(8,128)(2,1)S(1)}, u32[]{:S(2)}, u32[]{:S(2)}) collective-permute-start(bf16[96,768]{1,0:T(8,128)(2,1)S(1)} %get-tuple-element.59), channel_id=1, source_target_pairs={{0,8},{4,12},{8,16},{12,20},{16,24},{20,28},{24,0},{28,4},{32,40},... | collective-permute-start | bytes 442376 | tf_op jit(solution)/shard_map/ppermute | solution.py:514
  26.0 2.9 %collective-permute-start.11 = (bf16[96,768]{1,0:T(8,128)(2,1)S(1)}, bf16[96,768]{1,0:T(8,128)(2,1)S(1)}, u32[]{:S(2)}, u32[]{:S(2)}) collective-permute-start(bf16[96,768]{1,0:T(8,128)(2,1)S(1)} %get-tuple-element.60), channel_id=1, source_target_pairs={{0,16},{4,20},{8,24},{12,28},{16,0},{20,4},{24,8},{28,12},{32,48},... | collective-permute-start | bytes 442376 | tf_op jit(solution)/shard_map/ppermute | solution.py:514
  28.9 1.3 %collective-permute-start.12 = (bf16[96,768]{1,0:T(8,128)(2,1)S(1)}, bf16[96,768]{1,0:T(8,128)(2,1)S(1)}, u32[]{:S(2)}, u32[]{:S(2)}) collective-permute-start(bf16[96,768]{1,0:T(8,128)(2,1)S(1)} %get-tuple-element.61), channel_id=1, source_target_pairs={{0,24},{4,28},{8,0},{12,4},{16,8},{20,12},{24,16},{28,20},{32,56},... | collective-permute-start | bytes 442376 | tf_op jit(solution)/shard_map/ppermute | solution.py:514
  30.2 2.6 %collective-permute-start.3 = (bf16[880,128]{1,0:T(8,128)(2,1)S(1)}, bf16[880,128]{1,0:T(8,128)(2,1)S(1)}, u32[]{:S(2)}, u32[]{:S(2)}) collective-permute-start(bf16[880,128]{1,0:T(8,128)(2,1)S(1)} %get-tuple-element.52), channel_id=1, source_target_pairs={{0,1},{1,2},{2,3},{3,0},{4,5},{5,6},{6,7},{7,4},{8,9},{9,10},{10,1... | collective-permute-start | bytes 675848 | tf_op jit(solution)/shard_map/ppermute | solution.py:514
  32.9 0.8 collective-permute-start.4
  33.6 1.4 %collective-permute-start.5 = (bf16[880,128]{1,0:T(8,128)(2,1)S(1)}, bf16[880,128]{1,0:T(8,128)(2,1)S(1)}, u32[]{:S(2)}, u32[]{:S(2)}) collective-permute-start(bf16[880,128]{1,0:T(8,128)(2,1)S(1)} %get-tuple-element.54), channel_id=1, source_target_pairs={{0,3},{1,0},{2,1},{3,2},{4,7},{5,4},{6,5},{7,6},{8,11},{9,8},{10,9... | collective-permute-start | bytes 675848 | tf_op jit(solution)/shard_map/ppermute | solution.py:514
  35.0 1.3 %collective-permute-done.11.y2 = bf16[96,768]{1,0:T(8,128)(2,1)S(1)} collective-permute-done((bf16[96,768]{1,0:T(8,128)(2,1)S(1)}, bf16[96,768]{1,0:T(8,128)(2,1)S(1)}, u32[]{:S(2)}, u32[]{:S(2)}) %collective-permute-start.11) | collective-permute-done | bytes 147488 | tf_op jit(solution)/shard_map/ppermute | solution.py:514
  36.3 0.3 shard_map.127
  36.5 2.7 %collective-permute-start.13 = (bf16[32,768]{1,0:T(8,128)(2,1)S(1)}, bf16[32,768]{1,0:T(8,128)(2,1)S(1)}, u32[]{:S(2)}, u32[]{:S(2)}) collective-permute-start(bf16[32,768]{1,0:T(8,128)(2,1)S(1)} %get-tuple-element.65), channel_id=1, source_target_pairs={{0,1},{1,2},{2,3},{3,0},{4,5},{5,6},{6,7},{7,4},{8,9},{9,10},{10,1... | collective-permute-start | bytes 147464 | tf_op jit(solution)/shard_map/ppermute | solution.py:514
  39.2 0.8 collective-permute-start.14
  40.0 3.9 %collective-permute-done.3.x1 = bf16[880,128]{1,0:T(8,128)(2,1)S(1)} collective-permute-done((bf16[880,128]{1,0:T(8,128)(2,1)S(1)}, bf16[880,128]{1,0:T(8,128)(2,1)S(1)}, u32[]{:S(2)}, u32[]{:S(2)}) %collective-permute-start.3) | collective-permute-done | bytes 225312 | tf_op jit(solution)/shard_map/ppermute | solution.py:514
  43.9 2.1 %collective-permute-done.5.x3 = bf16[880,128]{1,0:T(8,128)(2,1)S(1)} collective-permute-done((bf16[880,128]{1,0:T(8,128)(2,1)S(1)}, bf16[880,128]{1,0:T(8,128)(2,1)S(1)}, u32[]{:S(2)}, u32[]{:S(2)}) %collective-permute-start.5) | collective-permute-done | bytes 225312 | tf_op jit(solution)/shard_map/ppermute | solution.py:514
  46.0 1.1 %shard_map.128 = (f32[576,768]{1,0:T(8,128)S(1)}, f32[80,768]{1,0:T(8,128)S(1)}) custom-call(bf16[880,128]{1,0:T(8,128)(2,1)S(1)} %get-tuple-element.51.wait0.x0, bf16[880,128]{1,0:T(8,128)(2,1)S(1)} %collective-permute-done.3.x1, bf16[880,128]{1,0:T(8,128)(2,1)S(1)} %collective-permute-done.4.x2, bf16[880,128]{1,0:T(8,128)(2,1)S(1)} %collective-permute-done.5.x3, ...), custom_call_target="tpu_custom_call" | custom-call | flops 15000000512 | bytes 15000000 | tf_op jit(solution)/shard_map/pallas_call | solution.py:478
  47.2 0.4 collective-permute-done.14.wait2.o2
  47.6 0.8 collective-permute-done.15.wait3.o3
  48.4 0.1 shard_map.129
  48.5 0.1 collective-permute-start.16
  48.6 1.9 %collective-permute-done.16.other_ref = bf16[320,768]{1,0:T(8,128)(2,1)S(1)} collective-permute-done((bf16[320,768]{1,0:T(8,128)(2,1)S(1)}, bf16[320,768]{1,0:T(8,128)(2,1)S(1)}, u32[]{:S(2)}, u32[]{:S(2)}) %collective-permute-start.16) | collective-permute-done | bytes 491552 | tf_op jit(solution)/shard_map/ppermute | solution.py:594
  50.5 0.2 shard_map.130
  50.6 0.4 collective-permute-start.17
  51.0 0.5 collective-permute-start.18
  51.6 2.7 %collective-permute-start.19 = (bf16[80,768]{1,0:T(8,128)(2,1)S(1)}, bf16[80,768]{1,0:T(8,128)(2,1)S(1)}, u32[]{:S(2)}, u32[]{:S(2)}) collective-permute-start(bf16[80,768]{1,0:T(8,128)(2,1)S(1)} %get-tuple-element.73), channel_id=1, source_target_pairs={{0,24},{4,28},{8,0},{12,4},{16,8},{20,12},{24,16},{28,20},{32,56},... | collective-permute-start | bytes 368648 | tf_op jit(solution)/shard_map/ppermute | solution.py:514
  54.3 4.2 %collective-permute-done.17.y1 = bf16[80,768]{1,0:T(8,128)(2,1)S(1)} collective-permute-done((bf16[80,768]{1,0:T(8,128)(2,1)S(1)}, bf16[80,768]{1,0:T(8,128)(2,1)S(1)}, u32[]{:S(2)}, u32[]{:S(2)}) %collective-permute-start.17) | collective-permute-done | bytes 122912 | tf_op jit(solution)/shard_map/ppermute | solution.py:514
  58.4 1.6 %collective-permute-done.18.y2 = bf16[80,768]{1,0:T(8,128)(2,1)S(1)} collective-permute-done((bf16[80,768]{1,0:T(8,128)(2,1)S(1)}, bf16[80,768]{1,0:T(8,128)(2,1)S(1)}, u32[]{:S(2)}, u32[]{:S(2)}) %collective-permute-start.18) | collective-permute-done | bytes 122912 | tf_op jit(solution)/shard_map/ppermute | solution.py:514
  60.1 0.3 shard_map.131
  60.3 18.7 %all_to_all.5.in_ref = bf16[8,16,768]{2,1,0:T(8,128)(2,1)S(1)} all-to-all(bf16[8,16,768]{2,1,0:T(8,128)(2,1)S(1)} %shard_map.131), channel_id=1, replica_groups={{0,32,64,96,128,160,192,224},{4,36,68,100,132,164,196,228},{8,40,72,104..., dimensions={0} | all-to-all | bytes 393216 | tf_op jit(solution)/shard_map/all_to_all | solution.py:602
  79.1 0.7 shard_map.132
  (28 shorter events, 0.1 us)
Async XLA Ops:
  0.6 14.2 %copy-start.2 = (bf16[1,128,1536]{2,1,0:T(8,128)(2,1)S(1)}, bf16[1,128,1536]{2,1,0:T(8,128)(2,1)}, u32[]{:S(2)}) copy-start(bf16[1,128,1536]{2,1,0:T(8,128)(2,1)} %tiles_ref.1) | copy-start | bytes 1179652
  0.6 14.2 %copy-start.4 = (s32[1,128]{1,0:T(1,128)S(1)}, s32[1,128]{1,0:T(1,128)}, u32[]{:S(2)}) copy-start(s32[1,128]{1,0:T(1,128)} %masked_ref.1) | copy-start | bytes 1540
  5.1 7.5 %collective-permute-start = (bf16[32,1536]{1,0:T(8,128)(2,1)}, bf16[32,1536]{1,0:T(8,128)(2,1)S(1)}, u32[]{:S(2)}, u32[]{:S(2)}) collective-permute-start(bf16[32,1536]{1,0:T(8,128)(2,1)} %get-tuple-element.40), channel_id=1, source_target_pairs={{0,2},{1,3},{2,0},{3,1},{4,6},{5,7},{6,4},{7,5},{8,10},{9,11},{10,... | collective-permute-start | bytes 294920 | tf_op jit(solution)/shard_map/ppermute | solution.py:514
  7.3 7.5 %collective-permute-start.1 = (bf16[32,1536]{1,0:T(8,128)(2,1)}, bf16[32,1536]{1,0:T(8,128)(2,1)S(1)}, u32[]{:S(2)}, u32[]{:S(2)}) collective-permute-start(bf16[32,1536]{1,0:T(8,128)(2,1)} %get-tuple-element.40), channel_id=1, source_target_pairs={{0,1},{1,2},{2,3},{3,0},{4,5},{5,6},{6,7},{7,4},{8,9},{9,10},{10,1... | collective-permute-start | bytes 294920 | tf_op jit(solution)/shard_map/ppermute | solution.py:514
  8.9 5.9 %collective-permute-start.2 = (bf16[32,1536]{1,0:T(8,128)(2,1)}, bf16[32,1536]{1,0:T(8,128)(2,1)S(1)}, u32[]{:S(2)}, u32[]{:S(2)}) collective-permute-start(bf16[32,1536]{1,0:T(8,128)(2,1)} %get-tuple-element.40), channel_id=1, source_target_pairs={{0,3},{1,0},{2,1},{3,2},{4,7},{5,4},{6,5},{7,6},{8,11},{9,8},{10,9... | collective-permute-start | bytes 294920 | tf_op jit(solution)/shard_map/ppermute | solution.py:514
  9.3 14.8 %collective-permute-start.6 = (bf16[128,768]{1,0:T(8,128)(2,1)}, bf16[128,768]{1,0:T(8,128)(2,1)S(1)}, u32[]{:S(2)}, u32[]{:S(2)}) collective-permute-start(bf16[128,768]{1,0:T(8,128)(2,1)} %get-tuple-element.55.n0), channel_id=1, source_target_pairs={{0,1},{1,2},{2,3},{3,0},{4,5},{5,6},{6,7},{7,4},{8,9},{9,10},{10,1... | collective-permute-start | bytes 589832 | tf_op jit(solution)/shard_map/ppermute | solution.py:514
  10.9 13.2 %collective-permute-start.7 = (bf16[128,768]{1,0:T(8,128)(2,1)}, bf16[128,768]{1,0:T(8,128)(2,1)S(1)}, u32[]{:S(2)}, u32[]{:S(2)}) collective-permute-start(bf16[128,768]{1,0:T(8,128)(2,1)} %get-tuple-element.55.n0), channel_id=1, source_target_pairs={{0,3},{1,0},{2,1},{3,2},{4,7},{5,4},{6,5},{7,6},{8,11},{9,8},{10,9... | collective-permute-start | bytes 589832 | tf_op jit(solution)/shard_map/ppermute | solution.py:514
  12.6 11.5 %collective-permute-start.8 = (bf16[128,768]{1,0:T(8,128)(2,1)}, bf16[128,768]{1,0:T(8,128)(2,1)S(1)}, u32[]{:S(2)}, u32[]{:S(2)}) collective-permute-start(bf16[128,768]{1,0:T(8,128)(2,1)} %get-tuple-element.55.n0), channel_id=1, source_target_pairs={{0,2},{1,3},{2,0},{3,1},{4,6},{5,7},{6,4},{7,5},{8,10},{9,11},{10,... | collective-permute-start | bytes 589832 | tf_op jit(solution)/shard_map/ppermute | solution.py:514
  14.9 1.1 %copy-start.9 = (bf16[128,2304]{1,0:T(8,128)(2,1)S(1)}, bf16[128,2304]{1,0:T(8,128)(2,1)}, u32[]{:S(2)}) copy-start(bf16[128,2304]{1,0:T(8,128)(2,1)} %get-tuple-element.39.proj_ref) | copy-start | bytes 1769476
  15.9 2.1 %copy-start = (bf16[1536,768]{1,0:T(8,128)(2,1)S(1)}, bf16[1536,768]{1,0:T(8,128)(2,1)}, u32[]{:S(2)}) copy-start(bf16[1536,768]{1,0:T(8,128)(2,1)} %w_in_ref.1) | copy-start | bytes 7077892
  15.9 2.1 %copy-start.1 = (bf16[768,768]{1,0:T(8,128)(2,1)S(1)}, bf16[768,768]{1,0:T(8,128)(2,1)}, u32[]{:S(2)}) copy-start(bf16[768,768]{1,0:T(8,128)(2,1)} %w_out_ref.1) | copy-start | bytes 3538948
  15.9 2.3 %copy-start.5 = (bf16[768,768]{1,0:T(8,128)(2,1)S(1)}, bf16[768,768]{1,0:T(8,128)(2,1)}, u32[]{:S(2)}) copy-start(bf16[768,768]{1,0:T(8,128)(2,1)} %constant.8.clone.order_ref) | copy-start | bytes 3538948
  15.9 2.3 %copy-start.11 = (bf16[128,768]{1,0:T(8,128)(2,1)S(1)}, bf16[128,768]{1,0:T(8,128)(2,1)}, u32[]{:S(2)}) copy-start(bf16[128,768]{1,0:T(8,128)(2,1)} %get-tuple-element.46.hidden_ref) | copy-start | bytes 589828
  18.3 3.0 %copy-start.6 = (bf16[384,384]{1,0:T(8,128)(2,1)S(1)}, bf16[384,384]{1,0:T(8,128)(2,1)}, u32[]{:S(2)}) copy-start(bf16[384,384]{1,0:T(8,128)(2,1)} %constant.9.clone.spread_ref) | copy-start | bytes 884740
  18.3 3.0 %copy-start.10 = (bf16[128,2304]{1,0:T(8,128)(2,1)S(1)}, bf16[128,2304]{1,0:T(8,128)(2,1)}, u32[]{:S(2)}) copy-start(bf16[128,2304]{1,0:T(8,128)(2,1)} %get-tuple-element.39.proj_ref) | copy-start | bytes 1769476
  21.0 3.2 %collective-permute-start.9 = (bf16[384,768]{1,0:T(8,128)(2,1)S(1)}, bf16[384,768]{1,0:T(8,128)(2,1)S(1)}, u32[]{:S(2)}, u32[]{:S(2)}) collective-permute-start(bf16[384,768]{1,0:T(8,128)(2,1)S(1)} %get-tuple-element.57), channel_id=1, source_target_pairs={{0,4},{4,0},{8,12},{12,8},{16,20},{20,16},{24,28},{28,24},{32,36},... | collective-permute-start | bytes 1769480 | tf_op jit(solution)/shard_map/ppermute | solution.py:561
  24.2 12.1 %copy-start.7 = (bf16[128,96]{1,0:T(8,128)(2,1)S(1)}, bf16[128,96]{1,0:T(8,128)(2,1)}, u32[]{:S(2)}) copy-start(bf16[128,96]{1,0:T(8,128)(2,1)} %constant.10.clone.order_ref) | copy-start | bytes 73732
  24.4 9.3 %collective-permute-start.10 = (bf16[96,768]{1,0:T(8,128)(2,1)S(1)}, bf16[96,768]{1,0:T(8,128)(2,1)S(1)}, u32[]{:S(2)}, u32[]{:S(2)}) collective-permute-start(bf16[96,768]{1,0:T(8,128)(2,1)S(1)} %get-tuple-element.59), channel_id=1, source_target_pairs={{0,8},{4,12},{8,16},{12,20},{16,24},{20,28},{24,0},{28,4},{32,40},... | collective-permute-start | bytes 442376 | tf_op jit(solution)/shard_map/ppermute | solution.py:514
  26.0 10.3 %collective-permute-start.11 = (bf16[96,768]{1,0:T(8,128)(2,1)S(1)}, bf16[96,768]{1,0:T(8,128)(2,1)S(1)}, u32[]{:S(2)}, u32[]{:S(2)}) collective-permute-start(bf16[96,768]{1,0:T(8,128)(2,1)S(1)} %get-tuple-element.60), channel_id=1, source_target_pairs={{0,16},{4,20},{8,24},{12,28},{16,0},{20,4},{24,8},{28,12},{32,48},... | collective-permute-start | bytes 442376 | tf_op jit(solution)/shard_map/ppermute | solution.py:514
  28.9 7.4 %collective-permute-start.12 = (bf16[96,768]{1,0:T(8,128)(2,1)S(1)}, bf16[96,768]{1,0:T(8,128)(2,1)S(1)}, u32[]{:S(2)}, u32[]{:S(2)}) collective-permute-start(bf16[96,768]{1,0:T(8,128)(2,1)S(1)} %get-tuple-element.61), channel_id=1, source_target_pairs={{0,24},{4,28},{8,0},{12,4},{16,8},{20,12},{24,16},{28,20},{32,56},... | collective-permute-start | bytes 442376 | tf_op jit(solution)/shard_map/ppermute | solution.py:514
  30.2 13.6 %collective-permute-start.3 = (bf16[880,128]{1,0:T(8,128)(2,1)S(1)}, bf16[880,128]{1,0:T(8,128)(2,1)S(1)}, u32[]{:S(2)}, u32[]{:S(2)}) collective-permute-start(bf16[880,128]{1,0:T(8,128)(2,1)S(1)} %get-tuple-element.52), channel_id=1, source_target_pairs={{0,1},{1,2},{2,3},{3,0},{4,5},{5,6},{6,7},{7,4},{8,9},{9,10},{10,1... | collective-permute-start | bytes 675848 | tf_op jit(solution)/shard_map/ppermute | solution.py:514
  32.9 11.0 %collective-permute-start.4 = (bf16[880,128]{1,0:T(8,128)(2,1)S(1)}, bf16[880,128]{1,0:T(8,128)(2,1)S(1)}, u32[]{:S(2)}, u32[]{:S(2)}) collective-permute-start(bf16[880,128]{1,0:T(8,128)(2,1)S(1)} %get-tuple-element.53), channel_id=1, source_target_pairs={{0,2},{1,3},{2,0},{3,1},{4,6},{5,7},{6,4},{7,5},{8,10},{9,11},{10,... | collective-permute-start | bytes 675848 | tf_op jit(solution)/shard_map/ppermute | solution.py:514
  33.6 12.4 %collective-permute-start.5 = (bf16[880,128]{1,0:T(8,128)(2,1)S(1)}, bf16[880,128]{1,0:T(8,128)(2,1)S(1)}, u32[]{:S(2)}, u32[]{:S(2)}) collective-permute-start(bf16[880,128]{1,0:T(8,128)(2,1)S(1)} %get-tuple-element.54), channel_id=1, source_target_pairs={{0,3},{1,0},{2,1},{3,2},{4,7},{5,4},{6,5},{7,6},{8,11},{9,8},{10,9... | collective-permute-start | bytes 675848 | tf_op jit(solution)/shard_map/ppermute | solution.py:514
  36.3 9.8 %copy-start.3 = (bf16[128,768]{1,0:T(8,128)(2,1)S(1)}, bf16[128,768]{1,0:T(8,128)(2,1)}, u32[]{:S(2)}) copy-start(bf16[128,768]{1,0:T(8,128)(2,1)} %get-tuple-element.55.n0) | copy-start | bytes 589828
  36.5 10.6 %collective-permute-start.13 = (bf16[32,768]{1,0:T(8,128)(2,1)S(1)}, bf16[32,768]{1,0:T(8,128)(2,1)S(1)}, u32[]{:S(2)}, u32[]{:S(2)}) collective-permute-start(bf16[32,768]{1,0:T(8,128)(2,1)S(1)} %get-tuple-element.65), channel_id=1, source_target_pairs={{0,1},{1,2},{2,3},{3,0},{4,5},{5,6},{6,7},{7,4},{8,9},{9,10},{10,1... | collective-permute-start | bytes 147464 | tf_op jit(solution)/shard_map/ppermute | solution.py:514
  39.2 8.4 %collective-permute-start.14 = (bf16[32,768]{1,0:T(8,128)(2,1)S(1)}, bf16[32,768]{1,0:T(8,128)(2,1)S(1)}, u32[]{:S(2)}, u32[]{:S(2)}) collective-permute-start(bf16[32,768]{1,0:T(8,128)(2,1)S(1)} %get-tuple-element.66), channel_id=1, source_target_pairs={{0,2},{1,3},{2,0},{3,1},{4,6},{5,7},{6,4},{7,5},{8,10},{9,11},{10,... | collective-permute-start | bytes 147464 | tf_op jit(solution)/shard_map/ppermute | solution.py:514
  43.9 4.5 %collective-permute-start.15 = (bf16[32,768]{1,0:T(8,128)(2,1)S(1)}, bf16[32,768]{1,0:T(8,128)(2,1)S(1)}, u32[]{:S(2)}, u32[]{:S(2)}) collective-permute-start(bf16[32,768]{1,0:T(8,128)(2,1)S(1)} %get-tuple-element.67), channel_id=1, source_target_pairs={{0,3},{1,0},{2,1},{3,2},{4,7},{5,4},{6,5},{7,6},{8,11},{9,8},{10,9... | collective-permute-start | bytes 147464 | tf_op jit(solution)/shard_map/ppermute | solution.py:514
  48.5 2.0 %collective-permute-start.16 = (bf16[320,768]{1,0:T(8,128)(2,1)S(1)}, bf16[320,768]{1,0:T(8,128)(2,1)S(1)}, u32[]{:S(2)}, u32[]{:S(2)}) collective-permute-start(bf16[320,768]{1,0:T(8,128)(2,1)S(1)} %get-tuple-element.69), channel_id=1, source_target_pairs={{0,4},{4,0},{8,12},{12,8},{16,20},{20,16},{24,28},{28,24},{32,36},... | collective-permute-start | bytes 1474568 | tf_op jit(solution)/shard_map/ppermute | solution.py:594
  50.5 9.6 %copy-start.8 = (bf16[96,80]{1,0:T(8,128)(2,1)S(1)}, bf16[96,80]{1,0:T(8,128)(2,1)}, u32[]{:S(2)}) copy-start(bf16[96,80]{1,0:T(8,128)(2,1)} %constant.11.clone.order_ref) | copy-start | bytes 46084
  50.6 7.8 %collective-permute-start.17 = (bf16[80,768]{1,0:T(8,128)(2,1)S(1)}, bf16[80,768]{1,0:T(8,128)(2,1)S(1)}, u32[]{:S(2)}, u32[]{:S(2)}) collective-permute-start(bf16[80,768]{1,0:T(8,128)(2,1)S(1)} %get-tuple-element.71), channel_id=1, source_target_pairs={{0,16},{4,20},{8,24},{12,28},{16,0},{20,4},{24,8},{28,12},{32,48},... | collective-permute-start | bytes 368648 | tf_op jit(solution)/shard_map/ppermute | solution.py:514
  51.0 9.0 %collective-permute-start.18 = (bf16[80,768]{1,0:T(8,128)(2,1)S(1)}, bf16[80,768]{1,0:T(8,128)(2,1)S(1)}, u32[]{:S(2)}, u32[]{:S(2)}) collective-permute-start(bf16[80,768]{1,0:T(8,128)(2,1)S(1)} %get-tuple-element.72), channel_id=1, source_target_pairs={{0,8},{4,12},{8,16},{12,20},{16,24},{20,28},{24,0},{28,4},{32,40},... | collective-permute-start | bytes 368648 | tf_op jit(solution)/shard_map/ppermute | solution.py:514
  51.6 8.5 %collective-permute-start.19 = (bf16[80,768]{1,0:T(8,128)(2,1)S(1)}, bf16[80,768]{1,0:T(8,128)(2,1)S(1)}, u32[]{:S(2)}, u32[]{:S(2)}) collective-permute-start(bf16[80,768]{1,0:T(8,128)(2,1)S(1)} %get-tuple-element.73), channel_id=1, source_target_pairs={{0,24},{4,28},{8,0},{12,4},{16,8},{20,12},{24,16},{28,20},{32,56},... | collective-permute-start | bytes 368648 | tf_op jit(solution)/shard_map/ppermute | solution.py:514

commit v15 on v14

--- a/solution.py
+++ b/solution.py
@@ -567,10 +567,10 @@
         8.0,
     )
     got = swap(sent, "seq", SEQ_TURNS)
-    out = call(out_core_kernel, [shape(SUB, D)] * NY, (out_mine, out_other, sent[0], norms[1], norms[3], norms[2]), unread=4)
+    out = call(out_core_kernel, [shape(SUB, D)] * NY, (out_mine, out_other, sent[0], norms[1], norms[3], norms[2]), unread=4, micros=0.01)
     out = swap(out, "slide", Y_TURNS)
     out_sums = call(
-        out_y_kernel, [shape(32, D)] * N_SEQ, (*out, out_pad_order())
+        out_y_kernel, [shape(32, D)] * N_SEQ, (*out, out_pad_order()), (), 0.01
     )
     out = swap(out_sums, "seq", SEQ_TURNS)
     whole, tail = call(

time: 80.4 us -> 80.8 us (level)
  starting transfers between devices: 27.1 us -> 30.8 us
  waiting for transfers between devices: 16.2 us -> 13.2 us
    ppermute x18, starting transfers between devices: 26.7 us -> 30.5 us  [swap(): got = {t: lax.ppermute(arrays[t], axis, turns[t]) for t in order}]
    ppermute x18, waiting for transfers between devices: 14.4 us -> 11.4 us  [swap(): got = {t: lax.ppermute(arrays[t], axis, turns[t]) for t in order}]
  transfers between devices with their start and end apart: 20 -> 20, of which waited for: 9 -> 8; matrix products, arithmetic and copies ran while one was open for 0% -> 0% of each run, Pallas kernels for 11% -> 11%
where the time goes in v15:
time: 80.8 us; the launch traced here: 79.9 us
  starting transfers between devices  30.8 us (38%)
  blocking collectives  18.2 us (23%)
  Pallas kernels  14.9 us (18%)
  waiting for transfers between devices  13.2 us (16%)
  between operations  1.51 us (2%)
  local copies, waits for them, and re-layouts  1.3 us (2%)
    ppermute x18, starting transfers between devices, swap(): got = {t: lax.ppermute(arrays[t], axis, turns[t]) for t in order}  30.5 us
    all_to_all x1, blocking collectives, per_device(): lax.all_to_all(by_z, 'slide', 0, 0, tiled=True, axis_index_groups=Z_GROUPS)  18.2 us
    pallas_call x11, Pallas kernels, call(): pl.pallas_call(kernel, out_shape=out_shapes, in_specs=specs, out_specs=[V...  14.9 us
    ppermute x18, waiting for transfers between devices, swap(): got = {t: lax.ppermute(arrays[t], axis, turns[t]) for t in order}  11.4 us
    ppermute x1, waiting for transfers between devices, per_device(): other = lax.ppermute(other, 'slide', CORE_PAIRS)  1.85 us
  transfers between devices with their start and end apart: 20, of which 8 were waited for; matrix products, arithmetic and copies ran while one was open for 0% of the time, Pallas kernels for 11%

profile of v15, /device:TPU:2, one launch (start us, length us, event | category | flops | bytes accessed | tf_op | source)
XLA Modules:
  0.0 79.9 jit_solution(9657098426397972532)
XLA Ops:
  0.7 4.4 %shard_map.122 = (bf16[128,768]{1,0:T(8,128)(2,1)}, bf16[128,768]{1,0:T(8,128)(2,1)}, bf16[128,2304]{1,0:T(8,128)(2,1)}, bf16[32,1536]{1,0:T(8,128)(2,1)}) custom-call(bf16[1,128,1536]{2,1,0:T(8,128)(2,1)} %tiles_ref.1, s32[1,128]{1,0:T(1,128)} %masked_ref.1, f32[768]{0:T(1024)} %gain_hbm.1, bf16[1536,768]{1,0:T(8,128)(2,1)} %w_in_ref.1, ...), custom_call_target="tpu_custom_call" | custom-call | flops 4000000000 | bytes 4000000 | tf_op jit(solution)/shard_map/pallas_call | solution.py:478
  5.1 2.2 %collective-permute-start = (bf16[32,1536]{1,0:T(8,128)(2,1)}, bf16[32,1536]{1,0:T(8,128)(2,1)S(1)}, u32[]{:S(2)}, u32[]{:S(2)}) collective-permute-start(bf16[32,1536]{1,0:T(8,128)(2,1)} %get-tuple-element.40), channel_id=1, source_target_pairs={{0,2},{1,3},{2,0},{3,1},{4,6},{5,7},{6,4},{7,5},{8,10},{9,11},{10,... | collective-permute-start | bytes 294920 | tf_op jit(solution)/shard_map/ppermute | solution.py:514
  7.3 1.6 %collective-permute-start.1 = (bf16[32,1536]{1,0:T(8,128)(2,1)}, bf16[32,1536]{1,0:T(8,128)(2,1)S(1)}, u32[]{:S(2)}, u32[]{:S(2)}) collective-permute-start(bf16[32,1536]{1,0:T(8,128)(2,1)} %get-tuple-element.40), channel_id=1, source_target_pairs={{0,1},{1,2},{2,3},{3,0},{4,5},{5,6},{6,7},{7,4},{8,9},{9,10},{10,1... | collective-permute-start | bytes 294920 | tf_op jit(solution)/shard_map/ppermute | solution.py:514
  8.9 0.4 collective-permute-start.2
  9.3 1.6 %collective-permute-start.6 = (bf16[128,768]{1,0:T(8,128)(2,1)}, bf16[128,768]{1,0:T(8,128)(2,1)S(1)}, u32[]{:S(2)}, u32[]{:S(2)}) collective-permute-start(bf16[128,768]{1,0:T(8,128)(2,1)} %get-tuple-element.55.n0), channel_id=1, source_target_pairs={{0,1},{1,2},{2,3},{3,0},{4,5},{5,6},{6,7},{7,4},{8,9},{9,10},{10,1... | collective-permute-start | bytes 589832 | tf_op jit(solution)/shard_map/ppermute | solution.py:514
  10.9 1.0 %collective-permute-start.7 = (bf16[128,768]{1,0:T(8,128)(2,1)}, bf16[128,768]{1,0:T(8,128)(2,1)S(1)}, u32[]{:S(2)}, u32[]{:S(2)}) collective-permute-start(bf16[128,768]{1,0:T(8,128)(2,1)} %get-tuple-element.55.n0), channel_id=1, source_target_pairs={{0,3},{1,0},{2,1},{3,2},{4,7},{5,4},{6,5},{7,6},{8,11},{9,8},{10,9... | collective-permute-start | bytes 589832 | tf_op jit(solution)/shard_map/ppermute | solution.py:514
  12.6 0.0 collective-permute-done.f2
  12.6 2.2 %collective-permute-start.8 = (bf16[128,768]{1,0:T(8,128)(2,1)}, bf16[128,768]{1,0:T(8,128)(2,1)S(1)}, u32[]{:S(2)}, u32[]{:S(2)}) collective-permute-start(bf16[128,768]{1,0:T(8,128)(2,1)} %get-tuple-element.55.n0), channel_id=1, source_target_pairs={{0,2},{1,3},{2,0},{3,1},{4,6},{5,7},{6,4},{7,5},{8,10},{9,11},{10,... | collective-permute-start | bytes 589832 | tf_op jit(solution)/shard_map/ppermute | solution.py:514
  14.8 0.1 collective-permute-done.2.f3
  14.9 1.1 %copy-done.9 = bf16[128,2304]{1,0:T(8,128)(2,1)S(1)} copy-done((bf16[128,2304]{1,0:T(8,128)(2,1)S(1)}, bf16[128,2304]{1,0:T(8,128)(2,1)}, u32[]{:S(2)}) %copy-start.9) | copy-done | bytes 589848
  15.9 2.1 %shard_map.123 = (bf16[128,768]{1,0:T(8,128)(2,1)S(1)}, bf16[128,768]{1,0:T(8,128)(2,1)S(1)}, f32[4,128,512]{2,1,0:T(8,128)S(1)}, f32[4,128,128]{2,1,0:T(8,128)S...) custom-call(s32[1,1]{1,0:T(1,128)} %bitcast.2.count_ref, ...), custom_call_target="tpu_custom_call" | custom-call | flops 2000000000 | bytes 2000000 | tf_op jit(solution)/shard_map/pallas_call | solution.py:478
  18.1 0.2 copy-done.6
  18.3 0.0 copy-done.11
  18.3 2.7 %shard_map.124 = (bf16[128,768]{1,0:T(8,128)(2,1)S(1)}, bf16[16,128]{1,0:T(8,128)(2,1)S(1)}, bf16[384,768]{1,0:T(8,128)(2,1)S(1)}, bf16[384,768]{1,0:T(8,128)(2,1)S(1)}) custom-call(bf16[128,768]{1,0:T(8,128)(2,1)S(1)} %get-tuple-element.45.att_ref, bf16[128,768]{1,0:T(8,128)(2,1)S(1)} %copy-done.11, bf16[128,1536]{1,0:T(8,128)(2,1)S(1)} %get-tuple-element.47.tiles_ref, ...), custom_call_target="tpu_custom_call" | custom-call | flops 3000000000 | bytes 3000000 | tf_op jit(solution)/shard_map/pallas_call | solution.py:478
  21.0 0.3 collective-permute-start.9
  21.3 2.8 %shard_map.125 = (bf16[880,128]{1,0:T(8,128)(2,1)S(1)}, bf16[880,128]{1,0:T(8,128)(2,1)S(1)}, bf16[880,128]{1,0:T(8,128)(2,1)S(1)}, bf16[880,128]{1,0:T(8,128)(2,1)S(1)}) custom-call(bf16[128,2304]{1,0:T(8,128)(2,1)S(1)} %copy-done.10, bf16[128,768]{1,0:T(8,128)(2,1)S(1)} %get-tuple-element.41.fk_ref, bf16[128,768]{1,0:T(8,128)(2,1)S(1)} %get-tuple-element.42.fv_ref, ...), custom_call_target="tpu_custom_call" | custom-call | flops 8000000000 | bytes 8000000 | tf_op jit(solution)/shard_map/pallas_call | solution.py:478
  24.2 0.0 copy-start
  24.2 0.0 collective-permute-done.6.wait1.n1
  24.2 0.0 collective-permute-done.7.wait2.n3
  24.2 0.0 collective-permute-done.9.other_ref
  24.2 0.2 shard_map.126
  24.4 1.6 %collective-permute-start.10 = (bf16[96,768]{1,0:T(8,128)(2,1)S(1)}, bf16[96,768]{1,0:T(8,128)(2,1)S(1)}, u32[]{:S(2)}, u32[]{:S(2)}) collective-permute-start(bf16[96,768]{1,0:T(8,128)(2,1)S(1)} %get-tuple-element.59), channel_id=1, source_target_pairs={{0,8},{4,12},{8,16},{12,20},{16,24},{20,28},{24,0},{28,4},{32,40},... | collective-permute-start | bytes 442376 | tf_op jit(solution)/shard_map/ppermute | solution.py:514
  26.0 2.6 %collective-permute-start.3 = (bf16[880,128]{1,0:T(8,128)(2,1)S(1)}, bf16[880,128]{1,0:T(8,128)(2,1)S(1)}, u32[]{:S(2)}, u32[]{:S(2)}) collective-permute-start(bf16[880,128]{1,0:T(8,128)(2,1)S(1)} %get-tuple-element.52), channel_id=1, source_target_pairs={{0,1},{1,2},{2,3},{3,0},{4,5},{5,6},{6,7},{7,4},{8,9},{9,10},{10,1... | collective-permute-start | bytes 675848 | tf_op jit(solution)/shard_map/ppermute | solution.py:514
  28.6 0.8 collective-permute-start.4
  29.4 1.3 %collective-permute-start.5 = (bf16[880,128]{1,0:T(8,128)(2,1)S(1)}, bf16[880,128]{1,0:T(8,128)(2,1)S(1)}, u32[]{:S(2)}, u32[]{:S(2)}) collective-permute-start(bf16[880,128]{1,0:T(8,128)(2,1)S(1)} %get-tuple-element.54), channel_id=1, source_target_pairs={{0,3},{1,0},{2,1},{3,2},{4,7},{5,4},{6,5},{7,6},{8,11},{9,8},{10,9... | collective-permute-start | bytes 675848 | tf_op jit(solution)/shard_map/ppermute | solution.py:514
  30.7 2.9 %collective-permute-start.11 = (bf16[96,768]{1,0:T(8,128)(2,1)S(1)}, bf16[96,768]{1,0:T(8,128)(2,1)S(1)}, u32[]{:S(2)}, u32[]{:S(2)}) collective-permute-start(bf16[96,768]{1,0:T(8,128)(2,1)S(1)} %get-tuple-element.60), channel_id=1, source_target_pairs={{0,16},{4,20},{8,24},{12,28},{16,0},{20,4},{24,8},{28,12},{32,48},... | collective-permute-start | bytes 442376 | tf_op jit(solution)/shard_map/ppermute | solution.py:514
  33.6 0.0 collective-permute-done.10.y1
  33.6 1.3 %collective-permute-start.12 = (bf16[96,768]{1,0:T(8,128)(2,1)S(1)}, bf16[96,768]{1,0:T(8,128)(2,1)S(1)}, u32[]{:S(2)}, u32[]{:S(2)}) collective-permute-start(bf16[96,768]{1,0:T(8,128)(2,1)S(1)} %get-tuple-element.61), channel_id=1, source_target_pairs={{0,24},{4,28},{8,0},{12,4},{16,8},{20,12},{24,16},{28,20},{32,56},... | collective-permute-start | bytes 442376 | tf_op jit(solution)/shard_map/ppermute | solution.py:514
  35.0 2.6 %collective-permute-done.11.y2 = bf16[96,768]{1,0:T(8,128)(2,1)S(1)} collective-permute-done((bf16[96,768]{1,0:T(8,128)(2,1)S(1)}, bf16[96,768]{1,0:T(8,128)(2,1)S(1)}, u32[]{:S(2)}, u32[]{:S(2)}) %collective-permute-start.11) | collective-permute-done | bytes 147488 | tf_op jit(solution)/shard_map/ppermute | solution.py:514
  37.6 2.4 %collective-permute-done.12.y3 = bf16[96,768]{1,0:T(8,128)(2,1)S(1)} collective-permute-done((bf16[96,768]{1,0:T(8,128)(2,1)S(1)}, bf16[96,768]{1,0:T(8,128)(2,1)S(1)}, u32[]{:S(2)}, u32[]{:S(2)}) %collective-permute-start.12) | collective-permute-done | bytes 147488 | tf_op jit(solution)/shard_map/ppermute | solution.py:514
  40.0 0.3 shard_map.127
  40.2 0.4 collective-permute-start.13
  40.7 4.0 %collective-permute-start.14 = (bf16[32,768]{1,0:T(8,128)(2,1)S(1)}, bf16[32,768]{1,0:T(8,128)(2,1)S(1)}, u32[]{:S(2)}, u32[]{:S(2)}) collective-permute-start(bf16[32,768]{1,0:T(8,128)(2,1)S(1)} %get-tuple-element.66), channel_id=1, source_target_pairs={{0,2},{1,3},{2,0},{3,1},{4,6},{5,7},{6,4},{7,5},{8,10},{9,11},{10,... | collective-permute-start | bytes 147464 | tf_op jit(solution)/shard_map/ppermute | solution.py:514
  44.7 1.1 %shard_map.128 = (f32[576,768]{1,0:T(8,128)S(1)}, f32[80,768]{1,0:T(8,128)S(1)}) custom-call(bf16[880,128]{1,0:T(8,128)(2,1)S(1)} %get-tuple-element.51.wait0.x0, bf16[880,128]{1,0:T(8,128)(2,1)S(1)} %collective-permute-done.3.x1, bf16[880,128]{1,0:T(8,128)(2,1)S(1)} %collective-permute-done.4.x2, bf16[880,128]{1,0:T(8,128)(2,1)S(1)} %collective-permute-done.5.x3, ...), custom_call_target="tpu_custom_call" | custom-call | flops 15000000512 | bytes 15000000 | tf_op jit(solution)/shard_map/pallas_call | solution.py:478
  45.8 0.9 %collective-permute-done.14.wait2.o2 = bf16[32,768]{1,0:T(8,128)(2,1)S(1)} collective-permute-done((bf16[32,768]{1,0:T(8,128)(2,1)S(1)}, bf16[32,768]{1,0:T(8,128)(2,1)S(1)}, u32[]{:S(2)}, u32[]{:S(2)}) %collective-permute-start.14) | collective-permute-done | bytes 49184 | tf_op jit(solution)/shard_map/ppermute | solution.py:514
  46.7 2.0 %collective-permute-done.15.wait3.o3 = bf16[32,768]{1,0:T(8,128)(2,1)S(1)} collective-permute-done((bf16[32,768]{1,0:T(8,128)(2,1)S(1)}, bf16[32,768]{1,0:T(8,128)(2,1)S(1)}, u32[]{:S(2)}, u32[]{:S(2)}) %collective-permute-start.15) | collective-permute-done | bytes 49184 | tf_op jit(solution)/shard_map/ppermute | solution.py:514
  48.7 0.1 shard_map.129
  48.9 0.1 collective-permute-start.16
  49.0 1.9 %collective-permute-done.16.other_ref = bf16[320,768]{1,0:T(8,128)(2,1)S(1)} collective-permute-done((bf16[320,768]{1,0:T(8,128)(2,1)S(1)}, bf16[320,768]{1,0:T(8,128)(2,1)S(1)}, u32[]{:S(2)}, u32[]{:S(2)}) %collective-permute-start.16) | collective-permute-done | bytes 491552 | tf_op jit(solution)/shard_map/ppermute | solution.py:594
  50.8 0.2 shard_map.130
  51.0 3.2 %collective-permute-start.17 = (bf16[80,768]{1,0:T(8,128)(2,1)S(1)}, bf16[80,768]{1,0:T(8,128)(2,1)S(1)}, u32[]{:S(2)}, u32[]{:S(2)}) collective-permute-start(bf16[80,768]{1,0:T(8,128)(2,1)S(1)} %get-tuple-element.71), channel_id=1, source_target_pairs={{0,16},{4,20},{8,24},{12,28},{16,0},{20,4},{24,8},{28,12},{32,48},... | collective-permute-start | bytes 368648 | tf_op jit(solution)/shard_map/ppermute | solution.py:514
  54.2 0.4 collective-permute-start.18
  54.6 2.8 %collective-permute-start.19 = (bf16[80,768]{1,0:T(8,128)(2,1)S(1)}, bf16[80,768]{1,0:T(8,128)(2,1)S(1)}, u32[]{:S(2)}, u32[]{:S(2)}) collective-permute-start(bf16[80,768]{1,0:T(8,128)(2,1)S(1)} %get-tuple-element.73), channel_id=1, source_target_pairs={{0,24},{4,28},{8,0},{12,4},{16,8},{20,12},{24,16},{28,20},{32,56},... | collective-permute-start | bytes 368648 | tf_op jit(solution)/shard_map/ppermute | solution.py:514
  57.4 1.1 %collective-permute-done.17.y1 = bf16[80,768]{1,0:T(8,128)(2,1)S(1)} collective-permute-done((bf16[80,768]{1,0:T(8,128)(2,1)S(1)}, bf16[80,768]{1,0:T(8,128)(2,1)S(1)}, u32[]{:S(2)}, u32[]{:S(2)}) %collective-permute-start.17) | collective-permute-done | bytes 122912 | tf_op jit(solution)/shard_map/ppermute | solution.py:514
  58.5 2.3 %collective-permute-done.18.y2 = bf16[80,768]{1,0:T(8,128)(2,1)S(1)} collective-permute-done((bf16[80,768]{1,0:T(8,128)(2,1)S(1)}, bf16[80,768]{1,0:T(8,128)(2,1)S(1)}, u32[]{:S(2)}, u32[]{:S(2)}) %collective-permute-start.18) | collective-permute-done | bytes 122912 | tf_op jit(solution)/shard_map/ppermute | solution.py:514
  60.8 0.3 shard_map.131
  61.1 18.2 %all_to_all.5.in_ref = bf16[8,16,768]{2,1,0:T(8,128)(2,1)S(1)} all-to-all(bf16[8,16,768]{2,1,0:T(8,128)(2,1)S(1)} %shard_map.131), channel_id=1, replica_groups={{0,32,64,96,128,160,192,224},{4,36,68,100,132,164,196,228},{8,40,72,104..., dimensions={0} | all-to-all | bytes 393216 | tf_op jit(solution)/shard_map/all_to_all | solution.py:602
  79.3 0.7 shard_map.132
  (28 shorter events, 0.1 us)
Async XLA Ops:
  0.6 14.2 %copy-start.3 = (bf16[1,128,1536]{2,1,0:T(8,128)(2,1)S(1)}, bf16[1,128,1536]{2,1,0:T(8,128)(2,1)}, u32[]{:S(2)}) copy-start(bf16[1,128,1536]{2,1,0:T(8,128)(2,1)} %tiles_ref.1) | copy-start | bytes 1179652
  0.6 14.2 %copy-start.5 = (s32[1,128]{1,0:T(1,128)S(1)}, s32[1,128]{1,0:T(1,128)}, u32[]{:S(2)}) copy-start(s32[1,128]{1,0:T(1,128)} %masked_ref.1) | copy-start | bytes 1540
  5.1 7.5 %collective-permute-start = (bf16[32,1536]{1,0:T(8,128)(2,1)}, bf16[32,1536]{1,0:T(8,128)(2,1)S(1)}, u32[]{:S(2)}, u32[]{:S(2)}) collective-permute-start(bf16[32,1536]{1,0:T(8,128)(2,1)} %get-tuple-element.40), channel_id=1, source_target_pairs={{0,2},{1,3},{2,0},{3,1},{4,6},{5,7},{6,4},{7,5},{8,10},{9,11},{10,... | collective-permute-start | bytes 294920 | tf_op jit(solution)/shard_map/ppermute | solution.py:514
  7.3 7.5 %collective-permute-start.1 = (bf16[32,1536]{1,0:T(8,128)(2,1)}, bf16[32,1536]{1,0:T(8,128)(2,1)S(1)}, u32[]{:S(2)}, u32[]{:S(2)}) collective-permute-start(bf16[32,1536]{1,0:T(8,128)(2,1)} %get-tuple-element.40), channel_id=1, source_target_pairs={{0,1},{1,2},{2,3},{3,0},{4,5},{5,6},{6,7},{7,4},{8,9},{9,10},{10,1... | collective-permute-start | bytes 294920 | tf_op jit(solution)/shard_map/ppermute | solution.py:514
  8.9 5.9 %collective-permute-start.2 = (bf16[32,1536]{1,0:T(8,128)(2,1)}, bf16[32,1536]{1,0:T(8,128)(2,1)S(1)}, u32[]{:S(2)}, u32[]{:S(2)}) collective-permute-start(bf16[32,1536]{1,0:T(8,128)(2,1)} %get-tuple-element.40), channel_id=1, source_target_pairs={{0,3},{1,0},{2,1},{3,2},{4,7},{5,4},{6,5},{7,6},{8,11},{9,8},{10,9... | collective-permute-start | bytes 294920 | tf_op jit(solution)/shard_map/ppermute | solution.py:514
  9.3 14.9 %collective-permute-start.6 = (bf16[128,768]{1,0:T(8,128)(2,1)}, bf16[128,768]{1,0:T(8,128)(2,1)S(1)}, u32[]{:S(2)}, u32[]{:S(2)}) collective-permute-start(bf16[128,768]{1,0:T(8,128)(2,1)} %get-tuple-element.55.n0), channel_id=1, source_target_pairs={{0,1},{1,2},{2,3},{3,0},{4,5},{5,6},{6,7},{7,4},{8,9},{9,10},{10,1... | collective-permute-start | bytes 589832 | tf_op jit(solution)/shard_map/ppermute | solution.py:514
  10.9 13.3 %collective-permute-start.7 = (bf16[128,768]{1,0:T(8,128)(2,1)}, bf16[128,768]{1,0:T(8,128)(2,1)S(1)}, u32[]{:S(2)}, u32[]{:S(2)}) collective-permute-start(bf16[128,768]{1,0:T(8,128)(2,1)} %get-tuple-element.55.n0), channel_id=1, source_target_pairs={{0,3},{1,0},{2,1},{3,2},{4,7},{5,4},{6,5},{7,6},{8,11},{9,8},{10,9... | collective-permute-start | bytes 589832 | tf_op jit(solution)/shard_map/ppermute | solution.py:514
  12.6 11.6 %collective-permute-start.8 = (bf16[128,768]{1,0:T(8,128)(2,1)}, bf16[128,768]{1,0:T(8,128)(2,1)S(1)}, u32[]{:S(2)}, u32[]{:S(2)}) collective-permute-start(bf16[128,768]{1,0:T(8,128)(2,1)} %get-tuple-element.55.n0), channel_id=1, source_target_pairs={{0,2},{1,3},{2,0},{3,1},{4,6},{5,7},{6,4},{7,5},{8,10},{9,11},{10,... | collective-permute-start | bytes 589832 | tf_op jit(solution)/shard_map/ppermute | solution.py:514
  14.9 1.1 %copy-start.9 = (bf16[128,2304]{1,0:T(8,128)(2,1)S(1)}, bf16[128,2304]{1,0:T(8,128)(2,1)}, u32[]{:S(2)}) copy-start(bf16[128,2304]{1,0:T(8,128)(2,1)} %get-tuple-element.39.proj_ref) | copy-start | bytes 1769476
  15.9 2.1 %copy-start.1 = (bf16[1536,768]{1,0:T(8,128)(2,1)S(1)}, bf16[1536,768]{1,0:T(8,128)(2,1)}, u32[]{:S(2)}) copy-start(bf16[1536,768]{1,0:T(8,128)(2,1)} %w_in_ref.1) | copy-start | bytes 7077892
  15.9 2.1 %copy-start.2 = (bf16[768,768]{1,0:T(8,128)(2,1)S(1)}, bf16[768,768]{1,0:T(8,128)(2,1)}, u32[]{:S(2)}) copy-start(bf16[768,768]{1,0:T(8,128)(2,1)} %w_out_ref.1) | copy-start | bytes 3538948
  15.9 2.3 %copy-start.6 = (bf16[768,768]{1,0:T(8,128)(2,1)S(1)}, bf16[768,768]{1,0:T(8,128)(2,1)}, u32[]{:S(2)}) copy-start(bf16[768,768]{1,0:T(8,128)(2,1)} %constant.8.clone.order_ref) | copy-start | bytes 3538948
  15.9 2.3 %copy-start.11 = (bf16[128,768]{1,0:T(8,128)(2,1)S(1)}, bf16[128,768]{1,0:T(8,128)(2,1)}, u32[]{:S(2)}) copy-start(bf16[128,768]{1,0:T(8,128)(2,1)} %get-tuple-element.46.hidden_ref) | copy-start | bytes 589828
  18.3 3.0 %copy-start.7 = (bf16[384,384]{1,0:T(8,128)(2,1)S(1)}, bf16[384,384]{1,0:T(8,128)(2,1)}, u32[]{:S(2)}) copy-start(bf16[384,384]{1,0:T(8,128)(2,1)} %constant.9.clone.spread_ref) | copy-start | bytes 884740
  18.3 3.0 %copy-start.10 = (bf16[128,2304]{1,0:T(8,128)(2,1)S(1)}, bf16[128,2304]{1,0:T(8,128)(2,1)}, u32[]{:S(2)}) copy-start(bf16[128,2304]{1,0:T(8,128)(2,1)} %get-tuple-element.39.proj_ref) | copy-start | bytes 1769476
  21.0 3.2 %collective-permute-start.9 = (bf16[384,768]{1,0:T(8,128)(2,1)S(1)}, bf16[384,768]{1,0:T(8,128)(2,1)S(1)}, u32[]{:S(2)}, u32[]{:S(2)}) collective-permute-start(bf16[384,768]{1,0:T(8,128)(2,1)S(1)} %get-tuple-element.57), channel_id=1, source_target_pairs={{0,4},{4,0},{8,12},{12,8},{16,20},{20,16},{24,28},{28,24},{32,36},... | collective-permute-start | bytes 1769480 | tf_op jit(solution)/shard_map/ppermute | solution.py:561
  24.2 15.8 %copy-start = (bf16[128,96]{1,0:T(8,128)(2,1)S(1)}, bf16[128,96]{1,0:T(8,128)(2,1)}, u32[]{:S(2)}) copy-start(bf16[128,96]{1,0:T(8,128)(2,1)} %constant.10.clone.order_ref) | copy-start | bytes 73732
  24.2 20.5 %copy-start.4 = (bf16[128,768]{1,0:T(8,128)(2,1)S(1)}, bf16[128,768]{1,0:T(8,128)(2,1)}, u32[]{:S(2)}) copy-start(bf16[128,768]{1,0:T(8,128)(2,1)} %get-tuple-element.55.n0) | copy-start | bytes 589828
  24.4 9.3 %collective-permute-start.10 = (bf16[96,768]{1,0:T(8,128)(2,1)S(1)}, bf16[96,768]{1,0:T(8,128)(2,1)S(1)}, u32[]{:S(2)}, u32[]{:S(2)}) collective-permute-start(bf16[96,768]{1,0:T(8,128)(2,1)S(1)} %get-tuple-element.59), channel_id=1, source_target_pairs={{0,8},{4,12},{8,16},{12,20},{16,24},{20,28},{24,0},{28,4},{32,40},... | collective-permute-start | bytes 442376 | tf_op jit(solution)/shard_map/ppermute | solution.py:514
  26.0 18.7 %collective-permute-start.3 = (bf16[880,128]{1,0:T(8,128)(2,1)S(1)}, bf16[880,128]{1,0:T(8,128)(2,1)S(1)}, u32[]{:S(2)}, u32[]{:S(2)}) collective-permute-start(bf16[880,128]{1,0:T(8,128)(2,1)S(1)} %get-tuple-element.52), channel_id=1, source_target_pairs={{0,1},{1,2},{2,3},{3,0},{4,5},{5,6},{6,7},{7,4},{8,9},{9,10},{10,1... | collective-permute-start | bytes 675848 | tf_op jit(solution)/shard_map/ppermute | solution.py:514
  28.6 16.0 %collective-permute-start.4 = (bf16[880,128]{1,0:T(8,128)(2,1)S(1)}, bf16[880,128]{1,0:T(8,128)(2,1)S(1)}, u32[]{:S(2)}, u32[]{:S(2)}) collective-permute-start(bf16[880,128]{1,0:T(8,128)(2,1)S(1)} %get-tuple-element.53), channel_id=1, source_target_pairs={{0,2},{1,3},{2,0},{3,1},{4,6},{5,7},{6,4},{7,5},{8,10},{9,11},{10,... | collective-permute-start | bytes 675848 | tf_op jit(solution)/shard_map/ppermute | solution.py:514
  29.4 15.3 %collective-permute-start.5 = (bf16[880,128]{1,0:T(8,128)(2,1)S(1)}, bf16[880,128]{1,0:T(8,128)(2,1)S(1)}, u32[]{:S(2)}, u32[]{:S(2)}) collective-permute-start(bf16[880,128]{1,0:T(8,128)(2,1)S(1)} %get-tuple-element.54), channel_id=1, source_target_pairs={{0,3},{1,0},{2,1},{3,2},{4,7},{5,4},{6,5},{7,6},{8,11},{9,8},{10,9... | collective-permute-start | bytes 675848 | tf_op jit(solution)/shard_map/ppermute | solution.py:514
  30.7 6.8 %collective-permute-start.11 = (bf16[96,768]{1,0:T(8,128)(2,1)S(1)}, bf16[96,768]{1,0:T(8,128)(2,1)S(1)}, u32[]{:S(2)}, u32[]{:S(2)}) collective-permute-start(bf16[96,768]{1,0:T(8,128)(2,1)S(1)} %get-tuple-element.60), channel_id=1, source_target_pairs={{0,16},{4,20},{8,24},{12,28},{16,0},{20,4},{24,8},{28,12},{32,48},... | collective-permute-start | bytes 442376 | tf_op jit(solution)/shard_map/ppermute | solution.py:514
  33.6 6.3 %collective-permute-start.12 = (bf16[96,768]{1,0:T(8,128)(2,1)S(1)}, bf16[96,768]{1,0:T(8,128)(2,1)S(1)}, u32[]{:S(2)}, u32[]{:S(2)}) collective-permute-start(bf16[96,768]{1,0:T(8,128)(2,1)S(1)} %get-tuple-element.61), channel_id=1, source_target_pairs={{0,24},{4,28},{8,0},{12,4},{16,8},{20,12},{24,16},{28,20},{32,56},... | collective-permute-start | bytes 442376 | tf_op jit(solution)/shard_map/ppermute | solution.py:514
  40.2 5.6 %collective-permute-start.13 = (bf16[32,768]{1,0:T(8,128)(2,1)S(1)}, bf16[32,768]{1,0:T(8,128)(2,1)S(1)}, u32[]{:S(2)}, u32[]{:S(2)}) collective-permute-start(bf16[32,768]{1,0:T(8,128)(2,1)S(1)} %get-tuple-element.65), channel_id=1, source_target_pairs={{0,1},{1,2},{2,3},{3,0},{4,5},{5,6},{6,7},{7,4},{8,9},{9,10},{10,1... | collective-permute-start | bytes 147464 | tf_op jit(solution)/shard_map/ppermute | solution.py:514
  40.7 6.0 %collective-permute-start.14 = (bf16[32,768]{1,0:T(8,128)(2,1)S(1)}, bf16[32,768]{1,0:T(8,128)(2,1)S(1)}, u32[]{:S(2)}, u32[]{:S(2)}) collective-permute-start(bf16[32,768]{1,0:T(8,128)(2,1)S(1)} %get-tuple-element.66), channel_id=1, source_target_pairs={{0,2},{1,3},{2,0},{3,1},{4,6},{5,7},{6,4},{7,5},{8,10},{9,11},{10,... | collective-permute-start | bytes 147464 | tf_op jit(solution)/shard_map/ppermute | solution.py:514
  44.6 4.1 %collective-permute-start.15 = (bf16[32,768]{1,0:T(8,128)(2,1)S(1)}, bf16[32,768]{1,0:T(8,128)(2,1)S(1)}, u32[]{:S(2)}, u32[]{:S(2)}) collective-permute-start(bf16[32,768]{1,0:T(8,128)(2,1)S(1)} %get-tuple-element.67), channel_id=1, source_target_pairs={{0,3},{1,0},{2,1},{3,2},{4,7},{5,4},{6,5},{7,6},{8,11},{9,8},{10,9... | collective-permute-start | bytes 147464 | tf_op jit(solution)/shard_map/ppermute | solution.py:514
  48.9 2.0 %collective-permute-start.16 = (bf16[320,768]{1,0:T(8,128)(2,1)S(1)}, bf16[320,768]{1,0:T(8,128)(2,1)S(1)}, u32[]{:S(2)}, u32[]{:S(2)}) collective-permute-start(bf16[320,768]{1,0:T(8,128)(2,1)S(1)} %get-tuple-element.69), channel_id=1, source_target_pairs={{0,4},{4,0},{8,12},{12,8},{16,20},{20,16},{24,28},{28,24},{32,36},... | collective-permute-start | bytes 1474568 | tf_op jit(solution)/shard_map/ppermute | solution.py:594
  50.8 10.0 %copy-start.8 = (bf16[96,80]{1,0:T(8,128)(2,1)S(1)}, bf16[96,80]{1,0:T(8,128)(2,1)}, u32[]{:S(2)}) copy-start(bf16[96,80]{1,0:T(8,128)(2,1)} %constant.11.clone.order_ref) | copy-start | bytes 46084
  51.0 7.5 %collective-permute-start.17 = (bf16[80,768]{1,0:T(8,128)(2,1)S(1)}, bf16[80,768]{1,0:T(8,128)(2,1)S(1)}, u32[]{:S(2)}, u32[]{:S(2)}) collective-permute-start(bf16[80,768]{1,0:T(8,128)(2,1)S(1)} %get-tuple-element.71), channel_id=1, source_target_pairs={{0,16},{4,20},{8,24},{12,28},{16,0},{20,4},{24,8},{28,12},{32,48},... | collective-permute-start | bytes 368648 | tf_op jit(solution)/shard_map/ppermute | solution.py:514
  54.2 6.6 %collective-permute-start.18 = (bf16[80,768]{1,0:T(8,128)(2,1)S(1)}, bf16[80,768]{1,0:T(8,128)(2,1)S(1)}, u32[]{:S(2)}, u32[]{:S(2)}) collective-permute-start(bf16[80,768]{1,0:T(8,128)(2,1)S(1)} %get-tuple-element.72), channel_id=1, source_target_pairs={{0,8},{4,12},{8,16},{12,20},{16,24},{20,28},{24,0},{28,4},{32,40},... | collective-permute-start | bytes 368648 | tf_op jit(solution)/shard_map/ppermute | solution.py:514
  54.6 6.2 %collective-permute-start.19 = (bf16[80,768]{1,0:T(8,128)(2,1)S(1)}, bf16[80,768]{1,0:T(8,128)(2,1)S(1)}, u32[]{:S(2)}, u32[]{:S(2)}) collective-permute-start(bf16[80,768]{1,0:T(8,128)(2,1)S(1)} %get-tuple-element.73), channel_id=1, source_target_pairs={{0,24},{4,28},{8,0},{12,4},{16,8},{20,12},{24,16},{28,20},{32,56},... | collective-permute-start | bytes 368648 | tf_op jit(solution)/shard_map/ppermute | solution.py:514

commit v16 on v14

--- a/solution.py
+++ b/solution.py
@@ -389,14 +389,15 @@
         ref[...] = resplit(mine_ref[rows].astype(F32) + other_ref[rows].astype(F32))[0].astype(BF)
 
 
-def y_kernel(y0, y1, y2, y3, o0, o1, o2, o3, order_ref, out_ref):
+def y_kernel(y0, y2, y1, y3, o0, o1, o2, o3, out_ref):
     total = y0[...].astype(F32) + y1[...].astype(F32) + y2[...].astype(F32) + y3[...].astype(F32)
-    total, loss = resplit(total)
-    out_ref[0:6] = nn(order_ref[...], total.astype(BF)).astype(BF).reshape(6, 16, D)
+    total, _ = resplit(total)
     out = o0[...].astype(F32) + o1[...].astype(F32) + o2[...].astype(F32) + o3[...].astype(F32)
-    tail = split_rows(jnp.broadcast_to(loss, (16, D)), (16, D), 12)
-    for half in range(2):
-        out_ref[6 + half] = (out[16 * half : 16 * (half + 1)] + tail).astype(BF)
+    tail = total[72:, 0:128]
+    for z in range(NZ):
+        rows = total[12 * z : 12 * (z + 1)] if z < 6 else out[16 * (z - 6) : 16 * (z - 6) + 12]
+        pieces = [rows[:, 128 * block : 128 * (block + 1)] for block in range(6)]
+        out_ref[z] = jnp.concatenate(pieces + [tail], 0).astype(BF)
 
 
 def out_core_kernel(mine_ref, other_ref, wait0, wait1, wait2, wait3, y0, y1, y2, y3):
@@ -419,8 +420,9 @@
     total = in_ref[0].astype(F32)
     for src in range(1, NZ):
         total = total + in_ref[src].astype(F32)
-    out_ref[...] = total[0:12]
-    loss_ref[...] = jnp.sum(total[12:15, 0:1], axis=0, keepdims=True)
+    for block in range(6):
+        out_ref[:, 128 * block : 128 * (block + 1)] = total[12 * block : 12 * (block + 1)]
+    loss_ref[...] = jnp.sum(total[72:75, 0:1], axis=0, keepdims=True)
 
 
 def spread_order():
@@ -452,16 +454,6 @@
         for half in range(2):
             for r in range(12):
                 place[j * 32 + half * 16 + r, j * 24 + half * 12 + r] = 1.0
-    return jnp.asarray(place, BF)
-
-
-def pad_order():
-    place = np.zeros((SUB, YROWS), np.float32)
-    for z in range(6):
-        for r in range(12):
-            place[z * 16 + r, z * 12 + r] = 1.0
-        for r in range(3):
-            place[z * 16 + 12 + r, 72 + r] = 1.0
     return jnp.asarray(place, BF)
 
 
@@ -596,8 +588,8 @@
     by_y = swap(by_y, "slide", Y_TURNS)
     (by_z,) = call(
         y_kernel,
-        [shape(NZ, 16, D)],
-        (by_y[0], by_y[2], by_y[1], by_y[3], *out, pad_order()),
+        [shape(NZ, 80, 128)],
+        (by_y[0], by_y[2], by_y[1], by_y[3], *out),
     )
     by_z = lax.all_to_all(by_z, "slide", 0, 0, tiled=True, axis_index_groups=Z_GROUPS)
     gradients, loss = call(z_kernel, [shape(12, D, dtype=F32), shape(1, 1, dtype=F32)], (by_z,))

time: 80.4 us -> 79.6 us (0.990)
  no operation moved by 1% of the time
where the time goes in v16:
time: 79.6 us; the launch traced here: 78.9 us
  starting transfers between devices  27.1 us (34%)
  blocking collectives  18 us (23%)
  waiting for transfers between devices  16.2 us (20%)
  Pallas kernels  14.7 us (18%)
  between operations  1.49 us (2%)
  local copies, waits for them, and re-layouts  1.29 us (2%)
    ppermute x18, starting transfers between devices, swap(): got = {t: lax.ppermute(arrays[t], axis, turns[t]) for t in order}  26.8 us
    all_to_all x1, blocking collectives, per_device(): lax.all_to_all(by_z, 'slide', 0, 0, tiled=True, axis_index_groups=Z_GROUPS)  18 us
    pallas_call x11, Pallas kernels, call(): pl.pallas_call(kernel, out_shape=out_shapes, in_specs=specs, out_specs=[V...  14.7 us
    ppermute x18, waiting for transfers between devices, swap(): got = {t: lax.ppermute(arrays[t], axis, turns[t]) for t in order}  14.4 us
    ppermute x1, waiting for transfers between devices, per_device(): other = lax.ppermute(other, 'slide', CORE_PAIRS)  1.85 us
  transfers between devices with their start and end apart: 20, of which 9 were waited for; matrix products, arithmetic and copies ran while one was open for 0% of the time, Pallas kernels for 11%

profile of v16, /device:TPU:2, one launch (start us, length us, event | category | flops | bytes accessed | tf_op | source)
XLA Modules:
  0.0 78.9 jit_solution(2218888185852884339)
XLA Ops:
  0.7 4.5 %shard_map.113 = (bf16[128,768]{1,0:T(8,128)(2,1)}, bf16[128,768]{1,0:T(8,128)(2,1)}, bf16[128,2304]{1,0:T(8,128)(2,1)}, bf16[32,1536]{1,0:T(8,128)(2,1)}) custom-call(bf16[1,128,1536]{2,1,0:T(8,128)(2,1)} %tiles_ref.1, s32[1,128]{1,0:T(1,128)} %masked_ref.1, f32[768]{0:T(1024)} %gain_hbm.1, bf16[1536,768]{1,0:T(8,128)(2,1)} %w_in_ref.1, ...), custom_call_target="tpu_custom_call" | custom-call | flops 4000000000 | bytes 4000000 | tf_op jit(solution)/shard_map/pallas_call | solution.py:470
  5.1 2.2 %collective-permute-start = (bf16[32,1536]{1,0:T(8,128)(2,1)}, bf16[32,1536]{1,0:T(8,128)(2,1)S(1)}, u32[]{:S(2)}, u32[]{:S(2)}) collective-permute-start(bf16[32,1536]{1,0:T(8,128)(2,1)} %get-tuple-element.40), channel_id=1, source_target_pairs={{0,2},{1,3},{2,0},{3,1},{4,6},{5,7},{6,4},{7,5},{8,10},{9,11},{10,... | collective-permute-start | bytes 294920 | tf_op jit(solution)/shard_map/ppermute | solution.py:506
  7.3 1.6 %collective-permute-start.1 = (bf16[32,1536]{1,0:T(8,128)(2,1)}, bf16[32,1536]{1,0:T(8,128)(2,1)S(1)}, u32[]{:S(2)}, u32[]{:S(2)}) collective-permute-start(bf16[32,1536]{1,0:T(8,128)(2,1)} %get-tuple-element.40), channel_id=1, source_target_pairs={{0,1},{1,2},{2,3},{3,0},{4,5},{5,6},{6,7},{7,4},{8,9},{9,10},{10,1... | collective-permute-start | bytes 294920 | tf_op jit(solution)/shard_map/ppermute | solution.py:506
  8.9 0.4 collective-permute-start.2
  9.4 1.6 %collective-permute-start.6 = (bf16[128,768]{1,0:T(8,128)(2,1)}, bf16[128,768]{1,0:T(8,128)(2,1)S(1)}, u32[]{:S(2)}, u32[]{:S(2)}) collective-permute-start(bf16[128,768]{1,0:T(8,128)(2,1)} %get-tuple-element.55.n0), channel_id=1, source_target_pairs={{0,1},{1,2},{2,3},{3,0},{4,5},{5,6},{6,7},{7,4},{8,9},{9,10},{10,1... | collective-permute-start | bytes 589832 | tf_op jit(solution)/shard_map/ppermute | solution.py:506
  11.0 1.0 %collective-permute-start.7 = (bf16[128,768]{1,0:T(8,128)(2,1)}, bf16[128,768]{1,0:T(8,128)(2,1)S(1)}, u32[]{:S(2)}, u32[]{:S(2)}) collective-permute-start(bf16[128,768]{1,0:T(8,128)(2,1)} %get-tuple-element.55.n0), channel_id=1, source_target_pairs={{0,3},{1,0},{2,1},{3,2},{4,7},{5,4},{6,5},{7,6},{8,11},{9,8},{10,9... | collective-permute-start | bytes 589832 | tf_op jit(solution)/shard_map/ppermute | solution.py:506
  12.7 2.2 %collective-permute-start.8 = (bf16[128,768]{1,0:T(8,128)(2,1)}, bf16[128,768]{1,0:T(8,128)(2,1)S(1)}, u32[]{:S(2)}, u32[]{:S(2)}) collective-permute-start(bf16[128,768]{1,0:T(8,128)(2,1)} %get-tuple-element.55.n0), channel_id=1, source_target_pairs={{0,2},{1,3},{2,0},{3,1},{4,6},{5,7},{6,4},{7,5},{8,10},{9,11},{10,... | collective-permute-start | bytes 589832 | tf_op jit(solution)/shard_map/ppermute | solution.py:506
  14.8 0.1 collective-permute-done.2.f3
  14.9 1.1 %copy-done.8 = bf16[128,2304]{1,0:T(8,128)(2,1)S(1)} copy-done((bf16[128,2304]{1,0:T(8,128)(2,1)S(1)}, bf16[128,2304]{1,0:T(8,128)(2,1)}, u32[]{:S(2)}) %copy-start.8) | copy-done | bytes 589848
  16.0 2.1 %shard_map.114 = (bf16[128,768]{1,0:T(8,128)(2,1)S(1)}, bf16[128,768]{1,0:T(8,128)(2,1)S(1)}, f32[4,128,512]{2,1,0:T(8,128)S(1)}, f32[4,128,128]{2,1,0:T(8,128)S...) custom-call(s32[1,1]{1,0:T(1,128)} %bitcast.2.count_ref, ...), custom_call_target="tpu_custom_call" | custom-call | flops 2000000000 | bytes 2000000 | tf_op jit(solution)/shard_map/pallas_call | solution.py:470
  18.1 0.2 copy-done.5
  18.3 0.0 copy-done.10
  18.3 2.7 %shard_map.115 = (bf16[128,768]{1,0:T(8,128)(2,1)S(1)}, bf16[16,128]{1,0:T(8,128)(2,1)S(1)}, bf16[384,768]{1,0:T(8,128)(2,1)S(1)}, bf16[384,768]{1,0:T(8,128)(2,1)S(1)}) custom-call(bf16[128,768]{1,0:T(8,128)(2,1)S(1)} %get-tuple-element.45.att_ref, bf16[128,768]{1,0:T(8,128)(2,1)S(1)} %copy-done.10, bf16[128,1536]{1,0:T(8,128)(2,1)S(1)} %get-tuple-element.47.tiles_ref, ...), custom_call_target="tpu_custom_call" | custom-call | flops 3000000000 | bytes 3000000 | tf_op jit(solution)/shard_map/pallas_call | solution.py:470
  21.0 0.3 collective-permute-start.9
  21.3 2.8 %shard_map.116 = (bf16[880,128]{1,0:T(8,128)(2,1)S(1)}, bf16[880,128]{1,0:T(8,128)(2,1)S(1)}, bf16[880,128]{1,0:T(8,128)(2,1)S(1)}, bf16[880,128]{1,0:T(8,128)(2,1)S(1)}) custom-call(bf16[128,2304]{1,0:T(8,128)(2,1)S(1)} %copy-done.9, bf16[128,768]{1,0:T(8,128)(2,1)S(1)} %get-tuple-element.41.fk_ref, bf16[128,768]{1,0:T(8,128)(2,1)S(1)} %get-tuple-element.42.fv_ref, ...), custom_call_target="tpu_custom_call" | custom-call | flops 8000000000 | bytes 8000000 | tf_op jit(solution)/shard_map/pallas_call | solution.py:470
  24.2 0.0 collective-permute-done.6.wait1.n1
  24.2 0.0 collective-permute-done.8.wait3.n2
  24.2 0.0 collective-permute-done.9.other_ref
  24.2 0.0 copy-start.7
  24.2 0.2 shard_map.117
  24.4 1.6 %collective-permute-start.10 = (bf16[96,768]{1,0:T(8,128)(2,1)S(1)}, bf16[96,768]{1,0:T(8,128)(2,1)S(1)}, u32[]{:S(2)}, u32[]{:S(2)}) collective-permute-start(bf16[96,768]{1,0:T(8,128)(2,1)S(1)} %get-tuple-element.59), channel_id=1, source_target_pairs={{0,8},{4,12},{8,16},{12,20},{16,24},{20,28},{24,0},{28,4},{32,40},... | collective-permute-start | bytes 442376 | tf_op jit(solution)/shard_map/ppermute | solution.py:506
  26.0 2.9 %collective-permute-start.11 = (bf16[96,768]{1,0:T(8,128)(2,1)S(1)}, bf16[96,768]{1,0:T(8,128)(2,1)S(1)}, u32[]{:S(2)}, u32[]{:S(2)}) collective-permute-start(bf16[96,768]{1,0:T(8,128)(2,1)S(1)} %get-tuple-element.60), channel_id=1, source_target_pairs={{0,16},{4,20},{8,24},{12,28},{16,0},{20,4},{24,8},{28,12},{32,48},... | collective-permute-start | bytes 442376 | tf_op jit(solution)/shard_map/ppermute | solution.py:506
  28.9 1.3 %collective-permute-start.12 = (bf16[96,768]{1,0:T(8,128)(2,1)S(1)}, bf16[96,768]{1,0:T(8,128)(2,1)S(1)}, u32[]{:S(2)}, u32[]{:S(2)}) collective-permute-start(bf16[96,768]{1,0:T(8,128)(2,1)S(1)} %get-tuple-element.61), channel_id=1, source_target_pairs={{0,24},{4,28},{8,0},{12,4},{16,8},{20,12},{24,16},{28,20},{32,56},... | collective-permute-start | bytes 442376 | tf_op jit(solution)/shard_map/ppermute | solution.py:506
  30.2 2.6 %collective-permute-start.3 = (bf16[880,128]{1,0:T(8,128)(2,1)S(1)}, bf16[880,128]{1,0:T(8,128)(2,1)S(1)}, u32[]{:S(2)}, u32[]{:S(2)}) collective-permute-start(bf16[880,128]{1,0:T(8,128)(2,1)S(1)} %get-tuple-element.52), channel_id=1, source_target_pairs={{0,1},{1,2},{2,3},{3,0},{4,5},{5,6},{6,7},{7,4},{8,9},{9,10},{10,1... | collective-permute-start | bytes 675848 | tf_op jit(solution)/shard_map/ppermute | solution.py:506
  32.9 0.8 collective-permute-start.4
  33.7 1.3 %collective-permute-start.5 = (bf16[880,128]{1,0:T(8,128)(2,1)S(1)}, bf16[880,128]{1,0:T(8,128)(2,1)S(1)}, u32[]{:S(2)}, u32[]{:S(2)}) collective-permute-start(bf16[880,128]{1,0:T(8,128)(2,1)S(1)} %get-tuple-element.54), channel_id=1, source_target_pairs={{0,3},{1,0},{2,1},{3,2},{4,7},{5,4},{6,5},{7,6},{8,11},{9,8},{10,9... | collective-permute-start | bytes 675848 | tf_op jit(solution)/shard_map/ppermute | solution.py:506
  35.0 1.3 %collective-permute-done.11.y2 = bf16[96,768]{1,0:T(8,128)(2,1)S(1)} collective-permute-done((bf16[96,768]{1,0:T(8,128)(2,1)S(1)}, bf16[96,768]{1,0:T(8,128)(2,1)S(1)}, u32[]{:S(2)}, u32[]{:S(2)}) %collective-permute-start.11) | collective-permute-done | bytes 147488 | tf_op jit(solution)/shard_map/ppermute | solution.py:506
  36.3 0.0 collective-permute-done.12.y3
  36.3 0.3 shard_map.118
  36.5 2.7 %collective-permute-start.13 = (bf16[32,768]{1,0:T(8,128)(2,1)S(1)}, bf16[32,768]{1,0:T(8,128)(2,1)S(1)}, u32[]{:S(2)}, u32[]{:S(2)}) collective-permute-start(bf16[32,768]{1,0:T(8,128)(2,1)S(1)} %get-tuple-element.65), channel_id=1, source_target_pairs={{0,1},{1,2},{2,3},{3,0},{4,5},{5,6},{6,7},{7,4},{8,9},{9,10},{10,1... | collective-permute-start | bytes 147464 | tf_op jit(solution)/shard_map/ppermute | solution.py:506
  39.3 0.8 collective-permute-start.14
  40.0 3.9 %collective-permute-done.3.x1 = bf16[880,128]{1,0:T(8,128)(2,1)S(1)} collective-permute-done((bf16[880,128]{1,0:T(8,128)(2,1)S(1)}, bf16[880,128]{1,0:T(8,128)(2,1)S(1)}, u32[]{:S(2)}, u32[]{:S(2)}) %collective-permute-start.3) | collective-permute-done | bytes 225312 | tf_op jit(solution)/shard_map/ppermute | solution.py:506
  43.9 2.1 %collective-permute-done.5.x3 = bf16[880,128]{1,0:T(8,128)(2,1)S(1)} collective-permute-done((bf16[880,128]{1,0:T(8,128)(2,1)S(1)}, bf16[880,128]{1,0:T(8,128)(2,1)S(1)}, u32[]{:S(2)}, u32[]{:S(2)}) %collective-permute-start.5) | collective-permute-done | bytes 225312 | tf_op jit(solution)/shard_map/ppermute | solution.py:506
  46.0 1.1 %shard_map.119 = (f32[576,768]{1,0:T(8,128)S(1)}, f32[80,768]{1,0:T(8,128)S(1)}) custom-call(bf16[880,128]{1,0:T(8,128)(2,1)S(1)} %get-tuple-element.51.wait0.x0, bf16[880,128]{1,0:T(8,128)(2,1)S(1)} %collective-permute-done.3.x1, bf16[880,128]{1,0:T(8,128)(2,1)S(1)} %collective-permute-done.4.x2, bf16[880,128]{1,0:T(8,128)(2,1)S(1)} %collective-permute-done.5.x3, ...), custom_call_target="tpu_custom_call" | custom-call | flops 15000000512 | bytes 15000000 | tf_op jit(solution)/shard_map/pallas_call | solution.py:470
  47.2 0.4 collective-permute-done.14.wait2.o2
  47.6 0.8 %collective-permute-done.15.wait3.o3 = bf16[32,768]{1,0:T(8,128)(2,1)S(1)} collective-permute-done((bf16[32,768]{1,0:T(8,128)(2,1)S(1)}, bf16[32,768]{1,0:T(8,128)(2,1)S(1)}, u32[]{:S(2)}, u32[]{:S(2)}) %collective-permute-start.15) | collective-permute-done | bytes 49184 | tf_op jit(solution)/shard_map/ppermute | solution.py:506
  48.4 0.1 shard_map.120
  48.5 0.1 collective-permute-start.16
  48.6 1.9 %collective-permute-done.16.other_ref = bf16[320,768]{1,0:T(8,128)(2,1)S(1)} collective-permute-done((bf16[320,768]{1,0:T(8,128)(2,1)S(1)}, bf16[320,768]{1,0:T(8,128)(2,1)S(1)}, u32[]{:S(2)}, u32[]{:S(2)}) %collective-permute-start.16) | collective-permute-done | bytes 491552 | tf_op jit(solution)/shard_map/ppermute | solution.py:586
  50.5 0.2 shard_map.121
  50.7 0.4 collective-permute-start.17
  51.0 0.5 collective-permute-start.18
  51.6 2.7 %collective-permute-start.19 = (bf16[80,768]{1,0:T(8,128)(2,1)S(1)}, bf16[80,768]{1,0:T(8,128)(2,1)S(1)}, u32[]{:S(2)}, u32[]{:S(2)}) collective-permute-start(bf16[80,768]{1,0:T(8,128)(2,1)S(1)} %get-tuple-element.73), channel_id=1, source_target_pairs={{0,24},{4,28},{8,0},{12,4},{16,8},{20,12},{24,16},{28,20},{32,56},... | collective-permute-start | bytes 368648 | tf_op jit(solution)/shard_map/ppermute | solution.py:506
  54.3 4.2 %collective-permute-done.17.y2 = bf16[80,768]{1,0:T(8,128)(2,1)S(1)} collective-permute-done((bf16[80,768]{1,0:T(8,128)(2,1)S(1)}, bf16[80,768]{1,0:T(8,128)(2,1)S(1)}, u32[]{:S(2)}, u32[]{:S(2)}) %collective-permute-start.17) | collective-permute-done | bytes 122912 | tf_op jit(solution)/shard_map/ppermute | solution.py:506
  58.5 1.6 %collective-permute-done.18.y1 = bf16[80,768]{1,0:T(8,128)(2,1)S(1)} collective-permute-done((bf16[80,768]{1,0:T(8,128)(2,1)S(1)}, bf16[80,768]{1,0:T(8,128)(2,1)S(1)}, u32[]{:S(2)}, u32[]{:S(2)}) %collective-permute-start.18) | collective-permute-done | bytes 122912 | tf_op jit(solution)/shard_map/ppermute | solution.py:506
  60.1 0.1 shard_map.122
  60.2 18.0 %all_to_all.5.in_ref = bf16[8,80,128]{2,1,0:T(8,128)(2,1)S(1)} all-to-all(bf16[8,80,128]{2,1,0:T(8,128)(2,1)S(1)} %shard_map.122), channel_id=1, replica_groups={{0,32,64,96,128,160,192,224},{4,36,68,100,132,164,196,228},{8,40,72,104..., dimensions={0} | all-to-all | bytes 327680 | tf_op jit(solution)/shard_map/all_to_all | solution.py:594
  78.2 0.6 shard_map.123
  (26 shorter events, 0.1 us)
Async XLA Ops:
  0.6 14.3 %copy-start.2 = (bf16[1,128,1536]{2,1,0:T(8,128)(2,1)S(1)}, bf16[1,128,1536]{2,1,0:T(8,128)(2,1)}, u32[]{:S(2)}) copy-start(bf16[1,128,1536]{2,1,0:T(8,128)(2,1)} %tiles_ref.1) | copy-start | bytes 1179652
  0.6 14.2 %copy-start.4 = (s32[1,128]{1,0:T(1,128)S(1)}, s32[1,128]{1,0:T(1,128)}, u32[]{:S(2)}) copy-start(s32[1,128]{1,0:T(1,128)} %masked_ref.1) | copy-start | bytes 1540
  5.1 7.5 %collective-permute-start = (bf16[32,1536]{1,0:T(8,128)(2,1)}, bf16[32,1536]{1,0:T(8,128)(2,1)S(1)}, u32[]{:S(2)}, u32[]{:S(2)}) collective-permute-start(bf16[32,1536]{1,0:T(8,128)(2,1)} %get-tuple-element.40), channel_id=1, source_target_pairs={{0,2},{1,3},{2,0},{3,1},{4,6},{5,7},{6,4},{7,5},{8,10},{9,11},{10,... | collective-permute-start | bytes 294920 | tf_op jit(solution)/shard_map/ppermute | solution.py:506
  7.3 7.5 %collective-permute-start.1 = (bf16[32,1536]{1,0:T(8,128)(2,1)}, bf16[32,1536]{1,0:T(8,128)(2,1)S(1)}, u32[]{:S(2)}, u32[]{:S(2)}) collective-permute-start(bf16[32,1536]{1,0:T(8,128)(2,1)} %get-tuple-element.40), channel_id=1, source_target_pairs={{0,1},{1,2},{2,3},{3,0},{4,5},{5,6},{6,7},{7,4},{8,9},{9,10},{10,1... | collective-permute-start | bytes 294920 | tf_op jit(solution)/shard_map/ppermute | solution.py:506
  8.9 5.9 %collective-permute-start.2 = (bf16[32,1536]{1,0:T(8,128)(2,1)}, bf16[32,1536]{1,0:T(8,128)(2,1)S(1)}, u32[]{:S(2)}, u32[]{:S(2)}) collective-permute-start(bf16[32,1536]{1,0:T(8,128)(2,1)} %get-tuple-element.40), channel_id=1, source_target_pairs={{0,3},{1,0},{2,1},{3,2},{4,7},{5,4},{6,5},{7,6},{8,11},{9,8},{10,9... | collective-permute-start | bytes 294920 | tf_op jit(solution)/shard_map/ppermute | solution.py:506
  9.4 14.8 %collective-permute-start.6 = (bf16[128,768]{1,0:T(8,128)(2,1)}, bf16[128,768]{1,0:T(8,128)(2,1)S(1)}, u32[]{:S(2)}, u32[]{:S(2)}) collective-permute-start(bf16[128,768]{1,0:T(8,128)(2,1)} %get-tuple-element.55.n0), channel_id=1, source_target_pairs={{0,1},{1,2},{2,3},{3,0},{4,5},{5,6},{6,7},{7,4},{8,9},{9,10},{10,1... | collective-permute-start | bytes 589832 | tf_op jit(solution)/shard_map/ppermute | solution.py:506
  11.0 13.2 %collective-permute-start.7 = (bf16[128,768]{1,0:T(8,128)(2,1)}, bf16[128,768]{1,0:T(8,128)(2,1)S(1)}, u32[]{:S(2)}, u32[]{:S(2)}) collective-permute-start(bf16[128,768]{1,0:T(8,128)(2,1)} %get-tuple-element.55.n0), channel_id=1, source_target_pairs={{0,3},{1,0},{2,1},{3,2},{4,7},{5,4},{6,5},{7,6},{8,11},{9,8},{10,9... | collective-permute-start | bytes 589832 | tf_op jit(solution)/shard_map/ppermute | solution.py:506
  12.7 11.5 %collective-permute-start.8 = (bf16[128,768]{1,0:T(8,128)(2,1)}, bf16[128,768]{1,0:T(8,128)(2,1)S(1)}, u32[]{:S(2)}, u32[]{:S(2)}) collective-permute-start(bf16[128,768]{1,0:T(8,128)(2,1)} %get-tuple-element.55.n0), channel_id=1, source_target_pairs={{0,2},{1,3},{2,0},{3,1},{4,6},{5,7},{6,4},{7,5},{8,10},{9,11},{10,... | collective-permute-start | bytes 589832 | tf_op jit(solution)/shard_map/ppermute | solution.py:506
  14.9 1.1 %copy-start.8 = (bf16[128,2304]{1,0:T(8,128)(2,1)S(1)}, bf16[128,2304]{1,0:T(8,128)(2,1)}, u32[]{:S(2)}) copy-start(bf16[128,2304]{1,0:T(8,128)(2,1)} %get-tuple-element.39.proj_ref) | copy-start | bytes 1769476
  16.0 2.1 %copy-start = (bf16[1536,768]{1,0:T(8,128)(2,1)S(1)}, bf16[1536,768]{1,0:T(8,128)(2,1)}, u32[]{:S(2)}) copy-start(bf16[1536,768]{1,0:T(8,128)(2,1)} %w_in_ref.1) | copy-start | bytes 7077892
  16.0 2.1 %copy-start.1 = (bf16[768,768]{1,0:T(8,128)(2,1)S(1)}, bf16[768,768]{1,0:T(8,128)(2,1)}, u32[]{:S(2)}) copy-start(bf16[768,768]{1,0:T(8,128)(2,1)} %w_out_ref.1) | copy-start | bytes 3538948
  16.0 2.3 %copy-start.5 = (bf16[768,768]{1,0:T(8,128)(2,1)S(1)}, bf16[768,768]{1,0:T(8,128)(2,1)}, u32[]{:S(2)}) copy-start(bf16[768,768]{1,0:T(8,128)(2,1)} %constant.6.clone.order_ref) | copy-start | bytes 3538948
  16.0 2.3 %copy-start.10 = (bf16[128,768]{1,0:T(8,128)(2,1)S(1)}, bf16[128,768]{1,0:T(8,128)(2,1)}, u32[]{:S(2)}) copy-start(bf16[128,768]{1,0:T(8,128)(2,1)} %get-tuple-element.46.hidden_ref) | copy-start | bytes 589828
  18.3 3.0 %copy-start.6 = (bf16[384,384]{1,0:T(8,128)(2,1)S(1)}, bf16[384,384]{1,0:T(8,128)(2,1)}, u32[]{:S(2)}) copy-start(bf16[384,384]{1,0:T(8,128)(2,1)} %constant.7.clone.spread_ref) | copy-start | bytes 884740
  18.3 3.0 %copy-start.9 = (bf16[128,2304]{1,0:T(8,128)(2,1)S(1)}, bf16[128,2304]{1,0:T(8,128)(2,1)}, u32[]{:S(2)}) copy-start(bf16[128,2304]{1,0:T(8,128)(2,1)} %get-tuple-element.39.proj_ref) | copy-start | bytes 1769476
  21.0 3.2 %collective-permute-start.9 = (bf16[384,768]{1,0:T(8,128)(2,1)S(1)}, bf16[384,768]{1,0:T(8,128)(2,1)S(1)}, u32[]{:S(2)}, u32[]{:S(2)}) collective-permute-start(bf16[384,768]{1,0:T(8,128)(2,1)S(1)} %get-tuple-element.57), channel_id=1, source_target_pairs={{0,4},{4,0},{8,12},{12,8},{16,20},{20,16},{24,28},{28,24},{32,36},... | collective-permute-start | bytes 1769480 | tf_op jit(solution)/shard_map/ppermute | solution.py:553
  24.2 12.0 %copy-start.7 = (bf16[128,96]{1,0:T(8,128)(2,1)S(1)}, bf16[128,96]{1,0:T(8,128)(2,1)}, u32[]{:S(2)}) copy-start(bf16[128,96]{1,0:T(8,128)(2,1)} %constant.8.clone.order_ref) | copy-start | bytes 73732
  24.4 9.3 %collective-permute-start.10 = (bf16[96,768]{1,0:T(8,128)(2,1)S(1)}, bf16[96,768]{1,0:T(8,128)(2,1)S(1)}, u32[]{:S(2)}, u32[]{:S(2)}) collective-permute-start(bf16[96,768]{1,0:T(8,128)(2,1)S(1)} %get-tuple-element.59), channel_id=1, source_target_pairs={{0,8},{4,12},{8,16},{12,20},{16,24},{20,28},{24,0},{28,4},{32,40},... | collective-permute-start | bytes 442376 | tf_op jit(solution)/shard_map/ppermute | solution.py:506
  26.0 10.3 %collective-permute-start.11 = (bf16[96,768]{1,0:T(8,128)(2,1)S(1)}, bf16[96,768]{1,0:T(8,128)(2,1)S(1)}, u32[]{:S(2)}, u32[]{:S(2)}) collective-permute-start(bf16[96,768]{1,0:T(8,128)(2,1)S(1)} %get-tuple-element.60), channel_id=1, source_target_pairs={{0,16},{4,20},{8,24},{12,28},{16,0},{20,4},{24,8},{28,12},{32,48},... | collective-permute-start | bytes 442376 | tf_op jit(solution)/shard_map/ppermute | solution.py:506
  28.9 7.4 %collective-permute-start.12 = (bf16[96,768]{1,0:T(8,128)(2,1)S(1)}, bf16[96,768]{1,0:T(8,128)(2,1)S(1)}, u32[]{:S(2)}, u32[]{:S(2)}) collective-permute-start(bf16[96,768]{1,0:T(8,128)(2,1)S(1)} %get-tuple-element.61), channel_id=1, source_target_pairs={{0,24},{4,28},{8,0},{12,4},{16,8},{20,12},{24,16},{28,20},{32,56},... | collective-permute-start | bytes 442376 | tf_op jit(solution)/shard_map/ppermute | solution.py:506
  30.2 13.7 %collective-permute-start.3 = (bf16[880,128]{1,0:T(8,128)(2,1)S(1)}, bf16[880,128]{1,0:T(8,128)(2,1)S(1)}, u32[]{:S(2)}, u32[]{:S(2)}) collective-permute-start(bf16[880,128]{1,0:T(8,128)(2,1)S(1)} %get-tuple-element.52), channel_id=1, source_target_pairs={{0,1},{1,2},{2,3},{3,0},{4,5},{5,6},{6,7},{7,4},{8,9},{9,10},{10,1... | collective-permute-start | bytes 675848 | tf_op jit(solution)/shard_map/ppermute | solution.py:506
  32.9 11.0 %collective-permute-start.4 = (bf16[880,128]{1,0:T(8,128)(2,1)S(1)}, bf16[880,128]{1,0:T(8,128)(2,1)S(1)}, u32[]{:S(2)}, u32[]{:S(2)}) collective-permute-start(bf16[880,128]{1,0:T(8,128)(2,1)S(1)} %get-tuple-element.53), channel_id=1, source_target_pairs={{0,2},{1,3},{2,0},{3,1},{4,6},{5,7},{6,4},{7,5},{8,10},{9,11},{10,... | collective-permute-start | bytes 675848 | tf_op jit(solution)/shard_map/ppermute | solution.py:506
  33.7 12.4 %collective-permute-start.5 = (bf16[880,128]{1,0:T(8,128)(2,1)S(1)}, bf16[880,128]{1,0:T(8,128)(2,1)S(1)}, u32[]{:S(2)}, u32[]{:S(2)}) collective-permute-start(bf16[880,128]{1,0:T(8,128)(2,1)S(1)} %get-tuple-element.54), channel_id=1, source_target_pairs={{0,3},{1,0},{2,1},{3,2},{4,7},{5,4},{6,5},{7,6},{8,11},{9,8},{10,9... | collective-permute-start | bytes 675848 | tf_op jit(solution)/shard_map/ppermute | solution.py:506
  36.3 9.8 %copy-start.3 = (bf16[128,768]{1,0:T(8,128)(2,1)S(1)}, bf16[128,768]{1,0:T(8,128)(2,1)}, u32[]{:S(2)}) copy-start(bf16[128,768]{1,0:T(8,128)(2,1)} %get-tuple-element.55.n0) | copy-start | bytes 589828
  36.5 10.6 %collective-permute-start.13 = (bf16[32,768]{1,0:T(8,128)(2,1)S(1)}, bf16[32,768]{1,0:T(8,128)(2,1)S(1)}, u32[]{:S(2)}, u32[]{:S(2)}) collective-permute-start(bf16[32,768]{1,0:T(8,128)(2,1)S(1)} %get-tuple-element.65), channel_id=1, source_target_pairs={{0,1},{1,2},{2,3},{3,0},{4,5},{5,6},{6,7},{7,4},{8,9},{9,10},{10,1... | collective-permute-start | bytes 147464 | tf_op jit(solution)/shard_map/ppermute | solution.py:506
  39.3 8.4 %collective-permute-start.14 = (bf16[32,768]{1,0:T(8,128)(2,1)S(1)}, bf16[32,768]{1,0:T(8,128)(2,1)S(1)}, u32[]{:S(2)}, u32[]{:S(2)}) collective-permute-start(bf16[32,768]{1,0:T(8,128)(2,1)S(1)} %get-tuple-element.66), channel_id=1, source_target_pairs={{0,2},{1,3},{2,0},{3,1},{4,6},{5,7},{6,4},{7,5},{8,10},{9,11},{10,... | collective-permute-start | bytes 147464 | tf_op jit(solution)/shard_map/ppermute | solution.py:506
  43.9 4.5 %collective-permute-start.15 = (bf16[32,768]{1,0:T(8,128)(2,1)S(1)}, bf16[32,768]{1,0:T(8,128)(2,1)S(1)}, u32[]{:S(2)}, u32[]{:S(2)}) collective-permute-start(bf16[32,768]{1,0:T(8,128)(2,1)S(1)} %get-tuple-element.67), channel_id=1, source_target_pairs={{0,3},{1,0},{2,1},{3,2},{4,7},{5,4},{6,5},{7,6},{8,11},{9,8},{10,9... | collective-permute-start | bytes 147464 | tf_op jit(solution)/shard_map/ppermute | solution.py:506
  48.5 2.0 %collective-permute-start.16 = (bf16[320,768]{1,0:T(8,128)(2,1)S(1)}, bf16[320,768]{1,0:T(8,128)(2,1)S(1)}, u32[]{:S(2)}, u32[]{:S(2)}) collective-permute-start(bf16[320,768]{1,0:T(8,128)(2,1)S(1)} %get-tuple-element.69), channel_id=1, source_target_pairs={{0,4},{4,0},{8,12},{12,8},{16,20},{20,16},{24,28},{28,24},{32,36},... | collective-permute-start | bytes 1474568 | tf_op jit(solution)/shard_map/ppermute | solution.py:586
  50.7 7.8 %collective-permute-start.17 = (bf16[80,768]{1,0:T(8,128)(2,1)S(1)}, bf16[80,768]{1,0:T(8,128)(2,1)S(1)}, u32[]{:S(2)}, u32[]{:S(2)}) collective-permute-start(bf16[80,768]{1,0:T(8,128)(2,1)S(1)} %get-tuple-element.71), channel_id=1, source_target_pairs={{0,16},{4,20},{8,24},{12,28},{16,0},{20,4},{24,8},{28,12},{32,48},... | collective-permute-start | bytes 368648 | tf_op jit(solution)/shard_map/ppermute | solution.py:506
  51.0 9.0 %collective-permute-start.18 = (bf16[80,768]{1,0:T(8,128)(2,1)S(1)}, bf16[80,768]{1,0:T(8,128)(2,1)S(1)}, u32[]{:S(2)}, u32[]{:S(2)}) collective-permute-start(bf16[80,768]{1,0:T(8,128)(2,1)S(1)} %get-tuple-element.72), channel_id=1, source_target_pairs={{0,8},{4,12},{8,16},{12,20},{16,24},{20,28},{24,0},{28,4},{32,40},... | collective-permute-start | bytes 368648 | tf_op jit(solution)/shard_map/ppermute | solution.py:506
  51.6 8.5 %collective-permute-start.19 = (bf16[80,768]{1,0:T(8,128)(2,1)S(1)}, bf16[80,768]{1,0:T(8,128)(2,1)S(1)}, u32[]{:S(2)}, u32[]{:S(2)}) collective-permute-start(bf16[80,768]{1,0:T(8,128)(2,1)S(1)} %get-tuple-element.73), channel_id=1, source_target_pairs={{0,24},{4,28},{8,0},{12,4},{16,8},{20,12},{24,16},{28,20},{32,56},... | collective-permute-start | bytes 368648 | tf_op jit(solution)/shard_map/ppermute | solution.py:506
